TPU v7x, 32 devices: a whole 2x2x4 slice. The times are simulated.
32 devices in a mesh: dp: 8 (over z, x), group: 4 (over y, core).
Axes of the slice: x: 2, y: 2, z: 4, core: 2. Of those that a mesh axis runs over, the one named last changes fastest.
Arguments:
- series_in: bfloat16 [73728, 512], P(('dp', 'group')), may hold values from -6 to 6
- block_kinds: int32 [384], P(('dp', 'group')), may hold values from 0 to 2, as said below
- out_grad: bfloat16 [73728, 512], P(('dp', 'group')), may hold values from -6 to 6
- fine_shrink: bfloat16 [6144, 512], P('dp'), may hold values from -0.078125 to 0.078125
- coarse_shrink: bfloat16 [8192, 512], P('dp'), may hold values from -0.0625 to 0.0625
- fine_isometric: bfloat16 [8192, 512], P('dp'), may hold values from -0.0625 to 0.0625
- coarse_isometric: bfloat16 [6144, 512], P('dp'), may hold values from -0.078125 to 0.078125
- fine_grow: bfloat16 [512, 6144], P('dp'), may hold values from -0.25 to 0.25
- coarse_grow: bfloat16 [512, 8192], P('dp'), may hold values from -0.25 to 0.25
- merge_weight: bfloat16 [1024, 512], P('dp'), may hold values from -0.1875 to 0.1875
- expand_weight: bfloat16 [512, 2048], P('dp'), may hold values from -0.25 to 0.25
- contract_weight: bfloat16 [2048, 512], P('dp'), may hold values from -0.125 to 0.125
- trend_weight: bfloat16 [512, 512], P('dp'), may hold values from -1.25 to 1.25
- branch_gain: bfloat16 [512], P('dp'), may hold values from 0.099609375 to 1.8984375
- middle_gain: bfloat16 [512], P('dp'), may hold values from 0.099609375 to 1.8984375
- output_gain: bfloat16 [512], P('dp'), may hold values from 0.099609375 to 1.8984375
Outputs:
- series_out: bfloat16 [73728, 512], P(('dp', 'group'))
- series_grad: bfloat16 [73728, 512], P(('dp', 'group'))
- fine_shrink_grad: float32 [6144, 512], P('dp')
- coarse_shrink_grad: float32 [8192, 512], P('dp')
- fine_isometric_grad: float32 [8192, 512], P('dp')
- coarse_isometric_grad: float32 [6144, 512], P('dp')
- fine_grow_grad: float32 [512, 6144], P('dp')
- coarse_grow_grad: float32 [512, 8192], P('dp')
- merge_grad: float32 [1024, 512], P('dp')
- expand_grad: float32 [512, 2048], P('dp')
- contract_grad: float32 [2048, 512], P('dp')
- trend_grad: float32 [512, 512], P('dp')
- branch_gain_grad: float32 [512], P('dp')
- middle_gain_grad: float32 [512], P('dp')
- output_gain_grad: float32 [512], P('dp')
Inputs may be any that keep to these rules, and one draw needn't show every extreme that they name: `block_kinds`: 0 starts an hourly series of one block, 1 starts a fifteen-minute series of four blocks, 2 continues the series of the block before; every aligned group of four blocks begins a series.
All inputs are finite; a program needn't handle non-finite values.
Results may differ from a plain program's by a relative error of at most 0.02.
Values may be sent and summed in bfloat16 or wider, within the bound.
No kernel may reach another device: no remote copies, remote signals or barrier semaphores. Data moves between devices by JAX's collectives and lax.ppermute only.
A program may use at most 320 MiB of HBM per device.

v0:
```python
import jax
import jax.numpy as jnp
from jax import lax
from jax.sharding import PartitionSpec as P

S1 = 12
S2 = 16
WINDOW = 25


def layer_norm(values, gain):
    center = jnp.mean(values, axis=-1, keepdims=True)
    centered = values - center
    spread = jnp.mean(centered * centered, axis=-1, keepdims=True)
    return centered * lax.rsqrt(spread + 1e-05) * gain


def exact_gelu(values):
    return jax.nn.gelu(values, approximate=False)


def previous_block(blocks, follows):
    earlier = jnp.concatenate([jnp.zeros_like(blocks[:1]), blocks[:-1]], axis=0)
    return earlier * follows.astype(blocks.dtype)[:, None, None]


def moving_average(blocks, follows):
    half_window = WINDOW // 2
    block_len = blocks.shape[1]
    leading = jnp.concatenate([follows[1:], jnp.zeros_like(follows[:1])])
    before_rim = (
        previous_block(blocks, follows)[:, block_len - half_window :]
        + (1.0 - follows)[:, None, None] * blocks[:, :1]
    )
    following = (
        jnp.concatenate([blocks[1:], jnp.zeros_like(blocks[:1])], axis=0) * leading[:, None, None]
    )
    after_rim = (
        following[:, :half_window] + (1.0 - leading)[:, None, None] * blocks[:, block_len - 1 :]
    )
    padded = jnp.concatenate([before_rim, blocks, after_rim], axis=1)
    running = padded[:, 0:block_len]
    for offset in range(1, WINDOW):
        running = running + padded[:, offset : offset + block_len]
    return running / WINDOW


def unfold(lowered, follows):
    positions = lowered.shape[1]
    extended = jnp.concatenate([previous_block(lowered, follows), lowered], axis=1)
    return jnp.concatenate(
        [extended[:, 1 + offset : 1 + offset + positions] for offset in range(positions)], axis=2
    )


def plain_dot(left, right):
    return jnp.dot(left, right, preferred_element_type=jnp.float32)


def weight_dot(inputs, grads):
    return lax.dot_general(
        inputs, grads, (((0,), (0,)), ((), ())), preferred_element_type=jnp.float32
    )


def back_dot(grads, weight):
    return lax.dot_general(
        grads, weight, (((1,), (1,)), ((), ())), preferred_element_type=jnp.float32
    )


def keep_local(item):
    return item


def branch_forward(season_low, season, follows, shrink, isometric, grow, gain, stride):
    block_count, block_len, feature_width = season.shape
    positions = block_len // stride
    shrink_rows = season_low.reshape(block_count * positions, stride * feature_width)
    shrunk = jnp.tanh(plain_dot(shrink_rows, shrink))
    shrunk_low = shrunk.astype(jnp.bfloat16).reshape(block_count, positions, feature_width)
    stacked = unfold(shrunk_low, follows).reshape(
        block_count * positions, positions * feature_width
    )
    isolocal = jnp.tanh(plain_dot(stacked, isometric))
    mixed_out, mixed_pull = jax.vjp(layer_norm, isolocal + shrunk, gain)
    mixed_low = mixed_out.astype(jnp.bfloat16)
    upward = jnp.tanh(plain_dot(mixed_low, grow)).reshape(block_count, block_len, feature_width)
    result, result_pull = jax.vjp(layer_norm, upward + season, gain)
    saved = (
        shrink_rows,
        shrunk,
        shrunk_low,
        stacked,
        isolocal,
        mixed_pull,
        mixed_low,
        upward,
        result_pull,
    )
    return (result, saved)


def branch_backward(saved, result_grad, follows, shrink, isometric, grow, stride, settle):
    (
        shrink_rows,
        shrunk,
        shrunk_low,
        stacked,
        isolocal,
        mixed_pull,
        mixed_low,
        upward,
        result_pull,
    ) = saved
    block_count, block_len, feature_width = result_grad.shape
    positions = block_len // stride
    summed, gain_first = result_pull(result_grad)
    grow_pre = (
        (summed * (1.0 - upward * upward))
        .reshape(block_count * positions, stride * feature_width)
        .astype(jnp.bfloat16)
    )
    grow_grad = settle(weight_dot(mixed_low, grow_pre))
    mixed_back = back_dot(grow_pre, grow)
    joint_grad, gain_second = mixed_pull(mixed_back)
    iso_pre = (joint_grad * (1.0 - isolocal * isolocal)).astype(jnp.bfloat16)
    isometric_grad = settle(weight_dot(stacked, iso_pre))
    stack_back = back_dot(iso_pre, isometric).reshape(
        block_count, positions, positions * feature_width
    )
    ignored, unfold_pull = jax.vjp(
        lambda values: unfold(values, follows), shrunk_low.astype(jnp.float32)
    )
    (shrunk_back,) = unfold_pull(stack_back)
    shrunk_total = shrunk_back.reshape(block_count * positions, feature_width) + joint_grad
    shrink_pre = (shrunk_total * (1.0 - shrunk * shrunk)).astype(jnp.bfloat16)
    shrink_grad = settle(weight_dot(shrink_rows, shrink_pre))
    season_back = (
        back_dot(shrink_pre, shrink).reshape(block_count, block_len, feature_width) + summed
    )
    return (season_back, shrink_grad, isometric_grad, grow_grad, gain_first + gain_second)


def on_device(
    series_in,
    block_kinds,
    out_grad,
    fine_shrink,
    coarse_shrink,
    fine_isometric,
    coarse_isometric,
    fine_grow,
    coarse_grow,
    merge_weight,
    expand_weight,
    contract_weight,
    trend_weight,
    branch_gain,
    middle_gain,
    output_gain,
):
    whole = (
        lax.all_gather(fine_shrink, "dp", axis=0, tiled=True),
        lax.all_gather(coarse_shrink, "dp", axis=0, tiled=True),
        lax.all_gather(fine_isometric, "dp", axis=0, tiled=True),
        lax.all_gather(coarse_isometric, "dp", axis=0, tiled=True),
        lax.all_gather(fine_grow, "dp", axis=0, tiled=True),
        lax.all_gather(coarse_grow, "dp", axis=0, tiled=True),
        lax.all_gather(merge_weight, "dp", axis=0, tiled=True),
        lax.all_gather(expand_weight, "dp", axis=0, tiled=True),
        lax.all_gather(contract_weight, "dp", axis=0, tiled=True),
        lax.all_gather(trend_weight, "dp", axis=0, tiled=True),
        lax.all_gather(branch_gain, "dp", axis=0, tiled=True),
        lax.all_gather(middle_gain, "dp", axis=0, tiled=True),
        lax.all_gather(output_gain, "dp", axis=0, tiled=True),
    )
    (
        f_shrink,
        c_shrink,
        f_iso,
        c_iso,
        f_grow,
        c_grow,
        merge_full,
        expand_full,
        contract_full,
        trend_full,
    ) = whole[:10]
    gain_branch = whole[10].astype(jnp.float32)
    gain_middle = whole[11].astype(jnp.float32)
    gain_output = whole[12].astype(jnp.float32)
    block_count = block_kinds.shape[0]
    feature_width = series_in.shape[1]
    block_len = series_in.shape[0] // block_count
    follows = (block_kinds == 2).astype(jnp.float32)
    blocks = series_in.astype(jnp.float32).reshape(block_count, block_len, feature_width)
    trend, average_pull = jax.vjp(lambda values: moving_average(values, follows), blocks)
    season = blocks - trend
    season_low = season.astype(jnp.bfloat16)
    fine_out, fine_saved = branch_forward(
        season_low, season, follows, f_shrink, f_iso, f_grow, gain_branch, S1
    )
    coarse_out, coarse_saved = branch_forward(
        season_low, season, follows, c_shrink, c_iso, c_grow, gain_branch, S2
    )
    joined = (
        jnp.concatenate([fine_out, coarse_out], axis=2)
        .astype(jnp.bfloat16)
        .reshape(-1, 2 * feature_width)
    )
    merged = plain_dot(joined, merge_full)
    middle, middle_pull = jax.vjp(layer_norm, merged, gain_middle)
    middle_low = middle.astype(jnp.bfloat16)
    hidden, gelu_pull = jax.vjp(exact_gelu, plain_dot(middle_low, expand_full))
    hidden_low = hidden.astype(jnp.bfloat16)
    lifted = plain_dot(hidden_low, contract_full)
    seasonal, output_pull = jax.vjp(layer_norm, middle + lifted, gain_output)
    trend_low = trend.reshape(-1, feature_width).astype(jnp.bfloat16)
    projected = plain_dot(trend_low, trend_full)
    series_out = (seasonal + projected).astype(jnp.bfloat16)
    trend_weight_grad = keep_local(weight_dot(trend_low, out_grad))
    trend_back = back_dot(out_grad, trend_full)
    summed_grad, output_gain_raw = output_pull(out_grad.astype(jnp.float32))
    output_gain_grad = keep_local(output_gain_raw)
    lifted_low = summed_grad.astype(jnp.bfloat16)
    contract_grad = keep_local(weight_dot(hidden_low, lifted_low))
    (hidden_pre_grad,) = gelu_pull(back_dot(lifted_low, contract_full))
    hidden_grad_low = hidden_pre_grad.astype(jnp.bfloat16)
    expand_grad = keep_local(weight_dot(middle_low, hidden_grad_low))
    middle_back = summed_grad + back_dot(hidden_grad_low, expand_full)
    merged_grad, middle_gain_raw = middle_pull(middle_back)
    middle_gain_grad = keep_local(middle_gain_raw)
    merged_low = merged_grad.astype(jnp.bfloat16)
    merge_grad = keep_local(weight_dot(joined, merged_low))
    joined_back = back_dot(merged_low, merge_full).reshape(
        block_count, block_len, 2 * feature_width
    )
    fine_season, fine_shrink_g, fine_iso_g, fine_grow_g, fine_gain_g = branch_backward(
        fine_saved,
        joined_back[:, :, :feature_width],
        follows,
        f_shrink,
        f_iso,
        f_grow,
        S1,
        keep_local,
    )
    coarse_season, coarse_shrink_g, coarse_iso_g, coarse_grow_g, coarse_gain_g = branch_backward(
        coarse_saved,
        joined_back[:, :, feature_width:],
        follows,
        c_shrink,
        c_iso,
        c_grow,
        S2,
        keep_local,
    )
    branch_gain_grad = keep_local(fine_gain_g + coarse_gain_g)
    season_grad = fine_season + coarse_season
    trend_total = trend_back.reshape(block_count, block_len, feature_width) - season_grad
    (averaged,) = average_pull(trend_total)
    series_grad = (season_grad + averaged).reshape(-1, feature_width).astype(jnp.bfloat16)
    grads = (
        fine_shrink_g,
        coarse_shrink_g,
        fine_iso_g,
        coarse_iso_g,
        fine_grow_g,
        coarse_grow_g,
        merge_grad,
        expand_grad,
        contract_grad,
        trend_weight_grad,
        branch_gain_grad,
        middle_gain_grad,
        output_gain_grad,
    )
    shares = (
        lax.psum_scatter(
            grads[0].astype(jnp.bfloat16), "dp", scatter_dimension=0, tiled=True
        ).astype(jnp.float32),
        lax.psum_scatter(
            grads[1].astype(jnp.bfloat16), "dp", scatter_dimension=0, tiled=True
        ).astype(jnp.float32),
        lax.psum_scatter(
            grads[2].astype(jnp.bfloat16), "dp", scatter_dimension=0, tiled=True
        ).astype(jnp.float32),
        lax.psum_scatter(
            grads[3].astype(jnp.bfloat16), "dp", scatter_dimension=0, tiled=True
        ).astype(jnp.float32),
        lax.psum_scatter(
            grads[4].astype(jnp.bfloat16), "dp", scatter_dimension=0, tiled=True
        ).astype(jnp.float32),
        lax.psum_scatter(
            grads[5].astype(jnp.bfloat16), "dp", scatter_dimension=0, tiled=True
        ).astype(jnp.float32),
        lax.psum_scatter(
            grads[6].astype(jnp.bfloat16), "dp", scatter_dimension=0, tiled=True
        ).astype(jnp.float32),
        lax.psum_scatter(
            grads[7].astype(jnp.bfloat16), "dp", scatter_dimension=0, tiled=True
        ).astype(jnp.float32),
        lax.psum_scatter(
            grads[8].astype(jnp.bfloat16), "dp", scatter_dimension=0, tiled=True
        ).astype(jnp.float32),
        lax.psum_scatter(
            grads[9].astype(jnp.bfloat16), "dp", scatter_dimension=0, tiled=True
        ).astype(jnp.float32),
        lax.psum_scatter(
            grads[10].astype(jnp.bfloat16), "dp", scatter_dimension=0, tiled=True
        ).astype(jnp.float32),
        lax.psum_scatter(
            grads[11].astype(jnp.bfloat16), "dp", scatter_dimension=0, tiled=True
        ).astype(jnp.float32),
        lax.psum_scatter(
            grads[12].astype(jnp.bfloat16), "dp", scatter_dimension=0, tiled=True
        ).astype(jnp.float32),
    )
    shares = (
        lax.psum(shares[0].astype(jnp.bfloat16), "group").astype(jnp.float32),
        lax.psum(shares[1].astype(jnp.bfloat16), "group").astype(jnp.float32),
        lax.psum(shares[2].astype(jnp.bfloat16), "group").astype(jnp.float32),
        lax.psum(shares[3].astype(jnp.bfloat16), "group").astype(jnp.float32),
        lax.psum(shares[4].astype(jnp.bfloat16), "group").astype(jnp.float32),
        lax.psum(shares[5].astype(jnp.bfloat16), "group").astype(jnp.float32),
        lax.psum(shares[6].astype(jnp.bfloat16), "group").astype(jnp.float32),
        lax.psum(shares[7].astype(jnp.bfloat16), "group").astype(jnp.float32),
        lax.psum(shares[8].astype(jnp.bfloat16), "group").astype(jnp.float32),
        lax.psum(shares[9].astype(jnp.bfloat16), "group").astype(jnp.float32),
        lax.psum(shares[10].astype(jnp.bfloat16), "group").astype(jnp.float32),
        lax.psum(shares[11].astype(jnp.bfloat16), "group").astype(jnp.float32),
        lax.psum(shares[12].astype(jnp.bfloat16), "group").astype(jnp.float32),
    )
    return (
        series_out,
        series_grad,
        shares[0],
        shares[1],
        shares[2],
        shares[3],
        shares[4],
        shares[5],
        shares[6],
        shares[7],
        shares[8],
        shares[9],
        shares[10],
        shares[11],
        shares[12],
    )


def solution(mesh):
    return jax.shard_map(
        on_device,
        mesh=mesh,
        in_specs=(
            P(("dp", "group"), None),
            P(("dp", "group")),
            P(("dp", "group"), None),
            P("dp", None),
            P("dp", None),
            P("dp", None),
            P("dp", None),
            P("dp", None),
            P("dp", None),
            P("dp", None),
            P("dp", None),
            P("dp", None),
            P("dp", None),
            P("dp"),
            P("dp"),
            P("dp"),
        ),
        out_specs=(
            P(("dp", "group"), None),
            P(("dp", "group"), None),
            P("dp", None),
            P("dp", None),
            P("dp", None),
            P("dp", None),
            P("dp", None),
            P("dp", None),
            P("dp", None),
            P("dp", None),
            P("dp", None),
            P("dp", None),
            P("dp"),
            P("dp"),
            P("dp"),
        ),
        check_vma=False,
    )
```

profile of v0, /device:TPU:0, one launch (start us, length us, event | category | flops | bytes accessed | tf_op | source)
XLA Modules:
  0.0 2062.1 jit_solution(10966191787939402608)
XLA Ops:
  16.3 14.8 fusion.116
  38.8 5.9 reshape.366
  51.1 23.9 %all-reduce.72 = (bf16[512]{0:T(512)(128)(2,1)S(1)}, bf16[512]{0:T(512)(128)(2,1)S(1)}, bf16[512]{0:T(512)(128)(2,1)S(1)}) all-reduce(bf16[512]{0:T(512)(128)(2,1)S(1)} %dynamic-update-slice, bf16[512]{0:T(512)(128)(2,1)S(1)} %dynamic-update-slice.1, bf16[512]{0:T(512)(128)(2,1)S(1)} %dynamic-update-slice.2), channel_id=1, replica_groups=mesh['dp'=8,'group'=4] {'dp'}, use_global_device_ids=true, to_apply=%add.65 | all-reduce | flops 1536 | bytes 6144
  75.6 37.1 %all-gather.10.cloned.1.call-done = bf16[6144,512]{1,0:T(8,128)(2,1)} async-done(((bf16[768,512]{1,0:T(8,128)(2,1)}), bf16[6144,512]{1,0:T(8,128)(2,1)}) %all-gather.10.cloned.1.call-update) | async-done | bytes 6291472 | tf_op jit(solution)/shard_map/all_gather | solution.py:164
  112.6 5.6 fusion.122
  130.8 107.1 %all-gather.16.cloned.1.call-done = bf16[8192,512]{1,0:T(8,128)(2,1)} async-done(((bf16[1024,512]{1,0:T(8,128)(2,1)}), bf16[8192,512]{1,0:T(8,128)(2,1)}) %all-gather.16.cloned.1.call-update) | async-done | bytes 8388624 | tf_op jit(solution)/shard_map/all_gather | solution.py:165
  254.2 83.1 %all-gather.18.cloned.1.call-done = bf16[6144,512]{1,0:T(8,128)(2,1)} async-done(((bf16[768,512]{1,0:T(8,128)(2,1)}), bf16[6144,512]{1,0:T(8,128)(2,1)}) %all-gather.18.cloned.1.call-update) | async-done | bytes 6291472 | tf_op jit(solution)/shard_map/all_gather | solution.py:167
  342.1 120.3 %all-gather.20.cloned.1.call-done = bf16[512,8192]{1,0:T(8,128)(2,1)} async-done(((bf16[64,8192]{1,0:T(8,128)(2,1)}), bf16[512,8192]{1,0:T(8,128)(2,1)}) %all-gather.20.cloned.1.call-update) | async-done | bytes 8388624 | tf_op jit(solution)/shard_map/all_gather | solution.py:169
  462.4 7.0 convolution_tanh_fusion
  469.4 6.3 reshape.371
  475.7 111.8 %all-gather.12.cloned.1.call-done = bf16[8192,512]{1,0:T(8,128)(2,1)} async-done(((bf16[1024,512]{1,0:T(8,128)(2,1)}), bf16[8192,512]{1,0:T(8,128)(2,1)}) %all-gather.12.cloned.1.call-update) | async-done | bytes 8388624 | tf_op jit(solution)/shard_map/all_gather | solution.py:166
  587.6 6.9 fusion.113
  594.7 92.1 %all-gather.14.cloned.1.call-done = bf16[512,6144]{1,0:T(8,128)(2,1)} async-done(((bf16[64,6144]{1,0:T(8,128)(2,1)}), bf16[512,6144]{1,0:T(8,128)(2,1)}) %all-gather.14.cloned.1.call-update) | async-done | bytes 6291472 | tf_op jit(solution)/shard_map/all_gather | solution.py:168
  686.8 6.4 convolution_tanh_fusion.1
  693.2 6.0 reshape.368
  699.3 8.2 fusion.112
  717.5 9.9 all-gather.22.cloned.1.call-done
  735.8 41.7 %all-gather.24.cloned.1.call-done = bf16[512,2048]{1,0:T(8,128)(2,1)} async-done(((bf16[64,2048]{1,0:T(8,128)(2,1)}), bf16[512,2048]{1,0:T(8,128)(2,1)}) %all-gather.24.cloned.1.call-update) | async-done | bytes 2097168 | tf_op jit(solution)/shard_map/all_gather | solution.py:171
  777.5 50.1 %multiply_convert_fusion = (bf16[2304,2048]{1,0:T(8,128)(2,1)}, f32[2304,2048]{1,0:T(8,128)}, f32[2304,2048]{1,0:T(8,128)}) fusion(bf16[512,2048]{1,0:T(8,128)(2,1)} %all-gather.24.cloned.1.call-done, f32[2304,512]{0,1:T(8,128)} %copy-done.10, f32[512]{0:T(512)S(1)} %convert_element_type.206, f32[2304]{0:T(1024)S(1)} %fusion.97, ...), kind=kOutput, calls=%fused_computation.25 | convolution fusion | flops 5143265280 | bytes 54022144 | tf_op jit(solution)/shard_map/dot_general | solution.py:57
  827.7 11.0 fusion.125
  842.6 24.6 %add_convert_fusion = bf16[2304,2048]{1,0:T(8,128)(2,1)} fusion(f32[2304,2048]{1,0:T(8,128)} %get-tuple-element.95, f32[2304,2048]{1,0:T(8,128)} %get-tuple-element.189, bf16[2048,512]{1,0:T(8,128)(2,1)} %all-gather.26.cloned.1.call-done, f32[2304]{0:T(1024)S(1)} %negate_multiply_fusion.4, bf16[2304,512]{0,1:T(8,128)(2,1)S(1)} %copy-done.6, ...), kind=kOutput, calls=%fused_computation.24 | convolution fusion | flops 4908515328 | bytes 56399872 | tf_op jit(solution)/shard_map/dot_general | solution.py:67
  867.2 13.6 multiply_reduce_fusion
  890.5 11.8 convolution_convert_fusion.6
  902.4 10.8 convolution_convert_fusion.7
  918.5 6.9 multiply_reduce_fusion.1
  925.4 8.6 fusion.107
  956.1 7.2 multiply_reduce_fusion.13
  969.9 6.4 multiply_reduce_fusion.10
  976.7 6.3 fusion.126
  990.8 5.8 convolution_convert_fusion
  996.8 7.6 convolution_convert_fusion.1
  1018.5 5.7 convolution_convert_fusion.2
  1025.1 32.2 %all_gather.51 = bf16[512,512]{1,0:T(8,128)(2,1)S(1)} all-gather(bf16[64,512]{1,0:T(8,128)(2,1)S(1)} %copy-done.61), channel_id=1, replica_groups=mesh['dp'=8,'group'=4] {'dp'}, dimensions={0}, use_global_device_ids=true | all-gather | bytes 589824 | tf_op jit(solution)/shard_map/all_gather | solution.py:173
  1061.0 19.2 all-reduce.71
  1080.5 5.9 all-reduce.73
  1087.9 7.1 fusion.127
  1095.0 5.6 reshape.375
  1100.6 8.4 fusion.129
  1109.0 6.3 reshape.378
  1125.1 12.7 subtract_multiply_fusion
  1137.9 83.7 %reduce-scatter.19.cloned.1.call-done = bf16[64,6144]{1,0:T(8,128)(2,1)} async-done(((bf16[512,6144]{1,0:T(8,128)(2,1)}), bf16[64,6144]{1,0:T(8,128)(2,1)}) %reduce-scatter.19.cloned.1.call-update) | async-done | bytes 786448 | tf_op jit(solution)/shard_map/reduce_scatter | solution.py:292
  1221.6 120.6 %reduce-scatter.17.cloned.1.call-done = bf16[768,512]{1,0:T(8,128)(2,1)} async-done(((bf16[6144,512]{1,0:T(8,128)(2,1)}), bf16[768,512]{1,0:T(8,128)(2,1)}) %reduce-scatter.17.cloned.1.call-update) | async-done | bytes 786448 | tf_op jit(solution)/shard_map/reduce_scatter | solution.py:289
  1342.2 120.6 %reduce-scatter.11.cloned.1.call-done = bf16[768,512]{1,0:T(8,128)(2,1)} async-done(((bf16[6144,512]{1,0:T(8,128)(2,1)}), bf16[768,512]{1,0:T(8,128)(2,1)}) %reduce-scatter.11.cloned.1.call-update) | async-done | bytes 786448 | tf_op jit(solution)/shard_map/reduce_scatter | solution.py:280
  1462.7 151.6 %reduce-scatter.21.cloned.1.call-done = bf16[64,8192]{1,0:T(8,128)(2,1)} async-done(((bf16[512,8192]{1,0:T(8,128)(2,1)}), bf16[64,8192]{1,0:T(8,128)(2,1)}) %reduce-scatter.21.cloned.1.call-update) | async-done | bytes 1048592 | tf_op jit(solution)/shard_map/reduce_scatter | solution.py:295
  1614.4 152.0 %reduce-scatter.15.cloned.1.call-done = bf16[1024,512]{1,0:T(8,128)(2,1)} async-done(((bf16[8192,512]{1,0:T(8,128)(2,1)}), bf16[1024,512]{1,0:T(8,128)(2,1)}) %reduce-scatter.15.cloned.1.call-update) | async-done | bytes 1048592 | tf_op jit(solution)/shard_map/reduce_scatter | solution.py:286
  1766.4 151.6 %reduce-scatter.13.cloned.1.call-done = bf16[1024,512]{1,0:T(8,128)(2,1)} async-done(((bf16[8192,512]{1,0:T(8,128)(2,1)}), bf16[1024,512]{1,0:T(8,128)(2,1)}) %reduce-scatter.13.cloned.1.call-update) | async-done | bytes 1048592 | tf_op jit(solution)/shard_map/reduce_scatter | solution.py:283
  1918.0 60.3 %pad_add_fusion = f32[12,216,512]{2,1,0:T(8,128)S(1)} fusion(f32[12,192,512]{2,1,0:T(8,128)} %get-tuple-element.82), kind=kLoop, calls=%fused_computation.55 | loop fusion | flops 31850496 | bytes 10027008 | tf_op jit(solution)/shard_map/transpose(jvp())/add_any | solution.py:42
  1984.6 55.8 %all-reduce.77.cloned.1.call-done = (bf16[768,512]{1,0:T(8,128)(2,1)}, bf16[1024,512]{1,0:T(8,128)(2,1)}, bf16[1024,512]{1,0:T(8,128)(2,1)}, bf16[768,512]{1,0:T...) async-done(((bf16[768,512]{1,0:T(8,128)(2,1)}, ...) | async-done | bytes 6225936 | tf_op jit(solution)/shard_map/psum | solution.py:321
  (422 shorter events, 179.9 us)
Async XLA Ops:
  7.2 105.4 %all-gather.10.cloned.1.call-start = ((), (), s32[]{:S(2)}) async-start(), calls=%async_computation.10 | async-start | bytes 7077888 | tf_op jit(solution)/shard_map/all_gather | solution.py:164
  7.9 229.9 %all-gather.16.cloned.1.call-start = ((), (), s32[]{:S(2)}) async-start(), calls=%async_computation.13 | async-start | bytes 9437184 | tf_op jit(solution)/shard_map/all_gather | solution.py:165
  8.7 328.6 %all-gather.18.cloned.1.call-start = ((), (), s32[]{:S(2)}) async-start(), calls=%async_computation.14 | async-start | bytes 7077888 | tf_op jit(solution)/shard_map/all_gather | solution.py:167
  9.4 453.0 %all-gather.20.cloned.1.call-start = ((), (), s32[]{:S(2)}) async-start(), calls=%async_computation.15 | async-start | bytes 9437184 | tf_op jit(solution)/shard_map/all_gather | solution.py:169
  10.0 577.6 %all-gather.12.cloned.1.call-start = ((), (), s32[]{:S(2)}) async-start(), calls=%async_computation.11 | async-start | bytes 9437184 | tf_op jit(solution)/shard_map/all_gather | solution.py:166
  10.6 676.2 %all-gather.14.cloned.1.call-start = ((), (), s32[]{:S(2)}) async-start(), calls=%async_computation.12 | async-start | bytes 7077888 | tf_op jit(solution)/shard_map/all_gather | solution.py:168
  11.2 716.2 %all-gather.22.cloned.1.call-start = ((), (), s32[]{:S(2)}) async-start(), calls=%async_computation.16 | async-start | bytes 1179648 | tf_op jit(solution)/shard_map/all_gather | solution.py:170
  11.9 765.6 %all-gather.24.cloned.1.call-start = ((), (), s32[]{:S(2)}) async-start(), calls=%async_computation.17 | async-start | bytes 2359296 | tf_op jit(solution)/shard_map/all_gather | solution.py:171
  12.7 815.0 %all-gather.26.cloned.1.call-start = ((), (), s32[]{:S(2)}) async-start(), calls=%async_computation.18 | async-start | bytes 2359296 | tf_op jit(solution)/shard_map/all_gather | solution.py:172
  13.4 1124.4 %reduce-scatter.29.cloned.1.call-start = ((), (), s32[]{:S(2)}) async-start(), calls=%async_computation.28 | async-start | bytes 589824 | tf_op jit(solution)/shard_map/reduce_scatter | solution.py:307
  16.3 14.8 copy-start.12
  35.0 1102.8 %reduce-scatter.23.cloned.1.call-start = ((), (), s32[]{:S(2)}) async-start(), calls=%async_computation.25 | async-start | bytes 1179648 | tf_op jit(solution)/shard_map/reduce_scatter | solution.py:298
  38.8 199.1 %copy-start.4 = (bf16[144,8192]{1,0:T(8,128)(2,1)}, bf16[144,8192]{1,0:T(8,128)(2,1)S(1)}, u32[]{:S(2)}) copy-start(bf16[144,8192]{1,0:T(8,128)(2,1)S(1)} %reshape.369) | copy-start | bytes 7077892
  38.8 11.5 copy-start.100
  38.8 11.8 copy-start.101
  38.8 12.0 copy-start.102
  75.0 639.0 %copy-start.31 = (f32[512]{0:T(512)}, f32[512]{0:T(512)S(1)}, u32[]{:S(2)}) copy-start(f32[512]{0:T(512)S(1)} %convert_element_type.202) | copy-start | bytes 6148
  242.7 94.6 %copy-start.22 = (f32[144,512]{1,0:T(8,128)}, f32[144,512]{1,0:T(8,128)S(1)}, u32[]{:S(2)}) copy-start(f32[144,512]{1,0:T(8,128)S(1)} %get-tuple-element.185) | copy-start | bytes 884740
  254.2 87.7 %copy-start.7 = (bf16[144,6144]{1,0:T(8,128)(2,1)}, bf16[144,6144]{1,0:T(8,128)(2,1)S(1)}, u32[]{:S(2)}) copy-start(bf16[144,6144]{1,0:T(8,128)(2,1)S(1)} %constant_dynamic-update-slice_fusion.16) | copy-start | bytes 5308420
  341.9 127.5 %copy-start.14 = (f32[144,512]{1,0:T(8,128)}, f32[144,512]{1,0:T(8,128)S(1)}, u32[]{:S(2)}) copy-start(f32[144,512]{1,0:T(8,128)S(1)} %get-tuple-element.103) | copy-start | bytes 884740
  341.9 120.5 %copy-start.63 = (f32[144]{0:T(256)}, f32[144]{0:T(256)S(1)}, u32[]{:S(2)}) copy-start(f32[144]{0:T(256)S(1)} %broadcast_multiply_fusion.4) | copy-start | bytes 1732
  342.1 120.3 %copy-start.79 = (f32[144]{0:T(256)}, f32[144]{0:T(256)S(1)}, u32[]{:S(2)}) copy-start(f32[144]{0:T(256)S(1)} %multiply_reduce_fusion.15) | copy-start | bytes 1732
  342.1 120.3 %copy-start.67 = (f32[144]{0:T(256)}, f32[144]{0:T(256)S(1)}, u32[]{:S(2)}) copy-start(f32[144]{0:T(256)S(1)} %fusion.100) | copy-start | bytes 1732
  469.4 118.1 %copy-start.42 = (f32[192,512]{1,0:T(8,128)S(1)}, f32[192,512]{1,0:T(8,128)}, u32[]{:S(2)}) copy-start(f32[192,512]{1,0:T(8,128)} %get-tuple-element.182) | copy-start | bytes 1179652
  594.4 98.8 %copy-start.17 = (f32[192,512]{1,0:T(8,128)}, f32[192,512]{1,0:T(8,128)S(1)}, u32[]{:S(2)}) copy-start(f32[192,512]{1,0:T(8,128)S(1)} %get-tuple-element.99) | copy-start | bytes 1179652
  594.5 98.8 %copy-start.65 = (f32[192]{0:T(256)}, f32[192]{0:T(256)S(1)}, u32[]{:S(2)}) copy-start(f32[192]{0:T(256)S(1)} %broadcast_multiply_fusion.5) | copy-start | bytes 2308
  594.7 98.6 %copy-start.77 = (f32[192]{0:T(256)}, f32[192]{0:T(256)S(1)}, u32[]{:S(2)}) copy-start(f32[192]{0:T(256)S(1)} %multiply_reduce_fusion.12) | copy-start | bytes 2308
  594.7 98.6 %copy-start.71 = (f32[192]{0:T(256)}, f32[192]{0:T(256)S(1)}, u32[]{:S(2)}) copy-start(f32[192]{0:T(256)S(1)} %fusion.99) | copy-start | bytes 2308
  827.7 11.0 copy-start.73
  838.7 51.8 %copy-start.57 = (f32[2304]{0:T(1024)}, f32[2304]{0:T(1024)S(1)}, u32[]{:S(2)}) copy-start(f32[2304]{0:T(1024)S(1)} %broadcast_multiply_fusion.2) | copy-start | bytes 27652
  839.9 50.6 %copy-start.69 = (f32[2304]{0:T(1024)}, f32[2304]{0:T(1024)S(1)}, u32[]{:S(2)}) copy-start(f32[2304]{0:T(1024)S(1)} %get-tuple-element.172) | copy-start | bytes 27652
  842.6 24.6 %copy-start.97 = (bf16[512,2048]{1,0:T(8,128)(2,1)S(1)}, bf16[512,2048]{1,0:T(8,128)(2,1)}, u32[]{:S(2)}) copy-start(bf16[512,2048]{1,0:T(8,128)(2,1)} %all-gather.24.cloned.1.call-done) | copy-start | bytes 6291460
  867.2 13.7 copy-start.60
  890.4 247.4 %reduce-scatter.27.cloned.1.call-start = ((), (), s32[]{:S(2)}) async-start(), calls=%async_computation.27 | async-start | bytes 2359296 | tf_op jit(solution)/shard_map/reduce_scatter | solution.py:304
  902.4 11.0 copy-start.98
  902.4 235.5 %reduce-scatter.25.cloned.1.call-start = ((), (), s32[]{:S(2)}) async-start(), calls=%async_computation.26 | async-start | bytes 2359296 | tf_op jit(solution)/shard_map/reduce_scatter | solution.py:301
  913.3 308.3 %reduce-scatter.19.cloned.1.call-start = ((), (), s32[]{:S(2)}) async-start(), calls=%async_computation.23 | async-start | bytes 7077888 | tf_op jit(solution)/shard_map/reduce_scatter | solution.py:292
  918.5 17.6 slice-start
  947.0 395.2 %reduce-scatter.17.cloned.1.call-start = ((), (), s32[]{:S(2)}) async-start(), calls=%async_computation.22 | async-start | bytes 7077888 | tf_op jit(solution)/shard_map/reduce_scatter | solution.py:289
  969.6 493.1 %reduce-scatter.11.cloned.1.call-start = ((), (), s32[]{:S(2)}) async-start(), calls=%async_computation.19 | async-start | bytes 7077888 | tf_op jit(solution)/shard_map/reduce_scatter | solution.py:280
  990.7 623.7 %reduce-scatter.21.cloned.1.call-start = ((), (), s32[]{:S(2)}) async-start(), calls=%async_computation.24 | async-start | bytes 9437184 | tf_op jit(solution)/shard_map/reduce_scatter | solution.py:295
  996.6 769.8 %reduce-scatter.15.cloned.1.call-start = ((), (), s32[]{:S(2)}) async-start(), calls=%async_computation.21 | async-start | bytes 9437184 | tf_op jit(solution)/shard_map/reduce_scatter | solution.py:286
  1004.5 913.5 %reduce-scatter.13.cloned.1.call-start = ((), (), s32[]{:S(2)}) async-start(), calls=%async_computation.20 | async-start | bytes 9437184 | tf_op jit(solution)/shard_map/reduce_scatter | solution.py:283
  1024.2 33.1 %copy-start.13 = (bf16[2304,512]{1,0:T(8,128)(2,1)S(1)}, bf16[2304,512]{1,0:T(8,128)(2,1)}, u32[]{:S(2)}) copy-start(bf16[2304,512]{1,0:T(8,128)(2,1)} %param.18) | copy-start | bytes 7077892
  1024.3 1016.1 %all-reduce.77.cloned.1.call-start = ((), (), s32[]{:S(2)}) async-start(), calls=%async_computation.29 | async-start | bytes 12451840 | tf_op jit(solution)/shard_map/psum | solution.py:321
  1057.4 30.5 %copy-start.29 = (bf16[192,512]{1,0:T(8,128)(2,1)S(1)}, bf16[192,512]{1,0:T(8,128)(2,1)}, u32[]{:S(2)}) copy-start(bf16[192,512]{1,0:T(8,128)(2,1)} %copy-done.28) | copy-start | bytes 589828
  1918.0 60.5 %copy-start.90 = (f32[12]{0:T(128)S(1)}, f32[12]{0:T(128)}, u32[]{:S(2)}) copy-start(f32[12]{0:T(128)} %copy-done.89) | copy-start | bytes 148
  1918.0 60.6 %copy-start.93 = (f32[12]{0:T(128)S(1)}, f32[12]{0:T(128)}, u32[]{:S(2)}) copy-start(f32[12]{0:T(128)} %copy-done.92) | copy-start | bytes 148
  (79 other events, 345.6 us)
Sparse Core Ops, SparseCore 0:
  10.2 102.3 all-gather.9
  114.8 123.0 all-gather.15
  240.1 97.1 all-gather.17
  339.3 123.1 all-gather.19
  464.4 123.1 all-gather.11
  589.6 97.1 all-gather.13
  689.0 38.3 all-gather.21
  729.5 48.0 all-gather.23
  779.7 47.7 all-gather.25
  831.2 60.4 reduce-scatter.28
  896.1 62.4 reduce-scatter.22
  962.5 66.9 reduce-scatter.26
  1033.7 67.4 reduce-scatter.24
  1104.5 117.0 reduce-scatter.18
  1225.0 117.0 reduce-scatter.16
  1345.6 117.0 reduce-scatter.10
  1466.2 148.1 reduce-scatter.20
  1618.3 148.0 reduce-scatter.14
  1770.0 147.9 reduce-scatter.12
  1921.2 119.1 all-reduce.76
where the time goes:
time: 2070 us; the launch traced here: 2060 us
  waiting for transfers between devices  1450 us (70%)
  matrix products  257 us (12%)
  other arithmetic  167 us (8%)
  local copies, waits for them, and re-layouts  93 us (4%)
  blocking collectives  81.2 us (4%)
    reduce_scatter x1, waiting for transfers between devices, on_device(): lax.psum_scatter(grads[2].astype(jnp.bfloat16), 'dp', scatter_dimension=0...  152 us
    reduce_scatter x1, waiting for transfers between devices, on_device(): lax.psum_scatter(grads[5].astype(jnp.bfloat16), 'dp', scatter_dimension=0...  152 us
    reduce_scatter x1, waiting for transfers between devices, on_device(): lax.psum_scatter(grads[1].astype(jnp.bfloat16), 'dp', scatter_dimension=0...  152 us
    reduce_scatter x1, waiting for transfers between devices, on_device(): lax.psum_scatter(grads[3].astype(jnp.bfloat16), 'dp', scatter_dimension=0...  121 us
    reduce_scatter x1, waiting for transfers between devices, on_device(): lax.psum_scatter(grads[0].astype(jnp.bfloat16), 'dp', scatter_dimension=0...  121 us
    all_gather x1, waiting for transfers between devices, on_device(): lax.all_gather(coarse_grow, 'dp', axis=0, tiled=True)  120 us
    all_gather x1, waiting for transfers between devices, on_device(): lax.all_gather(fine_isometric, 'dp', axis=0, tiled=True)  112 us
    all_gather x1, waiting for transfers between devices, on_device(): lax.all_gather(coarse_shrink, 'dp', axis=0, tiled=True)  107 us
  transfers between devices with their start and end apart: 20, of which 15 were waited for; matrix products, arithmetic and copies ran while one was open for 24% of the time, Pallas kernels for 0%

commit v1 on v0

v1 whole, which is shorter than its diff:
```python
import jax
import jax.numpy as jnp
from jax import lax
from jax.experimental import pallas as pl
from jax.experimental.pallas import tpu as pltpu
from jax.sharding import PartitionSpec as P

S1 = 12
S2 = 16
WINDOW = 25
HALF = WINDOW // 2
GROUP = 4
BF = jnp.bfloat16
F32 = jnp.float32


def layer_norm(values, gain):
    center = jnp.mean(values, axis=-1, keepdims=True)
    centered = values - center
    spread = jnp.mean(centered * centered, axis=-1, keepdims=True)
    return centered * lax.rsqrt(spread + 1e-05) * gain


def exact_gelu(values):
    return jax.nn.gelu(values, approximate=False)


def previous_block(blocks, follows):
    earlier = jnp.concatenate([jnp.zeros_like(blocks[:1]), blocks[:-1]], axis=0)
    return earlier * follows.astype(blocks.dtype)[:, None, None]


def average_matrix(kinds, block_len):
    follows = (kinds == 2).reshape(-1, GROUP)
    groups = follows.shape[0]
    length = GROUP * block_len
    first = jnp.zeros((groups, GROUP), jnp.int32)
    last = jnp.zeros((groups, GROUP), jnp.int32)
    start = jnp.zeros((groups,), jnp.int32)
    firsts = []
    for b in range(GROUP):
        start = jnp.where(follows[:, b], start, b * block_len) if b else jnp.zeros_like(start)
        firsts.append(start)
    stop = jnp.full((groups,), length - 1, jnp.int32)
    lasts = []
    for b in reversed(range(GROUP)):
        if b < GROUP - 1:
            stop = jnp.where(follows[:, b + 1], stop, (b + 1) * block_len - 1)
        lasts.append(stop)
    first = jnp.repeat(jnp.stack(firsts, 1), block_len, axis=1)
    last = jnp.repeat(jnp.stack(lasts[::-1], 1), block_len, axis=1)
    i = lax.broadcasted_iota(jnp.int32, (groups, length, length), 1)
    j = lax.broadcasted_iota(jnp.int32, (groups, length, length), 2)
    first = first[:, :, None]
    last = last[:, :, None]
    inside = (jnp.abs(i - j) <= HALF) & (j >= first) & (j <= last)
    count = inside.astype(jnp.int32)
    count = count + jnp.where(j == first, jnp.maximum(first - i + HALF, 0), 0)
    count = count + jnp.where(j == last, jnp.maximum(i + HALF - last, 0), 0)
    return count.astype(BF)


def unfold(lowered, follows):
    positions = lowered.shape[1]
    extended = jnp.concatenate([previous_block(lowered, follows), lowered], axis=1)
    return jnp.concatenate(
        [extended[:, 1 + offset : 1 + offset + positions] for offset in range(positions)], axis=2
    )


def plain_dot(left, right):
    return jnp.dot(left, right, preferred_element_type=F32)


def weight_dot(inputs, grads):
    return lax.dot_general(inputs, grads, (((0,), (0,)), ((), ())), preferred_element_type=F32)


def back_dot(grads, weight):
    return lax.dot_general(grads, weight, (((1,), (1,)), ((), ())), preferred_element_type=F32)


def branch_forward(season_low, season, follows, shrink, isometric, grow, gain, stride):
    block_count, block_len, feature_width = season.shape
    positions = block_len // stride
    shrink_rows = season_low.reshape(block_count * positions, stride * feature_width)
    shrunk = jnp.tanh(plain_dot(shrink_rows, shrink))
    shrunk_low = shrunk.astype(BF).reshape(block_count, positions, feature_width)
    stacked = unfold(shrunk_low, follows).reshape(
        block_count * positions, positions * feature_width
    )
    isolocal = jnp.tanh(plain_dot(stacked, isometric))
    mixed_out, mixed_pull = jax.vjp(layer_norm, isolocal + shrunk, gain)
    mixed_low = mixed_out.astype(BF)
    upward = jnp.tanh(plain_dot(mixed_low, grow)).reshape(block_count, block_len, feature_width)
    result, result_pull = jax.vjp(layer_norm, upward + season, gain)
    saved = (
        shrink_rows,
        shrunk,
        shrunk_low,
        stacked,
        isolocal,
        mixed_pull,
        mixed_low,
        upward,
        result_pull,
    )
    return (result, saved)


def branch_backward(saved, result_grad, follows, shrink, isometric, grow, stride):
    (
        shrink_rows,
        shrunk,
        shrunk_low,
        stacked,
        isolocal,
        mixed_pull,
        mixed_low,
        upward,
        result_pull,
    ) = saved
    block_count, block_len, feature_width = result_grad.shape
    positions = block_len // stride
    summed, gain_first = result_pull(result_grad)
    grow_pre = (
        (summed * (1.0 - upward * upward))
        .reshape(block_count * positions, stride * feature_width)
        .astype(BF)
    )
    grow_grad = weight_dot(mixed_low, grow_pre).astype(BF)
    mixed_back = back_dot(grow_pre, grow)
    joint_grad, gain_second = mixed_pull(mixed_back)
    iso_pre = (joint_grad * (1.0 - isolocal * isolocal)).astype(BF)
    isometric_grad = weight_dot(stacked, iso_pre).astype(BF)
    stack_back = back_dot(iso_pre, isometric).reshape(
        block_count, positions, positions * feature_width
    )
    ignored, unfold_pull = jax.vjp(
        lambda values: unfold(values, follows), shrunk_low.astype(F32)
    )
    (shrunk_back,) = unfold_pull(stack_back)
    shrunk_total = shrunk_back.reshape(block_count * positions, feature_width) + joint_grad
    shrink_pre = (shrunk_total * (1.0 - shrunk * shrunk)).astype(BF)
    shrink_grad = weight_dot(shrink_rows, shrink_pre).astype(BF)
    season_back = (
        back_dot(shrink_pre, shrink).reshape(block_count, block_len, feature_width) + summed
    )
    return (season_back, shrink_grad, isometric_grad, grow_grad, gain_first + gain_second)


CORE_SWAP = ((0, 1), (1, 0), (2, 3), (3, 2))
Y_SWAP = ((0, 2), (2, 0), (1, 3), (3, 1))


def swap_core(v):
    return lax.ppermute(v, "group", CORE_SWAP)


def swap_y(v):
    return lax.ppermute(v, "group", Y_SWAP)


class Ring:
    def __init__(self, n):
        self.n = n
        order = list(range(0, n, 2)) + list(range(n - 1, 0, -2))
        self.right = [(order[k], order[(k + 1) % n]) for k in range(n)]
        self.left = [(b, a) for a, b in self.right]
        d = lax.axis_index("dp")
        self.me = d
        self.pos = jnp.where(d % 2 == 0, d // 2, n - 1 - d // 2)

    def index(self, offset):
        r = (self.pos + offset) % self.n
        return jnp.where(r < self.n // 2, 2 * r, 2 * (self.n - 1 - r) + 1)

    def steps(self, long_right):
        longer, shorter = self.n // 2, self.n - 1 - self.n // 2
        return (longer, shorter) if long_right else (shorter, longer)

    def go_right(self, v):
        return lax.ppermute(v, "dp", self.right)

    def go_left(self, v):
        return lax.ppermute(v, "dp", self.left)


def gather_pieces(ring, own, split_y, long_right):
    to_right, to_left = ring.steps(long_right)
    found = []

    def spread(piece):
        if split_y:
            other = swap_y(piece)
            return [piece, other, swap_core(piece), swap_core(other)]
        return [piece, swap_core(piece)]

    right = left = own
    for k in range(1, max(to_right, to_left) + 1):
        if k <= to_right:
            right = ring.go_right(right)
            found.append((-k, spread(right)))
        if k <= to_left:
            left = ring.go_left(left)
            found.append((k, spread(left)))
    return found


def place(name, shards, found, parts, ring, core, y, split_y):
    n = ring.n
    offsets = [offset for offset, _ in found]
    where = jnp.stack([ring.me, core, y] + [ring.index(offset) for offset in offsets])
    buffers = [b for _, bufs in found for b in bufs]
    count = len(buffers) // len(offsets)
    whole = [
        jax.ShapeDtypeStruct((shard.shape[0] * n, shard.shape[1]), shard.dtype) for shard in shards
    ]

    def body(where_ref, *refs):
        own = refs[: len(shards)]
        pieces = refs[len(shards) : len(shards) + len(buffers)]
        outs = refs[len(shards) + len(buffers) : -1]
        sems = refs[-1]
        me, c, h = where_ref[0], where_ref[1], where_ref[2]
        for t, shard in enumerate(shards):
            rows = shard.shape[0]
            start = pl.multiple_of(me * rows, rows)
            pltpu.make_async_copy(own[t], outs[t].at[pl.ds(start, rows)], sems.at[t]).start()
        for o in range(len(offsets)):
            source = where_ref[3 + o]
            for b in range(count):
                if split_y:
                    cc, hh = (c if b < 2 else 1 - c), (h if b % 2 == 0 else 1 - h)
                else:
                    cc, hh = (c if b == 0 else 1 - c), None
                piece = pieces[o * count + b]
                for t, cuts in enumerate(parts):
                    rows = shards[t].shape[0]
                    for r0, nr, c0, nc, fn, align_r, align_c in cuts:
                        row, col = fn(cc, hh)
                        row = pl.multiple_of(source * rows + row, align_r)
                        if not isinstance(col, int):
                            col = pl.multiple_of(col, align_c)
                        pltpu.make_async_copy(
                            piece.at[pl.ds(r0, nr), pl.ds(c0, nc)],
                            outs[t].at[pl.ds(row, nr), pl.ds(col, nc)],
                            sems.at[t],
                        ).start()
        for t in range(len(shards)):
            pltpu.make_async_copy(outs[t], outs[t], sems.at[t]).wait()

    total = sum(w.shape[0] * w.shape[1] * 4 for w in whole)
    return pl.pallas_call(
        body,
        out_shape=whole,
        grid_spec=pltpu.PrefetchScalarGridSpec(
            num_scalar_prefetch=1,
            grid=(),
            in_specs=[pl.BlockSpec(memory_space=pl.ANY)] * (len(shards) + len(buffers)),
            out_specs=[pl.BlockSpec(memory_space=pltpu.VMEM)] * len(whole),
            scratch_shapes=[pltpu.SemaphoreType.DMA((len(shards),))],
        ),
        cost_estimate=pl.CostEstimate(flops=0, bytes_accessed=total, transcendentals=0),
        compiler_params=pltpu.CompilerParams(vmem_limit_bytes=40 * 1024 * 1024),
        name=name,
    )(where, *shards, *buffers)


def cut(v, index, size, axis):
    return lax.dynamic_slice_in_dim(v, index, size, axis=axis)


def gather_row_pair(name, ring, first, second, core, y, split_y, long_right):
    share = 4 if split_y else 2
    ra, rb = first.shape[0] // share, second.shape[0] // share
    slot = core * 2 + y if split_y else core
    own = jnp.concatenate([cut(first, slot * ra, ra, 0), cut(second, slot * rb, rb, 0)], axis=0)
    width = first.shape[1]
    found = gather_pieces(ring, own, split_y, long_right)

    def at(rows):
        if split_y:
            return lambda c, h: ((c * 2 + h) * rows, 0)
        return lambda c, h: (c * rows, 0)

    parts = [[(0, ra, 0, width, at(ra), ra, 1)], [(ra, rb, 0, width, at(rb), rb, 1)]]
    return place(name, [first, second], found, parts, ring, core, y, split_y)


def gather_column_pair(name, ring, first, second, core, y, split_y, long_right):
    share = 4 if split_y else 2
    ca, cb = first.shape[1] // share, second.shape[1] // share
    slot = core * 2 + y if split_y else core
    own = jnp.concatenate([cut(first, slot * ca, ca, 1), cut(second, slot * cb, cb, 1)], axis=1)
    rows = first.shape[0]
    found = gather_pieces(ring, own, split_y, long_right)

    def at(cols):
        if split_y:
            return lambda c, h: (0, (c * 2 + h) * cols)
        return lambda c, h: (0, c * cols)

    parts = [[(0, rows, 0, ca, at(ca), rows, ca)], [(0, rows, ca, cb, at(cb), rows, cb)]]
    return place(name, [first, second], found, parts, ring, core, y, split_y)


def gather_rest(name, ring, merge, contract, trend, expand, core, y, long_right):
    half = merge.shape[1] // 2
    wide = expand.shape[1] // 2
    chunks = wide // half
    stack = [cut(v, core * half, half, 1) for v in (merge, contract, trend)]
    stack += [cut(expand, core * wide + j * half, half, 1) for j in range(chunks)]
    own = jnp.concatenate(stack, axis=0)
    found = gather_pieces(ring, own, False, long_right)
    parts, start = [], 0
    for v in (merge, contract, trend):
        rows = v.shape[0]
        parts.append([(start, rows, 0, half, lambda c, h: (0, c * half), rows, half)])
        start += rows
    rows = expand.shape[0]
    cuts = []
    for j in range(chunks):
        cuts.append(
            (start, rows, 0, half, lambda c, h, j=j: (0, c * wide + j * half), rows, half)
        )
        start += rows
    parts.append(cuts)
    return place(name, [merge, contract, trend, expand], found, parts, ring, core, y, False)


def reduce_tensor(ring, grad, by_rows, core, y, split_y, long_right):
    n = ring.n
    rows, cols = grad.shape[0] // n, grad.shape[1]
    if by_rows:
        full = grad.reshape(n, 2, rows // 2, cols)
        take = lambda v, c: lax.dynamic_index_in_dim(v, c, axis=1, keepdims=False)
        give = take(full, 1 - core)
        keep = take(full, core)
        got = swap_core(give)
        if split_y:
            quarter = rows // 4
            piece = lambda v, h: cut(v, h * quarter, quarter, 1)
        axis = 0
    else:
        half = cols // 2
        full = grad.reshape(n, rows, cols)
        take = lambda v, c: cut(v, c * half, half, 2)
        give = take(full, 1 - core)
        keep = take(full, core)
        got = swap_core(give)
        if split_y:
            quarter = half // 2
            piece = lambda v, h: cut(v, h * quarter, quarter, 2)
        axis = 1
    terms = [keep, got]
    if split_y:
        give_y = (piece(keep, 1 - y).astype(F32) + piece(got, 1 - y).astype(F32)).astype(BF)
        got_y = swap_y(give_y)
        terms = [piece(keep, y), piece(got, y), got_y]

    def local(offset):
        at = ring.me if offset == 0 else ring.index(offset)
        total = None
        for t in terms:
            v = lax.dynamic_index_in_dim(t, at, axis=0, keepdims=False).astype(F32)
            total = v if total is None else total + v
        return total

    to_right, to_left = ring.steps(long_right)
    longest = max(to_right, to_left)
    right = left = None
    for k in range(longest, 0, -1):
        if k <= to_right:
            part = local(k)
            if right is not None:
                part = part + right.astype(F32)
            right = ring.go_right(part.astype(BF))
        if k <= to_left:
            part = local(-k)
            if left is not None:
                part = part + left.astype(F32)
            left = ring.go_left(part.astype(BF))
    mine = (local(0) + right.astype(F32) + left.astype(F32)).astype(BF)
    other = swap_y(mine)
    if split_y:
        half_sum = jnp.where(
            y == 0,
            jnp.concatenate([mine, other], axis=axis),
            jnp.concatenate([other, mine], axis=axis),
        )
    else:
        half_sum = (mine.astype(F32) + other.astype(F32)).astype(BF)
    sibling = swap_core(half_sum)
    return jnp.where(
        core == 0,
        jnp.concatenate([half_sum, sibling], axis=axis),
        jnp.concatenate([sibling, half_sum], axis=axis),
    ).astype(F32)


def add_over(v, axis, size):
    step = 1
    while step < size:
        v = v + lax.ppermute(v, axis, [(i, i ^ step) for i in range(size)])
        step *= 2
    return v


def on_device(
    n,
    series_in,
    block_kinds,
    out_grad,
    fine_shrink,
    coarse_shrink,
    fine_isometric,
    coarse_isometric,
    fine_grow,
    coarse_grow,
    merge_weight,
    expand_weight,
    contract_weight,
    trend_weight,
    branch_gain,
    middle_gain,
    output_gain,
):
    ring = Ring(n)
    member = lax.axis_index("group")
    core, y = member % 2, member // 2
    me = ring.me
    block_count = block_kinds.shape[0]
    feature_width = series_in.shape[1]
    block_len = series_in.shape[0] // block_count
    share = branch_gain.shape[0]

    gains = jnp.stack([branch_gain, middle_gain, output_gain]).astype(F32)
    gains = lax.dynamic_update_slice(
        jnp.zeros((3, feature_width), F32), gains, (jnp.int32(0), me * share)
    )
    gains = add_over(gains, "dp", n)
    gain_branch, gain_middle, gain_output = gains[0], gains[1], gains[2]

    f_shrink, c_shrink = gather_row_pair(
        "place_shrink", ring, fine_shrink, coarse_shrink, core, y, True, False
    )
    f_grow, c_grow = gather_column_pair(
        "place_grow", ring, fine_grow, coarse_grow, core, y, True, False
    )
    f_iso, c_iso = gather_row_pair(
        "place_iso", ring, fine_isometric, coarse_isometric, core, y, False, True
    )
    merge_full, contract_full, trend_full, expand_full = gather_rest(
        "place_rest",
        ring,
        merge_weight,
        contract_weight,
        trend_weight,
        expand_weight,
        core,
        y,
        False,
    )

    follows = (block_kinds == 2).astype(F32)
    blocks = series_in.astype(F32).reshape(block_count, block_len, feature_width)
    counts = average_matrix(block_kinds, block_len)
    grouped = series_in.reshape(-1, GROUP * block_len, feature_width)
    trend = jnp.einsum("gij,gjd->gid", counts, grouped, preferred_element_type=F32)
    trend = (trend * (1.0 / WINDOW)).reshape(block_count, block_len, feature_width)
    season = blocks - trend
    season_low = season.astype(BF)
    fine_out, fine_saved = branch_forward(
        season_low, season, follows, f_shrink, f_iso, f_grow, gain_branch, S1
    )
    coarse_out, coarse_saved = branch_forward(
        season_low, season, follows, c_shrink, c_iso, c_grow, gain_branch, S2
    )
    joined = (
        jnp.concatenate([fine_out, coarse_out], axis=2).astype(BF).reshape(-1, 2 * feature_width)
    )
    merged = plain_dot(joined, merge_full)
    middle, middle_pull = jax.vjp(layer_norm, merged, gain_middle)
    middle_low = middle.astype(BF)
    hidden, gelu_pull = jax.vjp(exact_gelu, plain_dot(middle_low, expand_full))
    hidden_low = hidden.astype(BF)
    lifted = plain_dot(hidden_low, contract_full)
    seasonal, output_pull = jax.vjp(layer_norm, middle + lifted, gain_output)
    trend_low = trend.reshape(-1, feature_width).astype(BF)
    projected = plain_dot(trend_low, trend_full)
    series_out = (seasonal + projected).astype(BF)
    trend_grad = weight_dot(trend_low, out_grad).astype(BF)
    trend_back = back_dot(out_grad, trend_full)
    summed_grad, output_gain_raw = output_pull(out_grad.astype(F32))
    lifted_low = summed_grad.astype(BF)
    contract_grad = weight_dot(hidden_low, lifted_low).astype(BF)
    (hidden_pre_grad,) = gelu_pull(back_dot(lifted_low, contract_full))
    hidden_grad_low = hidden_pre_grad.astype(BF)
    expand_grad = weight_dot(middle_low, hidden_grad_low).astype(BF)
    middle_back = summed_grad + back_dot(hidden_grad_low, expand_full)
    merged_grad, middle_gain_raw = middle_pull(middle_back)
    merged_low = merged_grad.astype(BF)
    merge_grad = weight_dot(joined, merged_low).astype(BF)
    joined_back = back_dot(merged_low, merge_full).reshape(
        block_count, block_len, 2 * feature_width
    )
    fine_season, fine_shrink_g, fine_iso_g, fine_grow_g, fine_gain_g = branch_backward(
        fine_saved, joined_back[:, :, :feature_width], follows, f_shrink, f_iso, f_grow, S1
    )
    coarse_season, coarse_shrink_g, coarse_iso_g, coarse_grow_g, coarse_gain_g = branch_backward(
        coarse_saved, joined_back[:, :, feature_width:], follows, c_shrink, c_iso, c_grow, S2
    )
    season_grad = fine_season + coarse_season
    trend_total = trend_back.reshape(block_count, block_len, feature_width) - season_grad
    spread = (trend_total * (1.0 / WINDOW)).astype(BF)
    averaged = jnp.einsum(
        "gij,gid->gjd",
        counts,
        spread.reshape(grouped.shape),
        preferred_element_type=F32,
    )
    series_grad = (season_grad + averaged.reshape(season_grad.shape)).reshape(
        -1, feature_width
    ).astype(BF)

    def reduced(grad, by_rows, split_y, long_right):
        return reduce_tensor(ring, grad, by_rows, core, y, split_y, long_right)

    contract_share = reduced(contract_grad, True, False, True)
    expand_share = reduced(expand_grad, False, False, False)
    merge_share = reduced(merge_grad, True, False, False)
    trend_share = reduced(trend_grad, True, False, False)
    fine_grow_share = reduced(fine_grow_g, False, True, True)
    coarse_grow_share = reduced(coarse_grow_g, False, True, False)
    fine_iso_share = reduced(fine_iso_g, True, True, True)
    coarse_iso_share = reduced(coarse_iso_g, True, True, False)
    fine_shrink_share = reduced(fine_shrink_g, True, False, True)
    coarse_shrink_share = reduced(coarse_shrink_g, True, False, False)

    gain_grads = jnp.stack([fine_gain_g + coarse_gain_g, middle_gain_raw, output_gain_raw])
    gain_grads = add_over(add_over(gain_grads, "dp", n), "group", 4)
    gain_grads = lax.dynamic_slice(gain_grads, (jnp.int32(0), me * share), (3, share))
    return (
        series_out,
        series_grad,
        fine_shrink_share,
        coarse_shrink_share,
        fine_iso_share,
        coarse_iso_share,
        fine_grow_share,
        coarse_grow_share,
        merge_share,
        expand_share,
        contract_share,
        trend_share,
        gain_grads[0],
        gain_grads[1],
        gain_grads[2],
    )


def solution(mesh):
    n = mesh.shape["dp"]
    rows = P(("dp", "group"), None)
    weight = P("dp", None)
    return jax.shard_map(
        lambda *args: on_device(n, *args),
        mesh=mesh,
        in_specs=(rows, P(("dp", "group")), rows) + (weight,) * 10 + (P("dp"),) * 3,
        out_specs=(rows, rows) + (weight,) * 10 + (P("dp"),) * 3,
        check_vma=False,
    )
```

time: 2070 us -> 1160 us (0.56)
  waiting for transfers between devices: 1450 us -> 331 us
  starting transfers between devices: 1.18 us -> 151 us
  local copies, waits for them, and re-layouts: 93 us -> 195 us
  blocking collectives: 81.2 us -> 0 us
  other arithmetic: 167 us -> 199 us
  Pallas kernels: 0 us -> 31 us
  matrix products: 257 us -> 235 us
    reduce_scatter x10 -> x0, waiting for transfers between devices: 780 us -> none  [the longest x1 152 us: on_device(): lax.psum_scatter(grads[2].astype(jnp.bfloat16), 'dp', scatter_dimension=0...]
    all_gather x9 -> x0, waiting for transfers between devices: 603 us -> none  [the longest x1 120 us: on_device(): lax.all_gather(coarse_grow, 'dp', axis=0, tiled=True)]
    ppermute x0 -> x196, waiting for transfers between devices: none -> 331 us  [the longest x51 124 us: go_left(): return lax.ppermute(v, 'dp', self.left)]
    ppermute x0 -> x196, starting transfers between devices: none -> 151 us  [the longest x51 68.9 us: go_left(): return lax.ppermute(v, 'dp', self.left)]
    convert_element_type x25 -> x99, other arithmetic: 36.8 us -> 135 us  [the longest x34 36.8 us: reduce_tensor(): right = ring.go_right(part.astype(BF))]
    add_any x1 -> x0, other arithmetic: 60.3 us -> none  [moving_average(): running = padded[:, 0:block_len]]
    psum x1 -> x0, waiting for transfers between devices: 55.8 us -> none  [on_device(): lax.psum(shares[0].astype(jnp.bfloat16), 'group').astype(jnp.float32)]
    unnamed x2 -> x0, blocking collectives: 43.1 us -> none
  transfers between devices with their start and end apart: 20 -> 196, of which waited for: 15 -> 78; matrix products, arithmetic and copies ran while one was open for 24% -> 24% of each run, Pallas kernels for 0% -> 2%
where the time goes in v1:
time: 1160 us; the launch traced here: 1150 us
  waiting for transfers between devices  331 us (29%)
  matrix products  235 us (20%)
  other arithmetic  199 us (17%)
  local copies, waits for them, and re-layouts  195 us (17%)
  starting transfers between devices  151 us (13%)
  Pallas kernels  31 us (3%)
    ppermute x51, waiting for transfers between devices, go_left(): return lax.ppermute(v, 'dp', self.left)  124 us
    ppermute x28, waiting for transfers between devices, swap_y(): return lax.ppermute(v, 'group', Y_SWAP)  109 us
    dot_general x10, matrix products, plain_dot(): return jnp.dot(left, right, preferred_element_type=F32)  95.5 us
    ppermute x47, waiting for transfers between devices, go_right(): return lax.ppermute(v, 'dp', self.right)  94.7 us
    dot_general x10, matrix products, back_dot(): lax.dot_general(grads, weight, (((1,), (1,)), ((), ())), preferred_elemen...  76.4 us
    unnamed x460, local copies, waits for them, and re-layouts  70.2 us
    ppermute x51, starting transfers between devices, go_left(): return lax.ppermute(v, 'dp', self.left)  68.9 us
    dot_general x10, matrix products, weight_dot(): lax.dot_general(inputs, grads, (((0,), (0,)), ((), ())), preferred_elemen...  54.4 us
  transfers between devices with their start and end apart: 196, of which 78 were waited for; matrix products, arithmetic and copies ran while one was open for 24% of the time, Pallas kernels for 2%

profile of v1, /device:TPU:0, one launch (start us, length us, event | category | flops | bytes accessed | tf_op | source)
XLA Modules:
  0.0 1145.5 jit_solution(16670969474797324406)
XLA Ops:
  27.2 6.6 collective-permute-done.182
  119.2 6.0 reshape.895
  136.3 5.7 subtract_convert_fusion
  142.0 6.2 reshape.887
  148.1 5.6 reshape.884
  158.2 5.7 subtract_convert_fusion.1
  213.5 6.0 copy.39
  234.3 10.8 place_shrink.1
  245.1 5.6 fusion.237
  281.9 5.8 fusion.236
  293.0 8.3 collective-permute-done.58.refs_15_
  309.9 14.9 %collective-permute-done.34.refs_8_ = bf16[896,512]{1,0:T(8,128)(2,1)S(1)} collective-permute-done((bf16[896,512]{1,0:T(8,128)(2,1)}, bf16[896,512]{1,0:T(8,128)(2,1)S(1)}, u32[]{:S(2)}, u32[]{:S(2)}) %collective-permute-start.34) | collective-permute-done | bytes 917536 | tf_op jit(solution)/shard_map/ppermute | solution.py:186
  324.8 7.4 collective-permute-done.69.refs_26_
  336.4 9.4 collective-permute-done.70.refs_27_
  349.1 6.3 collective-permute-done.36.refs_10_
  357.5 8.2 place_grow.1
  383.2 9.0 place_iso.1
  402.0 6.0 reshape.898
  408.0 6.2 reshape.897
  414.1 7.0 fusion.230
  425.5 5.5 reshape.891
  436.6 10.9 fusion.229
  452.6 6.5 multiply_convert_fusion.5
  465.2 48.3 %multiply_convert_fusion = (bf16[2304,2048]{1,0:T(8,128)(2,1)}, f32[2304,2048]{1,0:T(8,128)}, f32[2304,2048]{1,0:T(8,128)}) fusion(bf16[512,2048]{1,0:T(8,128)(2,1)S(1)} %copy-done.51, f32[2304,512]{0,1:T(8,128)S(1)} %get-tuple-element.213, f32[512]{0:T(512)S(1)} %bitcast.826, f32[2304]{0:T(1024)S(1)} %fusion.209, f32[2304]{0:T(1024)S(1)} %broadcast_multiply_fusion.4), kind=kOutput, calls=%fused_computation.3 | convolution fusion | flops 5143265280 | bytes 54022144 | tf_op jit(solution)/shard_map/dot_general | solution.py:72
  513.5 10.7 fusion.239
  529.7 8.0 convolution_convert_fusion.6
  537.7 23.5 %add_convert_fusion = bf16[2304,2048]{1,0:T(8,128)(2,1)} fusion(f32[2304,2048]{1,0:T(8,128)} %get-tuple-element.94, f32[2304,2048]{1,0:T(8,128)} %get-tuple-element.214, bf16[2048,512]{1,0:T(8,128)(2,1)S(1)} %copy-done.53, f32[2304]{0:T(1024)S(1)} %negate_multiply_fusion.4, bf16[2304,512]{0,1:T(8,128)(2,1)S(1)} %copy-done.63, f32[2304,512]{0,1:T(8,128)} %copy-done.67, ...), kind=kOutput, calls=%fused_computation.2 | convolution fusion | flops 4908515328 | bytes 56399872 | tf_op jit(solution)/shard_map/dot_general | solution.py:80
  561.2 13.6 %multiply_reduce_fusion = (f32[512]{0:T(512)}, f32[2304]{0:T(1024)S(1)}, f32[2304,512]{0,1:T(8,128)S(1)}) fusion(f32[2304,512]{0,1:T(8,128)} %copy-done.68, f32[2304]{0:T(1024)S(1)} %fusion.209, f32[2304]{0:T(1024)S(1)} %broadcast_multiply_fusion.4, f32[512]{0:T(512)S(1)} %bitcast.828, bf16[2304,2048]{1,0:T(8,128)(2,1)} %add_convert_fusion, ...), kind=kOutput, calls=%fused_computation.48 | convolution fusion | flops 4850709504 | bytes 28120064 | tf_op jit(solution)/shard_map/dot_general | solution.py:80
  574.8 10.9 convolution_convert_fusion.7
  585.8 5.9 fusion.227
  617.4 7.2 multiply_reduce_fusion.13
  624.6 5.7 convolution_convert_fusion
  638.8 5.7 multiply_reduce_fusion.10
  681.1 5.7 convolution_convert_fusion.2
  686.9 8.7 fusion.243
  698.8 5.5 reshape.902
  704.3 6.0 reshape.905
  715.3 10.6 multiply_convert_fusion.1
  886.6 12.7 %collective-permute-done.130 = bf16[8,64,1536]{2,1,0:T(8,128)(2,1)} collective-permute-done((bf16[8,64,1536]{2,1,0:T(8,128)(2,1)}, bf16[8,64,1536]{2,1,0:T(8,128)(2,1)}, u32[]{:S(2)}, u32[]{:S(2)}) %collective-permute-start.130) | collective-permute-done | bytes 1572896 | tf_op jit(solution)/shard_map/ppermute | solution.py:161
  902.1 30.8 %collective-permute-done.119 = bf16[8,192,512]{2,1,0:T(8,128)(2,1)} collective-permute-done((bf16[8,192,512]{2,1,0:T(8,128)(2,1)}, bf16[8,192,512]{2,1,0:T(8,128)(2,1)}, u32[]{:S(2)}, u32[]{:S(2)}) %collective-permute-start.119) | collective-permute-done | bytes 1572896 | tf_op jit(solution)/shard_map/ppermute | solution.py:161
  946.8 11.9 %collective-permute-done.132 = bf16[64,1536]{1,0:T(8,128)(2,1)S(1)} collective-permute-done((bf16[64,1536]{1,0:T(8,128)(2,1)S(1)}, bf16[64,1536]{1,0:T(8,128)(2,1)S(1)}, u32[]{:S(2)}, u32[]{:S(2)}) %collective-permute-start.132) | collective-permute-done | bytes 196640 | tf_op jit(solution)/shard_map/ppermute | solution.py:183
  984.2 6.2 collective-permute-done.124
  1004.4 9.2 collective-permute-done.125
  1030.5 7.3 collective-permute-done.138
  1059.4 6.0 collective-permute-done.109
  1078.3 8.3 collective-permute-done.146
  1110.6 9.1 collective-permute-done.104
  1125.9 6.4 collective-permute-done.115
  (1101 shorter events, 687.8 us)
Async XLA Ops:
  19.9 39.8 %collective-permute-start.75 = (bf16[704,256]{1,0:T(8,128)(2,1)}, bf16[704,256]{1,0:T(8,128)(2,1)}, u32[]{:S(2)}, u32[]{:S(2)}) collective-permute-start(bf16[704,256]{1,0:T(8,128)(2,1)} %constant_dynamic-update-slice_fusion.28), channel_id=1, source_target_pairs={{8,0},{16,8},{24,16},{28,24},{20,28},{12,20},{4,12},{0,4},{9,1},{1... | collective-permute-start | bytes 1081352 | tf_op jit(solution)/shard_map/ppermute | solution.py:186
  22.4 40.0 %collective-permute-start.73 = (bf16[704,256]{1,0:T(8,128)(2,1)}, bf16[704,256]{1,0:T(8,128)(2,1)S(1)}, u32[]{:S(2)}, u32[]{:S(2)}) collective-permute-start(bf16[704,256]{1,0:T(8,128)(2,1)} %constant_dynamic-update-slice_fusion.28), channel_id=1, source_target_pairs={{0,8},{8,16},{16,24},{24,28},{28,20},{20,12},{12,4},{4,0},{1,9},{9... | collective-permute-start | bytes 1081352 | tf_op jit(solution)/shard_map/ppermute | solution.py:183
  27.1 36.9 %collective-permute-start.4 = (bf16[448,512]{1,0:T(8,128)(2,1)}, bf16[448,512]{1,0:T(8,128)(2,1)S(1)}, u32[]{:S(2)}, u32[]{:S(2)}) collective-permute-start(bf16[448,512]{1,0:T(8,128)(2,1)} %pad_maximum_fusion.6), channel_id=1, source_target_pairs={{8,0},{16,8},{24,16},{28,24},{20,28},{12,20},{4,12},{0,4},{9,1},{1... | collective-permute-start | bytes 1376264 | tf_op jit(solution)/shard_map/ppermute | solution.py:186
  66.4 24.5 %collective-permute-start.12 = (bf16[448,512]{1,0:T(8,128)(2,1)S(1)}, bf16[448,512]{1,0:T(8,128)(2,1)S(1)}, u32[]{:S(2)}, u32[]{:S(2)}) collective-permute-start(bf16[448,512]{1,0:T(8,128)(2,1)S(1)} %collective-permute-done.4.refs_6_), channel_id=1, source_target_pairs={{8,0},{16,8},{24,16},{28,24},{20,28},{12,20},{4,12},{0,4},{9,1},{1... | collective-permute-start | bytes 1376264 | tf_op jit(solution)/shard_map/ppermute | solution.py:186
  130.3 25.3 %collective-permute-start.7 = (bf16[448,512]{1,0:T(8,128)(2,1)}, bf16[448,512]{1,0:T(8,128)(2,1)}, u32[]{:S(2)}, u32[]{:S(2)}) collective-permute-start(bf16[448,512]{1,0:T(8,128)(2,1)} %collective-permute-done.5.refs_7_), channel_id=1, source_target_pairs={{0,1},{1,0},{2,3},{3,2},{4,5},{5,4},{6,7},{7,6},{8,9},{9,8},{10,11... | collective-permute-start | bytes 1376264 | tf_op jit(solution)/shard_map/ppermute | solution.py:157
  179.3 27.0 %collective-permute-start.22 = (bf16[448,512]{1,0:T(8,128)(2,1)S(1)}, bf16[448,512]{1,0:T(8,128)(2,1)S(1)}, u32[]{:S(2)}, u32[]{:S(2)}) collective-permute-start(bf16[448,512]{1,0:T(8,128)(2,1)S(1)} %copy-done.18), channel_id=1, source_target_pairs={{0,1},{1,0},{2,3},{3,2},{4,5},{5,4},{6,7},{7,6},{8,9},{9,8},{10,11... | collective-permute-start | bytes 1376264 | tf_op jit(solution)/shard_map/ppermute | solution.py:157
  179.4 28.2 %collective-permute-start.19 = (bf16[448,512]{1,0:T(8,128)(2,1)}, bf16[448,512]{1,0:T(8,128)(2,1)S(1)}, u32[]{:S(2)}, u32[]{:S(2)}) collective-permute-start(bf16[448,512]{1,0:T(8,128)(2,1)} %collective-permute-done.17.refs_19_), channel_id=1, source_target_pairs={{0,1},{1,0},{2,3},{3,2},{4,5},{5,4},{6,7},{7,6},{8,9},{9,8},{10,11... | collective-permute-start | bytes 1376264 | tf_op jit(solution)/shard_map/ppermute | solution.py:157
  183.0 37.0 %collective-permute-start.26 = (bf16[448,512]{1,0:T(8,128)(2,1)}, bf16[448,512]{1,0:T(8,128)(2,1)}, u32[]{:S(2)}, u32[]{:S(2)}) collective-permute-start(bf16[448,512]{1,0:T(8,128)(2,1)} %collective-permute-done.24.refs_26_), channel_id=1, source_target_pairs={{0,1},{1,0},{2,3},{3,2},{4,5},{5,4},{6,7},{7,6},{8,9},{9,8},{10,11... | collective-permute-start | bytes 1376264 | tf_op jit(solution)/shard_map/ppermute | solution.py:157
  183.8 35.7 %collective-permute-start.23 = (bf16[448,512]{1,0:T(8,128)(2,1)}, bf16[448,512]{1,0:T(8,128)(2,1)}, u32[]{:S(2)}, u32[]{:S(2)}) collective-permute-start(bf16[448,512]{1,0:T(8,128)(2,1)} %collective-permute-done.21.refs_23_), channel_id=1, source_target_pairs={{0,1},{1,0},{2,3},{3,2},{4,5},{5,4},{6,7},{7,6},{8,9},{9,8},{10,11... | collective-permute-start | bytes 1376264 | tf_op jit(solution)/shard_map/ppermute | solution.py:157
  189.4 32.1 %collective-permute-start.27 = (bf16[448,512]{1,0:T(8,128)(2,1)}, bf16[448,512]{1,0:T(8,128)(2,1)}, u32[]{:S(2)}, u32[]{:S(2)}) collective-permute-start(bf16[448,512]{1,0:T(8,128)(2,1)} %collective-permute-done.25.refs_27_), channel_id=1, source_target_pairs={{0,1},{1,0},{2,3},{3,2},{4,5},{5,4},{6,7},{7,6},{8,9},{9,8},{10,11... | collective-permute-start | bytes 1376264 | tf_op jit(solution)/shard_map/ppermute | solution.py:157
  207.1 45.0 %collective-permute-start.28 = (bf16[896,512]{1,0:T(8,128)(2,1)}, bf16[896,512]{1,0:T(8,128)(2,1)S(1)}, u32[]{:S(2)}, u32[]{:S(2)}) collective-permute-start(bf16[896,512]{1,0:T(8,128)(2,1)} %pad_maximum_fusion.5), channel_id=1, source_target_pairs={{0,8},{8,16},{16,24},{24,28},{28,20},{20,12},{12,4},{4,0},{1,9},{9... | collective-permute-start | bytes 2752520 | tf_op jit(solution)/shard_map/ppermute | solution.py:183
  208.4 44.3 %collective-permute-start.30 = (bf16[896,512]{1,0:T(8,128)(2,1)}, bf16[896,512]{1,0:T(8,128)(2,1)}, u32[]{:S(2)}, u32[]{:S(2)}) collective-permute-start(bf16[896,512]{1,0:T(8,128)(2,1)} %pad_maximum_fusion.5), channel_id=1, source_target_pairs={{8,0},{16,8},{24,16},{28,24},{20,28},{12,20},{4,12},{0,4},{9,1},{1... | collective-permute-start | bytes 2752520 | tf_op jit(solution)/shard_map/ppermute | solution.py:186
  219.5 33.7 %collective-permute-start.53 = (bf16[64,3584]{1,0:T(8,128)(2,1)}, bf16[64,3584]{1,0:T(8,128)(2,1)}, u32[]{:S(2)}, u32[]{:S(2)}) collective-permute-start(bf16[64,3584]{1,0:T(8,128)(2,1)} %collective-permute-done.45.refs_2_), channel_id=1, source_target_pairs={{0,8},{8,16},{16,24},{24,28},{28,20},{20,12},{12,4},{4,0},{1,9},{9... | collective-permute-start | bytes 1376264 | tf_op jit(solution)/shard_map/ppermute | solution.py:183
  220.0 57.7 %collective-permute-start.46 = (bf16[64,3584]{1,0:T(8,128)(2,1)}, bf16[64,3584]{1,0:T(8,128)(2,1)}, u32[]{:S(2)}, u32[]{:S(2)}) collective-permute-start(bf16[64,3584]{1,0:T(8,128)(2,1)} %collective-permute-done.45.refs_2_), channel_id=1, source_target_pairs={{0,2},{2,0},{1,3},{3,1},{4,6},{6,4},{5,7},{7,5},{8,10},{10,8},{9,1... | collective-permute-start | bytes 1376264 | tf_op jit(solution)/shard_map/ppermute | solution.py:161
  221.5 31.2 %collective-permute-start.57 = (bf16[64,3584]{1,0:T(8,128)(2,1)}, bf16[64,3584]{1,0:T(8,128)(2,1)}, u32[]{:S(2)}, u32[]{:S(2)}) collective-permute-start(bf16[64,3584]{1,0:T(8,128)(2,1)} %collective-permute-done.49.refs_6_), channel_id=1, source_target_pairs={{8,0},{16,8},{24,16},{28,24},{20,28},{12,20},{4,12},{0,4},{9,1},{1... | collective-permute-start | bytes 1376264 | tf_op jit(solution)/shard_map/ppermute | solution.py:186
  252.1 27.2 %collective-permute-start.50 = (bf16[64,3584]{1,0:T(8,128)(2,1)}, bf16[64,3584]{1,0:T(8,128)(2,1)S(1)}, u32[]{:S(2)}, u32[]{:S(2)}) collective-permute-start(bf16[64,3584]{1,0:T(8,128)(2,1)} %collective-permute-done.49.refs_6_), channel_id=1, source_target_pairs={{0,2},{2,0},{1,3},{3,1},{4,6},{6,4},{5,7},{7,5},{8,10},{10,8},{9,1... | collective-permute-start | bytes 1376264 | tf_op jit(solution)/shard_map/ppermute | solution.py:161
  252.7 28.2 %collective-permute-start.47 = (bf16[64,3584]{1,0:T(8,128)(2,1)}, bf16[64,3584]{1,0:T(8,128)(2,1)}, u32[]{:S(2)}, u32[]{:S(2)}) collective-permute-start(bf16[64,3584]{1,0:T(8,128)(2,1)} %collective-permute-done.45.refs_2_), channel_id=1, source_target_pairs={{0,1},{1,0},{2,3},{3,2},{4,5},{5,4},{6,7},{7,6},{8,9},{9,8},{10,11... | collective-permute-start | bytes 1376264 | tf_op jit(solution)/shard_map/ppermute | solution.py:157
  252.7 28.7 %collective-permute-start.51 = (bf16[64,3584]{1,0:T(8,128)(2,1)}, bf16[64,3584]{1,0:T(8,128)(2,1)}, u32[]{:S(2)}, u32[]{:S(2)}) collective-permute-start(bf16[64,3584]{1,0:T(8,128)(2,1)} %collective-permute-done.49.refs_6_), channel_id=1, source_target_pairs={{0,1},{1,0},{2,3},{3,2},{4,5},{5,4},{6,7},{7,6},{8,9},{9,8},{10,11... | collective-permute-start | bytes 1376264 | tf_op jit(solution)/shard_map/ppermute | solution.py:157
  253.2 28.6 %collective-permute-start.65 = (bf16[64,3584]{1,0:T(8,128)(2,1)}, bf16[64,3584]{1,0:T(8,128)(2,1)}, u32[]{:S(2)}, u32[]{:S(2)}) collective-permute-start(bf16[64,3584]{1,0:T(8,128)(2,1)} %collective-permute-done.57.refs_14_), channel_id=1, source_target_pairs={{8,0},{16,8},{24,16},{28,24},{20,28},{12,20},{4,12},{0,4},{9,1},{1... | collective-permute-start | bytes 1376264 | tf_op jit(solution)/shard_map/ppermute | solution.py:186
  281.3 28.5 %collective-permute-start.32 = (bf16[896,512]{1,0:T(8,128)(2,1)S(1)}, bf16[896,512]{1,0:T(8,128)(2,1)S(1)}, u32[]{:S(2)}, u32[]{:S(2)}) collective-permute-start(bf16[896,512]{1,0:T(8,128)(2,1)S(1)} %collective-permute-done.28.refs_2_), channel_id=1, source_target_pairs={{0,8},{8,16},{16,24},{24,28},{28,20},{20,12},{12,4},{4,0},{1,9},{9... | collective-permute-start | bytes 2752520 | tf_op jit(solution)/shard_map/ppermute | solution.py:183
  303.5 28.6 %collective-permute-start.69 = (bf16[64,3584]{1,0:T(8,128)(2,1)}, bf16[64,3584]{1,0:T(8,128)(2,1)S(1)}, u32[]{:S(2)}, u32[]{:S(2)}) collective-permute-start(bf16[64,3584]{1,0:T(8,128)(2,1)} %collective-permute-done.65.refs_22_), channel_id=1, source_target_pairs={{8,0},{16,8},{24,16},{28,24},{20,28},{12,20},{4,12},{0,4},{9,1},{1... | collective-permute-start | bytes 1376264 | tf_op jit(solution)/shard_map/ppermute | solution.py:186
  304.5 28.2 %collective-permute-start.66 = (bf16[64,3584]{1,0:T(8,128)(2,1)}, bf16[64,3584]{1,0:T(8,128)(2,1)S(1)}, u32[]{:S(2)}, u32[]{:S(2)}) collective-permute-start(bf16[64,3584]{1,0:T(8,128)(2,1)} %collective-permute-done.65.refs_22_), channel_id=1, source_target_pairs={{0,2},{2,0},{1,3},{3,1},{4,6},{6,4},{5,7},{7,5},{8,10},{10,8},{9,1... | collective-permute-start | bytes 1376264 | tf_op jit(solution)/shard_map/ppermute | solution.py:161
  306.0 26.2 %collective-permute-start.62 = (bf16[64,3584]{1,0:T(8,128)(2,1)S(1)}, bf16[64,3584]{1,0:T(8,128)(2,1)S(1)}, u32[]{:S(2)}, u32[]{:S(2)}) collective-permute-start(bf16[64,3584]{1,0:T(8,128)(2,1)S(1)} %collective-permute-done.61.refs_18_), channel_id=1, source_target_pairs={{0,2},{2,0},{1,3},{3,1},{4,6},{6,4},{5,7},{7,5},{8,10},{10,8},{9,1... | collective-permute-start | bytes 1376264 | tf_op jit(solution)/shard_map/ppermute | solution.py:161
  348.7 34.4 %collective-permute-start.33 = (bf16[896,512]{1,0:T(8,128)(2,1)S(1)}, bf16[896,512]{1,0:T(8,128)(2,1)S(1)}, u32[]{:S(2)}, u32[]{:S(2)}) collective-permute-start(bf16[896,512]{1,0:T(8,128)(2,1)S(1)} %collective-permute-done.32.refs_6_), channel_id=1, source_target_pairs={{0,1},{1,0},{2,3},{3,2},{4,5},{5,4},{6,7},{7,6},{8,9},{9,8},{10,11... | collective-permute-start | bytes 2752520 | tf_op jit(solution)/shard_map/ppermute | solution.py:157
  695.7 47.1 %collective-permute-start.191 = (f32[3,512]{1,0:T(4,128)S(1)}, f32[3,512]{1,0:T(4,128)S(1)}, u32[]{:S(2)}, u32[]{:S(2)}) collective-permute-start(f32[3,512]{1,0:T(4,128)S(1)} %pad_maximum_fusion.10), channel_id=1, source_target_pairs={{0,4},{4,0},{8,12},{12,8},{16,20},{20,16},{24,28},{28,24},{1,5},{5... | collective-permute-start | bytes 18440 | tf_op jit(solution)/shard_map/ppermute | solution.py:405
  697.4 70.8 %collective-permute-start.161 = (bf16[8,64,1024]{2,1,0:T(8,128)(2,1)}, bf16[8,64,1024]{2,1,0:T(8,128)(2,1)}, u32[]{:S(2)}, u32[]{:S(2)}) collective-permute-start(bf16[8,64,1024]{2,1,0:T(8,128)(2,1)} %constant_dynamic-slice_fusion.2), channel_id=1, source_target_pairs={{0,1},{1,0},{2,3},{3,2},{4,5},{5,4},{6,7},{7,6},{8,9},{9,8},{10,11... | collective-permute-start | bytes 3145736 | tf_op jit(solution)/shard_map/ppermute | solution.py:157
  698.5 31.2 %collective-permute-start.151 = (bf16[8,64,512]{2,1,0:T(8,128)(2,1)}, bf16[8,64,512]{2,1,0:T(8,128)(2,1)}, u32[]{:S(2)}, u32[]{:S(2)}) collective-permute-start(bf16[8,64,512]{2,1,0:T(8,128)(2,1)} %dynamic-slice_bitcast_fusion.5), channel_id=1, source_target_pairs={{0,1},{1,0},{2,3},{3,2},{4,5},{5,4},{6,7},{7,6},{8,9},{9,8},{10,11... | collective-permute-start | bytes 1572872 | tf_op jit(solution)/shard_map/ppermute | solution.py:157
  727.0 35.7 %collective-permute-start.171 = (bf16[8,128,512]{2,1,0:T(8,128)(2,1)}, bf16[8,128,512]{2,1,0:T(8,128)(2,1)S(1)}, u32[]{:S(2)}, u32[]{:S(2)}) collective-permute-start(bf16[8,128,512]{2,1,0:T(8,128)(2,1)} %dynamic-slice_bitcast_fusion.4), channel_id=1, source_target_pairs={{0,1},{1,0},{2,3},{3,2},{4,5},{5,4},{6,7},{7,6},{8,9},{9,8},{10,11... | collective-permute-start | bytes 3145736 | tf_op jit(solution)/shard_map/ppermute | solution.py:157
  759.3 113.2 %collective-permute-start.140 = (bf16[8,64,4096]{2,1,0:T(8,128)(2,1)}, bf16[8,64,4096]{2,1,0:T(8,128)(2,1)}, u32[]{:S(2)}, u32[]{:S(2)}) collective-permute-start(bf16[8,64,4096]{2,1,0:T(8,128)(2,1)} %constant_dynamic-slice_fusion), channel_id=1, source_target_pairs={{0,1},{1,0},{2,3},{3,2},{4,5},{5,4},{6,7},{7,6},{8,9},{9,8},{10,11... | collective-permute-start | bytes 12582920 | tf_op jit(solution)/shard_map/ppermute | solution.py:157
  760.3 96.6 %collective-permute-start.129 = (bf16[8,64,3072]{2,1,0:T(8,128)(2,1)}, bf16[8,64,3072]{2,1,0:T(8,128)(2,1)}, u32[]{:S(2)}, u32[]{:S(2)}) collective-permute-start(bf16[8,64,3072]{2,1,0:T(8,128)(2,1)} %constant_dynamic-slice_fusion.3), channel_id=1, source_target_pairs={{0,1},{1,0},{2,3},{3,2},{4,5},{5,4},{6,7},{7,6},{8,9},{9,8},{10,11... | collective-permute-start | bytes 9437192 | tf_op jit(solution)/shard_map/ppermute | solution.py:157
  761.8 63.4 %collective-permute-start.87 = (bf16[8,384,512]{2,1,0:T(8,128)(2,1)S(1)}, bf16[8,384,512]{2,1,0:T(8,128)(2,1)S(1)}, u32[]{:S(2)}, u32[]{:S(2)}) collective-permute-start(bf16[8,384,512]{2,1,0:T(8,128)(2,1)S(1)} %dynamic-slice_bitcast_fusion.3), channel_id=1, source_target_pairs={{0,1},{1,0},{2,3},{3,2},{4,5},{5,4},{6,7},{7,6},{8,9},{9,8},{10,11... | collective-permute-start | bytes 9437192 | tf_op jit(solution)/shard_map/ppermute | solution.py:157
  831.8 30.0 %collective-permute-start.118 = (bf16[8,384,512]{2,1,0:T(8,128)(2,1)}, bf16[8,384,512]{2,1,0:T(8,128)(2,1)}, u32[]{:S(2)}, u32[]{:S(2)}) collective-permute-start(bf16[8,384,512]{2,1,0:T(8,128)(2,1)} %dynamic-slice_bitcast_fusion.2), channel_id=1, source_target_pairs={{0,1},{1,0},{2,3},{3,2},{4,5},{5,4},{6,7},{7,6},{8,9},{9,8},{10,11... | collective-permute-start | bytes 9437192 | tf_op jit(solution)/shard_map/ppermute | solution.py:157
  831.9 46.0 %collective-permute-start.107 = (bf16[8,512,512]{2,1,0:T(8,128)(2,1)}, bf16[8,512,512]{2,1,0:T(8,128)(2,1)}, u32[]{:S(2)}, u32[]{:S(2)}) collective-permute-start(bf16[8,512,512]{2,1,0:T(8,128)(2,1)} %dynamic-slice_bitcast_fusion), channel_id=1, source_target_pairs={{0,1},{1,0},{2,3},{3,2},{4,5},{5,4},{6,7},{7,6},{8,9},{9,8},{10,11... | collective-permute-start | bytes 12582920 | tf_op jit(solution)/shard_map/ppermute | solution.py:157
  837.0 45.7 %collective-permute-start.97 = (bf16[8,512,512]{2,1,0:T(8,128)(2,1)}, bf16[8,512,512]{2,1,0:T(8,128)(2,1)}, u32[]{:S(2)}, u32[]{:S(2)}) collective-permute-start(bf16[8,512,512]{2,1,0:T(8,128)(2,1)} %dynamic-slice_bitcast_fusion.1), channel_id=1, source_target_pairs={{0,1},{1,0},{2,3},{3,2},{4,5},{5,4},{6,7},{7,6},{8,9},{9,8},{10,11... | collective-permute-start | bytes 12582920 | tf_op jit(solution)/shard_map/ppermute | solution.py:157
  861.7 37.5 %collective-permute-start.130 = (bf16[8,64,1536]{2,1,0:T(8,128)(2,1)}, bf16[8,64,1536]{2,1,0:T(8,128)(2,1)}, u32[]{:S(2)}, u32[]{:S(2)}) collective-permute-start(bf16[8,64,1536]{2,1,0:T(8,128)(2,1)} %add_convert_fusion.8), channel_id=1, source_target_pairs={{0,2},{2,0},{1,3},{3,1},{4,6},{6,4},{5,7},{7,5},{8,10},{10,8},{9,1... | collective-permute-start | bytes 4718600 | tf_op jit(solution)/shard_map/ppermute | solution.py:161
  868.5 64.5 %collective-permute-start.119 = (bf16[8,192,512]{2,1,0:T(8,128)(2,1)}, bf16[8,192,512]{2,1,0:T(8,128)(2,1)}, u32[]{:S(2)}, u32[]{:S(2)}) collective-permute-start(bf16[8,192,512]{2,1,0:T(8,128)(2,1)} %fusion.16), channel_id=1, source_target_pairs={{0,2},{2,0},{1,3},{3,1},{4,6},{6,4},{5,7},{7,5},{8,10},{10,8},{9,1... | collective-permute-start | bytes 4718600 | tf_op jit(solution)/shard_map/ppermute | solution.py:161
  877.9 167.6 %collective-permute-start.141 = (bf16[8,64,2048]{2,1,0:T(8,128)(2,1)}, bf16[8,64,2048]{2,1,0:T(8,128)(2,1)}, u32[]{:S(2)}, u32[]{:S(2)}) collective-permute-start(bf16[8,64,2048]{2,1,0:T(8,128)(2,1)} %add_convert_fusion.5), channel_id=1, source_target_pairs={{0,2},{2,0},{1,3},{3,1},{4,6},{6,4},{5,7},{7,5},{8,10},{10,8},{9,1... | collective-permute-start | bytes 6291464 | tf_op jit(solution)/shard_map/ppermute | solution.py:161
  882.7 165.2 %collective-permute-start.108 = (bf16[8,256,512]{2,1,0:T(8,128)(2,1)}, bf16[8,256,512]{2,1,0:T(8,128)(2,1)S(1)}, u32[]{:S(2)}, u32[]{:S(2)}) collective-permute-start(bf16[8,256,512]{2,1,0:T(8,128)(2,1)} %fusion.13), channel_id=1, source_target_pairs={{0,2},{2,0},{1,3},{3,1},{4,6},{6,4},{5,7},{7,5},{8,10},{10,8},{9,1... | collective-permute-start | bytes 6291464 | tf_op jit(solution)/shard_map/ppermute | solution.py:161
  884.8 50.0 %collective-permute-start.98 = (bf16[512,512]{1,0:T(8,128)(2,1)S(1)}, bf16[512,512]{1,0:T(8,128)(2,1)S(1)}, u32[]{:S(2)}, u32[]{:S(2)}) collective-permute-start(bf16[512,512]{1,0:T(8,128)(2,1)S(1)} %fusion.30), channel_id=1, source_target_pairs={{0,8},{8,16},{16,24},{24,28},{28,20},{20,12},{12,4},{4,0},{1,9},{9... | collective-permute-start | bytes 1572872 | tf_op jit(solution)/shard_map/ppermute | solution.py:183
  899.2 37.8 %collective-permute-start.92 = (bf16[384,512]{1,0:T(8,128)(2,1)S(1)}, bf16[384,512]{1,0:T(8,128)(2,1)S(1)}, u32[]{:S(2)}, u32[]{:S(2)}) collective-permute-start(bf16[384,512]{1,0:T(8,128)(2,1)S(1)} %get-tuple-element.120), channel_id=1, source_target_pairs={{8,0},{16,8},{24,16},{28,24},{20,28},{12,20},{4,12},{0,4},{9,1},{1... | collective-permute-start | bytes 1179656 | tf_op jit(solution)/shard_map/ppermute | solution.py:186
  937.0 32.2 %collective-permute-start.99 = (bf16[512,512]{1,0:T(8,128)(2,1)S(1)}, bf16[512,512]{1,0:T(8,128)(2,1)S(1)}, u32[]{:S(2)}, u32[]{:S(2)}) collective-permute-start(bf16[512,512]{1,0:T(8,128)(2,1)S(1)} %fusion.32), channel_id=1, source_target_pairs={{0,8},{8,16},{16,24},{24,28},{28,20},{20,12},{12,4},{4,0},{1,9},{9... | collective-permute-start | bytes 1572872 | tf_op jit(solution)/shard_map/ppermute | solution.py:183
  940.8 25.4 %collective-permute-start.93 = (bf16[384,512]{1,0:T(8,128)(2,1)S(1)}, bf16[384,512]{1,0:T(8,128)(2,1)S(1)}, u32[]{:S(2)}, u32[]{:S(2)}) collective-permute-start(bf16[384,512]{1,0:T(8,128)(2,1)S(1)} %fusion.44), channel_id=1, source_target_pairs={{8,0},{16,8},{24,16},{28,24},{20,28},{12,20},{4,12},{0,4},{9,1},{1... | collective-permute-start | bytes 1179656 | tf_op jit(solution)/shard_map/ppermute | solution.py:186
  964.4 36.6 %collective-permute-start.91 = (bf16[384,512]{1,0:T(8,128)(2,1)S(1)}, bf16[384,512]{1,0:T(8,128)(2,1)S(1)}, u32[]{:S(2)}, u32[]{:S(2)}) collective-permute-start(bf16[384,512]{1,0:T(8,128)(2,1)S(1)} %get-tuple-element.119), channel_id=1, source_target_pairs={{0,8},{8,16},{16,24},{24,28},{28,20},{20,12},{12,4},{4,0},{1,9},{9... | collective-permute-start | bytes 1179656 | tf_op jit(solution)/shard_map/ppermute | solution.py:183
  976.9 24.5 %collective-permute-start.94 = (bf16[384,512]{1,0:T(8,128)(2,1)S(1)}, bf16[384,512]{1,0:T(8,128)(2,1)S(1)}, u32[]{:S(2)}, u32[]{:S(2)}) collective-permute-start(bf16[384,512]{1,0:T(8,128)(2,1)S(1)} %fusion.46), channel_id=1, source_target_pairs={{8,0},{16,8},{24,16},{28,24},{20,28},{12,20},{4,12},{0,4},{9,1},{1... | collective-permute-start | bytes 1179656 | tf_op jit(solution)/shard_map/ppermute | solution.py:186
  998.0 24.7 %collective-permute-start.101 = (bf16[512,512]{1,0:T(8,128)(2,1)S(1)}, bf16[512,512]{1,0:T(8,128)(2,1)S(1)}, u32[]{:S(2)}, u32[]{:S(2)}) collective-permute-start(bf16[512,512]{1,0:T(8,128)(2,1)S(1)} %get-tuple-element.110), channel_id=1, source_target_pairs={{8,0},{16,8},{24,16},{28,24},{20,28},{12,20},{4,12},{0,4},{9,1},{1... | collective-permute-start | bytes 1572872 | tf_op jit(solution)/shard_map/ppermute | solution.py:186
  1021.1 89.4 %collective-permute-start.100 = (bf16[512,512]{1,0:T(8,128)(2,1)S(1)}, bf16[512,512]{1,0:T(8,128)(2,1)S(1)}, u32[]{:S(2)}, u32[]{:S(2)}) collective-permute-start(bf16[512,512]{1,0:T(8,128)(2,1)S(1)} %get-tuple-element.109), channel_id=1, source_target_pairs={{0,8},{8,16},{16,24},{24,28},{28,20},{20,12},{12,4},{4,0},{1,9},{9... | collective-permute-start | bytes 1572872 | tf_op jit(solution)/shard_map/ppermute | solution.py:183
  1045.5 25.8 %collective-permute-start.96 = (bf16[384,512]{1,0:T(8,128)(2,1)S(1)}, bf16[384,512]{1,0:T(8,128)(2,1)S(1)}, u32[]{:S(2)}, u32[]{:S(2)}) collective-permute-start(bf16[384,512]{1,0:T(8,128)(2,1)S(1)} %add_convert_fusion.16), channel_id=1, source_target_pairs={{0,1},{1,0},{2,3},{3,2},{4,5},{5,4},{6,7},{7,6},{8,9},{9,8},{10,11... | collective-permute-start | bytes 1179656 | tf_op jit(solution)/shard_map/ppermute | solution.py:157
  1066.6 32.4 %collective-permute-start.103 = (bf16[512,512]{1,0:T(8,128)(2,1)S(1)}, bf16[512,512]{1,0:T(8,128)(2,1)S(1)}, u32[]{:S(2)}, u32[]{:S(2)}) collective-permute-start(bf16[512,512]{1,0:T(8,128)(2,1)S(1)} %fusion.27), channel_id=1, source_target_pairs={{8,0},{16,8},{24,16},{28,24},{20,28},{12,20},{4,12},{0,4},{9,1},{1... | collective-permute-start | bytes 1572872 | tf_op jit(solution)/shard_map/ppermute | solution.py:186
  (361 other events, 4523.5 us)

commit v2 on v0

v2 whole, which is shorter than its diff:
```python
import functools
import math

import jax
import jax.numpy as jnp
from jax import lax
from jax.experimental import pallas as pl
from jax.experimental.pallas import tpu as pltpu
from jax.sharding import PartitionSpec as P

STRIDES = (12, 16)
WINDOW = 25
HALF = WINDOW // 2
GROUP = 4
BF = jnp.bfloat16
F32 = jnp.float32
MIB = 1024 * 1024
CORE_SWAP = ((0, 1), (1, 0), (2, 3), (3, 2))
Y_SWAP = ((0, 2), (2, 0), (1, 3), (3, 1))


class Layout:
    def __init__(self, n, width, block_len, ff):
        self.n, self.width, self.block_len = n, width, block_len
        self.length = GROUP * block_len
        self.taps = tuple(block_len // s for s in STRIDES)
        self.shrink = tuple(s * width for s in STRIDES)
        self.iso = tuple(p * width for p in self.taps)
        self.si_half = (self.shrink[0] + self.iso[0]) // (2 * n)
        self.k = width // n
        self.g_half = max(STRIDES) // 2 * self.k
        self.chunks = ff // width
        self.merge, self.contract = 2 * width // n, ff // n
        self.f_half = max(self.contract + self.merge, self.k * (1 + self.chunks))
        self.npos = tuple(GROUP * p for p in self.taps)

    def si_parts(self, b):
        s, i = self.shrink[b] // self.n, self.iso[b] // self.n
        return [(0, s // 2, 0, s), (s // 2, i // 2, self.shrink[b], i)]

    def g_parts(self, b):
        return [(j * self.k, self.k, j) for j in range(STRIDES[b] // 2)]

    def f_parts(self, h):
        base = self.g_half
        if h == 0:
            return [
                (base, self.contract, "contract", 0),
                (base + self.contract, self.merge, "merge", 0),
            ]
        found = [(base, self.k, "trend", 0)]
        for j in range(self.chunks):
            found.append((base + (1 + j) * self.k, self.k, "expand", j))
        return found


def held(*values):
    return lax.optimization_barrier(values)


class Ring:
    def __init__(self, n):
        self.n = n
        order = list(range(0, n, 2)) + list(range(n - 1, 0, -2))
        self.right = [(order[k], order[(k + 1) % n]) for k in range(n)]
        self.left = [(b, a) for a, b in self.right]
        d = lax.axis_index("dp")
        self.me = d
        self.pos = jnp.where(d % 2 == 0, d // 2, n - 1 - d // 2)

    def index(self, offset):
        if offset == 0:
            return self.me
        r = (self.pos + offset) % self.n
        return jnp.where(r < self.n // 2, 2 * r, 2 * (self.n - 1 - r) + 1)


def slot(sends, work=None, given=()):
    names = list(sends)
    tied = held(*[sends[k][0] for k in names], *given)
    moved = [sends[k][1](v) for k, v in zip(names, tied)]
    done = tuple(work(*tied[len(names) :])) if work is not None else ()
    out = held(*moved, *done)
    return dict(zip(names, out[: len(names)])), out[len(names) :]


def swap_core(v):
    return lax.ppermute(v, "group", CORE_SWAP)


def swap_y(v):
    return lax.ppermute(v, "group", Y_SWAP)


def dot(a, b):
    return jnp.dot(a, b, preferred_element_type=F32)


def dot_t(a, b):
    return lax.dot_general(a, b, (((1,), (1,)), ((), ())), preferred_element_type=F32)


def dot_w(a, b):
    return lax.dot_general(a, b, (((0,), (0,)), ((), ())), preferred_element_type=F32)


def normal(v):
    center = jnp.mean(v, axis=-1, keepdims=True)
    centered = v - center
    inverse = lax.rsqrt(jnp.mean(centered * centered, axis=-1, keepdims=True) + 1e-05)
    return centered * inverse, inverse


def normal_back(grad, hat, inverse, gain):
    g = grad * gain
    a = jnp.mean(g, axis=-1, keepdims=True)
    b = jnp.mean(g * hat, axis=-1, keepdims=True)
    return inverse * (g - a - hat * b)


def erf_pair(h):
    x = jnp.abs(h) * (1.0 / math.sqrt(2.0))
    d = 1.0 + 0.3275911 * x
    t = pl.reciprocal(d, approx=True)
    t = t * (2.0 - d * t)
    e = jnp.exp(-0.5 * h * h)
    p = t * (
        0.254829592
        + t * (-0.284496736 + t * (1.421413741 + t * (-1.453152027 + t * 1.061405429)))
    )
    q = 0.5 * p * e
    return jnp.where(h >= 0, 1.0 - q, q), h * e * (1.0 / math.sqrt(2.0 * math.pi))


def over(parts, first, rows):
    for part in parts:
        lo, hi = max(first, part[0]), min(first + rows, part[0] + part[1])
        if lo < hi:
            yield lo - first, hi - lo, lo - part[0], part


def start_copy(piece, row, rows, whole, at, sem):
    at = at if isinstance(at, int) else pl.multiple_of(at, 16)
    pltpu.make_async_copy(
        piece.at[pl.ds(row, rows)], whole.at[pl.ds(at, rows)], sem
    ).start()


def wait_rows(whole, first, rows, sem):
    view = whole.at[pl.ds(first, rows)]
    pltpu.make_async_copy(view, view, sem).wait()


class Pieces:
    def __init__(self):
        self.meta, self.arrays = [], []

    def add(self, source, other, first, array):
        self.meta.append((source, other, first, array.shape[0]))
        self.arrays.append(array)


def load_si(lay, b, where, meta, refs, whole, sems):
    core = where[1]
    for (source, other, first, rows), ref in zip(meta, refs):
        src = where[2 + source]
        h = 1 - core if other else core
        for row, count, inside, part in over(lay.si_parts(b), first, rows):
            _, half, base, shard = part
            at = base + src * shard + h * half + inside
            start_copy(ref, row, count, whole, at, sems.at[0 if base == 0 else 1])


def load_g(lay, b, where, meta, refs, whole, sem):
    core = where[1]
    for (source, other, first, rows), ref in zip(meta, refs):
        src = where[2 + source]
        h = 1 - core if other else core
        for row, count, inside, part in over(lay.g_parts(b), first, rows):
            at = (h * (STRIDES[b] // 2) + part[2]) * lay.width + src * lay.k + inside
            start_copy(ref, row, count, whole, at, sem)


def load_f(lay, c, where, meta, refs, wholes, sems):
    names = ("merge", "contract", "trend", "expand")
    for (source, other, first, rows), ref in zip(meta, refs):
        src = where[2 + source]
        h = 1 - c if other else c
        for row, count, inside, part in over(lay.f_parts(h), first, rows):
            t = names.index(part[2])
            at = part[3] * lay.width + src * part[1] + inside
            start_copy(ref, row, count, wholes[t], at, sems.at[t])


def any_spec():
    return pl.BlockSpec(memory_space=pl.ANY)


def vmem_spec():
    return pl.BlockSpec(memory_space=pltpu.VMEM)


def smem_spec():
    return pl.BlockSpec(memory_space=pltpu.SMEM)


def cost(flops, moved):
    return pl.CostEstimate(flops=int(flops), bytes_accessed=int(moved), transcendentals=0)


def by_branch(where, body):
    for b in range(2):
        pl.when(where[0] == b)(functools.partial(body, b))


def tap_rows(x, age, k):
    if k == 0:
        return x
    return jnp.where(age >= k, pltpu.roll(x, k, 0), 0.0)


def shrink_forward(lay, where, si, season_low, age, gain):
    n, width = lay.n, lay.width
    groups = season_low.shape[0]
    most = groups * max(lay.npos)
    count = len(si.arrays)

    def kernel(where, age_ref, gain_ref, season_ref, *refs):
        pieces, (shrunk_ref, iso_ref, mixed_ref, whole, sems) = refs[:count], refs[count:]

        def body(b):
            load_si(lay, b, where, si.meta, pieces, whole, sems)
            npos = lay.npos[b]
            m = groups * npos
            wait_rows(whole, 0, lay.shrink[b], sems.at[0])
            z = jnp.zeros((m, width), F32)
            for s in range(STRIDES[b]):
                x = season_ref[:, s * npos : (s + 1) * npos, :].reshape(m, width)
                z += dot(x, whole[s * width : (s + 1) * width])
            shrunk = jnp.tanh(z)
            shrunk_ref[:m] = shrunk
            low = shrunk.astype(BF).astype(F32)
            wait_rows(whole, lay.shrink[b], lay.iso[b], sems.at[1])
            taps = lay.taps[b]
            base = lay.shrink[b]
            age = age_ref[:m]
            e = jnp.zeros((m, width), F32)
            for k in range(taps):
                at = base + (taps - 1 - k) * width
                e += dot(tap_rows(low, age, k).astype(BF), whole[at : at + width])
            iso = jnp.tanh(e)
            iso_ref[:m] = iso
            hat, _ = normal(iso + shrunk)
            mixed_ref[:m] = (hat * gain_ref[...]).astype(BF)

        by_branch(where, body)

    total = lay.shrink[0] + lay.iso[0]
    return pl.pallas_call(
        kernel,
        out_shape=[
            jax.ShapeDtypeStruct((most, width), F32),
            jax.ShapeDtypeStruct((most, width), F32),
            jax.ShapeDtypeStruct((most, width), BF),
        ],
        in_specs=[smem_spec(), vmem_spec(), vmem_spec(), vmem_spec()] + [any_spec()] * count,
        out_specs=[vmem_spec()] * 3,
        scratch_shapes=[pltpu.VMEM((total, width), BF), pltpu.SemaphoreType.DMA((2,))],
        compiler_params=pltpu.CompilerParams(vmem_limit_bytes=44 * MIB),
        cost_estimate=cost(2 * most * width * total, 2 * total * width),
        name="shrink_forward",
    )(where, age, gain, season_low, *si.arrays)


def grow_forward(lay, where, gf, part, mixed, season, order, gain):
    width = lay.width
    groups = season.shape[0] // 2
    length = lay.length
    count = len(gf.arrays)

    def kernel(where, gain_ref, order_ref, mixed_ref, season_ref, *refs):
        pieces, (out_ref, up_ref, whole, rows_ref, sem) = refs[:count], refs[count:]

        def body(b):
            load_g(lay, b, where, gf.meta, pieces, whole, sem)
            npos = lay.npos[b]
            m = groups * npos
            x = mixed_ref[part * m : (part + 1) * m]
            wait_rows(whole, 0, STRIDES[b] * width, sem)
            for s in range(STRIDES[b]):
                cut = slice(s * npos, (s + 1) * npos)
                up = jnp.tanh(dot(x, whole[s * width : (s + 1) * width]))
                up_ref[:, cut, :] = up.reshape(groups, npos, width)
                hat, _ = normal(up + season_ref[:, cut, :].reshape(m, width))
                rows_ref[:, cut, :] = (hat * gain_ref[...]).astype(BF).reshape(groups, npos, width)

        by_branch(where, body)
        for g in range(groups):
            out_ref[g] = dot_w(order_ref[...], rows_ref[g]).astype(BF)

    most = max(STRIDES) * width
    return pl.pallas_call(
        kernel,
        grid=(1,),
        out_shape=[
            jax.ShapeDtypeStruct((groups, length, width), BF),
            jax.ShapeDtypeStruct((groups, length, width), F32),
        ],
        in_specs=[
            smem_spec(),
            vmem_spec(),
            vmem_spec(),
            vmem_spec(),
            pl.BlockSpec((groups, length, width), lambda g: (part, 0, 0)),
        ]
        + [any_spec()] * count,
        out_specs=[vmem_spec()] * 2,
        scratch_shapes=[
            pltpu.VMEM((most, width), BF),
            pltpu.VMEM((groups, length, width), BF),
            pltpu.SemaphoreType.DMA,
        ],
        compiler_params=pltpu.CompilerParams(vmem_limit_bytes=52 * MIB),
        cost_estimate=cost(
            2 * groups * length * width * (width + length), 2 * most * width + 14 * groups * length * width
        ),
        name="grow_forward",
    )(where, gain, order, mixed, season, *gf.arrays)


def grow_backward(lay, where, gf, part, grad, up, season, order, gain):
    width = lay.width
    groups = season.shape[0] // 2
    length = lay.length
    count = len(gf.arrays)
    most = groups * max(lay.npos)

    def kernel(where, gain_ref, order_ref, grad_ref, up_ref, season_ref, *refs):
        pieces, rest = refs[:count], refs[count:]
        (pre_ref, back_ref, sum_ref, gain_grad_ref, whole, rows_ref, sem) = rest

        def order_rows():
            for g in range(groups):
                rows_ref[g] = dot(order_ref[...], grad_ref[g]).astype(BF)

        def body(b):
            load_g(lay, b, where, gf.meta, pieces, whole, sem)
            order_rows()
            npos = lay.npos[b]
            m = groups * npos
            wait_rows(whole, 0, STRIDES[b] * width, sem)
            total = jnp.zeros((m, width), F32)
            gains = jnp.zeros((1, width), F32)
            for s in range(STRIDES[b]):
                cut = slice(s * npos, (s + 1) * npos)
                up = up_ref[:, cut, :].reshape(m, width)
                hat, inverse = normal(up + season_ref[:, cut, :].reshape(m, width))
                g = rows_ref[:, cut, :].reshape(m, width).astype(F32)
                gains += jnp.sum(g * hat, axis=0, keepdims=True)
                d = normal_back(g, hat, inverse, gain_ref[...])
                sum_ref[:, cut, :] = d.reshape(groups, npos, width)
                pre = (d * (1.0 - up * up)).astype(BF)
                pre_ref[:, cut, :] = pre.reshape(groups, npos, width)
                total += dot_t(pre, whole[s * width : (s + 1) * width])
            back_ref[:m] = total
            gain_grad_ref[...] = gains

        by_branch(where, body)

    whole_rows = max(STRIDES) * width
    return pl.pallas_call(
        kernel,
        grid=(1,),
        out_shape=[
            jax.ShapeDtypeStruct((groups, length, width), BF),
            jax.ShapeDtypeStruct((most, width), F32),
            jax.ShapeDtypeStruct((groups, length, width), F32),
            jax.ShapeDtypeStruct((1, width), F32),
        ],
        in_specs=[
            smem_spec(),
            vmem_spec(),
            vmem_spec(),
            vmem_spec(),
            vmem_spec(),
            pl.BlockSpec((groups, length, width), lambda g: (part, 0, 0)),
        ]
        + [any_spec()] * count,
        out_specs=[vmem_spec()] * 4,
        scratch_shapes=[
            pltpu.VMEM((whole_rows, width), BF),
            pltpu.VMEM((groups, length, width), BF),
            pltpu.SemaphoreType.DMA,
        ],
        compiler_params=pltpu.CompilerParams(vmem_limit_bytes=58 * MIB),
        cost_estimate=cost(
            2 * groups * length * width * (width + length),
            2 * whole_rows * width + 18 * groups * length * width,
        ),
        name="grow_backward",
    )(where, gain, order, grad, up, season, *gf.arrays)


def grow_weight(lay, where, places, mixed, pre_own, pre_other):
    n, width, k = lay.n, lay.width, lay.k
    groups = pre_own.shape[0]

    def kernel(where, places_ref, mixed_ref, own_ref, other_ref, out_ref):
        def body(b):
            npos = lay.npos[b]
            m = groups * npos
            x0, x1 = mixed_ref[:m], mixed_ref[m : 2 * m]
            steps = STRIDES[b] // 2
            for s in range(STRIDES[b]):
                cut = slice(s * npos, (s + 1) * npos)
                d = dot_w(x0, own_ref[:, cut, :].reshape(m, width))
                d += dot_w(x1, other_ref[:, cut, :].reshape(m, width))
                side = jnp.where(where[1] == s // steps, 0, 1)
                at = (s % steps) * k
                for shard in range(n):
                    out_ref[side, places_ref[shard], at : at + k, :] = d[
                        shard * k : (shard + 1) * k
                    ].astype(BF)
            rest = lay.g_half - steps * k
            if rest:
                out_ref[:, :, steps * k :, :] = jnp.zeros((2, n, rest, width), BF)

        by_branch(where, body)

    return pl.pallas_call(
        kernel,
        out_shape=jax.ShapeDtypeStruct((2, n, lay.g_half, width), BF),
        in_specs=[smem_spec(), smem_spec()] + [vmem_spec()] * 3,
        out_specs=vmem_spec(),
        compiler_params=pltpu.CompilerParams(vmem_limit_bytes=44 * MIB),
        cost_estimate=cost(4 * groups * lay.length * width * width, 2 * 2 * n * lay.g_half * width),
        name="grow_weight",
    )(where, places, mixed, pre_own, pre_other)


def shrink_backward(lay, where, places, si, back_own, back_other, shrunk, iso, season_low, age, gain):
    n, width = lay.n, lay.width
    most = shrunk.shape[0]
    groups = season_low.shape[0]
    count = len(si.arrays)

    def kernel(where, places_ref, age_ref, gain_ref, b0, b1, shrunk_ref, iso_ref, season_ref, *refs):
        pieces, (pre_ref, grad_ref, gain_grad_ref, whole, sems) = refs[:count], refs[count:]

        def body(b):
            load_si(lay, b, where, si.meta, pieces, whole, sems)
            npos, taps = lay.npos[b], lay.taps[b]
            m = groups * npos
            mixed_back = jnp.concatenate([b0[: m // 2], b1[: m // 2]], axis=0)
            shrunk, iso = shrunk_ref[:m], iso_ref[:m]
            hat, inverse = normal(iso + shrunk)
            gain_grad_ref[...] = jnp.sum(mixed_back * hat, axis=0, keepdims=True)
            joint = normal_back(mixed_back, hat, inverse, gain_ref[...])
            iso_pre = (joint * (1.0 - iso * iso)).astype(BF)
            low = shrunk.astype(BF).astype(F32)
            age = age_ref[:m]

            def store(part, row, d):
                first, half, _, shard = part
                lo = row
                while lo < row + width:
                    dp, h, r = lo // shard, (lo % shard) // half, lo % half
                    rows = min(half - r, row + width - lo)
                    side = jnp.where(where[1] == h, 0, 1)
                    grad_ref[side, places_ref[dp], first + r : first + r + rows, :] = d[
                        lo - row : lo - row + rows
                    ].astype(BF)
                    lo += rows

            part_s, part_i = lay.si_parts(b)
            base = lay.shrink[b]
            wait_rows(whole, 0, base, sems.at[0])
            wait_rows(whole, base, lay.iso[b], sems.at[1])
            total = joint
            for k in range(taps):
                tap = taps - 1 - k
                back = dot_t(iso_pre, whole[base + tap * width : base + (tap + 1) * width])
                if k:
                    back = pltpu.roll(jnp.where(age >= k, back, 0.0), m - k, 0)
                total += back
                store(part_i, tap * width, dot_w(tap_rows(low, age, k).astype(BF), iso_pre))
            pre = (total * (1.0 - shrunk * shrunk)).astype(BF)
            pre_ref[:m] = pre
            for s in range(STRIDES[b]):
                x = season_ref[:, s * npos : (s + 1) * npos, :].reshape(m, width)
                store(part_s, s * width, dot_w(x, pre))

        by_branch(where, body)

    total = lay.shrink[0] + lay.iso[0]
    return pl.pallas_call(
        kernel,
        out_shape=[
            jax.ShapeDtypeStruct((most, width), BF),
            jax.ShapeDtypeStruct((2, n, lay.si_half, width), BF),
            jax.ShapeDtypeStruct((1, width), F32),
        ],
        in_specs=[smem_spec(), smem_spec()] + [vmem_spec()] * 7 + [any_spec()] * count,
        out_specs=[vmem_spec()] * 3,
        scratch_shapes=[pltpu.VMEM((total, width), BF), pltpu.SemaphoreType.DMA((2,))],
        compiler_params=pltpu.CompilerParams(vmem_limit_bytes=58 * MIB),
        cost_estimate=cost(6 * most * width * total // 2, 4 * total * width),
        name="shrink_backward",
    )(where, places, age, gain, back_own, back_other, shrunk, iso, season_low, *si.arrays)


def season_backward(lay, where, si, pre, sum_own, sum_other, order):
    width, length = lay.width, lay.length
    groups = sum_own.shape[0]
    count = len(si.arrays)

    def kernel(where, order_ref, pre_ref, own_ref, other_ref, *refs):
        pieces, (own_out, other_out, whole, rows_ref, sems) = refs[:count], refs[count:]

        def body(b):
            core = where[1]
            npos = lay.npos[b]
            m = groups * npos
            parts = lay.si_parts(b)[:1]
            for (source, other, first, rows), ref in zip(si.meta, pieces):
                src = where[2 + source]
                h = 1 - core if other else core
                for row, rows_in, inside, part in over(parts, first, rows):
                    at = src * part[3] + h * part[1] + inside
                    start_copy(ref, row, rows_in, whole, at, sems)
            wait_rows(whole, 0, lay.shrink[b], sems)
            for s in range(STRIDES[b]):
                cut = slice(s * npos, (s + 1) * npos)
                d = dot_t(pre_ref[: 2 * m], whole[s * width : (s + 1) * width])
                rows_ref[:groups, cut, :] = (
                    d[:m].reshape(groups, npos, width) + own_ref[:, cut, :]
                ).astype(BF)
                rows_ref[groups:, cut, :] = (
                    d[m:].reshape(groups, npos, width) + other_ref[:, cut, :]
                ).astype(BF)

        by_branch(where, body)
        for g in range(groups):
            own_out[g] = dot_w(order_ref[...], rows_ref[g]).astype(BF)
            other_out[g] = dot_w(order_ref[...], rows_ref[groups + g]).astype(BF)

    most = max(lay.shrink)
    return pl.pallas_call(
        kernel,
        out_shape=[jax.ShapeDtypeStruct((groups, length, width), BF)] * 2,
        in_specs=[smem_spec()] + [vmem_spec()] * 4 + [any_spec()] * count,
        out_specs=[vmem_spec()] * 2,
        scratch_shapes=[
            pltpu.VMEM((most, width), BF),
            pltpu.VMEM((2 * groups, length, width), BF),
            pltpu.SemaphoreType.DMA,
        ],
        compiler_params=pltpu.CompilerParams(vmem_limit_bytes=52 * MIB),
        cost_estimate=cost(
            4 * groups * length * width * (width + length), 2 * most * width + 24 * groups * length * width
        ),
        name="season_backward",
    )(where, order, pre, sum_own, sum_other, *si.arrays)


def dense(lay, where, gf, tile, mine, received, trend_low, out_grad, gain_middle, gain_output):
    width, length, chunks = lay.width, lay.length, lay.chunks
    count = len(gf.arrays)
    part = length // 2
    ff = width * chunks

    def kernel(where, gm_ref, go_ref, mine_ref, got_ref, trend_ref, grad_ref, *refs):
        pieces, rest = refs[:count], refs[count:]
        (out_ref, jm_ref, js_ref, tb_ref, ml_ref, hid_ref, hg_ref, ll_ref, mg_ref) = rest[:9]
        (gains_ref, merge, contract, trend, expand, slope_ref, sems) = rest[9:]
        for c in range(2):
            pl.when(where[1] == c)(
                functools.partial(
                    load_f, lay, c, where, gf.meta, pieces, (merge, contract, trend, expand), sems
                )
            )
        b = where[0]
        for t, (w, rows) in enumerate(
            ((merge, 2 * width), (contract, ff), (trend, width), (expand, ff))
        ):
            wait_rows(w, 0, rows, sems.at[t])
        gm, go = gm_ref[...], go_ref[...]
        at_mine = pl.multiple_of(b * width, width)
        at_other = pl.multiple_of((1 - b) * width, width)

        def block(i, gains):
            rows = pl.ds(pl.multiple_of(i * part, part), part)
            merged = dot(mine_ref[0, rows, :], merge[pl.ds(at_mine, width)])
            merged += dot(got_ref[0, rows, :], merge[pl.ds(at_other, width)])
            mhat, minv = normal(merged)
            middle = mhat * gm
            mlow = middle.astype(BF)
            ml_ref[rows, :] = mlow
            lifted = jnp.zeros((part, width), F32)
            for j in range(chunks):
                cols = slice(j * width, (j + 1) * width)
                h = dot(mlow, expand[cols])
                phi, dens = erf_pair(h)
                hid = (h * phi).astype(BF)
                slope_ref[:, cols] = phi + dens
                hid_ref[rows, cols] = hid
                lifted += dot(hid, contract[cols])
            ohat, oinv = normal(middle + lifted)
            g_low = grad_ref[0, rows, :]
            projected = dot(trend_ref[0, rows, :], trend[...])
            out_ref[rows, :] = (ohat * go + projected).astype(BF)
            g = g_low.astype(F32)
            tb_ref[rows, :] = dot_t(g_low, trend[...])
            d = normal_back(g, ohat, oinv, go)
            llow = d.astype(BF)
            ll_ref[rows, :] = llow
            back = d
            for j in range(chunks):
                cols = slice(j * width, (j + 1) * width)
                hg = (dot_t(llow, contract[cols]) * slope_ref[:, cols]).astype(BF)
                hg_ref[rows, cols] = hg
                back += dot_t(hg, expand[cols])
            mg = normal_back(back, mhat, minv, gm).astype(BF)
            mg_ref[rows, :] = mg
            jm_ref[rows, :] = dot_t(mg, merge[pl.ds(at_mine, width)]).astype(BF)
            js_ref[rows, :] = dot_t(mg, merge[pl.ds(at_other, width)]).astype(BF)
            return (
                gains[0] + jnp.sum(back * mhat, axis=0, keepdims=True),
                gains[1] + jnp.sum(g * ohat, axis=0, keepdims=True),
            )

        zero = jnp.zeros((1, width), F32)
        a, c = lax.fori_loop(0, length // part, block, (zero, zero))
        gains_ref[0:1, :] = a
        gains_ref[1:2, :] = c

    block_spec = pl.BlockSpec((1, length, width), lambda g: (tile, 0, 0))
    whole_spec = pl.BlockSpec((1, length, width), lambda g: (0, 0, 0))
    shapes = [(width, BF)] * 3 + [(width, F32), (width, BF), (ff, BF), (ff, BF), (width, BF), (width, BF)]
    return pl.pallas_call(
        kernel,
        grid=(1,),
        out_shape=[jax.ShapeDtypeStruct((length, w), t) for w, t in shapes]
        + [jax.ShapeDtypeStruct((2, width), F32)],
        in_specs=[
            smem_spec(),
            vmem_spec(),
            vmem_spec(),
            block_spec,
            whole_spec,
            block_spec,
            block_spec,
        ]
        + [any_spec()] * count,
        out_specs=[vmem_spec()] * 10,
        scratch_shapes=[
            pltpu.VMEM((2 * width, width), BF),
            pltpu.VMEM((ff, width), BF),
            pltpu.VMEM((width, width), BF),
            pltpu.VMEM((ff, width), BF),
            pltpu.VMEM((part, ff), F32),
            pltpu.SemaphoreType.DMA((4,)),
        ],
        compiler_params=pltpu.CompilerParams(vmem_limit_bytes=56 * MIB),
        cost_estimate=cost(
            2 * length * width * (4 * width + 4 * ff + 2 * width), 12 * MIB + 20 * MIB
        ),
        name="dense_%d" % tile,
    )(where, gain_middle, gain_output, mine, received, trend_low, out_grad, *gf.arrays)


def dense_weights(lay, where, places, mine, received, trend_low, out_grad, saved):
    n, width, chunks, length = lay.n, lay.width, lay.chunks, lay.length
    groups = len(saved)

    def kernel(where, places_ref, mine_ref, trend_ref, grad_ref, *refs):
        got = refs[:groups]
        kept = [refs[groups + 5 * g : groups + 5 * (g + 1)] for g in range(groups)]
        out_ref = refs[-1]
        core = where[1]

        def store(h, first, shard, row, d):
            side = jnp.where(core == h, 0, 1)
            lo = row
            while lo < row + d.shape[0]:
                dp, r = lo // shard, lo % shard
                rows = min(shard - r, row + d.shape[0] - lo)
                out_ref[side, places_ref[dp], first + r : first + r + rows, :] = d[
                    lo - row : lo - row + rows
                ].astype(BF)
                lo += rows

        def total(pairs):
            d = None
            for x, g in pairs:
                v = dot_w(x, g)
                d = v if d is None else d + v
            return d

        base = -lay.g_half
        for h in range(2):
            used = 0
            for first, rows, name, j in lay.f_parts(h):
                first += base
                used = first + rows
                if name == "contract":
                    for q in range(chunks):
                        cols = slice(q * width, (q + 1) * width)
                        d = total([(k[1][:, cols], k[3][...]) for k in kept])
                        store(h, first, rows, q * width, d)
                elif name == "merge":
                    for q in range(2):
                        first_half = where[0] == q

                        def one(arrays, q=q, first=first, rows=rows):
                            store(h, first, rows, q * width, total(list(zip(arrays, [k[4][...] for k in kept]))))

                        pl.when(first_half)(lambda: one([mine_ref[g] for g in range(groups)]))
                        pl.when(jnp.logical_not(first_half))(lambda: one([v[0] for v in got]))
                elif name == "trend":
                    d = total([(trend_ref[g], grad_ref[g]) for g in range(groups)])
                    store(h, first, rows, 0, d)
                else:
                    cols = slice(j * width, (j + 1) * width)
                    d = total([(k[0][...], k[2][:, cols]) for k in kept])
                    store(h, first, rows, 0, d)
            rest = lay.f_half - used
            if rest:
                side = jnp.where(core == h, 0, 1)
                out_ref[side, :, used:, :] = jnp.zeros((n, rest, width), BF)

    flat = [v for s in saved for v in s]
    ff = chunks * width
    return pl.pallas_call(
        kernel,
        out_shape=jax.ShapeDtypeStruct((2, n, lay.f_half, width), BF),
        in_specs=[smem_spec(), smem_spec()] + [vmem_spec()] * (3 + groups + len(flat)),
        out_specs=vmem_spec(),
        compiler_params=pltpu.CompilerParams(vmem_limit_bytes=58 * MIB),
        cost_estimate=cost(
            2 * groups * length * width * (2 * width + 2 * ff + width), 45 * MIB
        ),
        name="dense_weights",
    )(where, places, mine, trend_low, out_grad, *received, *flat)


def series_bounds(kinds):
    follows = kinds == 2
    start = jnp.zeros_like(kinds[:, 0])
    firsts = []
    for b in range(GROUP):
        start = jnp.where(follows[:, b], start, b) if b else start
        firsts.append(start)
    stop = jnp.full_like(start, GROUP - 1)
    lasts = [stop]
    for b in reversed(range(GROUP - 1)):
        stop = jnp.where(follows[:, b + 1], stop, b)
        lasts.append(stop)
    return jnp.stack(firsts, 1), jnp.stack(lasts[::-1], 1)


def pick(table, block):
    found = jnp.zeros((table.shape[0], block.shape[0]), table.dtype)
    for b in range(GROUP):
        found = jnp.where(block[None, :] == b, table[:, b : b + 1], found)
    return found


def window_counts(kinds, block_len, step):
    firsts, lasts = series_bounds(kinds)
    length = GROUP * block_len
    block = step // block_len
    first = pick(firsts, block)[:, :, None] * block_len
    last = pick(lasts, block)[:, :, None] * block_len + (block_len - 1)
    i = step[None, :, None]
    j = jnp.arange(length, dtype=jnp.int32)[None, None, :]
    count = ((jnp.abs(i - j) <= HALF) & (j >= first) & (j <= last)).astype(jnp.int32)
    count += jnp.where(j == first, jnp.maximum(first - i + HALF, 0), 0)
    count += jnp.where(j == last, jnp.maximum(i + HALF - last, 0), 0)
    return count.astype(F32).astype(BF)


def exchange(axis, size, step):
    return lambda v: lax.ppermute(v, axis, [(i, i ^ step) for i in range(size)])


def on_device(
    n,
    series_in,
    block_kinds,
    out_grad,
    fine_shrink,
    coarse_shrink,
    fine_isometric,
    coarse_isometric,
    fine_grow,
    coarse_grow,
    merge_weight,
    expand_weight,
    contract_weight,
    trend_weight,
    branch_gain,
    middle_gain,
    output_gain,
):
    ring = Ring(n)
    member = lax.axis_index("group")
    core, y = member % 2, member // 2
    block_count = block_kinds.shape[0]
    width = series_in.shape[1]
    block_len = series_in.shape[0] // block_count
    groups = block_count // GROUP
    lay = Layout(n, width, block_len, expand_weight.shape[1])
    length = lay.length
    share = branch_gain.shape[0]
    fine = y == 0

    def right(v):
        return lax.ppermute(v, "dp", ring.right)

    def left(v):
        return lax.ppermute(v, "dp", ring.left)

    def cut(v, h, rows):
        return lax.dynamic_slice_in_dim(v, h * rows, rows, axis=0)

    def si_half(h):
        s, i = (STRIDES[0] * width // n) // 2, (lay.taps[0] * width // n) // 2
        s2, i2 = (STRIDES[1] * width // n) // 2, (lay.taps[1] * width // n) // 2
        return jnp.where(
            fine,
            jnp.concatenate([cut(fine_shrink, h, s), cut(fine_isometric, h, i)]),
            jnp.concatenate([cut(coarse_shrink, h, s2), cut(coarse_isometric, h, i2)]),
        )

    def blocks_of(v, first, count):
        v = lax.dynamic_slice_in_dim(v, first * width, count * width, axis=1)
        return jnp.concatenate([v[:, j * width : (j + 1) * width] for j in range(count)])

    def gf_half(h):
        a, b = STRIDES[0] // 2, STRIDES[1] // 2
        fine_part = blocks_of(fine_grow, h * a, a)
        fine_part = jnp.pad(fine_part, ((0, lay.g_half - fine_part.shape[0]), (0, 0)))
        grow = jnp.where(fine, fine_part, blocks_of(coarse_grow, h * b, b))
        first = jnp.concatenate([contract_weight, merge_weight])
        second = jnp.concatenate([trend_weight, blocks_of(expand_weight, 0, lay.chunks)])
        first = jnp.pad(first, ((0, lay.f_half - first.shape[0]), (0, 0)))
        second = jnp.pad(second, ((0, lay.f_half - second.shape[0]), (0, 0)))
        return jnp.concatenate([grow, jnp.where(h == 0, first, second)])

    si_own, gf_own = si_half(core), gf_half(core)
    offsets = [0]
    si, gf = Pieces(), Pieces()
    si.add(0, 0, 0, si_own)
    si.add(0, 1, 0, si_half(1 - core))
    gf.add(0, 0, 0, gf_own)
    gf.add(0, 1, 0, gf_half(1 - core))
    for k in range(1, n // 2):
        offsets += [-k, k]
    offsets.append(n // 2)

    def source(offset):
        return offsets.index(offset if abs(offset) < n // 2 else n // 2)

    where = jnp.stack([y, core] + [ring.index(o) for o in offsets]).astype(jnp.int32)

    gains = jnp.stack([branch_gain, middle_gain, output_gain]).astype(F32)
    gains = lax.dynamic_update_slice(
        jnp.zeros((3, width), F32), gains, (jnp.int32(0), ring.me * share)
    )
    x_own = series_in.reshape(groups, length, width)
    kinds_own = block_kinds.reshape(groups, GROUP)
    x_other = []
    kinds_other = None
    last = n // 2
    ways = {"r": {}, "l": {}}
    got = {}
    si_r = si_l = si_own
    gf_r = gf_l = gf_own
    step_index = 1
    prepared = None
    hat_rows = lay.si_half // 2
    gf_rows = (lay.g_half + lay.f_half) // 2

    def prepare(kinds_other, *xs):
        other = jnp.stack(xs)
        x_all = jnp.concatenate([x_own, other])
        kinds = jnp.concatenate([kinds_own, kinds_other.astype(jnp.int32).reshape(groups, GROUP)])
        r = jnp.arange(length, dtype=jnp.int32)
        npos = jnp.where(fine, lay.npos[0], lay.npos[1])
        stride = jnp.where(fine, STRIDES[0], STRIDES[1])
        taps = jnp.where(fine, lay.taps[0], lay.taps[1])
        step = (r % npos) * stride + r // npos
        order = (step[:, None] == r[None, :]).astype(F32).astype(BF)
        counts = window_counts(kinds, block_len, step)
        mean = jnp.einsum("grj,gjd->grd", counts, x_all, preferred_element_type=F32)
        season = jnp.einsum("rj,gjd->grd", order, x_all, preferred_element_type=F32)
        season = season - mean * (1.0 / WINDOW)
        own_counts = window_counts(kinds_own, block_len, r)
        trend = jnp.einsum("gij,gjd->gid", own_counts, x_own, preferred_element_type=F32)
        trend_low = (trend * (1.0 / WINDOW)).astype(BF)
        q = jnp.arange(2 * groups * max(lay.npos), dtype=jnp.int32)
        group = q // npos
        pos = q % npos
        block = pos // taps
        firsts, _ = series_bounds(kinds)
        first = jnp.zeros_like(q)
        for g in range(2 * groups):
            for b in range(GROUP):
                first = jnp.where((group == g) & (block == b), firsts[g, b], first)
        age = (pos - first * taps)[:, None]
        return season, season.astype(BF), order, own_counts, trend_low, age

    doublings = []
    size = 1
    while size < n:
        doublings.append(size)
        size *= 2
    for t in range(1, last + 3):
        sends = {}
        if t <= last:
            if t < last:
                sends["sr"], sends["sl"] = (si_r, right), (si_l, left)
            else:
                sends["sr"], sends["sl"] = (si_r[:hat_rows], right), (si_l[hat_rows:], left)
        if 1 <= t - 1 <= last:
            if t - 1 < last:
                sends["gr"], sends["gl"] = (gf_r, right), (gf_l, left)
            else:
                sends["gr"], sends["gl"] = (gf_r[:gf_rows], right), (gf_l[gf_rows:], left)
            sends["csr"], sends["csl"] = (si_r, swap_core), (si_l, swap_core)
        if 1 <= t - 2 <= last:
            sends["cgr"], sends["cgl"] = (gf_r, swap_core), (gf_l, swap_core)
        if t <= groups:
            sends["x"] = (x_own[t - 1], swap_y)
        if t == 1:
            sends["k"] = (block_kinds.astype(F32), swap_y)
        if t <= len(doublings):
            sends["gain"] = (gains, exchange("dp", n, doublings[t - 1]))
        work, given = None, ()
        if t == last + 1:
            work, given = prepare, (kinds_other, *x_other)
        arrived, done = slot(sends, work, given)
        if done:
            prepared = done
        if "x" in arrived:
            x_other.append(arrived["x"])
        if "k" in arrived:
            kinds_other = arrived["k"]
        if "gain" in arrived:
            gains = gains + arrived["gain"]

        def keep(pieces, step, other, a, b, half):
            pieces.add(source(-step), other, 0, a)
            pieces.add(source(step), other, half if step == last else 0, b)

        if "csr" in arrived:
            keep(si, t - 1, 1, arrived["csr"], arrived["csl"], hat_rows)
        if "cgr" in arrived:
            keep(gf, t - 2, 1, arrived["cgr"], arrived["cgl"], gf_rows)
        if "sr" in arrived:
            si_r, si_l = arrived["sr"], arrived["sl"]
            keep(si, t, 0, si_r, si_l, hat_rows)
        if "gr" in arrived:
            gf_r, gf_l = arrived["gr"], arrived["gl"]
            keep(gf, t - 1, 0, gf_r, gf_l, gf_rows)
    season, season_low, order, own_counts, trend_low, age = prepared
    gain_b, gain_m, gain_o = gains[0:1], gains[1:2], gains[2:3]

    shrunk, iso, mixed = shrink_forward(lay, where, si, season_low, age, gain_b)
    branch_other, up_other = grow_forward(lay, where, gf, 1, mixed, season, order, gain_b)
    parts = [branch_other[g : g + 1] for g in range(groups)]
    received = [swap_y(p) for p in parts]
    branch_own, up_own = grow_forward(lay, where, gf, 0, mixed, season, order, gain_b)

    grads_in = out_grad.reshape(groups, length, width)
    outs, back_own, back_got, trend_back, saved, dense_gains = [], [], [], [], [], None
    for g in range(groups):
        made = dense(
            lay, where, gf, g, branch_own, received[g], trend_low, grads_in, gain_m, gain_o
        )
        outs.append(made[0])
        back_own.append(made[1])
        back_got.append(swap_y(made[2]))
        trend_back.append(made[3])
        saved.append(made[4:9])
        dense_gains = made[9] if dense_gains is None else dense_gains + made[9]
    series_out = jnp.concatenate(outs)

    ring_order = [n // 2]
    for k in range(n // 2 - 1, 0, -1):
        ring_order += [k, -k]
    ring_order.append(0)
    spot = jnp.zeros((n,), jnp.int32)
    for place, offset in enumerate(ring_order):
        spot = jnp.where(jnp.arange(n) == ring.index(offset), place, spot)
    f_local = dense_weights(lay, where, spot, branch_own, received, trend_low, grads_in, saved)

    pre_own, mixed_back_own, sum_own, gains_own = grow_backward(
        lay, where, gf, 0, jnp.stack(back_own), up_own, season, order, gain_b
    )
    pre_other, mixed_back_other, sum_other, gains_other = grow_backward(
        lay, where, gf, 1, jnp.stack(back_got), up_other, season, order, gain_b
    )
    g_local = grow_weight(lay, where, spot, mixed, pre_own, pre_other)
    shrink_pre, si_local, gains_si = shrink_backward(
        lay, where, spot, si, mixed_back_own, mixed_back_other, shrunk, iso, season_low, age, gain_b
    )

    class Chain:
        def __init__(self, local):
            self.local = local
            self.keep = local[0]
            self.got = None
            self.step = last
            self.r = self.l = None
            self.half = local.shape[2] // 2

        def give(self):
            return self.local[1]

        def here(self, place):
            return self.keep[place].astype(F32) + self.got[place].astype(F32)

        def sends(self):
            k = self.step
            if k == last:
                part = self.here(0)
                return part[: self.half].astype(BF), part[self.half :].astype(BF)
            place = 1 + 2 * (last - 1 - k)
            a, b = self.here(place), self.here(place + 1)
            if k == last - 1:
                h = self.half
                a = jnp.concatenate([a[:h] + self.r.astype(F32), a[h:]])
                b = jnp.concatenate([b[:h], b[h:] + self.l.astype(F32)])
            else:
                a, b = a + self.r.astype(F32), b + self.l.astype(F32)
            return a.astype(BF), b.astype(BF)

        def receive(self, r, l):
            self.r, self.l = r, l
            self.step -= 1

        def total(self):
            return (self.here(n - 1) + self.r.astype(F32) + self.l.astype(F32)).astype(BF)

    f, g, s = Chain(f_local), Chain(g_local), Chain(si_local)
    f.got = swap_core(f.give())

    def move(chains, extra=None, work=None, given=()):
        sends = dict(extra or {})
        for name, chain in chains.items():
            a, b = chain.sends()
            sends[name + "r"], sends[name + "l"] = (a, right), (b, left)
        arrived, done = slot(sends, work, given)
        for name, chain in chains.items():
            chain.receive(arrived[name + "r"], arrived[name + "l"])
        return arrived, done

    def season_work(pre, sum_own, sum_other):
        return season_backward(lay, where, si, pre, sum_own, sum_other, order)

    for _ in range(last - 2):
        move({"f": f})
    arrived, _ = move({"f": f}, {"g": (g.give(), swap_core)})
    g.got = arrived["g"]
    arrived, _ = move({"f": f, "g": g}, {"s": (s.give(), swap_core)})
    s.got = arrived["s"]
    f_mine = f.total()
    arrived, (season_own, season_send) = move(
        {"g": g, "s": s}, {"f": (f_mine, swap_y)}, season_work, (shrink_pre, sum_own, sum_other)
    )
    f_half = (f_mine.astype(F32) + arrived["f"].astype(F32)).astype(BF)
    tail_sends = [season_send[i] for i in range(groups)]
    tail = []
    extra = {"f": (f_half, swap_core)}
    f_other = g_y = g_core = None
    while s.step > 0:
        chains = {"s": s}
        if g.step > 0:
            chains["g"] = g
        elif g_y is None:
            g_mine = g.total()
            extra["g"] = (g_mine, swap_y)
        elif g_core is None:
            extra["gc"], extra["gd"] = (g_mine, swap_core), (g_y, swap_core)
        if tail_sends:
            extra["x"] = (tail_sends.pop(0), swap_y)
        arrived, _ = move(chains, extra)
        extra = {}
        if "f" in arrived:
            f_other = arrived["f"]
        if "g" in arrived:
            g_y = arrived["g"]
        if "gc" in arrived:
            g_core = (arrived["gc"], arrived["gd"])
        if "x" in arrived:
            tail.append(arrived["x"])
    s_mine = s.total()
    extra = {"s": (s_mine, swap_y)}
    if g_y is None:
        g_mine = g.total()
        g_y = swap_y(g_mine)
    if g_core is None:
        extra["gc"], extra["gd"] = (g_mine, swap_core), (g_y, swap_core)
    while tail_sends:
        tail.append(swap_y(tail_sends.pop(0)))

    def finish(*tail):
        total = season_own.astype(F32) + jnp.stack(tail).astype(F32)
        rest = jnp.stack(trend_back) - total
        spread = (rest * (1.0 / WINDOW)).astype(BF)
        averaged = jnp.einsum("gij,gid->gjd", own_counts, spread, preferred_element_type=F32)
        return ((total + averaged).astype(BF),)

    arrived, (series_grad,) = slot(extra, finish, tail)
    if "gc" in arrived:
        g_core = (arrived["gc"], arrived["gd"])
    s_y = arrived["s"]
    s_core = (swap_core(s_mine), swap_core(s_y))

    def both(mine, other):
        return jnp.where(core == 0, mine, other), jnp.where(core == 0, other, mine)

    def branches(mine, over_y):
        return jnp.where(fine, mine, over_y), jnp.where(fine, over_y, mine)

    s_fine, s_coarse = branches(s_mine, s_y)
    t_fine, t_coarse = branches(*s_core)
    g_fine, g_coarse = branches(g_mine, g_y)
    h_fine, h_coarse = branches(*g_core)

    def si_out(b, mine, other):
        lo, hi = both(mine, other)
        (f0, r0, _, _), (f1, r1, _, _) = lay.si_parts(b)
        shrink = jnp.concatenate([lo[f0 : f0 + r0], hi[f0 : f0 + r0]])
        return shrink.astype(F32), jnp.concatenate([lo[f1 : f1 + r1], hi[f1 : f1 + r1]]).astype(F32)

    def g_out(b, mine, other):
        lo, hi = both(mine, other)
        cols = [v[r : r + k] for v in (lo, hi) for r, k, _ in lay.g_parts(b)]
        return jnp.concatenate(cols, axis=1).astype(F32)

    fine_shrink_grad, fine_iso_grad = si_out(0, s_fine, t_fine)
    coarse_shrink_grad, coarse_iso_grad = si_out(1, s_coarse, t_coarse)
    fine_grow_grad, coarse_grow_grad = g_out(0, g_fine, h_fine), g_out(1, g_coarse, h_coarse)
    lo, hi = both(f_half, f_other)
    (a0, a1, _, _), (b0, b1, _, _) = lay.f_parts(0)
    z = lay.g_half
    contract_grad = lo[a0 - z : a0 - z + a1].astype(F32)
    merge_grad = lo[b0 - z : b0 - z + b1].astype(F32)
    rest = [hi[a - z : a - z + rows].astype(F32) for a, rows, _, _ in lay.f_parts(1)]
    trend_grad, expand_grad = rest[0], jnp.concatenate(rest[1:], axis=1)

    gain_grads = jnp.concatenate([gains_own + gains_other + gains_si, dense_gains])
    for size in doublings:
        gain_grads = gain_grads + exchange("dp", n, size)(gain_grads)
    for size in (1, 2):
        gain_grads = gain_grads + exchange("group", 4, size)(gain_grads)
    gain_grads = lax.dynamic_slice(gain_grads, (jnp.int32(0), ring.me * share), (3, share))
    return (
        series_out,
        series_grad.reshape(series_in.shape),
        fine_shrink_grad,
        coarse_shrink_grad,
        fine_iso_grad,
        coarse_iso_grad,
        fine_grow_grad,
        coarse_grow_grad,
        merge_grad,
        expand_grad,
        contract_grad,
        trend_grad,
        gain_grads[0],
        gain_grads[1],
        gain_grads[2],
    )


def solution(mesh):
    n = mesh.shape["dp"]
    rows = P(("dp", "group"), None)
    weight = P("dp", None)
    return jax.shard_map(
        lambda *args: on_device(n, *args),
        mesh=mesh,
        in_specs=(rows, P(("dp", "group")), rows) + (weight,) * 10 + (P("dp"),) * 3,
        out_specs=(rows, rows) + (weight,) * 10 + (P("dp"),) * 3,
        check_vma=False,
    )
```

time: 2070 us -> 773 us (0.37)
  waiting for transfers between devices: 1450 us -> 274 us
  matrix products: 257 us -> 33.4 us
  Pallas kernels: 0 us -> 214 us
  blocking collectives: 81.2 us -> 0 us
  other arithmetic: 167 us -> 86.3 us
  starting transfers between devices: 1.18 us -> 80 us
    reduce_scatter x10 -> x0, waiting for transfers between devices: 780 us -> none  [the longest x1 152 us: on_device(): lax.psum_scatter(grads[2].astype(jnp.bfloat16), 'dp', scatter_dimension=0...]
    all_gather x9 -> x0, waiting for transfers between devices: 603 us -> none  [the longest x1 120 us: on_device(): lax.all_gather(coarse_grow, 'dp', axis=0, tiled=True)]
    ppermute x0 -> x88, waiting for transfers between devices: none -> 274 us  [the longest x16 89.8 us: swap_y(): return lax.ppermute(v, 'group', Y_SWAP)]
    dot_general x30 -> x4, matrix products: 257 us -> 33.4 us  [the longest x1 13.3 us: prepare(): mean = jnp.einsum('grj,gjd->grd', counts, x_all, preferred_element_type=F32)]
    pallas_call x0 -> x12, Pallas kernels: none -> 214 us  [the longest x3 70.9 us: dense(): pl.pallas_call(kernel, grid=(1,), out_shape=[jax.ShapeDtypeStruct((length...]
    ppermute x0 -> x88, starting transfers between devices: none -> 80 us  [the longest x16 23.6 us: swap_y(): return lax.ppermute(v, 'group', Y_SWAP)]
    add_any x5 -> x0, other arithmetic: 62.7 us -> none  [the longest x1 60.3 us: moving_average(): running = padded[:, 0:block_len]]
    psum x1 -> x0, waiting for transfers between devices: 55.8 us -> none  [on_device(): lax.psum(shares[0].astype(jnp.bfloat16), 'group').astype(jnp.float32)]
  transfers between devices with their start and end apart: 20 -> 88, of which waited for: 15 -> 29; matrix products, arithmetic and copies ran while one was open for 24% -> 17% of each run, Pallas kernels for 0% -> 20%
where the time goes in v2:
time: 773 us; the launch traced here: 763 us
  waiting for transfers between devices  274 us (35%)
  Pallas kernels  214 us (28%)
  other arithmetic  86.3 us (11%)
  starting transfers between devices  80 us (10%)
  local copies, waits for them, and re-layouts  73.1 us (9%)
  matrix products  33.4 us (4%)
    ppermute x16, waiting for transfers between devices, swap_y(): return lax.ppermute(v, 'group', Y_SWAP)  89.8 us
    ppermute x20, waiting for transfers between devices, right(): return lax.ppermute(v, 'dp', ring.right)  86.6 us
    ppermute x8, waiting for transfers between devices, exchange(): return lambda v: lax.ppermute(v, axis, [(i, i ^ step) for i in range(size)])  74.4 us
    pallas_call x3, Pallas kernels, dense(): pl.pallas_call(kernel, grid=(1,), out_shape=[jax.ShapeDtypeStruct((length...  70.9 us
    pallas_call x2, Pallas kernels, grow_backward(): pl.pallas_call(kernel, grid=(1,), out_shape=[jax.ShapeDtypeStruct((groups...  30.1 us
    pallas_call x1, Pallas kernels, dense_weights(): pl.pallas_call(kernel, out_shape=jax.ShapeDtypeStruct((2, n, lay.f_half,...  28.3 us
    pallas_call x1, Pallas kernels, shrink_backward(): pl.pallas_call(kernel, out_shape=[jax.ShapeDtypeStruct((most, width), BF)...  26.4 us
    ppermute x16, starting transfers between devices, swap_y(): return lax.ppermute(v, 'group', Y_SWAP)  23.6 us
  transfers between devices with their start and end apart: 88, of which 29 were waited for; matrix products, arithmetic and copies ran while one was open for 17% of the time, Pallas kernels for 20%

profile of v2, /device:TPU:0, one launch (start us, length us, event | category | flops | bytes accessed | tf_op | source)
XLA Modules:
  0.0 762.9 jit_solution(4116851741602183025)
XLA Ops:
  1.9 2.8 fusion.99
  8.2 2.6 constant_dynamic-slice_fusion.3
  11.1 3.0 collective-permute-start.3
  54.8 15.7 %collective-permute-done.12 = f32[3,512]{1,0:T(4,128)S(1)} collective-permute-done((f32[3,512]{1,0:T(4,128)S(1)}, f32[3,512]{1,0:T(4,128)S(1)}, u32[]{:S(2)}, u32[]{:S(2)}) %collective-permute-start.12) | collective-permute-done | bytes 6176 | tf_op jit(solution)/shard_map/ppermute | solution.py:784
  76.1 12.2 %collective-permute-done.7.refs_2_ = bf16[896,512]{1,0:T(8,128)(2,1)} collective-permute-done((bf16[896,512]{1,0:T(8,128)(2,1)}, bf16[896,512]{1,0:T(8,128)(2,1)}, u32[]{:S(2)}, u32[]{:S(2)}) %collective-permute-start.7) | collective-permute-done | bytes 917536 | tf_op jit(solution)/shard_map/ppermute | solution.py:819
  88.4 4.1 collective-permute-done.8.refs_3_
  95.5 3.4 collective-permute-start.22
  99.0 30.4 %collective-permute-done.22 = f32[3,512]{1,0:T(4,128)S(1)} collective-permute-done((f32[3,512]{1,0:T(4,128)S(1)}, f32[3,512]{1,0:T(4,128)S(1)}, u32[]{:S(2)}, u32[]{:S(2)}) %collective-permute-start.22) | collective-permute-done | bytes 6176 | tf_op jit(solution)/shard_map/ppermute | solution.py:784
  129.4 2.7 collective-permute-start.16
  136.2 12.1 %collective-permute-done.16.refs_7_ = bf16[896,512]{1,0:T(8,128)(2,1)} collective-permute-done((bf16[896,512]{1,0:T(8,128)(2,1)}, bf16[896,512]{1,0:T(8,128)(2,1)}, u32[]{:S(2)}, u32[]{:S(2)}) %collective-permute-start.16) | collective-permute-done | bytes 917536 | tf_op jit(solution)/shard_map/ppermute | solution.py:822
  153.7 7.8 %multiply_convert_fusion.trend_ref = bf16[3,768,512]{2,1,0:T(8,128)(2,1)} fusion(bf16[3,768,512]{2,1,0:T(8,128)(2,1)} %bitcast.268, s32[3,768]{1,0:T(4,128)S(1)} %get-tuple-element.577, s32[3,768]{1,0:T(4,128)S(1)} %get-tuple-element.554, s32[3,768]{1,0:T(4,128)S(1)} %get-tuple-element.578, s32[3,768]{1,0:T(4,128)S(1)} %get-tuple-element.553, ...), kind=kOutput, calls=%fused_computation.29 | convolution fusion | flops 1837301760 | bytes 5345280 | tf_op jit(solution)/shard_map/gij,gjd->gid/dot_general | solution.py:900
  168.3 11.2 %collective-permute-done.23.refs_14_ = bf16[448,512]{1,0:T(8,128)(2,1)S(1)} collective-permute-done((bf16[448,512]{1,0:T(8,128)(2,1)}, bf16[448,512]{1,0:T(8,128)(2,1)S(1)}, u32[]{:S(2)}, u32[]{:S(2)}) %collective-permute-start.23) | collective-permute-done | bytes 458784 | tf_op jit(solution)/shard_map/ppermute | solution.py:819
  180.1 4.3 copy.42
  184.5 6.4 convert_convert_fusion.2
  198.9 13.3 %fusion.2 = f32[6,768,512]{2,1,0:T(8,128)S(1)} fusion(s32[6,768]{1,0:T(8,128)S(1)} %get-tuple-element.579, s32[6,768]{1,0:T(8,128)S(1)} %get-tuple-element.556, s32[6,768]{1,0:T(8,128)S(1)} %get-tuple-element.580, s32[6,768]{1,0:T(8,128)S(1)} %get-tuple-element.555, pred[768,768]{1,0:T(8,128)(4,1)} %get-tuple-element.576, bf16[1,768,512]{1,2,0:T(8,128)(2,1)} %bitcast.16, ...), kind=kOutput, calls=%fused_computation.9 | convolution fusion | flops 3676962816 | bytes 14819328 | tf_op jit(solution)/shard_map/grj,gjd->grd/dot_general | solution.py:896
  212.2 8.7 %fusion.107 = (bf16[6,768,512]{2,1,0:T(8,128)(2,1)}, f32[6,768,512]{2,1,0:T(8,128)}) fusion(f32[6,768,512]{2,1,0:T(8,128)S(1)} %fusion.2, s32[768]{0:T(1024)S(1)} %get-tuple-element.589, bf16[1,768,512]{1,2,0:T(8,128)(2,1)} %bitcast.16, bf16[1,768,512]{1,2,0:T(8,128)(2,1)S(1)} %bitcast.285, bf16[1,768,512]{1,2,0:T(8,128)(2,1)} %bitcast.14, ...), kind=kOutput, calls=%fused_computation.377 | convolution fusion | flops 3639803904 | bytes 28314624 | tf_op jit(solution)/shard_map/rj,gjd->grd/dot_general | solution.py:897
  223.2 17.4 %multiply_subtract_fusion.age_ref = s32[384,1]{1,0:T(8,128)S(1)} fusion(s32[]{:T(128)} %bitcast.36, s32[]{:T(128)} %bitcast.35, s32[]{:T(128)} %bitcast.34, s32[]{:T(128)} %bitcast.33, s32[]{:T(128)} %bitcast.32, s32[]{:T(128)} %bitcast.31, s32[]{:T(128)} %bitcast.30, s32[]{:T(128)} %bitcast.29, s32[]{:T(128)} %bitcast.28, s32[]{:T(128)} %bitcast.27, ...), kind=kLoop, calls=%fused_computation.190 | loop fusion | flops 30720 | bytes 1628 | tf_op jit(solution)/shard_map/sub | solution.py:911
  241.8 13.4 %shrink_forward.1 = (f32[384,512]{1,0:T(8,128)S(1)}, f32[384,512]{1,0:T(8,128)S(1)}, bf16[384,512]{1,0:T(8,128)(2,1)S(1)}) custom-call(s32[10]{0:T(128)S(1)} %stack.127.where, s32[384,1]{1,0:T(8,128)S(1)} %multiply_subtract_fusion.age_ref, f32[1,512]{1,0:T(1,128)S(1)} %get-tuple-element.546.gain_ref, bf16[6,768,512]{2,1,0:T(8,128)(2,1)} %get-tuple-element.296.season_ref, ...), custom_call_target="tpu_custom_call" | custom-call | flops 5637144576 | bytes 14680064 | tf_op jit(solution)/shard_map/shrink_forward/pallas_call | solution.py:259
  257.9 10.8 %grow_forward.3 = (bf16[3,768,512]{2,1,0:T(8,128)(2,1)}, f32[3,768,512]{2,1,0:T(8,128)}) custom-call(s32[10]{0:T(128)S(1)} %stack.127.where, f32[1,512]{1,0:T(1,128)S(1)} %get-tuple-element.546.gain_ref, bf16[768,768]{1,0:T(8,128)(2,1)} %get-tuple-element.294.order_ref, bf16[384,512]{1,0:T(8,128)(2,1)S(1)} %get-tuple-element.305.mixed_ref, ...), custom_call_target="tpu_custom_call" | custom-call | flops 3019898880 | bytes 24903680 | tf_op jit(solution)/shard_map/grow_forward/pallas_call | solution.py:302
  273.1 11.2 %grow_forward.2 = (bf16[3,768,512]{2,1,0:T(8,128)(2,1)}, f32[3,768,512]{2,1,0:T(8,128)}) custom-call(s32[10]{0:T(128)S(1)} %stack.127.where, f32[1,512]{1,0:T(1,128)S(1)} %get-tuple-element.546.gain_ref, bf16[768,768]{1,0:T(8,128)(2,1)} %get-tuple-element.294.order_ref, bf16[384,512]{1,0:T(8,128)(2,1)S(1)} %get-tuple-element.305.mixed_ref, ...), custom_call_target="tpu_custom_call" | custom-call | flops 3019898880 | bytes 24903680 | tf_op jit(solution)/shard_map/grow_forward/pallas_call | solution.py:302
  284.4 6.5 collective-permute-done.41.got_ref.refs_2_
  291.8 23.7 %dense_2.1 = (bf16[768,512]{1,0:T(8,128)(2,1)}, bf16[768,512]{1,0:T(8,128)(2,1)}, bf16[768,512]{1,0:T(8,128)(2,1)}, f32[768,512]{1,0:T(8,128)}, bf16[768,512]{1,...) custom-call(s32[10]{0:T(128)} %copy-done.18, ...), custom_call_target="tpu_custom_call" | custom-call | flops 8858370048 | bytes 33554432 | tf_op jit(solution)/shard_map/dense_2/pallas_call | solution.py:640
  315.5 8.3 %collective-permute-done.40.got_ref.refs_1_ = bf16[1,768,512]{2,1,0:T(8,128)(2,1)S(1)} collective-permute-done((bf16[1,768,512]{2,1,0:T(8,128)(2,1)S(1)}, bf16[1,768,512]{2,1,0:T(8,128)(2,1)S(1)}, u32[]{:S(2)}, u32[]{:S(2)}) %collective-permute-start.40) | collective-permute-done | bytes 786464 | tf_op jit(solution)/shard_map/ppermute | solution.py:92
  324.7 23.6 %dense_1.1 = (bf16[768,512]{1,0:T(8,128)(2,1)}, bf16[768,512]{1,0:T(8,128)(2,1)}, bf16[768,512]{1,0:T(8,128)(2,1)}, f32[768,512]{1,0:T(8,128)}, bf16[768,512]{1,...) custom-call(s32[10]{0:T(128)} %copy-done.18, ...), custom_call_target="tpu_custom_call" | custom-call | flops 8858370048 | bytes 33554432 | tf_op jit(solution)/shard_map/dense_1/pallas_call | solution.py:640
  349.2 23.7 %dense_0.1 = (bf16[768,512]{1,0:T(8,128)(2,1)}, bf16[768,512]{1,0:T(8,128)(2,1)}, bf16[768,512]{1,0:T(8,128)(2,1)}, f32[768,512]{1,0:T(8,128)}, bf16[768,512]{1,...) custom-call(s32[10]{0:T(128)} %copy-done.18, ...), custom_call_target="tpu_custom_call" | custom-call | flops 8858370048 | bytes 33554432 | tf_op jit(solution)/shard_map/dense_0/pallas_call | solution.py:640
  372.9 28.3 %dense_weights.1 = bf16[2,8,384,512]{3,2,1,0:T(8,128)(2,1)} custom-call(s32[10]{0:T(128)} %copy-done.18, s32[8]{0:T(128)} %compare_select_fusion.6.places_ref, bf16[3,768,512]{2,1,0:T(8,128)(2,1)} %get-tuple-element.319.mine_ref, bf16[3,768,512]{2,1,0:T(8,128)(2,1)} %multiply_convert_fusion.trend_ref, bf16[3,768,512]{2,1,0:T(8,128)(2,1)} %bitcast.283, ...), custom_call_target="tpu_custom_call" | custom-call | flops 13287555072 | bytes 47185920 | tf_op jit(solution)/shard_map/dense_weights/pallas_call | solution.py:734
  407.6 15.1 %grow_backward.2 = (bf16[3,768,512]{2,1,0:T(8,128)(2,1)}, f32[192,512]{1,0:T(8,128)}, f32[3,768,512]{2,1,0:T(8,128)}, f32[1,512]{1,0:T(1,128)}) custom-call(s32[10]{0:T(128)} %copy-done.18, f32[1,512]{1,0:T(1,128)} %copy-done.17, bf16[768,768]{1,0:T(8,128)(2,1)} %get-tuple-element.294.order_ref, bf16[3,768,512]{2,1,0:T(8,128)(2,1)} %pad_maximum_fusion.2.grad_ref, ...), custom_call_target="tpu_custom_call" | custom-call | flops 3019898880 | bytes 29622272 | tf_op jit(solution)/shard_map/grow_backward/pallas_call | solution.py:371
  424.2 17.0 %collective-permute-done.43 = bf16[768,512]{1,0:T(8,128)(2,1)} collective-permute-done((bf16[768,512]{1,0:T(8,128)(2,1)}, bf16[768,512]{1,0:T(8,128)(2,1)}, u32[]{:S(2)}, u32[]{:S(2)}) %collective-permute-start.43) | collective-permute-done | bytes 786464 | tf_op jit(solution)/shard_map/ppermute | solution.py:92
  441.2 16.4 %collective-permute-done.42 = bf16[768,512]{1,0:T(8,128)(2,1)} collective-permute-done((bf16[768,512]{1,0:T(8,128)(2,1)}, bf16[768,512]{1,0:T(8,128)(2,1)}, u32[]{:S(2)}, u32[]{:S(2)}) %collective-permute-start.42) | collective-permute-done | bytes 786464 | tf_op jit(solution)/shard_map/ppermute | solution.py:92
  457.6 3.0 pad_maximum_fusion.3.grad_ref
  460.6 15.1 %grow_backward.3 = (bf16[3,768,512]{2,1,0:T(8,128)(2,1)}, f32[192,512]{1,0:T(8,128)}, f32[3,768,512]{2,1,0:T(8,128)}, f32[1,512]{1,0:T(1,128)}) custom-call(s32[10]{0:T(128)} %copy-done.18, f32[1,512]{1,0:T(1,128)} %copy-done.17, bf16[768,768]{1,0:T(8,128)(2,1)} %get-tuple-element.294.order_ref, bf16[3,768,512]{2,1,0:T(8,128)(2,1)} %pad_maximum_fusion.3.grad_ref, ...), custom_call_target="tpu_custom_call" | custom-call | flops 3019898880 | bytes 29622272 | tf_op jit(solution)/shard_map/grow_backward/pallas_call | solution.py:371
  479.9 7.9 %grow_weight.1 = bf16[2,8,512,512]{3,2,1,0:T(8,128)(2,1)} custom-call(s32[10]{0:T(128)S(1)} %copy-done.19, s32[8]{0:T(128)S(1)} %copy-done.21, bf16[384,512]{1,0:T(8,128)(2,1)S(1)} %get-tuple-element.305.mixed_ref, bf16[3,768,512]{2,1,0:T(8,128)(2,1)S(1)} %copy-done.5, bf16[3,768,512]{2,1,0:T(8,128)(2,1)S(1)} %copy-done.6), custom_call_target="tpu_custom_call" | custom-call | flops 2415919104 | bytes 8388608 | tf_op jit(solution)/shard_map/grow_weight/pallas_call | solution.py:430
  492.6 5.6 collective-permute-done.48
  501.4 26.4 %shrink_backward.1 = (bf16[384,512]{1,0:T(8,128)(2,1)}, bf16[2,8,896,512]{3,2,1,0:T(8,128)(2,1)}, f32[1,512]{1,0:T(1,128)}) custom-call(s32[10]{0:T(128)} %copy-done.18, s32[8]{0:T(128)} %compare_select_fusion.6.places_ref, s32[384,1]{1,0:T(8,128)} %copy-done.16, f32[1,512]{1,0:T(1,128)} %copy-done.17, f32[192,512]{1,0:T(8,128)} %get-tuple-element.329.b0, ...), custom_call_target="tpu_custom_call" | custom-call | flops 8455716864 | bytes 29360128 | tf_op jit(solution)/shard_map/shrink_backward/pallas_call | solution.py:496
  529.9 6.5 slice_bitcast_fusion
  536.5 2.9 collective-permute-done.51
  550.2 12.5 %collective-permute-done.56 = bf16[256,512]{1,0:T(8,128)(2,1)S(1)} collective-permute-done((bf16[256,512]{1,0:T(8,128)(2,1)S(1)}, bf16[256,512]{1,0:T(8,128)(2,1)S(1)}, u32[]{:S(2)}, u32[]{:S(2)}) %collective-permute-start.56) | collective-permute-done | bytes 262176 | tf_op jit(solution)/shard_map/ppermute | solution.py:819
  570.8 8.9 %collective-permute-start.58 = (bf16[384,512]{1,0:T(8,128)(2,1)S(1)}, bf16[384,512]{1,0:T(8,128)(2,1)}, u32[]{:S(2)}, u32[]{:S(2)}) collective-permute-start(bf16[384,512]{1,0:T(8,128)(2,1)S(1)} %fusion.47), channel_id=1, source_target_pairs={{0,2},{2,0},{1,3},{3,1},{4,6},{6,4},{5,7},{7,5},{8,10},{10,8},{9,1... | collective-permute-start | bytes 1179656 | tf_op jit(solution)/shard_map/ppermute | solution.py:92
  584.0 14.8 %season_backward.1 = (bf16[3,768,512]{2,1,0:T(8,128)(2,1)}, bf16[3,768,512]{2,1,0:T(8,128)(2,1)}) custom-call(s32[10]{0:T(128)S(1)} %copy-done.20, bf16[768,768]{1,0:T(8,128)(2,1)} %get-tuple-element.294.order_ref, bf16[384,512]{1,0:T(8,128)(2,1)S(1)} %copy-done.15, f32[3,768,512]{2,1,0:T(8,128)} %get-tuple-element.388.own_ref, ...), custom_call_target="tpu_custom_call" | custom-call | flops 6039797760 | bytes 36700160 | tf_op jit(solution)/shard_map/season_backward/pallas_call | solution.py:548
  598.8 4.1 collective-permute-done.59
  613.8 19.0 %collective-permute-done.83 = f32[3,512]{1,0:T(4,128)S(1)} collective-permute-done((f32[3,512]{1,0:T(4,128)S(1)}, f32[3,512]{1,0:T(4,128)S(1)}, u32[]{:S(2)}, u32[]{:S(2)}) %collective-permute-start.83) | collective-permute-done | bytes 6176 | tf_op jit(solution)/shard_map/ppermute | solution.py:784
  632.9 3.6 collective-permute-done.84
  636.5 4.5 collective-permute-done.85
  644.4 11.8 %collective-permute-done.67 = bf16[512,512]{1,0:T(8,128)(2,1)S(1)} collective-permute-done((bf16[512,512]{1,0:T(8,128)(2,1)S(1)}, bf16[512,512]{1,0:T(8,128)(2,1)S(1)}, u32[]{:S(2)}, u32[]{:S(2)}) %collective-permute-start.67) | collective-permute-done | bytes 524320 | tf_op jit(solution)/shard_map/ppermute | solution.py:819
  669.0 26.0 %collective-permute-done.72 = bf16[512,512]{1,0:T(8,128)(2,1)S(1)} collective-permute-done((bf16[512,512]{1,0:T(8,128)(2,1)S(1)}, bf16[512,512]{1,0:T(8,128)(2,1)S(1)}, u32[]{:S(2)}, u32[]{:S(2)}) %collective-permute-start.72) | collective-permute-done | bytes 524320 | tf_op jit(solution)/shard_map/ppermute | solution.py:819
  706.4 21.4 %collective-permute-done.74 = bf16[512,512]{1,0:T(8,128)(2,1)S(1)} collective-permute-done((bf16[512,512]{1,0:T(8,128)(2,1)S(1)}, bf16[512,512]{1,0:T(8,128)(2,1)S(1)}, u32[]{:S(2)}, u32[]{:S(2)}) %collective-permute-start.74) | collective-permute-done | bytes 524320 | tf_op jit(solution)/shard_map/ppermute | solution.py:92
  730.6 3.6 add_convert_fusion
  734.1 18.7 %collective-permute-done.78 = bf16[896,512]{1,0:T(8,128)(2,1)S(1)} collective-permute-done((bf16[896,512]{1,0:T(8,128)(2,1)S(1)}, bf16[896,512]{1,0:T(8,128)(2,1)S(1)}, u32[]{:S(2)}, u32[]{:S(2)}) %collective-permute-start.78) | collective-permute-done | bytes 917536 | tf_op jit(solution)/shard_map/ppermute | solution.py:92
  (442 shorter events, 187.8 us)
Async XLA Ops:
  11.1 35.8 %collective-permute-start.3 = (f32[12]{0:T(128)}, f32[12]{0:T(128)}, u32[]{:S(2)}, u32[]{:S(2)}) collective-permute-start(f32[12]{0:T(128)} %convert_element_type.514), channel_id=1, source_target_pairs={{0,2},{2,0},{1,3},{3,1},{4,6},{6,4},{5,7},{7,5},{8,10},{10,8},{9,1... | collective-permute-start | bytes 152 | tf_op jit(solution)/shard_map/ppermute | solution.py:92
  14.1 32.7 %collective-permute-start.4 = (f32[3,512]{1,0:T(4,128)S(1)}, f32[3,512]{1,0:T(4,128)S(1)}, u32[]{:S(2)}, u32[]{:S(2)}) collective-permute-start(f32[3,512]{1,0:T(4,128)S(1)} %dynamic_update_slice.5), channel_id=1, source_target_pairs={{0,4},{4,0},{8,12},{12,8},{16,20},{20,16},{24,28},{28,24},{1,5},{5... | collective-permute-start | bytes 18440 | tf_op jit(solution)/shard_map/ppermute | solution.py:784
  15.7 31.2 %collective-permute-start.2 = (bf16[768,512]{0,1:T(8,128)(2,1)}, bf16[768,512]{0,1:T(8,128)(2,1)}, u32[]{:S(2)}, u32[]{:S(2)}) collective-permute-start(bf16[768,512]{0,1:T(8,128)(2,1)} %copy.50), channel_id=1, source_target_pairs={{0,2},{2,0},{1,3},{3,1},{4,6},{6,4},{5,7},{7,5},{8,10},{10,8},{9,1... | collective-permute-start | bytes 2359304 | tf_op jit(solution)/shard_map/ppermute | solution.py:92
  16.2 30.7 %collective-permute-start = (bf16[896,512]{1,0:T(8,128)(2,1)S(1)}, bf16[896,512]{1,0:T(8,128)(2,1)S(1)}, u32[]{:S(2)}, u32[]{:S(2)}) collective-permute-start(bf16[896,512]{1,0:T(8,128)(2,1)S(1)} %maximum_select_fusion.refs_0_), channel_id=1, source_target_pairs={{0,8},{8,16},{16,24},{24,28},{28,20},{20,12},{12,4},{4,0},{1,9},{9... | collective-permute-start | bytes 2752520 | tf_op jit(solution)/shard_map/ppermute | solution.py:819
  17.8 29.1 %collective-permute-start.1 = (bf16[896,512]{1,0:T(8,128)(2,1)S(1)}, bf16[896,512]{1,0:T(8,128)(2,1)S(1)}, u32[]{:S(2)}, u32[]{:S(2)}) collective-permute-start(bf16[896,512]{1,0:T(8,128)(2,1)S(1)} %maximum_select_fusion.refs_0_), channel_id=1, source_target_pairs={{8,0},{16,8},{24,16},{28,24},{20,28},{12,20},{4,12},{0,4},{9,1},{1... | collective-permute-start | bytes 2752520 | tf_op jit(solution)/shard_map/ppermute | solution.py:822
  47.9 23.6 %collective-permute-start.5 = (bf16[896,512]{1,0:T(8,128)(2,1)S(1)}, bf16[896,512]{1,0:T(8,128)(2,1)S(1)}, u32[]{:S(2)}, u32[]{:S(2)}) collective-permute-start(bf16[896,512]{1,0:T(8,128)(2,1)S(1)} %collective-permute-done.refs_2_), channel_id=1, source_target_pairs={{0,8},{8,16},{16,24},{24,28},{28,20},{20,12},{12,4},{4,0},{1,9},{9... | collective-permute-start | bytes 2752520 | tf_op jit(solution)/shard_map/ppermute | solution.py:819
  49.5 22.0 %collective-permute-start.11 = (bf16[768,512]{0,1:T(8,128)(2,1)}, bf16[768,512]{0,1:T(8,128)(2,1)S(1)}, u32[]{:S(2)}, u32[]{:S(2)}) collective-permute-start(bf16[768,512]{0,1:T(8,128)(2,1)} %copy.51), channel_id=1, source_target_pairs={{0,2},{2,0},{1,3},{3,1},{4,6},{6,4},{5,7},{7,5},{8,10},{10,8},{9,1... | collective-permute-start | bytes 2359304 | tf_op jit(solution)/shard_map/ppermute | solution.py:92
  52.7 23.4 %collective-permute-start.6 = (bf16[896,512]{1,0:T(8,128)(2,1)S(1)}, bf16[896,512]{1,0:T(8,128)(2,1)}, u32[]{:S(2)}, u32[]{:S(2)}) collective-permute-start(bf16[896,512]{1,0:T(8,128)(2,1)S(1)} %collective-permute-done.1.refs_3_), channel_id=1, source_target_pairs={{8,0},{16,8},{24,16},{28,24},{20,28},{12,20},{4,12},{0,4},{9,1},{1... | collective-permute-start | bytes 2752520 | tf_op jit(solution)/shard_map/ppermute | solution.py:822
  52.7 35.6 %collective-permute-start.7 = (bf16[896,512]{1,0:T(8,128)(2,1)}, bf16[896,512]{1,0:T(8,128)(2,1)}, u32[]{:S(2)}, u32[]{:S(2)}) collective-permute-start(bf16[896,512]{1,0:T(8,128)(2,1)} %get-tuple-element.243.refs_0_), channel_id=1, source_target_pairs={{0,8},{8,16},{16,24},{24,28},{28,20},{20,12},{12,4},{4,0},{1,9},{9... | collective-permute-start | bytes 2752520 | tf_op jit(solution)/shard_map/ppermute | solution.py:819
  70.5 22.0 %collective-permute-start.8 = (bf16[896,512]{1,0:T(8,128)(2,1)}, bf16[896,512]{1,0:T(8,128)(2,1)}, u32[]{:S(2)}, u32[]{:S(2)}) collective-permute-start(bf16[896,512]{1,0:T(8,128)(2,1)} %get-tuple-element.243.refs_0_), channel_id=1, source_target_pairs={{8,0},{16,8},{24,16},{28,24},{20,28},{12,20},{4,12},{0,4},{9,1},{1... | collective-permute-start | bytes 2752520 | tf_op jit(solution)/shard_map/ppermute | solution.py:822
  71.5 21.0 %collective-permute-start.9 = (bf16[896,512]{1,0:T(8,128)(2,1)S(1)}, bf16[896,512]{1,0:T(8,128)(2,1)}, u32[]{:S(2)}, u32[]{:S(2)}) collective-permute-start(bf16[896,512]{1,0:T(8,128)(2,1)S(1)} %collective-permute-done.refs_2_), channel_id=1, source_target_pairs={{0,1},{1,0},{2,3},{3,2},{4,5},{5,4},{6,7},{7,6},{8,9},{9,8},{10,11... | collective-permute-start | bytes 2752520 | tf_op jit(solution)/shard_map/ppermute | solution.py:88
  92.5 39.7 %collective-permute-start.13 = (bf16[896,512]{1,0:T(8,128)(2,1)}, bf16[896,512]{1,0:T(8,128)(2,1)}, u32[]{:S(2)}, u32[]{:S(2)}) collective-permute-start(bf16[896,512]{1,0:T(8,128)(2,1)} %copy-done.34), channel_id=1, source_target_pairs={{0,8},{8,16},{16,24},{24,28},{28,20},{20,12},{12,4},{4,0},{1,9},{9... | collective-permute-start | bytes 2752520 | tf_op jit(solution)/shard_map/ppermute | solution.py:819
  92.9 39.8 %collective-permute-start.14 = (bf16[896,512]{1,0:T(8,128)(2,1)}, bf16[896,512]{1,0:T(8,128)(2,1)}, u32[]{:S(2)}, u32[]{:S(2)}) collective-permute-start(bf16[896,512]{1,0:T(8,128)(2,1)} %collective-permute-done.6.refs_7_), channel_id=1, source_target_pairs={{8,0},{16,8},{24,16},{28,24},{20,28},{12,20},{4,12},{0,4},{9,1},{1... | collective-permute-start | bytes 2752520 | tf_op jit(solution)/shard_map/ppermute | solution.py:822
  94.5 38.2 %collective-permute-start.15 = (bf16[896,512]{1,0:T(8,128)(2,1)}, bf16[896,512]{1,0:T(8,128)(2,1)}, u32[]{:S(2)}, u32[]{:S(2)}) collective-permute-start(bf16[896,512]{1,0:T(8,128)(2,1)} %collective-permute-done.7.refs_2_), channel_id=1, source_target_pairs={{0,8},{8,16},{16,24},{24,28},{28,20},{20,12},{12,4},{4,0},{1,9},{9... | collective-permute-start | bytes 2752520 | tf_op jit(solution)/shard_map/ppermute | solution.py:819
  94.9 37.2 %collective-permute-start.21 = (bf16[768,512]{0,1:T(8,128)(2,1)}, bf16[768,512]{0,1:T(8,128)(2,1)}, u32[]{:S(2)}, u32[]{:S(2)}) collective-permute-start(bf16[768,512]{0,1:T(8,128)(2,1)} %copy.52), channel_id=1, source_target_pairs={{0,2},{2,0},{1,3},{3,1},{4,6},{6,4},{5,7},{7,5},{8,10},{10,8},{9,1... | collective-permute-start | bytes 2359304 | tf_op jit(solution)/shard_map/ppermute | solution.py:92
  95.5 33.9 %collective-permute-start.22 = (f32[3,512]{1,0:T(4,128)S(1)}, f32[3,512]{1,0:T(4,128)S(1)}, u32[]{:S(2)}, u32[]{:S(2)}) collective-permute-start(f32[3,512]{1,0:T(4,128)S(1)} %add.567), channel_id=1, source_target_pairs={{0,16},{4,20},{8,24},{12,28},{16,0},{20,4},{24,8},{28,12},{1,17},{... | collective-permute-start | bytes 18440 | tf_op jit(solution)/shard_map/ppermute | solution.py:784
  152.0 28.1 %collective-permute-start.25 = (bf16[896,512]{1,0:T(8,128)(2,1)}, bf16[896,512]{1,0:T(8,128)(2,1)}, u32[]{:S(2)}, u32[]{:S(2)}) collective-permute-start(bf16[896,512]{1,0:T(8,128)(2,1)} %collective-permute-done.15.refs_6_), channel_id=1, source_target_pairs={{0,8},{8,16},{16,24},{24,28},{28,20},{20,12},{12,4},{4,0},{1,9},{9... | collective-permute-start | bytes 2752520 | tf_op jit(solution)/shard_map/ppermute | solution.py:819
  167.6 23.9 %collective-permute-start.26 = (bf16[896,512]{1,0:T(8,128)(2,1)}, bf16[896,512]{1,0:T(8,128)(2,1)}, u32[]{:S(2)}, u32[]{:S(2)}) collective-permute-start(bf16[896,512]{1,0:T(8,128)(2,1)} %collective-permute-done.16.refs_7_), channel_id=1, source_target_pairs={{8,0},{16,8},{24,16},{28,24},{20,28},{12,20},{4,12},{0,4},{9,1},{1... | collective-permute-start | bytes 2752520 | tf_op jit(solution)/shard_map/ppermute | solution.py:822
  168.3 23.2 %collective-permute-start.27 = (bf16[896,512]{1,0:T(8,128)(2,1)}, bf16[896,512]{1,0:T(8,128)(2,1)}, u32[]{:S(2)}, u32[]{:S(2)}) collective-permute-start(bf16[896,512]{1,0:T(8,128)(2,1)} %collective-permute-done.13.refs_10_), channel_id=1, source_target_pairs={{0,1},{1,0},{2,3},{3,2},{4,5},{5,4},{6,7},{7,6},{8,9},{9,8},{10,11... | collective-permute-start | bytes 2752520 | tf_op jit(solution)/shard_map/ppermute | solution.py:88
  196.1 24.8 %collective-permute-start.31 = (bf16[448,512]{1,0:T(8,128)(2,1)}, bf16[448,512]{1,0:T(8,128)(2,1)S(1)}, u32[]{:S(2)}, u32[]{:S(2)}) collective-permute-start(bf16[448,512]{1,0:T(8,128)(2,1)} %slice.702), channel_id=1, source_target_pairs={{0,8},{8,16},{16,24},{24,28},{28,20},{20,12},{12,4},{4,0},{1,9},{9... | collective-permute-start | bytes 1376264 | tf_op jit(solution)/shard_map/ppermute | solution.py:819
  197.7 43.0 %collective-permute-start.32 = (bf16[448,512]{1,0:T(8,128)(2,1)}, bf16[448,512]{1,0:T(8,128)(2,1)S(1)}, u32[]{:S(2)}, u32[]{:S(2)}) collective-permute-start(bf16[448,512]{1,0:T(8,128)(2,1)} %slice.703), channel_id=1, source_target_pairs={{8,0},{16,8},{24,16},{28,24},{20,28},{12,20},{4,12},{0,4},{9,1},{1... | collective-permute-start | bytes 1376264 | tf_op jit(solution)/shard_map/ppermute | solution.py:822
  198.2 42.5 %collective-permute-start.33 = (bf16[448,512]{1,0:T(8,128)(2,1)S(1)}, bf16[448,512]{1,0:T(8,128)(2,1)S(1)}, u32[]{:S(2)}, u32[]{:S(2)}) collective-permute-start(bf16[448,512]{1,0:T(8,128)(2,1)S(1)} %collective-permute-done.23.refs_14_), channel_id=1, source_target_pairs={{0,1},{1,0},{2,3},{3,2},{4,5},{5,4},{6,7},{7,6},{8,9},{9,8},{10,11... | collective-permute-start | bytes 1376264 | tf_op jit(solution)/shard_map/ppermute | solution.py:88
  198.2 42.5 %collective-permute-start.35 = (bf16[896,512]{1,0:T(8,128)(2,1)}, bf16[896,512]{1,0:T(8,128)(2,1)S(1)}, u32[]{:S(2)}, u32[]{:S(2)}) collective-permute-start(bf16[896,512]{1,0:T(8,128)(2,1)} %collective-permute-done.25.refs_10_), channel_id=1, source_target_pairs={{0,1},{1,0},{2,3},{3,2},{4,5},{5,4},{6,7},{7,6},{8,9},{9,8},{10,11... | collective-permute-start | bytes 2752520 | tf_op jit(solution)/shard_map/ppermute | solution.py:88
  198.7 42.0 %collective-permute-start.36 = (bf16[896,512]{1,0:T(8,128)(2,1)}, bf16[896,512]{1,0:T(8,128)(2,1)S(1)}, u32[]{:S(2)}, u32[]{:S(2)}) collective-permute-start(bf16[896,512]{1,0:T(8,128)(2,1)} %collective-permute-done.26.refs_11_), channel_id=1, source_target_pairs={{0,1},{1,0},{2,3},{3,2},{4,5},{5,4},{6,7},{7,6},{8,9},{9,8},{10,11... | collective-permute-start | bytes 2752520 | tf_op jit(solution)/shard_map/ppermute | solution.py:88
  271.1 77.2 %collective-permute-start.39 = (bf16[1,768,512]{2,1,0:T(8,128)(2,1)S(1)}, bf16[1,768,512]{2,1,0:T(8,128)(2,1)S(1)}, u32[]{:S(2)}, u32[]{:S(2)}) collective-permute-start(bf16[1,768,512]{2,1,0:T(8,128)(2,1)S(1)} %get-tuple-element.489), channel_id=1, source_target_pairs={{0,2},{2,0},{1,3},{3,1},{4,6},{6,4},{5,7},{7,5},{8,10},{10,8},{9,1... | collective-permute-start | bytes 2359304 | tf_op jit(solution)/shard_map/ppermute | solution.py:92
  273.1 50.7 %collective-permute-start.40 = (bf16[1,768,512]{2,1,0:T(8,128)(2,1)S(1)}, bf16[1,768,512]{2,1,0:T(8,128)(2,1)S(1)}, u32[]{:S(2)}, u32[]{:S(2)}) collective-permute-start(bf16[1,768,512]{2,1,0:T(8,128)(2,1)S(1)} %get-tuple-element.491), channel_id=1, source_target_pairs={{0,2},{2,0},{1,3},{3,1},{4,6},{6,4},{5,7},{7,5},{8,10},{10,8},{9,1... | collective-permute-start | bytes 2359304 | tf_op jit(solution)/shard_map/ppermute | solution.py:92
  403.5 72.2 %collective-permute-start.45 = (bf16[8,384,512]{2,1,0:T(8,128)(2,1)S(1)}, bf16[8,384,512]{2,1,0:T(8,128)(2,1)}, u32[]{:S(2)}, u32[]{:S(2)}) collective-permute-start(bf16[8,384,512]{2,1,0:T(8,128)(2,1)S(1)} %slice_bitcast_fusion.2), channel_id=1, source_target_pairs={{0,1},{1,0},{2,3},{3,2},{4,5},{5,4},{6,7},{7,6},{8,9},{9,8},{10,11... | collective-permute-start | bytes 9437192 | tf_op jit(solution)/shard_map/ppermute | solution.py:88
  403.9 37.2 %collective-permute-start.43 = (bf16[768,512]{1,0:T(8,128)(2,1)}, bf16[768,512]{1,0:T(8,128)(2,1)}, u32[]{:S(2)}, u32[]{:S(2)}) collective-permute-start(bf16[768,512]{1,0:T(8,128)(2,1)} %get-tuple-element.331), channel_id=1, source_target_pairs={{0,2},{2,0},{1,3},{3,1},{4,6},{6,4},{5,7},{7,5},{8,10},{10,8},{9,1... | collective-permute-start | bytes 2359304 | tf_op jit(solution)/shard_map/ppermute | solution.py:92
  405.7 51.9 %collective-permute-start.42 = (bf16[768,512]{1,0:T(8,128)(2,1)}, bf16[768,512]{1,0:T(8,128)(2,1)}, u32[]{:S(2)}, u32[]{:S(2)}) collective-permute-start(bf16[768,512]{1,0:T(8,128)(2,1)} %get-tuple-element.330), channel_id=1, source_target_pairs={{0,2},{2,0},{1,3},{3,1},{4,6},{6,4},{5,7},{7,5},{8,10},{10,8},{9,1... | collective-permute-start | bytes 2359304 | tf_op jit(solution)/shard_map/ppermute | solution.py:92
  501.3 39.5 %collective-permute-start.50 = (bf16[8,512,512]{2,1,0:T(8,128)(2,1)S(1)}, bf16[8,512,512]{2,1,0:T(8,128)(2,1)}, u32[]{:S(2)}, u32[]{:S(2)}) collective-permute-start(bf16[8,512,512]{2,1,0:T(8,128)(2,1)S(1)} %slice_bitcast_fusion.1), channel_id=1, source_target_pairs={{0,1},{1,0},{2,3},{3,2},{4,5},{5,4},{6,7},{7,6},{8,9},{9,8},{10,11... | collective-permute-start | bytes 12582920 | tf_op jit(solution)/shard_map/ppermute | solution.py:88
  570.8 28.0 %collective-permute-start.58 = (bf16[384,512]{1,0:T(8,128)(2,1)S(1)}, bf16[384,512]{1,0:T(8,128)(2,1)}, u32[]{:S(2)}, u32[]{:S(2)}) collective-permute-start(bf16[384,512]{1,0:T(8,128)(2,1)S(1)} %fusion.47), channel_id=1, source_target_pairs={{0,2},{2,0},{1,3},{3,1},{4,6},{6,4},{5,7},{7,5},{8,10},{10,8},{9,1... | collective-permute-start | bytes 1179656 | tf_op jit(solution)/shard_map/ppermute | solution.py:92
  581.9 21.0 %collective-permute-start.59 = (bf16[512,512]{1,0:T(8,128)(2,1)}, bf16[512,512]{1,0:T(8,128)(2,1)}, u32[]{:S(2)}, u32[]{:S(2)}) collective-permute-start(bf16[512,512]{1,0:T(8,128)(2,1)} %pad_maximum_fusion.12), channel_id=1, source_target_pairs={{0,8},{8,16},{16,24},{24,28},{28,20},{20,12},{12,4},{4,0},{1,9},{9... | collective-permute-start | bytes 1572872 | tf_op jit(solution)/shard_map/ppermute | solution.py:819
  582.3 21.0 %collective-permute-start.60 = (bf16[512,512]{1,0:T(8,128)(2,1)}, bf16[512,512]{1,0:T(8,128)(2,1)}, u32[]{:S(2)}, u32[]{:S(2)}) collective-permute-start(bf16[512,512]{1,0:T(8,128)(2,1)} %pad_maximum_fusion.13), channel_id=1, source_target_pairs={{8,0},{16,8},{24,16},{28,24},{20,28},{12,20},{4,12},{0,4},{9,1},{1... | collective-permute-start | bytes 1572872 | tf_op jit(solution)/shard_map/ppermute | solution.py:822
  609.8 32.5 %collective-permute-start.63 = (bf16[384,512]{1,0:T(8,128)(2,1)S(1)}, bf16[384,512]{1,0:T(8,128)(2,1)S(1)}, u32[]{:S(2)}, u32[]{:S(2)}) collective-permute-start(bf16[384,512]{1,0:T(8,128)(2,1)S(1)} %add_convert_fusion.1), channel_id=1, source_target_pairs={{0,1},{1,0},{2,3},{3,2},{4,5},{5,4},{6,7},{7,6},{8,9},{9,8},{10,11... | collective-permute-start | bytes 1179656 | tf_op jit(solution)/shard_map/ppermute | solution.py:88
  609.9 46.7 %collective-permute-start.65 = (bf16[896,512]{1,0:T(8,128)(2,1)S(1)}, bf16[896,512]{1,0:T(8,128)(2,1)S(1)}, u32[]{:S(2)}, u32[]{:S(2)}) collective-permute-start(bf16[896,512]{1,0:T(8,128)(2,1)S(1)} %pad_maximum_fusion.8), channel_id=1, source_target_pairs={{0,8},{8,16},{16,24},{24,28},{28,20},{20,12},{12,4},{4,0},{1,9},{9... | collective-permute-start | bytes 2752520 | tf_op jit(solution)/shard_map/ppermute | solution.py:819
  610.3 46.3 %collective-permute-start.66 = (bf16[896,512]{1,0:T(8,128)(2,1)S(1)}, bf16[896,512]{1,0:T(8,128)(2,1)S(1)}, u32[]{:S(2)}, u32[]{:S(2)}) collective-permute-start(bf16[896,512]{1,0:T(8,128)(2,1)S(1)} %pad_maximum_fusion.9), channel_id=1, source_target_pairs={{8,0},{16,8},{24,16},{28,24},{20,28},{12,20},{4,12},{0,4},{9,1},{1... | collective-permute-start | bytes 2752520 | tf_op jit(solution)/shard_map/ppermute | solution.py:822
  612.0 44.6 %collective-permute-start.64 = (bf16[768,512]{1,0:T(8,128)(2,1)S(1)}, bf16[768,512]{1,0:T(8,128)(2,1)S(1)}, u32[]{:S(2)}, u32[]{:S(2)}) collective-permute-start(bf16[768,512]{1,0:T(8,128)(2,1)S(1)} %get-tuple-element.399), channel_id=1, source_target_pairs={{0,2},{2,0},{1,3},{3,1},{4,6},{6,4},{5,7},{7,5},{8,10},{10,8},{9,1... | collective-permute-start | bytes 2359304 | tf_op jit(solution)/shard_map/ppermute | solution.py:92
  660.9 34.4 %collective-permute-start.69 = (bf16[768,512]{1,0:T(8,128)(2,1)S(1)}, bf16[768,512]{1,0:T(8,128)(2,1)S(1)}, u32[]{:S(2)}, u32[]{:S(2)}) collective-permute-start(bf16[768,512]{1,0:T(8,128)(2,1)S(1)} %get-tuple-element.408), channel_id=1, source_target_pairs={{0,2},{2,0},{1,3},{3,1},{4,6},{6,4},{5,7},{7,5},{8,10},{10,8},{9,1... | collective-permute-start | bytes 2359304 | tf_op jit(solution)/shard_map/ppermute | solution.py:92
  662.7 32.6 %collective-permute-start.70 = (bf16[896,512]{1,0:T(8,128)(2,1)S(1)}, bf16[896,512]{1,0:T(8,128)(2,1)S(1)}, u32[]{:S(2)}, u32[]{:S(2)}) collective-permute-start(bf16[896,512]{1,0:T(8,128)(2,1)S(1)} %get-tuple-element.409), channel_id=1, source_target_pairs={{0,8},{8,16},{16,24},{24,28},{28,20},{20,12},{12,4},{4,0},{1,9},{9... | collective-permute-start | bytes 2752520 | tf_op jit(solution)/shard_map/ppermute | solution.py:819
  663.0 32.3 %collective-permute-start.71 = (bf16[896,512]{1,0:T(8,128)(2,1)S(1)}, bf16[896,512]{1,0:T(8,128)(2,1)S(1)}, u32[]{:S(2)}, u32[]{:S(2)}) collective-permute-start(bf16[896,512]{1,0:T(8,128)(2,1)S(1)} %get-tuple-element.410), channel_id=1, source_target_pairs={{8,0},{16,8},{24,16},{28,24},{20,28},{12,20},{4,12},{0,4},{9,1},{1... | collective-permute-start | bytes 2752520 | tf_op jit(solution)/shard_map/ppermute | solution.py:822
  666.3 28.7 %collective-permute-start.72 = (bf16[512,512]{1,0:T(8,128)(2,1)S(1)}, bf16[512,512]{1,0:T(8,128)(2,1)S(1)}, u32[]{:S(2)}, u32[]{:S(2)}) collective-permute-start(bf16[512,512]{1,0:T(8,128)(2,1)S(1)} %get-tuple-element.411), channel_id=1, source_target_pairs={{0,8},{8,16},{16,24},{24,28},{28,20},{20,12},{12,4},{4,0},{1,9},{9... | collective-permute-start | bytes 1572872 | tf_op jit(solution)/shard_map/ppermute | solution.py:819
  666.6 28.7 %collective-permute-start.73 = (bf16[512,512]{1,0:T(8,128)(2,1)S(1)}, bf16[512,512]{1,0:T(8,128)(2,1)S(1)}, u32[]{:S(2)}, u32[]{:S(2)}) collective-permute-start(bf16[512,512]{1,0:T(8,128)(2,1)S(1)} %get-tuple-element.412), channel_id=1, source_target_pairs={{8,0},{16,8},{24,16},{28,24},{20,28},{12,20},{4,12},{0,4},{9,1},{1... | collective-permute-start | bytes 1572872 | tf_op jit(solution)/shard_map/ppermute | solution.py:822
  699.2 28.6 %collective-permute-start.75 = (bf16[768,512]{1,0:T(8,128)(2,1)S(1)}, bf16[768,512]{1,0:T(8,128)(2,1)S(1)}, u32[]{:S(2)}, u32[]{:S(2)}) collective-permute-start(bf16[768,512]{1,0:T(8,128)(2,1)S(1)} %get-tuple-element.418), channel_id=1, source_target_pairs={{0,2},{2,0},{1,3},{3,1},{4,6},{6,4},{5,7},{7,5},{8,10},{10,8},{9,1... | collective-permute-start | bytes 2359304 | tf_op jit(solution)/shard_map/ppermute | solution.py:92
  699.6 28.2 %collective-permute-start.76 = (bf16[896,512]{1,0:T(8,128)(2,1)S(1)}, bf16[896,512]{1,0:T(8,128)(2,1)S(1)}, u32[]{:S(2)}, u32[]{:S(2)}) collective-permute-start(bf16[896,512]{1,0:T(8,128)(2,1)S(1)} %get-tuple-element.419), channel_id=1, source_target_pairs={{0,8},{8,16},{16,24},{24,28},{28,20},{20,12},{12,4},{4,0},{1,9},{9... | collective-permute-start | bytes 2752520 | tf_op jit(solution)/shard_map/ppermute | solution.py:819
  700.8 27.0 %collective-permute-start.77 = (bf16[896,512]{1,0:T(8,128)(2,1)S(1)}, bf16[896,512]{1,0:T(8,128)(2,1)S(1)}, u32[]{:S(2)}, u32[]{:S(2)}) collective-permute-start(bf16[896,512]{1,0:T(8,128)(2,1)S(1)} %get-tuple-element.420), channel_id=1, source_target_pairs={{8,0},{16,8},{24,16},{28,24},{20,28},{12,20},{4,12},{0,4},{9,1},{1... | collective-permute-start | bytes 2752520 | tf_op jit(solution)/shard_map/ppermute | solution.py:822
  702.3 25.5 %collective-permute-start.74 = (bf16[512,512]{1,0:T(8,128)(2,1)S(1)}, bf16[512,512]{1,0:T(8,128)(2,1)S(1)}, u32[]{:S(2)}, u32[]{:S(2)}) collective-permute-start(bf16[512,512]{1,0:T(8,128)(2,1)S(1)} %fusion.41), channel_id=1, source_target_pairs={{0,2},{2,0},{1,3},{3,1},{4,6},{6,4},{5,7},{7,5},{8,10},{10,8},{9,1... | collective-permute-start | bytes 1572872 | tf_op jit(solution)/shard_map/ppermute | solution.py:92
  729.5 26.6 %collective-permute-start.81 = (bf16[896,512]{1,0:T(8,128)(2,1)S(1)}, bf16[896,512]{1,0:T(8,128)(2,1)S(1)}, u32[]{:S(2)}, u32[]{:S(2)}) collective-permute-start(bf16[896,512]{1,0:T(8,128)(2,1)S(1)} %fusion.29), channel_id=1, source_target_pairs={{0,1},{1,0},{2,3},{3,2},{4,5},{5,4},{6,7},{7,6},{8,9},{9,8},{10,11... | collective-permute-start | bytes 2752520 | tf_op jit(solution)/shard_map/ppermute | solution.py:88
  730.2 22.7 %collective-permute-start.78 = (bf16[896,512]{1,0:T(8,128)(2,1)S(1)}, bf16[896,512]{1,0:T(8,128)(2,1)S(1)}, u32[]{:S(2)}, u32[]{:S(2)}) collective-permute-start(bf16[896,512]{1,0:T(8,128)(2,1)S(1)} %fusion.29), channel_id=1, source_target_pairs={{0,2},{2,0},{1,3},{3,1},{4,6},{6,4},{5,7},{7,5},{8,10},{10,8},{9,1... | collective-permute-start | bytes 2752520 | tf_op jit(solution)/shard_map/ppermute | solution.py:92
  (102 other events, 1968.3 us)

commit v3 on v2

v3 whole, which is shorter than its diff:
```python
import functools
import math

import jax
import jax.numpy as jnp
from jax import lax
from jax.experimental import pallas as pl
from jax.experimental.pallas import tpu as pltpu
from jax.sharding import PartitionSpec as P

STRIDES = (12, 16)
WINDOW = 25
HALF = WINDOW // 2
GROUP = 4
BF = jnp.bfloat16
F32 = jnp.float32
MIB = 1024 * 1024
CORE_SWAP = ((0, 1), (1, 0), (2, 3), (3, 2))
Y_SWAP = ((0, 2), (2, 0), (1, 3), (3, 1))


class Layout:
    def __init__(self, n, width, block_len, ff):
        self.n, self.width, self.block_len = n, width, block_len
        self.length = GROUP * block_len
        self.taps = tuple(block_len // s for s in STRIDES)
        self.shrink = tuple(s * width for s in STRIDES)
        self.iso = tuple(p * width for p in self.taps)
        self.si_half = (self.shrink[0] + self.iso[0]) // (2 * n)
        self.k = width // n
        self.g_half = max(STRIDES) // 2 * self.k
        self.chunks = ff // width
        self.merge, self.contract = 2 * width // n, ff // n
        self.f_half = max(self.contract + self.merge, self.k * (1 + self.chunks))
        self.npos = tuple(GROUP * p for p in self.taps)

    def si_parts(self, b):
        s, i = self.shrink[b] // self.n, self.iso[b] // self.n
        return [(0, s // 2, 0, s), (s // 2, i // 2, self.shrink[b], i)]

    def g_parts(self, b):
        return [(j * self.k, self.k, j) for j in range(STRIDES[b] // 2)]

    def f_parts(self, h):
        base = self.g_half
        if h == 0:
            return [
                (base, self.contract, "contract", 0),
                (base + self.contract, self.merge, "merge", 0),
            ]
        found = [(base, self.k, "trend", 0)]
        for j in range(self.chunks):
            found.append((base + (1 + j) * self.k, self.k, "expand", j))
        return found


def held(*values):
    return lax.optimization_barrier(values)


class Ring:
    def __init__(self, n):
        self.n = n
        order = list(range(0, n, 2)) + list(range(n - 1, 0, -2))
        self.right = [(order[k], order[(k + 1) % n]) for k in range(n)]
        self.left = [(b, a) for a, b in self.right]
        d = lax.axis_index("dp")
        self.me = d
        self.pos = jnp.where(d % 2 == 0, d // 2, n - 1 - d // 2)

    def index(self, offset):
        if offset == 0:
            return self.me
        r = (self.pos + offset) % self.n
        return jnp.where(r < self.n // 2, 2 * r, 2 * (self.n - 1 - r) + 1)


def slot(sends, work=None, given=()):
    names = list(sends)
    tied = held(*[sends[k][0] for k in names], *given)
    moved = [sends[k][1](v) for k, v in zip(names, tied)]
    done = tuple(work(*tied[len(names) :])) if work is not None else ()
    out = held(*moved, *done)
    return dict(zip(names, out[: len(names)])), out[len(names) :]


def swap_core(v):
    return lax.ppermute(v, "group", CORE_SWAP)


def swap_y(v):
    return lax.ppermute(v, "group", Y_SWAP)


def dot(a, b):
    return jnp.dot(a, b, preferred_element_type=F32)


def dot_t(a, b):
    return lax.dot_general(a, b, (((1,), (1,)), ((), ())), preferred_element_type=F32)


def dot_w(a, b):
    return lax.dot_general(a, b, (((0,), (0,)), ((), ())), preferred_element_type=F32)


def normal(v):
    center = jnp.mean(v, axis=-1, keepdims=True)
    centered = v - center
    inverse = lax.rsqrt(jnp.mean(centered * centered, axis=-1, keepdims=True) + 1e-05)
    return centered * inverse, inverse


def normal_back(grad, hat, inverse, gain):
    g = grad * gain
    a = jnp.mean(g, axis=-1, keepdims=True)
    b = jnp.mean(g * hat, axis=-1, keepdims=True)
    return inverse * (g - a - hat * b)


def erf_pair(h):
    x = jnp.abs(h) * (1.0 / math.sqrt(2.0))
    d = 1.0 + 0.3275911 * x
    t = pl.reciprocal(d, approx=True)
    t = t * (2.0 - d * t)
    e = jnp.exp(-0.5 * h * h)
    p = t * (
        0.254829592
        + t * (-0.284496736 + t * (1.421413741 + t * (-1.453152027 + t * 1.061405429)))
    )
    q = 0.5 * p * e
    return jnp.where(h >= 0, 1.0 - q, q), h * e * (1.0 / math.sqrt(2.0 * math.pi))


def over(parts, first, rows):
    for part in parts:
        lo, hi = max(first, part[0]), min(first + rows, part[0] + part[1])
        if lo < hi:
            yield lo - first, hi - lo, lo - part[0], part


def start_copy(piece, row, rows, whole, at, sem):
    at = at if isinstance(at, int) else pl.multiple_of(at, 16)
    pltpu.make_async_copy(
        piece.at[pl.ds(row, rows)], whole.at[pl.ds(at, rows)], sem
    ).start()


def wait_rows(whole, first, rows, sem):
    view = whole.at[pl.ds(first, rows)]
    pltpu.make_async_copy(view, view, sem).wait()


class Pieces:
    def __init__(self):
        self.meta, self.arrays = [], []

    def add(self, source, other, first, array):
        self.meta.append((source, other, first, array.shape[0]))
        self.arrays.append(array)


def load_si(lay, b, where, meta, refs, whole, sems):
    core = where[1]
    for (source, other, first, rows), ref in zip(meta, refs):
        src = where[2 + source]
        h = 1 - core if other else core
        for row, count, inside, part in over(lay.si_parts(b), first, rows):
            _, half, base, shard = part
            at = base + src * shard + h * half + inside
            start_copy(ref, row, count, whole, at, sems.at[0 if base == 0 else 1])


def load_g(lay, b, where, meta, refs, whole, sem):
    core = where[1]
    for (source, other, first, rows), ref in zip(meta, refs):
        src = where[2 + source]
        h = 1 - core if other else core
        for row, count, inside, part in over(lay.g_parts(b), first - lay.si_half, rows):
            at = (h * (STRIDES[b] // 2) + part[2]) * lay.width + src * lay.k + inside
            start_copy(ref, row, count, whole, at, sem)


def load_f(lay, c, where, meta, refs, wholes, sems):
    names = ("merge", "contract", "trend", "expand")
    for (source, other, first, rows), ref in zip(meta, refs):
        src = where[2 + source]
        h = 1 - c if other else c
        for row, count, inside, part in over(lay.f_parts(h), first - lay.si_half, rows):
            t = names.index(part[2])
            at = part[3] * lay.width + src * part[1] + inside
            start_copy(ref, row, count, wholes[t], at, sems.at[t])


def any_spec():
    return pl.BlockSpec(memory_space=pl.ANY)


def vmem_spec():
    return pl.BlockSpec(memory_space=pltpu.VMEM)


def smem_spec():
    return pl.BlockSpec(memory_space=pltpu.SMEM)


def cost(flops, moved):
    return pl.CostEstimate(flops=int(flops), bytes_accessed=int(moved), transcendentals=0)


def by_branch(where, body):
    for b in range(2):
        pl.when(where[0] == b)(functools.partial(body, b))


def half_of(lay, where, sibling, fs, cs, fi, ci, fg, cg, weights):
    width, k = lay.width, lay.k
    base = lay.si_half
    rows = base + lay.g_half + lay.f_half

    def kernel(where, fs, cs, fi, ci, fg, cg, contract, merge, trend, expand, out, sems):
        def moves(b, h):
            found = []
            for i, (first, half, _, _) in enumerate(lay.si_parts(b)):
                source = ((fs, fi), (cs, ci))[b][i]
                found.append((source.at[pl.ds(h * half, half)], out.at[pl.ds(first, half)]))
            for first, count, j in lay.g_parts(b):
                col = (h * (STRIDES[b] // 2) + j) * width
                source = (fg, cg)[b].at[:, pl.ds(col, width)]
                found.append((source, out.at[pl.ds(base + first, count)]))
            named = {"contract": contract, "merge": merge, "trend": trend}
            for first, count, name, j in lay.f_parts(h):
                source = expand.at[:, pl.ds(j * width, width)] if name == "expand" else named[name]
                found.append((source, out.at[pl.ds(base + first, count)]))
            return [(x, y, sems.at[i]) for i, (x, y) in enumerate(found)]

        for b in range(2):
            for h in range(2):

                @pl.when((where[0] == b) & (where[1] == (1 - h if sibling else h)))
                def _(b=b, h=h):
                    used = lay.g_parts(b)[-1][0] + k
                    if used < lay.g_half:
                        out[base + used : base + lay.g_half, :] = jnp.zeros(
                            (lay.g_half - used, width), BF
                        )
                    used = lay.f_parts(h)[-1][0] + lay.f_parts(h)[-1][1]
                    if used < lay.g_half + lay.f_half:
                        out[base + used :, :] = jnp.zeros((rows - base - used, width), BF)
                    for x, y, sem in moves(b, h):
                        pltpu.make_async_copy(x, y, sem).start()
                    for x, y, sem in moves(b, h):
                        pltpu.make_async_copy(x, y, sem).wait()

    return pl.pallas_call(
        kernel,
        out_shape=jax.ShapeDtypeStruct((rows, width), BF),
        in_specs=[smem_spec()] + [any_spec()] * 10,
        out_specs=vmem_spec(),
        scratch_shapes=[pltpu.SemaphoreType.DMA((8 + max(STRIDES),))],
        compiler_params=pltpu.CompilerParams(vmem_limit_bytes=60 * MIB),
        cost_estimate=cost(0, 4 * rows * width),
        name="sibling_half" if sibling else "own_half",
    )(where, fs, cs, fi, ci, fg, cg, *weights)


def bounds_of(kinds, base):
    firsts, lasts = [jnp.int32(0)], [jnp.int32(GROUP - 1)]
    for b in range(1, GROUP):
        firsts.append(jnp.where(kinds[base + b] == 2, firsts[-1], b))
    for b in reversed(range(GROUP - 1)):
        lasts.insert(0, jnp.where(kinds[base + b + 1] == 2, lasts[0], b))
    return firsts, lasts


def counts_of(lay, kinds, base, step):
    firsts, lasts = bounds_of(kinds, base)
    length = lay.length
    first = jnp.zeros_like(step)
    last = jnp.full_like(step, length - 1)
    for b in range(GROUP):
        inside = (step >= b * lay.block_len) & (step < (b + 1) * lay.block_len)
        first = jnp.where(inside, firsts[b] * lay.block_len, first)
        last = jnp.where(inside, lasts[b] * lay.block_len + (lay.block_len - 1), last)
    j = lax.broadcasted_iota(jnp.int32, (length, length), 1)
    low = jnp.maximum(step - HALF, first)
    high = jnp.minimum(step + HALF, last)
    count = jnp.where((j >= low) & (j <= high), 1.0, 0.0)
    before = jnp.maximum(first - step + HALF, 0).astype(F32)
    after = jnp.maximum(step + HALF - last, 0).astype(F32)
    count += jnp.where(j == first, before, 0.0)
    count += jnp.where(j == last, after, 0.0)
    return count.astype(BF)


def season_kernel(lay, kinds, step, x, with_trend):
    width, length = lay.width, lay.length
    groups = x.shape[0]

    def kernel(kinds_ref, step_ref, x_ref, season_ref, low_ref, *refs):
        base = pl.program_id(0) * GROUP
        step = step_ref[...]
        x = x_ref[0]
        j = lax.broadcasted_iota(jnp.int32, (length, length), 1)
        order = jnp.where(j == step, 1.0, 0.0).astype(BF)
        season = dot(order, x) - dot(counts_of(lay, kinds_ref, base, step), x) * (1.0 / WINDOW)
        season_ref[0] = season
        low_ref[0] = season.astype(BF)
        if with_trend:
            counts_ref, trend_ref, order_ref = refs
            order_ref[...] = order
            plain = lax.broadcasted_iota(jnp.int32, (length, 1), 0)
            counts = counts_of(lay, kinds_ref, base, plain)
            counts_ref[0] = counts
            trend_ref[0] = (dot(counts, x) * (1.0 / WINDOW)).astype(BF)

    group = pl.BlockSpec((1, length, width), lambda g: (g, 0, 0))
    square = pl.BlockSpec((1, length, length), lambda g: (g, 0, 0))
    shapes = [
        jax.ShapeDtypeStruct((groups, length, width), F32),
        jax.ShapeDtypeStruct((groups, length, width), BF),
    ]
    specs = [group, group]
    if with_trend:
        shapes += [
            jax.ShapeDtypeStruct((groups, length, length), BF),
            jax.ShapeDtypeStruct((groups, length, width), BF),
            jax.ShapeDtypeStruct((length, length), BF),
        ]
        specs += [square, group, pl.BlockSpec((length, length), lambda g: (0, 0))]
    return pl.pallas_call(
        kernel,
        grid=(groups,),
        out_shape=shapes,
        in_specs=[smem_spec(), pl.BlockSpec((length, 1), lambda g: (0, 0)), group],
        out_specs=specs,
        compiler_params=pltpu.CompilerParams(vmem_limit_bytes=60 * MIB),
        cost_estimate=cost(6 * groups * length * length * width, 12 * groups * length * width),
        name="season_trend" if with_trend else "season",
    )(kinds, step, x)


def tap_rows(x, age, k):
    if k == 0:
        return x
    return jnp.where(age >= k, pltpu.roll(x, k, 0), 0.0)


def step_rows(own, other, s, npos):
    cut = slice(s * npos, (s + 1) * npos)
    x = jnp.concatenate([own[:, cut, :], other[:, cut, :]], axis=0)
    return x.reshape(x.shape[0] * npos, x.shape[2])


def shrink_forward(lay, where, si, low_own, low_other, kinds_own, kinds_other, gain):
    n, width = lay.n, lay.width
    groups = 2 * low_own.shape[0]
    most = groups * max(lay.npos)
    count = len(si.arrays)
    total = lay.shrink[0] + lay.iso[0]

    def kernel(where, kinds_own, kinds_other, gain_ref, own_ref, other_ref, *refs):
        pieces, rest = refs[:count], refs[count:]
        shrunk_ref, iso_ref, mixed_ref, age_ref, whole_out, whole, sems = rest

        def body(b):
            load_si(lay, b, where, si.meta, pieces, whole, sems)
            npos = lay.npos[b]
            m = groups * npos
            wait_rows(whole, 0, lay.shrink[b], sems.at[0])
            z = jnp.zeros((m, width), F32)
            for s in range(STRIDES[b]):
                z += dot(step_rows(own_ref, other_ref, s, npos), whole[s * width : (s + 1) * width])
            shrunk = jnp.tanh(z)
            shrunk_ref[:m] = shrunk
            low = shrunk.astype(BF).astype(F32)
            wait_rows(whole, lay.shrink[b], lay.iso[b], sems.at[1])
            pltpu.make_async_copy(whole, whole_out, sems.at[2]).start()
            taps = lay.taps[b]
            base = lay.shrink[b]
            row = lax.broadcasted_iota(jnp.int32, (m, 1), 0)
            age = jnp.zeros_like(row)
            for g in range(groups):
                own = g < groups // 2
                kinds = kinds_own if own else kinds_other
                firsts, _ = bounds_of(kinds, (g if own else g - groups // 2) * GROUP)
                for i in range(GROUP):
                    lo = g * npos + i * taps
                    inside = (row >= lo) & (row < lo + taps)
                    age = jnp.where(inside, row - lo + (i - firsts[i]) * taps, age)
            age_ref[:m] = age
            e = jnp.zeros((m, width), F32)
            for k in range(taps):
                at = base + (taps - 1 - k) * width
                e += dot(tap_rows(low, age, k).astype(BF), whole[at : at + width])
            iso = jnp.tanh(e)
            iso_ref[:m] = iso
            hat, _ = normal(iso + shrunk)
            mixed_ref[:m] = (hat * gain_ref[...]).astype(BF)
            pltpu.make_async_copy(whole, whole_out, sems.at[2]).wait()

        by_branch(where, body)

    return pl.pallas_call(
        kernel,
        out_shape=[
            jax.ShapeDtypeStruct((most, width), F32),
            jax.ShapeDtypeStruct((most, width), F32),
            jax.ShapeDtypeStruct((most, width), BF),
            jax.ShapeDtypeStruct((most, 1), jnp.int32),
            jax.ShapeDtypeStruct((total, width), BF),
        ],
        in_specs=[smem_spec()] * 3 + [vmem_spec()] * 3 + [any_spec()] * count,
        out_specs=[vmem_spec()] * 4 + [any_spec()],
        scratch_shapes=[pltpu.VMEM((total, width), BF), pltpu.SemaphoreType.DMA((3,))],
        compiler_params=pltpu.CompilerParams(vmem_limit_bytes=60 * MIB),
        cost_estimate=cost(2 * most * width * total, 4 * total * width),
        name="shrink_forward",
    )(where, kinds_own, kinds_other, gain, low_own, low_other, *si.arrays)


def stage(lay, b, copies):
    def view(ref, first, rows, middle):
        return ref.at[:, pl.ds(first, rows), :] if middle else ref.at[pl.ds(first, rows)]

    def run(i):
        for source, target, rows, sems, middle in copies:
            yield pltpu.make_async_copy(
                view(source, i * 4 * rows, 4 * rows, middle),
                view(target, i * 4 * rows, 4 * rows, middle),
                sems.at[i],
            )

    def start(i):
        for c in run(i):
            c.start()

    def wait(i):
        for c in run(i):
            c.wait()

    return start, wait


def grow_forward(lay, where, gf, part, mixed, season, order, gain):
    width = lay.width
    groups = season.shape[0]
    length = lay.length
    pieces_in = isinstance(gf, Pieces)
    arrays = gf.arrays if pieces_in else [gf]
    count = len(arrays)
    most = max(STRIDES) * width
    runs = max(STRIDES) // 4

    def kernel(where, gain_ref, order_ref, mixed_ref, season_in, *refs):
        pieces, rest = refs[:count], refs[count:]
        outs, up_out = rest[:groups], rest[groups]
        scratch = rest[groups + 1 + pieces_in :]
        rows_ref, whole, season_ref, up_ref, in_sems, w_sems, up_sems, sems = scratch

        def body(b):
            npos = lay.npos[b]
            m = groups * npos
            copies = [(season_in, season_ref, npos, in_sems, True)]
            if not pieces_in:
                copies.append((pieces[0], whole, width, w_sems, False))
            start, wait = stage(lay, b, copies)
            up_start, up_wait = stage(lay, b, [(up_ref, up_out, npos, up_sems, True)])
            if pieces_in:
                load_g(lay, b, where, gf.meta, pieces, whole, sems.at[0])
            for i in range(STRIDES[b] // 4):
                start(i)
            if pieces_in:
                wait_rows(whole, 0, STRIDES[b] * width, sems.at[0])
                pltpu.make_async_copy(whole, rest[groups + 1], sems.at[1]).start()
            x = mixed_ref[part * m : (part + 1) * m]
            gain = gain_ref[...]
            for s in range(STRIDES[b]):
                if s % 4 == 0:
                    wait(s // 4)
                cut = slice(s * npos, (s + 1) * npos)
                up = jnp.tanh(dot(x, whole[s * width : (s + 1) * width]))
                up_ref[:, cut, :] = up.reshape(groups, npos, width)
                hat, _ = normal(up + season_ref[:, cut, :].reshape(m, width))
                rows_ref[:, cut, :] = (hat * gain).astype(BF).reshape(groups, npos, width)
                if s % 4 == 3:
                    up_start(s // 4)
            for g in range(groups):
                outs[g][0] = dot_w(order_ref[...], rows_ref[g]).astype(BF)
            for i in range(STRIDES[b] // 4):
                up_wait(i)
            if pieces_in:
                pltpu.make_async_copy(whole, rest[groups + 1], sems.at[1]).wait()

        by_branch(where, body)

    shapes = [jax.ShapeDtypeStruct((1, length, width), BF)] * groups
    shapes.append(jax.ShapeDtypeStruct((groups, length, width), F32))
    if pieces_in:
        shapes.append(jax.ShapeDtypeStruct((most, width), BF))
    return pl.pallas_call(
        kernel,
        out_shape=shapes,
        in_specs=[smem_spec()] + [vmem_spec()] * 3 + [any_spec()] * (1 + count),
        out_specs=[vmem_spec()] * groups + [any_spec()] * (1 + pieces_in),
        scratch_shapes=[
            pltpu.VMEM((groups, length, width), BF),
            pltpu.VMEM((most, width), BF),
            pltpu.VMEM((groups, length, width), F32),
            pltpu.VMEM((groups, length, width), F32),
        ]
        + [pltpu.SemaphoreType.DMA((runs,))] * 3
        + [pltpu.SemaphoreType.DMA((2,))],
        compiler_params=pltpu.CompilerParams(vmem_limit_bytes=60 * MIB),
        cost_estimate=cost(
            2 * groups * length * width * (width + length),
            2 * most * width + 14 * groups * length * width,
        ),
        name="grow_forward",
    )(where, gain, order, mixed, season, *arrays)


def grow_backward(lay, where, whole, grads, up, season, order, gain):
    width = lay.width
    groups = season.shape[0]
    length = lay.length
    most = groups * max(lay.npos)
    runs = max(STRIDES) // 4

    def kernel(where, gain_ref, order_ref, up_in, season_in, whole_in, *refs):
        grad_refs, rest = refs[:groups], refs[groups:]
        pre_ref, back_ref, sum_out, gain_grad_ref = rest[:4]
        rows_ref, whole, up_ref, season_ref, sum_ref = rest[4:9]
        sems, sum_sems = rest[9:12], rest[12]

        def body(b):
            npos = lay.npos[b]
            m = groups * npos
            start, wait = stage(
                lay,
                b,
                [
                    (up_in, up_ref, npos, sems[0], True),
                    (season_in, season_ref, npos, sems[1], True),
                    (whole_in, whole, width, sems[2], False),
                ],
            )
            sum_start, sum_wait = stage(lay, b, [(sum_ref, sum_out, npos, sum_sems, True)])
            for i in range(STRIDES[b] // 4):
                start(i)
            for g in range(groups):
                rows_ref[g] = dot(order_ref[...], grad_refs[g][...]).astype(BF)
            total = jnp.zeros((m, width), F32)
            gains = jnp.zeros((1, width), F32)
            for s in range(STRIDES[b]):
                if s % 4 == 0:
                    wait(s // 4)
                cut = slice(s * npos, (s + 1) * npos)
                up = up_ref[:, cut, :].reshape(m, width)
                hat, inverse = normal(up + season_ref[:, cut, :].reshape(m, width))
                g = rows_ref[:, cut, :].reshape(m, width).astype(F32)
                gains += jnp.sum(g * hat, axis=0, keepdims=True)
                d = normal_back(g, hat, inverse, gain_ref[...])
                sum_ref[:, cut, :] = d.reshape(groups, npos, width)
                pre = (d * (1.0 - up * up)).astype(BF)
                pre_ref[:, cut, :] = pre.reshape(groups, npos, width)
                total += dot_t(pre, whole[s * width : (s + 1) * width])
                if s % 4 == 3:
                    sum_start(s // 4)
            back_ref[:m] = total
            gain_grad_ref[...] = gains
            for i in range(STRIDES[b] // 4):
                sum_wait(i)

        by_branch(where, body)

    return pl.pallas_call(
        kernel,
        out_shape=[
            jax.ShapeDtypeStruct((groups, length, width), BF),
            jax.ShapeDtypeStruct((most, width), F32),
            jax.ShapeDtypeStruct((groups, length, width), F32),
            jax.ShapeDtypeStruct((1, width), F32),
        ],
        in_specs=[smem_spec()] + [vmem_spec()] * 2 + [any_spec()] * 3 + [vmem_spec()] * groups,
        out_specs=[vmem_spec(), vmem_spec(), any_spec(), vmem_spec()],
        scratch_shapes=[
            pltpu.VMEM((groups, length, width), BF),
            pltpu.VMEM((whole.shape[0], width), BF),
            pltpu.VMEM((groups, length, width), F32),
            pltpu.VMEM((groups, length, width), F32),
            pltpu.VMEM((groups, length, width), F32),
        ]
        + [pltpu.SemaphoreType.DMA((runs,))] * 4,
        compiler_params=pltpu.CompilerParams(vmem_limit_bytes=60 * MIB),
        cost_estimate=cost(
            2 * groups * length * width * (width + length),
            2 * whole.shape[0] * width + 18 * groups * length * width,
        ),
        name="grow_backward",
    )(where, gain, order, up, season, whole, *grads)


class Outlet:
    def __init__(self, n, rows, width, cuts):
        self.n, self.rows, self.width = n, rows, width
        self.bounds = [(0, n)] if cuts is None else cuts

    def shapes(self):
        sizes = [self.n] + [hi - lo for lo, hi in self.bounds]
        return [jax.ShapeDtypeStruct((c, self.rows, self.width), BF) for c in sizes]

    def scratch(self):
        return [
            pltpu.VMEM((2, self.n, self.rows, self.width), BF),
            pltpu.SemaphoreType.DMA((1 + len(self.bounds),)),
        ]

    def copies(self, held_ref, outs, sems):
        found = [pltpu.make_async_copy(held_ref.at[0], outs[0], sems.at[0])]
        for i, (lo, hi) in enumerate(self.bounds):
            source = held_ref.at[1, pl.ds(lo, hi - lo)]
            found.append(pltpu.make_async_copy(source, outs[1 + i], sems.at[1 + i]))
        return found

    def flush(self, held_ref, outs, sems):
        for c in self.copies(held_ref, outs, sems):
            c.start()
        for c in self.copies(held_ref, outs, sems):
            c.wait()


def grow_weight(lay, where, places, mixed, pre_own, pre_other, outlet):
    n, width, k = lay.n, lay.width, lay.k
    groups = pre_own.shape[0]
    made = len(outlet.shapes())

    def kernel(where, places_ref, mixed_ref, own_ref, other_ref, *refs):
        outs, (out_ref, sems) = refs[:made], refs[made:]

        def body(b):
            npos = lay.npos[b]
            x = mixed_ref[: 2 * groups * npos]
            steps = STRIDES[b] // 2
            for s in range(STRIDES[b]):
                d = dot_w(x, step_rows(own_ref, other_ref, s, npos)).astype(BF)
                side = jnp.where(where[1] == s // steps, 0, 1)
                at = (s % steps) * k
                for shard in range(n):
                    out_ref[side, places_ref[shard], at : at + k, :] = d[shard * k : (shard + 1) * k]
            rest = lay.g_half - steps * k
            if rest:
                out_ref[:, :, steps * k :, :] = jnp.zeros((2, n, rest, width), BF)

        by_branch(where, body)
        outlet.flush(out_ref, outs, sems)

    return pl.pallas_call(
        kernel,
        out_shape=outlet.shapes(),
        in_specs=[smem_spec(), smem_spec()] + [vmem_spec()] * 3,
        out_specs=[any_spec()] * made,
        scratch_shapes=outlet.scratch(),
        compiler_params=pltpu.CompilerParams(vmem_limit_bytes=60 * MIB),
        cost_estimate=cost(4 * groups * lay.length * width * width, 2 * 2 * n * lay.g_half * width),
        name="grow_weight",
    )(where, places, mixed, pre_own, pre_other)


def shrink_backward(lay, where, whole, back_own, back_other, shrunk, iso, age, gain):
    width = lay.width
    most = shrunk.shape[0]

    def kernel(where, age_ref, gain_ref, b0, b1, shrunk_ref, iso_ref, whole_in, *refs):
        pre_ref, iso_pre_ref, gain_grad_ref, whole, sem = refs

        def body(b):
            npos, taps = lay.npos[b], lay.taps[b]
            base = lay.shrink[b]
            source = whole_in.at[pl.ds(base, lay.iso[b])]
            fetch = pltpu.make_async_copy(source, whole.at[pl.ds(0, lay.iso[b])], sem)
            fetch.start()
            m = (most // max(lay.npos)) * npos
            mixed_back = jnp.concatenate([b0[: m // 2], b1[: m // 2]], axis=0)
            shrunk, iso = shrunk_ref[:m], iso_ref[:m]
            hat, inverse = normal(iso + shrunk)
            gain_grad_ref[...] = jnp.sum(mixed_back * hat, axis=0, keepdims=True)
            joint = normal_back(mixed_back, hat, inverse, gain_ref[...])
            iso_pre = (joint * (1.0 - iso * iso)).astype(BF)
            iso_pre_ref[:m] = iso_pre
            age = age_ref[:m]
            total = joint
            fetch.wait()
            for k in range(taps):
                tap = taps - 1 - k
                back = dot_t(iso_pre, whole[tap * width : (tap + 1) * width])
                if k:
                    back = pltpu.roll(jnp.where(age >= k, back, 0.0), m - k, 0)
                total += back
            pre_ref[:m] = (total * (1.0 - shrunk * shrunk)).astype(BF)

        by_branch(where, body)

    return pl.pallas_call(
        kernel,
        out_shape=[
            jax.ShapeDtypeStruct((most, width), BF),
            jax.ShapeDtypeStruct((most, width), BF),
            jax.ShapeDtypeStruct((1, width), F32),
        ],
        in_specs=[smem_spec()] + [vmem_spec()] * 6 + [any_spec()],
        out_specs=[vmem_spec()] * 3,
        scratch_shapes=[pltpu.VMEM((max(lay.iso), width), BF), pltpu.SemaphoreType.DMA],
        compiler_params=pltpu.CompilerParams(vmem_limit_bytes=60 * MIB),
        cost_estimate=cost(2 * most * width * lay.iso[0], 2 * lay.iso[0] * width),
        name="shrink_backward",
    )(where, age, gain, back_own, back_other, shrunk, iso, whole)


def shrink_weight(lay, where, places, iso_pre, pre, shrunk, low_own, low_other, gains, age, outlet):
    width = lay.width
    most = shrunk.shape[0]
    made = len(outlet.shapes())

    def kernel(where, places_ref, age_ref, gains_ref, iso_pre_ref, pre_ref, shrunk_ref, *refs):
        own_ref, other_ref = refs[:2]
        outs, (grad_ref, sems) = refs[2 : 2 + made], refs[2 + made :]
        extra = gains_ref[...].astype(BF)
        for side in range(2):
            for place in range(lay.n):
                grad_ref[side, place, lay.si_half :, :] = extra

        def body(b):
            npos, taps = lay.npos[b], lay.taps[b]
            m = (most // max(lay.npos)) * npos

            def store(part, row, d):
                first, half, _, shard = part
                d = d.astype(BF)
                lo = row
                while lo < row + width:
                    dp, h, r = lo // shard, (lo % shard) // half, lo % half
                    rows = min(half - r, row + width - lo)
                    side = jnp.where(where[1] == h, 0, 1)
                    grad_ref[side, places_ref[dp], first + r : first + r + rows, :] = d[
                        lo - row : lo - row + rows
                    ]
                    lo += rows

            part_s, part_i = lay.si_parts(b)
            low = shrunk_ref[:m].astype(BF).astype(F32)
            age = age_ref[:m]
            iso_pre, pre = iso_pre_ref[:m], pre_ref[:m]
            for k in range(taps):
                tap = taps - 1 - k
                store(part_i, tap * width, dot_w(tap_rows(low, age, k).astype(BF), iso_pre))
            for s in range(STRIDES[b]):
                store(part_s, s * width, dot_w(step_rows(own_ref, other_ref, s, npos), pre))

        by_branch(where, body)
        outlet.flush(grad_ref, outs, sems)

    return pl.pallas_call(
        kernel,
        out_shape=outlet.shapes(),
        in_specs=[smem_spec(), smem_spec()] + [vmem_spec()] * 7,
        out_specs=[any_spec()] * made,
        scratch_shapes=outlet.scratch(),
        compiler_params=pltpu.CompilerParams(vmem_limit_bytes=60 * MIB),
        cost_estimate=cost(2 * most * width * (lay.iso[0] + lay.shrink[0]), 30 * MIB),
        name="shrink_weight",
    )(where, places, age, gains, iso_pre, pre, shrunk, low_own, low_other)


def season_backward(lay, where, whole, pre, sum_own, sum_other, order):
    width, length = lay.width, lay.length
    groups = sum_own.shape[0]
    most = max(lay.shrink)

    def kernel(where, order_ref, pre_ref, own_ref, other_ref, whole_in, *refs):
        outs, (whole, rows_ref, sem) = refs[: groups + 1], refs[groups + 1 :]

        def body(b):
            fetch = pltpu.make_async_copy(
                whole_in.at[pl.ds(0, lay.shrink[b])], whole.at[pl.ds(0, lay.shrink[b])], sem
            )
            fetch.start()
            npos = lay.npos[b]
            m = groups * npos
            fetch.wait()
            for s in range(STRIDES[b]):
                cut = slice(s * npos, (s + 1) * npos)
                d = dot_t(pre_ref[: 2 * m], whole[s * width : (s + 1) * width])
                rows_ref[:groups, cut, :] = (
                    d[:m].reshape(groups, npos, width) + own_ref[:, cut, :]
                ).astype(BF)
                rows_ref[groups:, cut, :] = (
                    d[m:].reshape(groups, npos, width) + other_ref[:, cut, :]
                ).astype(BF)

        by_branch(where, body)
        for g in range(groups):
            outs[0][g] = dot_w(order_ref[...], rows_ref[g]).astype(BF)
            outs[1 + g][...] = dot_w(order_ref[...], rows_ref[groups + g]).astype(BF)

    return pl.pallas_call(
        kernel,
        out_shape=[jax.ShapeDtypeStruct((groups, length, width), BF)]
        + [jax.ShapeDtypeStruct((length, width), BF)] * groups,
        in_specs=[smem_spec()] + [vmem_spec()] * 4 + [any_spec()],
        out_specs=[vmem_spec()] * (1 + groups),
        scratch_shapes=[
            pltpu.VMEM((most, width), BF),
            pltpu.VMEM((2 * groups, length, width), BF),
            pltpu.SemaphoreType.DMA,
        ],
        compiler_params=pltpu.CompilerParams(vmem_limit_bytes=60 * MIB),
        cost_estimate=cost(
            4 * groups * length * width * (width + length),
            2 * most * width + 24 * groups * length * width,
        ),
        name="season_backward",
    )(where, order, pre, sum_own, sum_other, whole)


def dense_whole(lay, where, gf):
    width, ff = lay.width, lay.width * lay.chunks
    count = len(gf.arrays)
    sizes = (2 * width, ff, width, ff)

    def kernel(where, *refs):
        pieces, wholes, sems = refs[:count], refs[count:-1], refs[-1]
        for c in range(2):
            pl.when(where[1] == c)(
                functools.partial(load_f, lay, c, where, gf.meta, pieces, wholes, sems)
            )
        for t in range(4):
            wait_rows(wholes[t], 0, sizes[t], sems.at[t])

    return pl.pallas_call(
        kernel,
        out_shape=[jax.ShapeDtypeStruct((r, width), BF) for r in sizes],
        in_specs=[smem_spec()] + [any_spec()] * count,
        out_specs=[vmem_spec()] * 4,
        scratch_shapes=[pltpu.SemaphoreType.DMA((4,))],
        compiler_params=pltpu.CompilerParams(vmem_limit_bytes=60 * MIB),
        cost_estimate=cost(0, 4 * sum(sizes) * width),
        name="dense_whole",
    )(where, *gf.arrays)


def dense(lay, where, tile, wholes, mine, received, trend_low, out_grad, gain_middle, gain_output):
    width, length, chunks = lay.width, lay.length, lay.chunks
    cuts = 2
    part = length // cuts
    ff = width * chunks

    def kernel(where, tile_ref, gm_ref, go_ref, merge, contract, trend, expand, *refs):
        mine_ref, got_ref, trend_ref, grad_ref = refs[:4]
        (out_ref, jm_ref, js_ref, tb_ref, ml_ref, hid_ref, hg_ref, ll_ref, mg_ref) = refs[4:13]
        gains_ref, slope_ref = refs[13:]
        b = where[0]
        gm, go = gm_ref[...], go_ref[...]
        at_mine = pl.multiple_of(b * width, width)
        at_other = pl.multiple_of((1 - b) * width, width)

        merged = dot(mine_ref[...], merge[pl.ds(at_mine, width)])
        merged += dot(got_ref[...], merge[pl.ds(at_other, width)])
        mhat, minv = normal(merged)
        middle = mhat * gm
        mlow = middle.astype(BF)
        ml_ref[...] = mlow
        lifted = jnp.zeros((part, width), F32)
        for j in range(chunks):
            cols = slice(j * width, (j + 1) * width)
            h = dot(mlow, expand[cols])
            phi, dens = erf_pair(h)
            hid = (h * phi).astype(BF)
            slope_ref[:, cols] = phi + dens
            hid_ref[:, cols] = hid
            lifted += dot(hid, contract[cols])
        ohat, oinv = normal(middle + lifted)
        g_low = grad_ref[0]
        projected = dot(trend_ref[0], trend[...])
        out_ref[...] = (ohat * go + projected).astype(BF)
        g = g_low.astype(F32)
        tb_ref[...] = dot_t(g_low, trend[...])
        d = normal_back(g, ohat, oinv, go)
        llow = d.astype(BF)
        ll_ref[...] = llow
        back = d
        for j in range(chunks):
            cols = slice(j * width, (j + 1) * width)
            hg = (dot_t(llow, contract[cols]) * slope_ref[:, cols]).astype(BF)
            hg_ref[:, cols] = hg
            back += dot_t(hg, expand[cols])
        mg = normal_back(back, mhat, minv, gm).astype(BF)
        mg_ref[...] = mg
        jm_ref[...] = dot_t(mg, merge[pl.ds(at_mine, width)]).astype(BF)
        js_ref[...] = dot_t(mg, merge[pl.ds(at_other, width)]).astype(BF)

        @pl.when(pl.program_id(0) == 0)
        def _():
            gains_ref[...] = jnp.zeros_like(gains_ref)

        gains_ref[0:1, :] += jnp.sum(back * mhat, axis=0, keepdims=True)
        gains_ref[1:2, :] += jnp.sum(g * ohat, axis=0, keepdims=True)

    of_tile = pl.BlockSpec((1, part, width), lambda i, w, t: (t[0], i, 0))
    alone = pl.BlockSpec((part, width), lambda i, w, t: (i, 0))
    shapes = [(width, BF)] * 3 + [(width, F32), (width, BF), (ff, BF), (ff, BF), (width, BF), (width, BF)]
    return pl.pallas_call(
        kernel,
        grid_spec=pltpu.PrefetchScalarGridSpec(
            num_scalar_prefetch=2,
            grid=(cuts,),
            in_specs=[vmem_spec()] * 6 + [alone, alone, of_tile, of_tile],
            out_specs=[pl.BlockSpec((part, w), lambda i, w, t: (i, 0)) for w, _ in shapes]
            + [pl.BlockSpec((2, width), lambda i, w, t: (0, 0))],
            scratch_shapes=[pltpu.VMEM((part, ff), F32)],
        ),
        out_shape=[jax.ShapeDtypeStruct((length, w), t) for w, t in shapes]
        + [jax.ShapeDtypeStruct((2, width), F32)],
        compiler_params=pltpu.CompilerParams(vmem_limit_bytes=60 * MIB),
        cost_estimate=cost(
            2 * length * width * (4 * width + 4 * ff + 2 * width), 12 * MIB + 20 * MIB
        ),
        name="dense",
    )(where, tile, gain_middle, gain_output, *wholes, mine, received, trend_low, out_grad)


def dense_weights(lay, where, places, mine, received, trend_low, out_grad, saved, outlet):
    n, width, chunks, length = lay.n, lay.width, lay.chunks, lay.length
    groups = len(saved)
    made = len(outlet.shapes())
    base = lay.g_half
    (_, contract, _, _), (merge_at, merge, _, _) = lay.f_parts(0)
    merge_at -= base

    def kernel(where, places_ref, *refs):
        refs = list(refs)

        def take(count):
            out = refs[:count]
            del refs[:count]
            return out

        middle, lifted = take(groups), take(groups)
        hidden, slopes = take(groups), take(groups)
        late = take(3 * groups) + take(2)
        outs = take(made)
        out_ref, sems, mine_ref, got_ref, grad_ref, trend_ref, up_ref, late_sems = refs
        core, q = where[1], pl.program_id(0)

        def fetches():
            targets = [r.at[g] for r in (mine_ref, got_ref, grad_ref) for g in range(groups)]
            targets += [trend_ref, up_ref]
            return [
                pltpu.make_async_copy(x, y, late_sems.at[i])
                for i, (x, y) in enumerate(zip(late, targets))
            ]

        def side(h):
            return jnp.where(core == h, 0, 1)

        def total(xs, gs):
            d = None
            for x, g in zip(xs, gs):
                v = dot_w(x, g)
                d = v if d is None else d + v
            return d.astype(BF)

        @pl.when(q == 0)
        def _():
            for f in fetches():
                f.start()
            if merge_at + merge < lay.f_half:
                out_ref[side(0), :, merge_at + merge :, :] = jnp.zeros(
                    (n, lay.f_half - merge_at - merge, width), BF
                )

        d = total([r[...] for r in hidden], [r[...] for r in lifted])
        each = width // contract
        for i in range(each):
            out_ref[side(0), places_ref[q * each + i], 0:contract, :] = d[
                i * contract : (i + 1) * contract
            ]
        d = total([r[...] for r in middle], [r[...] for r in slopes])
        at = pl.ds(pl.multiple_of((1 + q) * lay.k, 16), lay.k)
        for dp in range(n):
            out_ref[side(1), places_ref[dp], at, :] = d[dp * lay.k : (dp + 1) * lay.k]

        @pl.when(q == chunks - 1)
        def _():
            for f in fetches():
                f.wait()
            d = total([trend_ref[g] for g in range(groups)], [up_ref[g] for g in range(groups)])
            for dp in range(n):
                out_ref[side(1), places_ref[dp], 0 : lay.k, :] = d[dp * lay.k : (dp + 1) * lay.k]
            each = width // merge
            for ref, first in ((mine_ref, where[0]), (got_ref, 1 - where[0])):
                d = total([ref[g] for g in range(groups)], [grad_ref[g] for g in range(groups)])
                for i in range(each):
                    out_ref[side(0), places_ref[first * each + i], merge_at : merge_at + merge, :] = d[
                        i * merge : (i + 1) * merge
                    ]
            used = (1 + chunks) * lay.k
            if used < lay.f_half:
                out_ref[side(1), :, used:, :] = jnp.zeros((n, lay.f_half - used, width), BF)
            outlet.flush(out_ref, outs, sems)

    whole = pl.BlockSpec((length, width), lambda q: (0, 0))
    column = pl.BlockSpec((length, width), lambda q: (0, q))
    arrays = [k[0] for k in saved] + [k[3] for k in saved]
    arrays += [k[1] for k in saved] + [k[2] for k in saved]
    arrays += [v.reshape(length, width) for v in mine] + list(received) + [k[4] for k in saved]
    arrays += [trend_low, out_grad]
    ff = chunks * width
    square = pltpu.VMEM((groups, length, width), BF)
    return pl.pallas_call(
        kernel,
        grid=(chunks,),
        out_shape=outlet.shapes(),
        in_specs=[smem_spec(), smem_spec()]
        + [whole] * (2 * groups)
        + [column] * (2 * groups)
        + [any_spec()] * (3 * groups + 2),
        out_specs=[any_spec()] * made,
        scratch_shapes=outlet.scratch()
        + [square] * 5
        + [pltpu.SemaphoreType.DMA((3 * groups + 2,))],
        compiler_params=pltpu.CompilerParams(vmem_limit_bytes=60 * MIB),
        cost_estimate=cost(
            2 * groups * length * width * (2 * width + 2 * ff + width), 45 * MIB
        ),
        name="dense_weights",
    )(where, places, *arrays)


def exchange(axis, size, step):
    return lambda v: lax.ppermute(v, axis, [(i, i ^ step) for i in range(size)])


def on_device(
    n,
    series_in,
    block_kinds,
    out_grad,
    fine_shrink,
    coarse_shrink,
    fine_isometric,
    coarse_isometric,
    fine_grow,
    coarse_grow,
    merge_weight,
    expand_weight,
    contract_weight,
    trend_weight,
    branch_gain,
    middle_gain,
    output_gain,
):
    ring = Ring(n)
    member = lax.axis_index("group")
    core, y = member % 2, member // 2
    block_count = block_kinds.shape[0]
    width = series_in.shape[1]
    block_len = series_in.shape[0] // block_count
    groups = block_count // GROUP
    lay = Layout(n, width, block_len, expand_weight.shape[1])
    length = lay.length
    share = branch_gain.shape[0]
    fine = y == 0

    def right(v):
        return lax.ppermute(v, "dp", ring.right)

    def left(v):
        return lax.ppermute(v, "dp", ring.left)

    shards = (fine_shrink, coarse_shrink, fine_isometric, coarse_isometric)
    shards += (fine_grow, coarse_grow)
    dense_shards = (contract_weight, merge_weight, trend_weight, expand_weight)
    member_ids = jnp.stack([y, core]).astype(jnp.int32)
    own = half_of(lay, member_ids, False, *shards, dense_shards)
    offsets = [0]
    pieces = Pieces()
    for k in range(1, n // 2):
        offsets += [-k, k]
    offsets.append(n // 2)

    def source(offset):
        return offsets.index(offset if abs(offset) < n // 2 else n // 2)

    where = jnp.stack([y, core] + [ring.index(o) for o in offsets]).astype(jnp.int32)

    x_own = series_in.reshape(groups, length, width)
    x_other = []
    last = n // 2

    def prepare_own(kinds, x):
        rows = jnp.arange(length, dtype=jnp.int32)
        npos = jnp.where(fine, lay.npos[0], lay.npos[1])
        stride = jnp.where(fine, STRIDES[0], STRIDES[1])
        step = ((rows % npos) * stride + rows // npos)[:, None]
        return (step, *season_kernel(lay, kinds, step, x, True))

    def prepare_other(step, kinds, *xs):
        kinds = kinds.astype(jnp.int32)
        return (kinds, *season_kernel(lay, kinds, step, jnp.stack(xs), False))

    def spread_gains(*parts):
        parts = jnp.stack(parts).astype(F32)
        return lax.dynamic_update_slice(
            jnp.zeros((3, width), F32), parts, (jnp.int32(0), ring.me * share)
        )

    doublings = []
    size = 1
    while size < n:
        doublings.append(size)
        size *= 2
    gains = spread_gains(branch_gain, middle_gain, output_gain)
    hops = [exchange("dp", n, d) for d in doublings]

    def hop(sends):
        if hops:
            sends["gain"] = (gains, hops.pop(0))

    whole_r = whole_l = own
    half_rows = (lay.g_half + lay.f_half) // 2
    si_rows = lay.si_half // 2
    for t in range(1, last):
        sends = {"r": (whole_r, right), "l": (whole_l, left)}
        if t > 1:
            sends["cr"], sends["cl"] = (whole_r, swap_core), (whole_l, swap_core)
        if t <= groups:
            sends["x"] = (x_own[t - 1], swap_y)
        work, given = None, ()
        if t == 1:
            sends["k"] = (block_kinds.astype(F32), swap_y)
            hop(sends)
            work = lambda *v: (half_of(lay, member_ids, True, *v[:6], v[6:]),)
            given = (*shards, *dense_shards)
        elif t == 2:
            work, given = prepare_own, (block_kinds, x_own)
        arrived, done = slot(sends, work, given)
        if t == 1:
            kinds_other = arrived["k"]
            pieces.add(0, 0, 0, own)
            pieces.add(0, 1, 0, done[0])
        elif t == 2:
            step, season_own, low_own, own_counts, trend_low, order = done
        if "x" in arrived:
            x_other.append(arrived["x"])
        if "gain" in arrived:
            gains = gains + arrived["gain"]
        if t > 1:
            pieces.add(source(1 - t), 1, 0, arrived["cr"])
            pieces.add(source(t - 1), 1, 0, arrived["cl"])
        whole_r, whole_l = arrived["r"], arrived["l"]
        pieces.add(source(-t), 0, 0, whole_r)
        pieces.add(source(t), 0, 0, whole_l)
    middle = lay.si_half
    sends = {"r": (whole_r[:si_rows], right), "l": (whole_l[si_rows:middle], left)}
    sends["cr"], sends["cl"] = (whole_r, swap_core), (whole_l, swap_core)
    hop(sends)
    arrived, done = slot(sends, prepare_other, (step, kinds_other, *x_other))
    kinds_other, season_other, low_other = done
    if "gain" in arrived:
        gains = gains + arrived["gain"]
    pieces.add(source(1 - last), 1, 0, arrived["cr"])
    pieces.add(source(last - 1), 1, 0, arrived["cl"])
    si_r, si_l = arrived["r"], arrived["l"]
    pieces.add(source(last), 0, 0, si_r)
    pieces.add(source(last), 0, si_rows, si_l)
    sends = {"cr": (si_r, swap_core), "cl": (si_l, swap_core)}
    hop(sends)
    arrived, _ = slot(sends)
    if "gain" in arrived:
        gains = gains + arrived["gain"]
    pieces.add(source(last), 1, 0, arrived["cr"])
    pieces.add(source(last), 1, si_rows, arrived["cl"])
    for move_gains in hops:
        gains = gains + move_gains(gains)
    gain_b, gain_m, gain_o = gains[0:1], gains[1:2], gains[2:3]

    def run_shrink(low_own, low_other, *arrays):
        pieces.arrays = list(arrays)
        return shrink_forward(
            lay, where, pieces, low_own, low_other, block_kinds, kinds_other, gain_b
        )

    cut_at = middle + half_rows
    sends = {"r": (whole_r[middle:cut_at], right), "l": (whole_l[cut_at:], left)}
    arrived, done = slot(sends, run_shrink, (low_own, low_other, *pieces.arrays))
    shrunk, iso, mixed, age, si_whole = done
    gf_r, gf_l = arrived["r"], arrived["l"]
    pieces.add(source(last), 0, middle, gf_r)
    pieces.add(source(last), 0, cut_at, gf_l)
    arrived, _ = slot({"cr": (gf_r, swap_core), "cl": (gf_l, swap_core)})
    pieces.add(source(last), 1, middle, arrived["cr"])
    pieces.add(source(last), 1, cut_at, arrived["cl"])
    gf = pieces

    *branch_other, up_other, g_whole = grow_forward(
        lay, where, gf, 1, mixed, season_other, order, gain_b
    )
    branch_other = [v.reshape(length, width) for v in branch_other]
    grads_in = out_grad.reshape(groups, length, width)

    def grow_own(mixed, g_whole, season_own, *arrays):
        gf.arrays = list(arrays)
        made = grow_forward(lay, where, g_whole, 0, mixed, season_own, order, gain_b)
        return (*made, *dense_whole(lay, where, gf))

    arrived, done = slot(
        {"b": (branch_other[0], swap_y)}, grow_own, (mixed, g_whole, season_own, *gf.arrays)
    )
    branch_own = [v.reshape(length, width) for v in done[:groups]]
    up_own, wholes = done[groups], done[groups + 1 :]
    received = [arrived["b"]]
    outs, back_own, back_got, waiting, trend_back, saved, dense_gains = [], [], [], [], [], [], None
    for g in range(groups):
        sends = {}
        if g + 1 < groups:
            sends["b"] = (branch_other[g + 1], swap_y)
        elif waiting:
            sends["j"] = (waiting.pop(0), swap_y)

        def run_dense(mine, got, *wholes, g=g):
            tile = jnp.full((1,), g, jnp.int32)
            return dense(
                lay, where, tile, wholes, mine, got, trend_low, grads_in, gain_m, gain_o
            )

        arrived, made = slot(sends, run_dense, (branch_own[g], received[g], *wholes))
        if "b" in arrived:
            received.append(arrived["b"])
        if "j" in arrived:
            back_got.append(arrived["j"])
        outs.append(made[0])
        back_own.append(made[1])
        waiting.append(made[2])
        trend_back.append(made[3])
        saved.append(made[4:9])
        dense_gains = made[9] if dense_gains is None else dense_gains + made[9]
    series_out = jnp.concatenate(outs)

    ring_order = [n // 2]
    for k in range(n // 2 - 1, 0, -1):
        ring_order += [k, -k]
    ring_order.append(0)
    spot = jnp.zeros((n,), jnp.int32)
    for place, offset in enumerate(ring_order):
        spot = jnp.where(jnp.arange(n) == ring.index(offset), place, spot)

    f_outlet = Outlet(n, lay.f_half, width, None)
    g_outlet = Outlet(n, lay.g_half, width, None)
    s_outlet = Outlet(n, lay.si_half + 16, width, None)

    def run_dense_weights(*arrays):
        mine, got, flat = arrays[:groups], arrays[groups : 2 * groups], arrays[2 * groups :]
        kept = [flat[5 * g : 5 * g + 5] for g in range(groups)]
        return dense_weights(
            lay, where, spot, mine, list(got), trend_low, grads_in, kept, f_outlet
        )

    arrived, (f_keep, f_give) = slot(
        {"j": (waiting.pop(0), swap_y)},
        run_dense_weights,
        (*branch_own, *received, *[v for k in saved for v in k]),
    )
    back_got.append(arrived["j"])

    class Chain:
        def __init__(self, keep):
            self.keep = keep
            self.got = []
            self.step = last
            self.r = self.l = None
            self.half = keep.shape[1] // 2

        def here(self, place):
            first = 0
            for v in self.got:
                if place < first + v.shape[0]:
                    got = v[place - first]
                    break
                first += v.shape[0]
            return self.keep[place].astype(F32) + got.astype(F32)

        def sends(self):
            k = self.step
            if k == last:
                part = self.here(0)
                return part[: self.half].astype(BF), part[self.half :].astype(BF)
            place = 1 + 2 * (last - 1 - k)
            a, b = self.here(place), self.here(place + 1)
            if k == last - 1:
                h = self.half
                a = jnp.concatenate([a[:h] + self.r.astype(F32), a[h:]])
                b = jnp.concatenate([b[:h], b[h:] + self.l.astype(F32)])
            else:
                a, b = a + self.r.astype(F32), b + self.l.astype(F32)
            return a.astype(BF), b.astype(BF)

        def total(self):
            return (self.here(n - 1) + self.r.astype(F32) + self.l.astype(F32)).astype(BF)

    def back_of(grads, g_whole, up, season):
        return grow_backward(lay, where, g_whole, grads, up, season, order, gain_b)

    arrived, done = slot(
        {"j": (waiting.pop(0), swap_y), "f": (f_give, swap_core)},
        lambda g_whole, up, season, *grads: back_of(grads, g_whole, up, season),
        (g_whole, up_own, season_own, *back_own),
    )
    back_got.append(arrived["j"])
    pre_own, mixed_back_own, sum_own, gains_own = done
    f = Chain(f_keep)
    f.got = [arrived["f"]]
    chains = {"f": f}
    starts = {"g": 3, "s": 5}
    kept = {}
    finals = {}
    t = 0
    while True:
        active = {k: c for k, c in chains.items() if c.step > 0}
        finishing = [k for k, c in chains.items() if c.step == 0 and k + "mine" not in finals]
        if not active and not finishing and "smine" in finals:
            break
        sends, work, given = {}, None, ()
        for name, chain in active.items():
            a, b = chain.sends()
            sends[name + "r"], sends[name + "l"] = (a, right), (b, left)
        for name in finishing:
            mine = chains[name].total()
            finals[name + "mine"] = mine
            sends[name + "y"] = (mine, swap_y)
            if name != "f":
                sends[name + "c"] = (mine, swap_core)
        for name in ("f", "g"):
            ready = name + "late" in finals and (t > 6 or name == "g")
            if ready and name + "sent" not in finals:
                sends[name + "d"] = (finals[name + "late"], swap_core)
                finals[name + "sent"] = True
        if t == 0:
            work = lambda g_whole, up, season, *grads: back_of(grads, g_whole, up, season)
            given = (g_whole, up_other, season_other, *back_got)
        elif t == 1:
            work = lambda *v: grow_weight(lay, where, spot, *v, g_outlet)
            given = (mixed, pre_own, pre_other)
        elif t == 2:
            work = lambda *v: shrink_backward(lay, where, *v, age, gain_b)
            given = (si_whole, mixed_back_own, mixed_back_other, shrunk, iso)
            sends["g"] = (g_give, swap_core)
        elif t == 3:
            work = lambda *v: shrink_weight(lay, where, spot, *v, age, s_outlet)
            given = (iso_pre, shrink_pre, shrunk, low_own, low_other, grad_gains)
        elif t == 4:
            work = lambda *v: season_backward(lay, where, *v, order)
            given = (si_whole, shrink_pre, sum_own, sum_other)
            sends["s0"] = (s_give, swap_core)
        if t in (5, 6, 8) and tail_sends:
            for i in range(len(tail_sends) if t == 8 else 1):
                sends["x%d" % i] = (tail_sends.pop(0), swap_y)
        if "s" in finishing:
            work, given = finish, (season_mine, own_counts, *trend_back, *tail)
        arrived, done = slot(sends, work, given)
        if t == 0:
            pre_other, mixed_back_other, sum_other, gains_other = done
        elif t == 1:
            g_keep, g_give = done
            chains["g"] = None
        elif t == 2:
            shrink_pre, iso_pre, gains_si = done
            chains["g"] = Chain(g_keep)
            chains["g"].got = [arrived["g"]]
            grad_gains = jnp.concatenate(
                [gains_own + gains_other + gains_si, dense_gains, jnp.zeros((13, width), F32)]
            )
        elif t == 3:
            s_keep, s_give = done
        elif t == 4:
            season_mine, *tail_sends = done
            tail = []
            chains["s"] = Chain(s_keep)
            chains["s"].got = [arrived["s0"]]

            def finish(season_mine, own_counts, *rest):
                backs, tail = rest[:groups], rest[groups:]
                total = season_mine.astype(F32) + jnp.stack(tail).astype(F32)
                rest = jnp.stack(backs) - total
                spread = (rest * (1.0 / WINDOW)).astype(BF)
                averaged = jnp.einsum(
                    "gij,gid->gjd", own_counts, spread, preferred_element_type=F32
                )
                return ((total + averaged).astype(BF),)

        for i in range(groups):
            if "x%d" % i in arrived:
                tail.append(arrived["x%d" % i])
        for name, chain in active.items():
            chain.r, chain.l = arrived[name + "r"], arrived[name + "l"]
            chain.step -= 1
        for name in ("f", "g"):
            if name + "d" in arrived:
                finals[name + "d"] = arrived[name + "d"]
        for name in finishing:
            finals[name + "y"] = arrived[name + "y"]
            if name != "f":
                finals[name + "c"] = arrived[name + "c"]
            if name == "f":
                mine = finals["fmine"].astype(F32) + arrived["fy"].astype(F32)
                finals["flate"] = mine.astype(BF)
            elif name == "g":
                finals["glate"] = arrived["gy"]
            else:
                (series_grad,) = done
        if chains.get("g", 0) is None:
            del chains["g"]
        t += 1
    s_mine, s_y = finals["smine"], finals["sy"]
    s_core = (finals["sc"], swap_core(s_y))
    f_half, f_other = finals["flate"], finals["fd"]
    g_mine, g_y = finals["gmine"], finals["gy"]
    g_core = (finals["gc"], finals["gd"])

    def both(mine, other):
        return jnp.where(core == 0, mine, other), jnp.where(core == 0, other, mine)

    def branches(mine, over_y):
        return jnp.where(fine, mine, over_y), jnp.where(fine, over_y, mine)

    s_fine, s_coarse = branches(s_mine, s_y)
    t_fine, t_coarse = branches(*s_core)
    g_fine, g_coarse = branches(g_mine, g_y)
    h_fine, h_coarse = branches(*g_core)

    def si_out(b, mine, other):
        lo, hi = both(mine, other)
        (f0, r0, _, _), (f1, r1, _, _) = lay.si_parts(b)
        shrink = jnp.concatenate([lo[f0 : f0 + r0], hi[f0 : f0 + r0]])
        return shrink.astype(F32), jnp.concatenate([lo[f1 : f1 + r1], hi[f1 : f1 + r1]]).astype(F32)

    def g_out(b, mine, other):
        lo, hi = both(mine, other)
        cols = [v[r : r + k] for v in (lo, hi) for r, k, _ in lay.g_parts(b)]
        return jnp.concatenate(cols, axis=1).astype(F32)

    fine_shrink_grad, fine_iso_grad = si_out(0, s_fine, t_fine)
    coarse_shrink_grad, coarse_iso_grad = si_out(1, s_coarse, t_coarse)
    fine_grow_grad, coarse_grow_grad = g_out(0, g_fine, h_fine), g_out(1, g_coarse, h_coarse)
    lo, hi = both(f_half, f_other)
    (a0, a1, _, _), (b0, b1, _, _) = lay.f_parts(0)
    z = lay.g_half
    contract_grad = lo[a0 - z : a0 - z + a1].astype(F32)
    merge_grad = lo[b0 - z : b0 - z + b1].astype(F32)
    rest = [hi[a - z : a - z + rows].astype(F32) for a, rows, _, _ in lay.f_parts(1)]
    trend_grad, expand_grad = rest[0], jnp.concatenate(rest[1:], axis=1)

    at = lay.si_half
    gain_grads = s_mine[at : at + 3].astype(F32) + s_y[at : at + 3].astype(F32)
    gain_grads = lax.dynamic_slice(gain_grads, (jnp.int32(0), ring.me * share), (3, share))
    return (
        series_out,
        series_grad.reshape(series_in.shape),
        fine_shrink_grad,
        coarse_shrink_grad,
        fine_iso_grad,
        coarse_iso_grad,
        fine_grow_grad,
        coarse_grow_grad,
        merge_grad,
        expand_grad,
        contract_grad,
        trend_grad,
        gain_grads[0],
        gain_grads[1],
        gain_grads[2],
    )


def solution(mesh):
    n = mesh.shape["dp"]
    rows = P(("dp", "group"), None)
    weight = P("dp", None)
    return jax.shard_map(
        lambda *args: on_device(n, *args),
        mesh=mesh,
        in_specs=(rows, P(("dp", "group")), rows) + (weight,) * 10 + (P("dp"),) * 3,
        out_specs=(rows, rows) + (weight,) * 10 + (P("dp"),) * 3,
        check_vma=False,
    )
```

time: 773 us -> 612 us (0.79)
  waiting for transfers between devices: 274 us -> 186 us
  local copies, waits for them, and re-layouts: 73.1 us -> 15.9 us
  Pallas kernels: 214 us -> 256 us
  matrix products: 33.4 us -> 4.53 us
  other arithmetic: 86.3 us -> 64.3 us
    pallas_call x9 -> x15, Pallas kernels: 159 us -> 214 us  [the longest x3 80.5 us: dense(): pl.pallas_call(kernel, grid_spec=pltpu.PrefetchScalarGridSpec(num_scalar_...]
    ppermute x8 -> x3, waiting for transfers between devices: 74.4 us -> 24.2 us  [exchange(): return lambda v: lax.ppermute(v, axis, [(i, i ^ step) for i in range(size)])]
    dot_general x3 -> x0, matrix products: 29.9 us -> none  [the longest x1 13.3 us: prepare(): mean = jnp.einsum('grj,gjd->grd', counts, x_all, preferred_element_type=F32)]
    ppermute x16, waiting for transfers between devices: 89.8 us -> 62.6 us  [swap_y(): return lax.ppermute(v, 'group', Y_SWAP)]
    sub x1 -> x0, other arithmetic: 17.4 us -> none  [prepare(): age = (pos - first * taps)[:, None]]
    pallas_call x1, Pallas kernels: 26.4 us -> 9.8 us  [shrink_backward(): pl.pallas_call(kernel, out_shape=[jax.ShapeDtypeStruct((most, width), BF)...]
    unnamed x167 -> x128, local copies, waits for them, and re-layouts: 22.1 us -> 5.45 us
    ppermute x20 -> x17, waiting for transfers between devices: 22.9 us -> 7.47 us  [left(): return lax.ppermute(v, 'dp', ring.left)]
  transfers between devices with their start and end apart: 88 -> 71, of which waited for: 29 -> 25; matrix products, arithmetic and copies ran while one was open for 17% -> 5% of each run, Pallas kernels for 20% -> 40%
where the time goes in v3:
time: 612 us; the launch traced here: 602 us
  Pallas kernels  256 us (42%)
  waiting for transfers between devices  186 us (30%)
  starting transfers between devices  72.8 us (12%)
  other arithmetic  64.3 us (11%)
  local copies, waits for them, and re-layouts  15.9 us (3%)
    ppermute x17, waiting for transfers between devices, right(): return lax.ppermute(v, 'dp', ring.right)  89.6 us
    pallas_call x3, Pallas kernels, dense(): pl.pallas_call(kernel, grid_spec=pltpu.PrefetchScalarGridSpec(num_scalar_...  80.5 us
    ppermute x16, waiting for transfers between devices, swap_y(): return lax.ppermute(v, 'group', Y_SWAP)  62.6 us
    ppermute x16, starting transfers between devices, swap_y(): return lax.ppermute(v, 'group', Y_SWAP)  29.1 us
    pallas_call x2, Pallas kernels, grow_backward(): pl.pallas_call(kernel, out_shape=[jax.ShapeDtypeStruct((groups, length, w...  25.4 us
    pallas_call x1, Pallas kernels, dense_weights(): pl.pallas_call(kernel, grid=(chunks,), out_shape=outlet.shapes(), in_spec...  24.3 us
    ppermute x3, waiting for transfers between devices, exchange(): return lambda v: lax.ppermute(v, axis, [(i, i ^ step) for i in range(size)])  24.2 us
    pallas_call x2, Pallas kernels, season_kernel(): pl.pallas_call(kernel, grid=(groups,), out_shape=shapes, in_specs=[smem_s...  22.5 us
  transfers between devices with their start and end apart: 71, of which 25 were waited for; matrix products, arithmetic and copies ran while one was open for 5% of the time, Pallas kernels for 40%

profile of v3, /device:TPU:0, one launch (start us, length us, event | category | flops | bytes accessed | tf_op | source)
XLA Modules:
  0.0 601.7 jit_solution(11176460117867120985)
XLA Ops:
  1.3 2.9 fusion.52
  5.1 3.5 own_half.1.refs_0_
  8.6 3.1 collective-permute-start
  15.7 3.5 sibling_half.1.refs_1_
  19.2 11.5 %collective-permute-done.3 = f32[12]{0:T(128)S(1)} collective-permute-done((f32[12]{0:T(128)S(1)}, f32[12]{0:T(128)S(1)}, u32[]{:S(2)}, u32[]{:S(2)}) %collective-permute-start.3) | collective-permute-done | bytes 80 | tf_op jit(solution)/shard_map/ppermute | solution.py:92
  30.7 21.3 %collective-permute-done.4 = f32[3,512]{1,0:T(4,128)S(1)} collective-permute-done((f32[3,512]{1,0:T(4,128)S(1)}, f32[3,512]{1,0:T(4,128)S(1)}, u32[]{:S(2)}, u32[]{:S(2)}) %collective-permute-start.4) | collective-permute-done | bytes 6176 | tf_op jit(solution)/shard_map/ppermute | solution.py:1041
  57.5 8.1 %fusion.36.step_ref = s32[768,1]{1,0:T(8,128)} fusion(s32[]{:T(128)S(6)} %select_n.261, s32[]{:T(128)S(6)} %sign.30, s32[]{:T(128)S(6)} %select_n.264, s32[]{:T(128)S(6)} %select_n.262), kind=kLoop, calls=%fused_computation.100 | loop fusion | flops 12288 | bytes 3088 | tf_op jit(solution)/shard_map/add | solution.py:1105
  65.6 12.8 %season_trend.1 = (f32[3,768,512]{2,1,0:T(8,128)}, bf16[3,768,512]{2,1,0:T(8,128)(2,1)}, bf16[3,768,768]{2,1,0:T(8,128)(2,1)}, bf16[3,768,512]{2,1,0:T(8,128)(2,1)}, bf16[768,768]{1,0:T(8,128)(2,1)}) custom-call(s32[12]{0:T(128)} %kinds_own.1, s32[768,1]{1,0:T(8,128)} %fusion.36.step_ref, bf16[3,768,512]{2,1,0:T(8,128)(2,1)} %bitcast.164), custom_call_target="tpu_custom_call" | custom-call | flops 5435817984 | bytes 14155776 | tf_op jit(solution)/shard_map/season_trend/pallas_call | solution.py:331
  78.4 15.5 %collective-permute-done.5.refs_6_ = bf16[1792,512]{1,0:T(8,128)(2,1)} collective-permute-done((bf16[1792,512]{1,0:T(8,128)(2,1)S(1)}, bf16[1792,512]{1,0:T(8,128)(2,1)}, u32[]{:S(2)}, u32[]{:S(2)}) %collective-permute-start.5) | collective-permute-done | bytes 1835040 | tf_op jit(solution)/shard_map/ppermute | solution.py:1076
  100.1 17.8 %collective-permute-done.14 = bf16[768,512]{1,0:T(8,128)(2,1)S(1)} collective-permute-done((bf16[768,512]{1,0:T(8,128)(2,1)}, bf16[768,512]{1,0:T(8,128)(2,1)S(1)}, u32[]{:S(2)}, u32[]{:S(2)}) %collective-permute-start.14) | collective-permute-done | bytes 786464 | tf_op jit(solution)/shard_map/ppermute | solution.py:92
  117.9 17.1 %collective-permute-done.10.refs_10_ = bf16[1792,512]{1,0:T(8,128)(2,1)S(1)} collective-permute-done((bf16[1792,512]{1,0:T(8,128)(2,1)}, bf16[1792,512]{1,0:T(8,128)(2,1)S(1)}, u32[]{:S(2)}, u32[]{:S(2)}) %collective-permute-start.10) | collective-permute-done | bytes 1835040 | tf_op jit(solution)/shard_map/ppermute | solution.py:1076
  136.8 2.3 fusion.53
  144.0 2.8 pad_maximum_fusion.x_ref
  146.7 9.7 %season.1 = (f32[3,768,512]{2,1,0:T(8,128)}, bf16[3,768,512]{2,1,0:T(8,128)(2,1)}) custom-call(s32[12]{0:T(128)} %convert_element_type.408.kinds_ref.kinds_other, s32[768,1]{1,0:T(8,128)} %fusion.36.step_ref, bf16[3,768,512]{2,1,0:T(8,128)(2,1)} %pad_maximum_fusion.x_ref), custom_call_target="tpu_custom_call" | custom-call | flops 5435817984 | bytes 14155776 | tf_op jit(solution)/shard_map/season/pallas_call | solution.py:331
  158.8 2.9 collective-permute-done.22
  164.4 17.0 %shrink_forward.1 = (f32[384,512]{1,0:T(8,128)}, f32[384,512]{1,0:T(8,128)}, bf16[384,512]{1,0:T(8,128)(2,1)}, s32[384,1]{1,0:T(8,128)}, bf16[14336,512]{1,0:T(8,128)(2,1)}) custom-call(s32[10]{0:T(128)} %stack.96.where, s32[12]{0:T(128)} %kinds_own.1, s32[12]{0:T(128)} %convert_element_type.408.kinds_ref.kinds_other, f32[1,512]{1,0:T(1,128)} %get-tuple-element.926.gain_ref, ...), custom_call_target="tpu_custom_call" | custom-call | flops 5637144576 | bytes 29360128 | tf_op jit(solution)/shard_map/shrink_forward/pallas_call | solution.py:404
  184.9 11.3 %grow_forward.2 = (bf16[1,768,512]{2,1,0:T(8,128)(2,1)}, bf16[1,768,512]{2,1,0:T(8,128)(2,1)}, bf16[1,768,512]{2,1,0:T(8,128)(2,1)}, f32[3,768,512]{2,1,0:T(8,128)}, bf16[8192,512]{1,0:T(8,128)(2,1)}) custom-call(s32[10]{0:T(128)} %stack.96.where, f32[1,512]{1,0:T(1,128)} %get-tuple-element.926.gain_ref, bf16[768,768]{1,0:T(8,128)(2,1)} %get-tuple-element.508.order_ref, ...), custom_call_target="tpu_custom_call" | custom-call | flops 3019898880 | bytes 24903680 | tf_op jit(solution)/shard_map/grow_forward/pallas_call | solution.py:501
  196.2 2.4 collective-permute-start.27
  199.2 5.8 dense_whole.1
  205.0 10.7 %grow_forward.3 = (bf16[1,768,512]{2,1,0:T(8,128)(2,1)}, bf16[1,768,512]{2,1,0:T(8,128)(2,1)}, bf16[1,768,512]{2,1,0:T(8,128)(2,1)}, f32[3,768,512]{2,1,0:T(8,128)}) custom-call(s32[10]{0:T(128)} %stack.96.where, f32[1,512]{1,0:T(1,128)} %get-tuple-element.926.gain_ref, bf16[768,768]{1,0:T(8,128)(2,1)} %get-tuple-element.508.order_ref, ...), custom_call_target="tpu_custom_call" | custom-call | flops 3019898880 | bytes 24903680 | tf_op jit(solution)/shard_map/grow_forward/pallas_call | solution.py:501
  218.5 22.9 %dense.3 = (bf16[768,512]{1,0:T(8,128)(2,1)}, bf16[768,512]{1,0:T(8,128)(2,1)}, bf16[768,512]{1,0:T(8,128)(2,1)}, f32[768,512]{1,0:T(8,128)}, bf16[768,512]{1,0:...) custom-call(s32[10]{0:T(128)} %stack.96.where, ...), custom_call_target="tpu_custom_call" | custom-call | flops 8858370048 | bytes 33554432 | tf_op jit(solution)/shard_map/dense/pallas_call | solution.py:912
  242.4 23.1 %dense.4 = (bf16[768,512]{1,0:T(8,128)(2,1)}, bf16[768,512]{1,0:T(8,128)(2,1)}, bf16[768,512]{1,0:T(8,128)(2,1)}, f32[768,512]{1,0:T(8,128)}, bf16[768,512]{1,0:...) custom-call(s32[10]{0:T(128)} %stack.96.where, ...), custom_call_target="tpu_custom_call" | custom-call | flops 8858370048 | bytes 33554432 | tf_op jit(solution)/shard_map/dense/pallas_call | solution.py:912
  266.7 34.5 %dense.5 = (bf16[768,512]{1,0:T(8,128)(2,1)}, bf16[768,512]{1,0:T(8,128)(2,1)}, bf16[768,512]{1,0:T(8,128)(2,1)}, f32[768,512]{1,0:T(8,128)}, bf16[768,512]{1,0:...) custom-call(s32[10]{0:T(128)} %stack.96.where, ...), custom_call_target="tpu_custom_call" | custom-call | flops 8858370048 | bytes 33554432 | tf_op jit(solution)/shard_map/dense/pallas_call | solution.py:912
  302.2 24.3 %dense_weights.1 = (bf16[8,384,512]{2,1,0:T(8,128)(2,1)}, bf16[8,384,512]{2,1,0:T(8,128)(2,1)}) custom-call(s32[10]{0:T(128)} %stack.96.where, s32[8]{0:T(128)} %compare_select_fusion.6.places_ref, bf16[768,512]{1,0:T(8,128)(2,1)} %get-tuple-element.678.refs_0_, bf16[768,512]{1,0:T(8,128)(2,1)} %get-tuple-element.679.refs_1_, ...), custom_call_target="tpu_custom_call" | custom-call | flops 13287555072 | bytes 47185920 | tf_op jit(solution)/shard_map/dense_weights/pallas_call | solution.py:1020
  328.5 12.7 %grow_backward.2 = (bf16[3,768,512]{2,1,0:T(8,128)(2,1)}, f32[192,512]{1,0:T(8,128)}, f32[3,768,512]{2,1,0:T(8,128)}, f32[1,512]{1,0:T(1,128)}) custom-call(s32[10]{0:T(128)} %stack.96.where, f32[1,512]{1,0:T(1,128)} %get-tuple-element.926.gain_ref, bf16[768,768]{1,0:T(8,128)(2,1)} %get-tuple-element.508.order_ref, f32[3,768,512]{2,1,0:T(8,128)} %get-tuple-element.710.up_in, ...), custom_call_target="tpu_custom_call" | custom-call | flops 3019898880 | bytes 29622272 | tf_op jit(solution)/shard_map/grow_backward/pallas_call | solution.py:577
  341.3 6.3 %collective-permute-done.32.refs_2_ = bf16[768,512]{1,0:T(8,128)(2,1)S(1)} collective-permute-done((bf16[768,512]{1,0:T(8,128)(2,1)}, bf16[768,512]{1,0:T(8,128)(2,1)S(1)}, u32[]{:S(2)}, u32[]{:S(2)}) %collective-permute-start.32) | collective-permute-done | bytes 786464 | tf_op jit(solution)/shard_map/ppermute | solution.py:92
  348.5 2.4 convert_add_fusion.5
  353.9 12.6 %grow_backward.3 = (bf16[3,768,512]{2,1,0:T(8,128)(2,1)}, f32[192,512]{1,0:T(8,128)}, f32[3,768,512]{2,1,0:T(8,128)}, f32[1,512]{1,0:T(1,128)}) custom-call(s32[10]{0:T(128)} %stack.96.where, f32[1,512]{1,0:T(1,128)} %get-tuple-element.926.gain_ref, bf16[768,768]{1,0:T(8,128)(2,1)} %get-tuple-element.508.order_ref, f32[3,768,512]{2,1,0:T(8,128)} %get-tuple-element.727.up_in, ...), custom_call_target="tpu_custom_call" | custom-call | flops 3019898880 | bytes 29622272 | tf_op jit(solution)/shard_map/grow_backward/pallas_call | solution.py:577
  373.2 9.6 %grow_weight.1 = (bf16[8,512,512]{2,1,0:T(8,128)(2,1)}, bf16[8,512,512]{2,1,0:T(8,128)(2,1)}) custom-call(s32[10]{0:T(128)} %stack.96.where, s32[8]{0:T(128)} %compare_select_fusion.6.places_ref, bf16[384,512]{1,0:T(8,128)(2,1)} %get-tuple-element.743.mixed_ref, bf16[3,768,512]{2,1,0:T(8,128)(2,1)} %get-tuple-element.744.own_ref, ...), custom_call_target="tpu_custom_call" | custom-call | flops 2415919104 | bytes 8388608 | tf_op jit(solution)/shard_map/grow_weight/pallas_call | solution.py:658
  383.6 2.3 fusion.26
  388.0 9.8 %shrink_backward.1 = (bf16[384,512]{1,0:T(8,128)(2,1)}, bf16[384,512]{1,0:T(8,128)(2,1)}, f32[1,512]{1,0:T(1,128)}) custom-call(s32[10]{0:T(128)} %stack.96.where, s32[384,1]{1,0:T(8,128)} %get-tuple-element.759.age_ref, f32[1,512]{1,0:T(1,128)} %get-tuple-element.926.gain_ref, f32[192,512]{1,0:T(8,128)} %get-tuple-element.760.b0, ...), custom_call_target="tpu_custom_call" | custom-call | flops 3221225472 | bytes 8388608 | tf_op jit(solution)/shard_map/shrink_backward/pallas_call | solution.py:704
  397.8 2.3 convert_add_fusion.3
  407.4 16.9 %shrink_weight.1 = (bf16[8,912,512]{2,1,0:T(8,128)(2,1)}, bf16[8,912,512]{2,1,0:T(8,128)(2,1)}) custom-call(s32[10]{0:T(128)} %stack.96.where, s32[8]{0:T(128)} %compare_select_fusion.6.places_ref, s32[384,1]{1,0:T(8,128)} %get-tuple-element.759.age_ref, f32[16,512]{1,0:T(8,128)} %maximum_maximum_fusion.gains_ref, ...), custom_call_target="tpu_custom_call" | custom-call | flops 5637144576 | bytes 31457280 | tf_op jit(solution)/shard_map/shrink_weight/pallas_call | solution.py:763
  427.9 9.9 %collective-permute-start.47 = (bf16[384,512]{1,0:T(8,128)(2,1)S(1)}, bf16[384,512]{1,0:T(8,128)(2,1)S(1)}, u32[]{:S(2)}, u32[]{:S(2)}) collective-permute-start(bf16[384,512]{1,0:T(8,128)(2,1)S(1)} %fusion.24), channel_id=1, source_target_pairs={{0,2},{2,0},{1,3},{3,1},{4,6},{6,4},{5,7},{7,5},{8,10},{10,8},{9,1... | collective-permute-start | bytes 1179656 | tf_op jit(solution)/shard_map/ppermute | solution.py:92
  439.9 14.8 %season_backward.1 = (bf16[3,768,512]{2,1,0:T(8,128)(2,1)}, bf16[768,512]{1,0:T(8,128)(2,1)}, bf16[768,512]{1,0:T(8,128)(2,1)}, bf16[768,512]{1,0:T(8,128)(2,1)}) custom-call(s32[10]{0:T(128)} %stack.96.where, bf16[768,768]{1,0:T(8,128)(2,1)} %get-tuple-element.508.order_ref, bf16[384,512]{1,0:T(8,128)(2,1)} %get-tuple-element.804.pre_ref, ...), custom_call_target="tpu_custom_call" | custom-call | flops 6039797760 | bytes 36700160 | tf_op jit(solution)/shard_map/season_backward/pallas_call | solution.py:806
  454.7 3.6 convert_add_fusion.1
  465.3 19.2 %collective-permute-done.51 = bf16[456,512]{1,0:T(8,128)(2,1)S(1)} collective-permute-done((bf16[456,512]{1,0:T(8,128)(2,1)S(1)}, bf16[456,512]{1,0:T(8,128)(2,1)S(1)}, u32[]{:S(2)}, u32[]{:S(2)}) %collective-permute-start.51) | collective-permute-done | bytes 466976 | tf_op jit(solution)/shard_map/ppermute | solution.py:1076
  493.3 26.8 %collective-permute-done.54 = bf16[512,512]{1,0:T(8,128)(2,1)S(1)} collective-permute-done((bf16[512,512]{1,0:T(8,128)(2,1)S(1)}, bf16[512,512]{1,0:T(8,128)(2,1)S(1)}, u32[]{:S(2)}, u32[]{:S(2)}) %collective-permute-start.54) | collective-permute-done | bytes 524320 | tf_op jit(solution)/shard_map/ppermute | solution.py:1076
  523.4 3.7 fusion.8
  530.6 3.2 pad_maximum_fusion.1
  533.8 5.7 collective-permute-done.61
  539.5 7.5 %collective-permute-done.59 = bf16[912,512]{1,0:T(8,128)(2,1)S(1)} collective-permute-done((bf16[912,512]{1,0:T(8,128)(2,1)}, bf16[912,512]{1,0:T(8,128)(2,1)S(1)}, u32[]{:S(2)}, u32[]{:S(2)}) %collective-permute-start.59) | collective-permute-done | bytes 933920 | tf_op jit(solution)/shard_map/ppermute | solution.py:1076
  547.3 3.1 fusion.7
  556.6 9.3 %collective-permute-done.67 = bf16[768,512]{1,0:T(8,128)(2,1)S(1)} collective-permute-done((bf16[768,512]{1,0:T(8,128)(2,1)S(1)}, bf16[768,512]{1,0:T(8,128)(2,1)S(1)}, u32[]{:S(2)}, u32[]{:S(2)}) %collective-permute-start.67) | collective-permute-done | bytes 786464 | tf_op jit(solution)/shard_map/ppermute | solution.py:92
  565.9 3.5 collective-permute-done.64
  570.1 2.1 fusion.12
  576.8 4.5 add_convert_fusion
  581.4 10.9 %collective-permute-done.68 = bf16[912,512]{1,0:T(8,128)(2,1)S(1)} collective-permute-done((bf16[912,512]{1,0:T(8,128)(2,1)S(1)}, bf16[912,512]{1,0:T(8,128)(2,1)S(1)}, u32[]{:S(2)}, u32[]{:S(2)}) %collective-permute-start.68) | collective-permute-done | bytes 933920 | tf_op jit(solution)/shard_map/ppermute | solution.py:92
  (325 shorter events, 109.7 us)
Async XLA Ops:
  8.6 43.4 %collective-permute-start = (bf16[1792,512]{1,0:T(8,128)(2,1)}, bf16[1792,512]{1,0:T(8,128)(2,1)S(1)}, u32[]{:S(2)}, u32[]{:S(2)}) collective-permute-start(bf16[1792,512]{1,0:T(8,128)(2,1)} %own_half.1.refs_0_), channel_id=1, source_target_pairs={{0,8},{8,16},{16,24},{24,28},{28,20},{20,12},{12,4},{4,0},{1,9},{9... | collective-permute-start | bytes 5505032 | tf_op jit(solution)/shard_map/ppermute | solution.py:1076
  11.6 41.7 %collective-permute-start.1 = (bf16[1792,512]{1,0:T(8,128)(2,1)}, bf16[1792,512]{1,0:T(8,128)(2,1)}, u32[]{:S(2)}, u32[]{:S(2)}) collective-permute-start(bf16[1792,512]{1,0:T(8,128)(2,1)} %own_half.1.refs_0_), channel_id=1, source_target_pairs={{8,0},{16,8},{24,16},{28,24},{20,28},{12,20},{4,12},{0,4},{9,1},{1... | collective-permute-start | bytes 5505032 | tf_op jit(solution)/shard_map/ppermute | solution.py:1079
  11.7 40.3 %collective-permute-start.2 = (bf16[768,512]{1,0:T(8,128)(2,1)S(1)}, bf16[768,512]{1,0:T(8,128)(2,1)S(1)}, u32[]{:S(2)}, u32[]{:S(2)}) collective-permute-start(bf16[768,512]{1,0:T(8,128)(2,1)S(1)} %get-tuple-element.447), channel_id=1, source_target_pairs={{0,2},{2,0},{1,3},{3,1},{4,6},{6,4},{5,7},{7,5},{8,10},{10,8},{9,1... | collective-permute-start | bytes 2359304 | tf_op jit(solution)/shard_map/ppermute | solution.py:92
  13.7 38.3 %collective-permute-start.4 = (f32[3,512]{1,0:T(4,128)S(1)}, f32[3,512]{1,0:T(4,128)S(1)}, u32[]{:S(2)}, u32[]{:S(2)}) collective-permute-start(f32[3,512]{1,0:T(4,128)S(1)} %dynamic_update_slice.5), channel_id=1, source_target_pairs={{0,4},{4,0},{8,12},{12,8},{16,20},{20,16},{24,28},{28,24},{1,5},{5... | collective-permute-start | bytes 18440 | tf_op jit(solution)/shard_map/ppermute | solution.py:1041
  53.4 40.6 %collective-permute-start.5 = (bf16[1792,512]{1,0:T(8,128)(2,1)S(1)}, bf16[1792,512]{1,0:T(8,128)(2,1)}, u32[]{:S(2)}, u32[]{:S(2)}) collective-permute-start(bf16[1792,512]{1,0:T(8,128)(2,1)S(1)} %collective-permute-done.refs_2_), channel_id=1, source_target_pairs={{0,8},{8,16},{16,24},{24,28},{28,20},{20,12},{12,4},{4,0},{1,9},{9... | collective-permute-start | bytes 5505032 | tf_op jit(solution)/shard_map/ppermute | solution.py:1076
  55.0 40.5 %collective-permute-start.6 = (bf16[1792,512]{1,0:T(8,128)(2,1)}, bf16[1792,512]{1,0:T(8,128)(2,1)}, u32[]{:S(2)}, u32[]{:S(2)}) collective-permute-start(bf16[1792,512]{1,0:T(8,128)(2,1)} %collective-permute-done.1.refs_3_), channel_id=1, source_target_pairs={{8,0},{16,8},{24,16},{28,24},{20,28},{12,20},{4,12},{0,4},{9,1},{1... | collective-permute-start | bytes 5505032 | tf_op jit(solution)/shard_map/ppermute | solution.py:1079
  55.4 40.1 %collective-permute-start.7 = (bf16[1792,512]{1,0:T(8,128)(2,1)S(1)}, bf16[1792,512]{1,0:T(8,128)(2,1)}, u32[]{:S(2)}, u32[]{:S(2)}) collective-permute-start(bf16[1792,512]{1,0:T(8,128)(2,1)S(1)} %collective-permute-done.refs_2_), channel_id=1, source_target_pairs={{0,1},{1,0},{2,3},{3,2},{4,5},{5,4},{6,7},{7,6},{8,9},{9,8},{10,11... | collective-permute-start | bytes 5505032 | tf_op jit(solution)/shard_map/ppermute | solution.py:88
  55.4 40.1 %collective-permute-start.8 = (bf16[1792,512]{1,0:T(8,128)(2,1)}, bf16[1792,512]{1,0:T(8,128)(2,1)}, u32[]{:S(2)}, u32[]{:S(2)}) collective-permute-start(bf16[1792,512]{1,0:T(8,128)(2,1)} %collective-permute-done.1.refs_3_), channel_id=1, source_target_pairs={{0,1},{1,0},{2,3},{3,2},{4,5},{5,4},{6,7},{7,6},{8,9},{9,8},{10,11... | collective-permute-start | bytes 5505032 | tf_op jit(solution)/shard_map/ppermute | solution.py:88
  55.9 22.5 %collective-permute-start.9 = (bf16[768,512]{1,0:T(8,128)(2,1)}, bf16[768,512]{1,0:T(8,128)(2,1)S(1)}, u32[]{:S(2)}, u32[]{:S(2)}) collective-permute-start(bf16[768,512]{1,0:T(8,128)(2,1)} %get-tuple-element.467), channel_id=1, source_target_pairs={{0,2},{2,0},{1,3},{3,1},{4,6},{6,4},{5,7},{7,5},{8,10},{10,8},{9,1... | collective-permute-start | bytes 2359304 | tf_op jit(solution)/shard_map/ppermute | solution.py:92
  95.5 39.6 %collective-permute-start.10 = (bf16[1792,512]{1,0:T(8,128)(2,1)}, bf16[1792,512]{1,0:T(8,128)(2,1)S(1)}, u32[]{:S(2)}, u32[]{:S(2)}) collective-permute-start(bf16[1792,512]{1,0:T(8,128)(2,1)} %collective-permute-done.5.refs_6_), channel_id=1, source_target_pairs={{0,8},{8,16},{16,24},{24,28},{28,20},{20,12},{12,4},{4,0},{1,9},{9... | collective-permute-start | bytes 5505032 | tf_op jit(solution)/shard_map/ppermute | solution.py:1076
  97.2 39.6 %collective-permute-start.11 = (bf16[1792,512]{1,0:T(8,128)(2,1)}, bf16[1792,512]{1,0:T(8,128)(2,1)}, u32[]{:S(2)}, u32[]{:S(2)}) collective-permute-start(bf16[1792,512]{1,0:T(8,128)(2,1)} %collective-permute-done.6.refs_7_), channel_id=1, source_target_pairs={{8,0},{16,8},{24,16},{28,24},{20,28},{12,20},{4,12},{0,4},{9,1},{1... | collective-permute-start | bytes 5505032 | tf_op jit(solution)/shard_map/ppermute | solution.py:1079
  97.8 39.1 %collective-permute-start.12 = (bf16[1792,512]{1,0:T(8,128)(2,1)}, bf16[1792,512]{1,0:T(8,128)(2,1)}, u32[]{:S(2)}, u32[]{:S(2)}) collective-permute-start(bf16[1792,512]{1,0:T(8,128)(2,1)} %collective-permute-done.5.refs_6_), channel_id=1, source_target_pairs={{0,1},{1,0},{2,3},{3,2},{4,5},{5,4},{6,7},{7,6},{8,9},{9,8},{10,11... | collective-permute-start | bytes 5505032 | tf_op jit(solution)/shard_map/ppermute | solution.py:88
  97.8 39.1 %collective-permute-start.13 = (bf16[1792,512]{1,0:T(8,128)(2,1)}, bf16[1792,512]{1,0:T(8,128)(2,1)}, u32[]{:S(2)}, u32[]{:S(2)}) collective-permute-start(bf16[1792,512]{1,0:T(8,128)(2,1)} %collective-permute-done.6.refs_7_), channel_id=1, source_target_pairs={{0,1},{1,0},{2,3},{3,2},{4,5},{5,4},{6,7},{7,6},{8,9},{9,8},{10,11... | collective-permute-start | bytes 5505032 | tf_op jit(solution)/shard_map/ppermute | solution.py:88
  98.3 19.7 %collective-permute-start.14 = (bf16[768,512]{1,0:T(8,128)(2,1)}, bf16[768,512]{1,0:T(8,128)(2,1)S(1)}, u32[]{:S(2)}, u32[]{:S(2)}) collective-permute-start(bf16[768,512]{1,0:T(8,128)(2,1)} %get-tuple-element.481), channel_id=1, source_target_pairs={{0,2},{2,0},{1,3},{3,1},{4,6},{6,4},{5,7},{7,5},{8,10},{10,8},{9,1... | collective-permute-start | bytes 2359304 | tf_op jit(solution)/shard_map/ppermute | solution.py:92
  139.1 17.4 %collective-permute-start.17 = (bf16[1792,512]{1,0:T(8,128)(2,1)S(1)}, bf16[1792,512]{1,0:T(8,128)(2,1)}, u32[]{:S(2)}, u32[]{:S(2)}) collective-permute-start(bf16[1792,512]{1,0:T(8,128)(2,1)S(1)} %collective-permute-done.10.refs_10_), channel_id=1, source_target_pairs={{0,1},{1,0},{2,3},{3,2},{4,5},{5,4},{6,7},{7,6},{8,9},{9,8},{10,11... | collective-permute-start | bytes 5505032 | tf_op jit(solution)/shard_map/ppermute | solution.py:88
  139.1 17.4 %collective-permute-start.18 = (bf16[1792,512]{1,0:T(8,128)(2,1)}, bf16[1792,512]{1,0:T(8,128)(2,1)}, u32[]{:S(2)}, u32[]{:S(2)}) collective-permute-start(bf16[1792,512]{1,0:T(8,128)(2,1)} %collective-permute-done.11.refs_11_), channel_id=1, source_target_pairs={{0,1},{1,0},{2,3},{3,2},{4,5},{5,4},{6,7},{7,6},{8,9},{9,8},{10,11... | collective-permute-start | bytes 5505032 | tf_op jit(solution)/shard_map/ppermute | solution.py:88
  140.2 16.3 %collective-permute-start.19 = (f32[3,512]{1,0:T(4,128)S(1)}, f32[3,512]{1,0:T(4,128)S(1)}, u32[]{:S(2)}, u32[]{:S(2)}) collective-permute-start(f32[3,512]{1,0:T(4,128)S(1)} %add.384), channel_id=1, source_target_pairs={{0,8},{4,12},{8,0},{12,4},{16,24},{20,28},{24,16},{28,20},{1,9},{5... | collective-permute-start | bytes 18440 | tf_op jit(solution)/shard_map/ppermute | solution.py:1041
  162.4 19.0 %collective-permute-start.23 = (bf16[448,512]{1,0:T(8,128)(2,1)}, bf16[448,512]{1,0:T(8,128)(2,1)S(1)}, u32[]{:S(2)}, u32[]{:S(2)}) collective-permute-start(bf16[448,512]{1,0:T(8,128)(2,1)} %get-tuple-element.520), channel_id=1, source_target_pairs={{0,8},{8,16},{16,24},{24,28},{28,20},{20,12},{12,4},{4,0},{1,9},{9... | collective-permute-start | bytes 1376264 | tf_op jit(solution)/shard_map/ppermute | solution.py:1076
  162.7 18.8 %collective-permute-start.24 = (bf16[448,512]{1,0:T(8,128)(2,1)S(1)}, bf16[448,512]{1,0:T(8,128)(2,1)S(1)}, u32[]{:S(2)}, u32[]{:S(2)}) collective-permute-start(bf16[448,512]{1,0:T(8,128)(2,1)S(1)} %copy-done.18), channel_id=1, source_target_pairs={{8,0},{16,8},{24,16},{28,24},{20,28},{12,20},{4,12},{0,4},{9,1},{1... | collective-permute-start | bytes 1376264 | tf_op jit(solution)/shard_map/ppermute | solution.py:1079
  196.2 20.5 %collective-permute-start.27 = (bf16[768,512]{1,0:T(8,128)(2,1)}, bf16[768,512]{1,0:T(8,128)(2,1)S(1)}, u32[]{:S(2)}, u32[]{:S(2)}) collective-permute-start(bf16[768,512]{1,0:T(8,128)(2,1)} %bitcast.189), channel_id=1, source_target_pairs={{0,2},{2,0},{1,3},{3,1},{4,6},{6,4},{5,7},{7,5},{8,10},{10,8},{9,1... | collective-permute-start | bytes 2359304 | tf_op jit(solution)/shard_map/ppermute | solution.py:92
  216.7 24.7 %collective-permute-start.28 = (bf16[768,512]{1,0:T(8,128)(2,1)S(1)}, bf16[768,512]{1,0:T(8,128)(2,1)S(1)}, u32[]{:S(2)}, u32[]{:S(2)}) collective-permute-start(bf16[768,512]{1,0:T(8,128)(2,1)S(1)} %bitcast.188), channel_id=1, source_target_pairs={{0,2},{2,0},{1,3},{3,1},{4,6},{6,4},{5,7},{7,5},{8,10},{10,8},{9,1... | collective-permute-start | bytes 2359304 | tf_op jit(solution)/shard_map/ppermute | solution.py:92
  241.4 24.1 %collective-permute-start.29 = (bf16[768,512]{1,0:T(8,128)(2,1)S(1)}, bf16[768,512]{1,0:T(8,128)(2,1)S(1)}, u32[]{:S(2)}, u32[]{:S(2)}) collective-permute-start(bf16[768,512]{1,0:T(8,128)(2,1)S(1)} %bitcast.181), channel_id=1, source_target_pairs={{0,2},{2,0},{1,3},{3,1},{4,6},{6,4},{5,7},{7,5},{8,10},{10,8},{9,1... | collective-permute-start | bytes 2359304 | tf_op jit(solution)/shard_map/ppermute | solution.py:92
  265.5 35.7 %collective-permute-start.30 = (bf16[768,512]{1,0:T(8,128)(2,1)S(1)}, bf16[768,512]{1,0:T(8,128)(2,1)S(1)}, u32[]{:S(2)}, u32[]{:S(2)}) collective-permute-start(bf16[768,512]{1,0:T(8,128)(2,1)S(1)} %copy-done.44), channel_id=1, source_target_pairs={{0,2},{2,0},{1,3},{3,1},{4,6},{6,4},{5,7},{7,5},{8,10},{10,8},{9,1... | collective-permute-start | bytes 2359304 | tf_op jit(solution)/shard_map/ppermute | solution.py:92
  301.3 25.2 %collective-permute-start.31 = (bf16[768,512]{1,0:T(8,128)(2,1)S(1)}, bf16[768,512]{1,0:T(8,128)(2,1)S(1)}, u32[]{:S(2)}, u32[]{:S(2)}) collective-permute-start(bf16[768,512]{1,0:T(8,128)(2,1)S(1)} %copy-done.42), channel_id=1, source_target_pairs={{0,2},{2,0},{1,3},{3,1},{4,6},{6,4},{5,7},{7,5},{8,10},{10,8},{9,1... | collective-permute-start | bytes 2359304 | tf_op jit(solution)/shard_map/ppermute | solution.py:92
  327.4 20.2 %collective-permute-start.33 = (bf16[8,384,512]{2,1,0:T(8,128)(2,1)}, bf16[8,384,512]{2,1,0:T(8,128)(2,1)}, u32[]{:S(2)}, u32[]{:S(2)}) collective-permute-start(bf16[8,384,512]{2,1,0:T(8,128)(2,1)} %get-tuple-element.709), channel_id=1, source_target_pairs={{0,1},{1,0},{2,3},{3,2},{4,5},{5,4},{6,7},{7,6},{8,9},{9,8},{10,11... | collective-permute-start | bytes 9437192 | tf_op jit(solution)/shard_map/ppermute | solution.py:88
  327.4 20.2 %collective-permute-start.32 = (bf16[768,512]{1,0:T(8,128)(2,1)}, bf16[768,512]{1,0:T(8,128)(2,1)S(1)}, u32[]{:S(2)}, u32[]{:S(2)}) collective-permute-start(bf16[768,512]{1,0:T(8,128)(2,1)} %get-tuple-element.708), channel_id=1, source_target_pairs={{0,2},{2,0},{1,3},{3,1},{4,6},{6,4},{5,7},{7,5},{8,10},{10,8},{9,1... | collective-permute-start | bytes 2359304 | tf_op jit(solution)/shard_map/ppermute | solution.py:92
  403.3 21.0 %collective-permute-start.43 = (bf16[256,512]{1,0:T(8,128)(2,1)}, bf16[256,512]{1,0:T(8,128)(2,1)}, u32[]{:S(2)}, u32[]{:S(2)}) collective-permute-start(bf16[256,512]{1,0:T(8,128)(2,1)} %get-tuple-element.782), channel_id=1, source_target_pairs={{0,8},{8,16},{16,24},{24,28},{28,20},{20,12},{12,4},{4,0},{1,9},{9... | collective-permute-start | bytes 786440 | tf_op jit(solution)/shard_map/ppermute | solution.py:1076
  404.2 20.1 %collective-permute-start.44 = (bf16[256,512]{1,0:T(8,128)(2,1)S(1)}, bf16[256,512]{1,0:T(8,128)(2,1)}, u32[]{:S(2)}, u32[]{:S(2)}) collective-permute-start(bf16[256,512]{1,0:T(8,128)(2,1)S(1)} %get-tuple-element.783), channel_id=1, source_target_pairs={{8,0},{16,8},{24,16},{28,24},{20,28},{12,20},{4,12},{0,4},{9,1},{1... | collective-permute-start | bytes 786440 | tf_op jit(solution)/shard_map/ppermute | solution.py:1079
  405.3 19.0 %collective-permute-start.41 = (bf16[384,512]{1,0:T(8,128)(2,1)S(1)}, bf16[384,512]{1,0:T(8,128)(2,1)S(1)}, u32[]{:S(2)}, u32[]{:S(2)}) collective-permute-start(bf16[384,512]{1,0:T(8,128)(2,1)S(1)} %get-tuple-element.780), channel_id=1, source_target_pairs={{0,8},{8,16},{16,24},{24,28},{28,20},{20,12},{12,4},{4,0},{1,9},{9... | collective-permute-start | bytes 1179656 | tf_op jit(solution)/shard_map/ppermute | solution.py:1076
  406.3 18.1 %collective-permute-start.42 = (bf16[384,512]{1,0:T(8,128)(2,1)S(1)}, bf16[384,512]{1,0:T(8,128)(2,1)S(1)}, u32[]{:S(2)}, u32[]{:S(2)}) collective-permute-start(bf16[384,512]{1,0:T(8,128)(2,1)S(1)} %get-tuple-element.781), channel_id=1, source_target_pairs={{8,0},{16,8},{24,16},{28,24},{20,28},{12,20},{4,12},{0,4},{9,1},{1... | collective-permute-start | bytes 1179656 | tf_op jit(solution)/shard_map/ppermute | solution.py:1079
  427.8 26.9 %collective-permute-start.48 = (bf16[8,912,512]{2,1,0:T(8,128)(2,1)}, bf16[8,912,512]{2,1,0:T(8,128)(2,1)}, u32[]{:S(2)}, u32[]{:S(2)}) collective-permute-start(bf16[8,912,512]{2,1,0:T(8,128)(2,1)} %get-tuple-element.803), channel_id=1, source_target_pairs={{0,1},{1,0},{2,3},{3,2},{4,5},{5,4},{6,7},{7,6},{8,9},{9,8},{10,11... | collective-permute-start | bytes 22413320 | tf_op jit(solution)/shard_map/ppermute | solution.py:88
  427.9 26.8 %collective-permute-start.47 = (bf16[384,512]{1,0:T(8,128)(2,1)S(1)}, bf16[384,512]{1,0:T(8,128)(2,1)S(1)}, u32[]{:S(2)}, u32[]{:S(2)}) collective-permute-start(bf16[384,512]{1,0:T(8,128)(2,1)S(1)} %fusion.24), channel_id=1, source_target_pairs={{0,2},{2,0},{1,3},{3,1},{4,6},{6,4},{5,7},{7,5},{8,10},{10,8},{9,1... | collective-permute-start | bytes 1179656 | tf_op jit(solution)/shard_map/ppermute | solution.py:92
  437.9 16.8 %collective-permute-start.45 = (bf16[512,512]{1,0:T(8,128)(2,1)S(1)}, bf16[512,512]{1,0:T(8,128)(2,1)S(1)}, u32[]{:S(2)}, u32[]{:S(2)}) collective-permute-start(bf16[512,512]{1,0:T(8,128)(2,1)S(1)} %pad_maximum_fusion.6), channel_id=1, source_target_pairs={{0,8},{8,16},{16,24},{24,28},{28,20},{20,12},{12,4},{4,0},{1,9},{9... | collective-permute-start | bytes 1572872 | tf_op jit(solution)/shard_map/ppermute | solution.py:1076
  460.3 24.9 %collective-permute-start.53 = (bf16[768,512]{1,0:T(8,128)(2,1)S(1)}, bf16[768,512]{1,0:T(8,128)(2,1)S(1)}, u32[]{:S(2)}, u32[]{:S(2)}) collective-permute-start(bf16[768,512]{1,0:T(8,128)(2,1)S(1)} %copy-done.39), channel_id=1, source_target_pairs={{0,2},{2,0},{1,3},{3,1},{4,6},{6,4},{5,7},{7,5},{8,10},{10,8},{9,1... | collective-permute-start | bytes 2359304 | tf_op jit(solution)/shard_map/ppermute | solution.py:92
  461.1 24.1 %collective-permute-start.49 = (bf16[512,512]{1,0:T(8,128)(2,1)S(1)}, bf16[512,512]{1,0:T(8,128)(2,1)S(1)}, u32[]{:S(2)}, u32[]{:S(2)}) collective-permute-start(bf16[512,512]{1,0:T(8,128)(2,1)S(1)} %get-tuple-element.816), channel_id=1, source_target_pairs={{0,8},{8,16},{16,24},{24,28},{28,20},{20,12},{12,4},{4,0},{1,9},{9... | collective-permute-start | bytes 1572872 | tf_op jit(solution)/shard_map/ppermute | solution.py:1076
  462.1 23.1 %collective-permute-start.50 = (bf16[512,512]{1,0:T(8,128)(2,1)S(1)}, bf16[512,512]{1,0:T(8,128)(2,1)S(1)}, u32[]{:S(2)}, u32[]{:S(2)}) collective-permute-start(bf16[512,512]{1,0:T(8,128)(2,1)S(1)} %get-tuple-element.817), channel_id=1, source_target_pairs={{8,0},{16,8},{24,16},{28,24},{20,28},{12,20},{4,12},{0,4},{9,1},{1... | collective-permute-start | bytes 1572872 | tf_op jit(solution)/shard_map/ppermute | solution.py:1079
  463.1 21.3 %collective-permute-start.51 = (bf16[456,512]{1,0:T(8,128)(2,1)S(1)}, bf16[456,512]{1,0:T(8,128)(2,1)S(1)}, u32[]{:S(2)}, u32[]{:S(2)}) collective-permute-start(bf16[456,512]{1,0:T(8,128)(2,1)S(1)} %get-tuple-element.818), channel_id=1, source_target_pairs={{0,8},{8,16},{16,24},{24,28},{28,20},{20,12},{12,4},{4,0},{1,9},{9... | collective-permute-start | bytes 1400840 | tf_op jit(solution)/shard_map/ppermute | solution.py:1076
  464.1 21.0 %collective-permute-start.52 = (bf16[456,512]{1,0:T(8,128)(2,1)S(1)}, bf16[456,512]{1,0:T(8,128)(2,1)S(1)}, u32[]{:S(2)}, u32[]{:S(2)}) collective-permute-start(bf16[456,512]{1,0:T(8,128)(2,1)S(1)} %get-tuple-element.819), channel_id=1, source_target_pairs={{8,0},{16,8},{24,16},{28,24},{20,28},{12,20},{4,12},{0,4},{9,1},{1... | collective-permute-start | bytes 1400840 | tf_op jit(solution)/shard_map/ppermute | solution.py:1079
  487.9 33.3 %collective-permute-start.56 = (bf16[912,512]{1,0:T(8,128)(2,1)S(1)}, bf16[912,512]{1,0:T(8,128)(2,1)S(1)}, u32[]{:S(2)}, u32[]{:S(2)}) collective-permute-start(bf16[912,512]{1,0:T(8,128)(2,1)S(1)} %pad_maximum_fusion.4), channel_id=1, source_target_pairs={{0,8},{8,16},{16,24},{24,28},{28,20},{20,12},{12,4},{4,0},{1,9},{9... | collective-permute-start | bytes 2801672 | tf_op jit(solution)/shard_map/ppermute | solution.py:1076
  489.3 31.9 %collective-permute-start.57 = (bf16[912,512]{1,0:T(8,128)(2,1)S(1)}, bf16[912,512]{1,0:T(8,128)(2,1)S(1)}, u32[]{:S(2)}, u32[]{:S(2)}) collective-permute-start(bf16[912,512]{1,0:T(8,128)(2,1)S(1)} %pad_maximum_fusion.5), channel_id=1, source_target_pairs={{8,0},{16,8},{24,16},{28,24},{20,28},{12,20},{4,12},{0,4},{9,1},{1... | collective-permute-start | bytes 2801672 | tf_op jit(solution)/shard_map/ppermute | solution.py:1079
  490.0 31.2 %collective-permute-start.58 = (bf16[768,512]{1,0:T(8,128)(2,1)S(1)}, bf16[768,512]{1,0:T(8,128)(2,1)S(1)}, u32[]{:S(2)}, u32[]{:S(2)}) collective-permute-start(bf16[768,512]{1,0:T(8,128)(2,1)S(1)} %copy-done.36), channel_id=1, source_target_pairs={{0,2},{2,0},{1,3},{3,1},{4,6},{6,4},{5,7},{7,5},{8,10},{10,8},{9,1... | collective-permute-start | bytes 2359304 | tf_op jit(solution)/shard_map/ppermute | solution.py:92
  491.1 29.0 %collective-permute-start.54 = (bf16[512,512]{1,0:T(8,128)(2,1)S(1)}, bf16[512,512]{1,0:T(8,128)(2,1)S(1)}, u32[]{:S(2)}, u32[]{:S(2)}) collective-permute-start(bf16[512,512]{1,0:T(8,128)(2,1)S(1)} %get-tuple-element.826), channel_id=1, source_target_pairs={{0,8},{8,16},{16,24},{24,28},{28,20},{20,12},{12,4},{4,0},{1,9},{9... | collective-permute-start | bytes 1572872 | tf_op jit(solution)/shard_map/ppermute | solution.py:1076
  492.5 28.7 %collective-permute-start.55 = (bf16[512,512]{1,0:T(8,128)(2,1)S(1)}, bf16[512,512]{1,0:T(8,128)(2,1)S(1)}, u32[]{:S(2)}, u32[]{:S(2)}) collective-permute-start(bf16[512,512]{1,0:T(8,128)(2,1)S(1)} %get-tuple-element.827), channel_id=1, source_target_pairs={{8,0},{16,8},{24,16},{28,24},{20,28},{12,20},{4,12},{0,4},{9,1},{1... | collective-permute-start | bytes 1572872 | tf_op jit(solution)/shard_map/ppermute | solution.py:1079
  527.1 19.9 %collective-permute-start.59 = (bf16[912,512]{1,0:T(8,128)(2,1)}, bf16[912,512]{1,0:T(8,128)(2,1)S(1)}, u32[]{:S(2)}, u32[]{:S(2)}) collective-permute-start(bf16[912,512]{1,0:T(8,128)(2,1)} %get-tuple-element.836), channel_id=1, source_target_pairs={{0,8},{8,16},{16,24},{24,28},{28,20},{20,12},{12,4},{4,0},{1,9},{9... | collective-permute-start | bytes 2801672 | tf_op jit(solution)/shard_map/ppermute | solution.py:1076
  527.7 19.6 %collective-permute-start.60 = (bf16[912,512]{1,0:T(8,128)(2,1)S(1)}, bf16[912,512]{1,0:T(8,128)(2,1)}, u32[]{:S(2)}, u32[]{:S(2)}) collective-permute-start(bf16[912,512]{1,0:T(8,128)(2,1)S(1)} %get-tuple-element.837), channel_id=1, source_target_pairs={{8,0},{16,8},{24,16},{28,24},{20,28},{12,20},{4,12},{0,4},{9,1},{1... | collective-permute-start | bytes 2801672 | tf_op jit(solution)/shard_map/ppermute | solution.py:1079
  551.2 18.1 %collective-permute-start.64 = (bf16[912,512]{1,0:T(8,128)(2,1)S(1)}, bf16[912,512]{1,0:T(8,128)(2,1)S(1)}, u32[]{:S(2)}, u32[]{:S(2)}) collective-permute-start(bf16[912,512]{1,0:T(8,128)(2,1)S(1)} %get-tuple-element.845), channel_id=1, source_target_pairs={{0,8},{8,16},{16,24},{24,28},{28,20},{20,12},{12,4},{4,0},{1,9},{9... | collective-permute-start | bytes 2801672 | tf_op jit(solution)/shard_map/ppermute | solution.py:1076
  551.8 18.3 %collective-permute-start.65 = (bf16[912,512]{1,0:T(8,128)(2,1)S(1)}, bf16[912,512]{1,0:T(8,128)(2,1)S(1)}, u32[]{:S(2)}, u32[]{:S(2)}) collective-permute-start(bf16[912,512]{1,0:T(8,128)(2,1)S(1)} %get-tuple-element.846), channel_id=1, source_target_pairs={{8,0},{16,8},{24,16},{28,24},{20,28},{12,20},{4,12},{0,4},{9,1},{1... | collective-permute-start | bytes 2801672 | tf_op jit(solution)/shard_map/ppermute | solution.py:1079
  575.1 17.1 %collective-permute-start.68 = (bf16[912,512]{1,0:T(8,128)(2,1)S(1)}, bf16[912,512]{1,0:T(8,128)(2,1)S(1)}, u32[]{:S(2)}, u32[]{:S(2)}) collective-permute-start(bf16[912,512]{1,0:T(8,128)(2,1)S(1)} %fusion.12), channel_id=1, source_target_pairs={{0,2},{2,0},{1,3},{3,1},{4,6},{6,4},{5,7},{7,5},{8,10},{10,8},{9,1... | collective-permute-start | bytes 2801672 | tf_op jit(solution)/shard_map/ppermute | solution.py:92
  (74 other events, 756.1 us)

commit v4 on v3

--- a/solution.py
+++ b/solution.py
@@ -15,6 +15,7 @@
 BF = jnp.bfloat16
 F32 = jnp.float32
 MIB = 1024 * 1024
+VMEM = 127 * MIB // 2
 CORE_SWAP = ((0, 1), (1, 0), (2, 3), (3, 2))
 Y_SWAP = ((0, 2), (2, 0), (1, 3), (3, 1))
 
@@ -119,17 +120,15 @@
 
 
 def erf_pair(h):
-    x = jnp.abs(h) * (1.0 / math.sqrt(2.0))
-    d = 1.0 + 0.3275911 * x
+    d = 1.0 + (0.3275911 / math.sqrt(2.0)) * jnp.abs(h)
     t = pl.reciprocal(d, approx=True)
     t = t * (2.0 - d * t)
-    e = jnp.exp(-0.5 * h * h)
-    p = t * (
-        0.254829592
-        + t * (-0.284496736 + t * (1.421413741 + t * (-1.453152027 + t * 1.061405429)))
-    )
-    q = 0.5 * p * e
-    return jnp.where(h >= 0, 1.0 - q, q), h * e * (1.0 / math.sqrt(2.0 * math.pi))
+    e = jnp.exp(-0.5 * (h * h))
+    p = 0.5 * -1.453152027 + t * (0.5 * 1.061405429)
+    p = 0.5 * 1.421413741 + t * p
+    p = 0.5 * -0.284496736 + t * p
+    q = (0.5 * 0.254829592 + t * p) * (t * e)
+    return jnp.where(h >= 0, 1.0 - q, q), (h * e) * (1.0 / math.sqrt(2.0 * math.pi))
 
 
 def over(parts, first, rows):
@@ -183,13 +182,15 @@
 
 def load_f(lay, c, where, meta, refs, wholes, sems):
     names = ("merge", "contract", "trend", "expand")
+    width = lay.width
     for (source, other, first, rows), ref in zip(meta, refs):
         src = where[2 + source]
         h = 1 - c if other else c
         for row, count, inside, part in over(lay.f_parts(h), first - lay.si_half, rows):
             t = names.index(part[2])
-            at = part[3] * lay.width + src * part[1] + inside
-            start_copy(ref, row, count, wholes[t], at, sems.at[t])
+            at = pl.multiple_of(src * part[1] + inside, 16)
+            target = wholes[t].at[pl.ds(at, count), pl.ds(part[3] * width, width)]
+            pltpu.make_async_copy(ref.at[pl.ds(row, count)], target, sems.at[t]).start()
 
 
 def any_spec():
@@ -258,7 +259,7 @@
         in_specs=[smem_spec()] + [any_spec()] * 10,
         out_specs=vmem_spec(),
         scratch_shapes=[pltpu.SemaphoreType.DMA((8 + max(STRIDES),))],
-        compiler_params=pltpu.CompilerParams(vmem_limit_bytes=60 * MIB),
+        compiler_params=pltpu.CompilerParams(vmem_limit_bytes=VMEM),
         cost_estimate=cost(0, 4 * rows * width),
         name="sibling_half" if sibling else "own_half",
     )(where, fs, cs, fi, ci, fg, cg, *weights)
@@ -334,7 +335,7 @@
         out_shape=shapes,
         in_specs=[smem_spec(), pl.BlockSpec((length, 1), lambda g: (0, 0)), group],
         out_specs=specs,
-        compiler_params=pltpu.CompilerParams(vmem_limit_bytes=60 * MIB),
+        compiler_params=pltpu.CompilerParams(vmem_limit_bytes=VMEM),
         cost_estimate=cost(6 * groups * length * length * width, 12 * groups * length * width),
         name="season_trend" if with_trend else "season",
     )(kinds, step, x)
@@ -350,6 +351,12 @@
     cut = slice(s * npos, (s + 1) * npos)
     x = jnp.concatenate([own[:, cut, :], other[:, cut, :]], axis=0)
     return x.reshape(x.shape[0] * npos, x.shape[2])
+
+
+def filled(x, rows):
+    if x.shape[0] == rows:
+        return x
+    return jnp.concatenate([x, jnp.zeros((rows - x.shape[0], x.shape[1]), x.dtype)], axis=0)
 
 
 def shrink_forward(lay, where, si, low_own, low_other, kinds_own, kinds_other, gain):
@@ -361,7 +368,7 @@
 
     def kernel(where, kinds_own, kinds_other, gain_ref, own_ref, other_ref, *refs):
         pieces, rest = refs[:count], refs[count:]
-        shrunk_ref, iso_ref, mixed_ref, age_ref, whole_out, whole, sems = rest
+        shrunk_ref, iso_ref, mixed_ref, age_ref, taps_out, whole_out, whole, taps_ref, sems = rest
 
         def body(b):
             load_si(lay, b, where, si.meta, pieces, whole, sems)
@@ -392,12 +399,19 @@
             e = jnp.zeros((m, width), F32)
             for k in range(taps):
                 at = base + (taps - 1 - k) * width
-                e += dot(tap_rows(low, age, k).astype(BF), whole[at : at + width])
+                x = tap_rows(low, age, k).astype(BF)
+                taps_ref[k, :m, :] = x
+                if m < most:
+                    taps_ref[k, m:, :] = jnp.zeros((most - m, width), BF)
+                e += dot(x, whole[at : at + width])
+            keep = pltpu.make_async_copy(taps_ref, taps_out, sems.at[3])
+            keep.start()
             iso = jnp.tanh(e)
             iso_ref[:m] = iso
             hat, _ = normal(iso + shrunk)
             mixed_ref[:m] = (hat * gain_ref[...]).astype(BF)
             pltpu.make_async_copy(whole, whole_out, sems.at[2]).wait()
+            keep.wait()
 
         by_branch(where, body)
 
@@ -408,12 +422,17 @@
             jax.ShapeDtypeStruct((most, width), F32),
             jax.ShapeDtypeStruct((most, width), BF),
             jax.ShapeDtypeStruct((most, 1), jnp.int32),
+            jax.ShapeDtypeStruct((max(lay.taps), most, width), BF),
             jax.ShapeDtypeStruct((total, width), BF),
         ],
         in_specs=[smem_spec()] * 3 + [vmem_spec()] * 3 + [any_spec()] * count,
-        out_specs=[vmem_spec()] * 4 + [any_spec()],
-        scratch_shapes=[pltpu.VMEM((total, width), BF), pltpu.SemaphoreType.DMA((3,))],
-        compiler_params=pltpu.CompilerParams(vmem_limit_bytes=60 * MIB),
+        out_specs=[vmem_spec()] * 4 + [any_spec()] * 2,
+        scratch_shapes=[
+            pltpu.VMEM((total, width), BF),
+            pltpu.VMEM((max(lay.taps), most, width), BF),
+            pltpu.SemaphoreType.DMA((4,)),
+        ],
+        compiler_params=pltpu.CompilerParams(vmem_limit_bytes=VMEM),
         cost_estimate=cost(2 * most * width * total, 4 * total * width),
         name="shrink_forward",
     )(where, kinds_own, kinds_other, gain, low_own, low_other, *si.arrays)
@@ -511,7 +530,7 @@
         ]
         + [pltpu.SemaphoreType.DMA((runs,))] * 3
         + [pltpu.SemaphoreType.DMA((2,))],
-        compiler_params=pltpu.CompilerParams(vmem_limit_bytes=60 * MIB),
+        compiler_params=pltpu.CompilerParams(vmem_limit_bytes=VMEM),
         cost_estimate=cost(
             2 * groups * length * width * (width + length),
             2 * most * width + 14 * groups * length * width,
@@ -592,7 +611,7 @@
             pltpu.VMEM((groups, length, width), F32),
         ]
         + [pltpu.SemaphoreType.DMA((runs,))] * 4,
-        compiler_params=pltpu.CompilerParams(vmem_limit_bytes=60 * MIB),
+        compiler_params=pltpu.CompilerParams(vmem_limit_bytes=VMEM),
         cost_estimate=cost(
             2 * groups * length * width * (width + length),
             2 * whole.shape[0] * width + 18 * groups * length * width,
@@ -640,10 +659,11 @@
 
         def body(b):
             npos = lay.npos[b]
-            x = mixed_ref[: 2 * groups * npos]
+            most = 2 * groups * max(lay.npos)
+            x = filled(mixed_ref[: 2 * groups * npos], most)
             steps = STRIDES[b] // 2
             for s in range(STRIDES[b]):
-                d = dot_w(x, step_rows(own_ref, other_ref, s, npos)).astype(BF)
+                d = dot_w(x, filled(step_rows(own_ref, other_ref, s, npos), most)).astype(BF)
                 side = jnp.where(where[1] == s // steps, 0, 1)
                 at = (s % steps) * k
                 for shard in range(n):
@@ -661,7 +681,7 @@
         in_specs=[smem_spec(), smem_spec()] + [vmem_spec()] * 3,
         out_specs=[any_spec()] * made,
         scratch_shapes=outlet.scratch(),
-        compiler_params=pltpu.CompilerParams(vmem_limit_bytes=60 * MIB),
+        compiler_params=pltpu.CompilerParams(vmem_limit_bytes=VMEM),
         cost_estimate=cost(4 * groups * lay.length * width * width, 2 * 2 * n * lay.g_half * width),
         name="grow_weight",
     )(where, places, mixed, pre_own, pre_other)
@@ -711,20 +731,22 @@
         in_specs=[smem_spec()] + [vmem_spec()] * 6 + [any_spec()],
         out_specs=[vmem_spec()] * 3,
         scratch_shapes=[pltpu.VMEM((max(lay.iso), width), BF), pltpu.SemaphoreType.DMA],
-        compiler_params=pltpu.CompilerParams(vmem_limit_bytes=60 * MIB),
+        compiler_params=pltpu.CompilerParams(vmem_limit_bytes=VMEM),
         cost_estimate=cost(2 * most * width * lay.iso[0], 2 * lay.iso[0] * width),
         name="shrink_backward",
     )(where, age, gain, back_own, back_other, shrunk, iso, whole)
 
 
-def shrink_weight(lay, where, places, iso_pre, pre, shrunk, low_own, low_other, gains, age, outlet):
+def shrink_weight(lay, where, places, iso_pre, pre, stacked, low_own, low_other, gains, outlet):
     width = lay.width
-    most = shrunk.shape[0]
+    most = stacked.shape[1]
     made = len(outlet.shapes())
 
-    def kernel(where, places_ref, age_ref, gains_ref, iso_pre_ref, pre_ref, shrunk_ref, *refs):
-        own_ref, other_ref = refs[:2]
-        outs, (grad_ref, sems) = refs[2 : 2 + made], refs[2 + made :]
+    def kernel(where, places_ref, gains_ref, iso_pre_ref, pre_ref, own_ref, other_ref, *refs):
+        stacked_in, outs = refs[0], refs[1 : 1 + made]
+        grad_ref, sems, taps_ref, taps_sem = refs[1 + made :]
+        fetch = pltpu.make_async_copy(stacked_in, taps_ref, taps_sem)
+        fetch.start()
         extra = gains_ref[...].astype(BF)
         for side in range(2):
             for place in range(lay.n):
@@ -748,14 +770,13 @@
                     lo += rows
 
             part_s, part_i = lay.si_parts(b)
-            low = shrunk_ref[:m].astype(BF).astype(F32)
-            age = age_ref[:m]
-            iso_pre, pre = iso_pre_ref[:m], pre_ref[:m]
+            iso_pre, pre = filled(iso_pre_ref[:m], most), filled(pre_ref[:m], most)
+            for s in range(STRIDES[b]):
+                x = filled(step_rows(own_ref, other_ref, s, npos), most)
+                store(part_s, s * width, dot_w(x, pre))
+            fetch.wait()
             for k in range(taps):
-                tap = taps - 1 - k
-                store(part_i, tap * width, dot_w(tap_rows(low, age, k).astype(BF), iso_pre))
-            for s in range(STRIDES[b]):
-                store(part_s, s * width, dot_w(step_rows(own_ref, other_ref, s, npos), pre))
+                store(part_i, (taps - 1 - k) * width, dot_w(taps_ref[k], iso_pre))
 
         by_branch(where, body)
         outlet.flush(grad_ref, outs, sems)
@@ -763,13 +784,14 @@
     return pl.pallas_call(
         kernel,
         out_shape=outlet.shapes(),
-        in_specs=[smem_spec(), smem_spec()] + [vmem_spec()] * 7,
+        in_specs=[smem_spec(), smem_spec()] + [vmem_spec()] * 5 + [any_spec()],
         out_specs=[any_spec()] * made,
-        scratch_shapes=outlet.scratch(),
-        compiler_params=pltpu.CompilerParams(vmem_limit_bytes=60 * MIB),
+        scratch_shapes=outlet.scratch()
+        + [pltpu.VMEM(stacked.shape, BF), pltpu.SemaphoreType.DMA],
+        compiler_params=pltpu.CompilerParams(vmem_limit_bytes=VMEM),
         cost_estimate=cost(2 * most * width * (lay.iso[0] + lay.shrink[0]), 30 * MIB),
         name="shrink_weight",
-    )(where, places, age, gains, iso_pre, pre, shrunk, low_own, low_other)
+    )(where, places, gains, iso_pre, pre, low_own, low_other, stacked)
 
 
 def season_backward(lay, where, whole, pre, sum_own, sum_other, order):
@@ -778,7 +800,7 @@
     most = max(lay.shrink)
 
     def kernel(where, order_ref, pre_ref, own_ref, other_ref, whole_in, *refs):
-        outs, (whole, rows_ref, sem) = refs[: groups + 1], refs[groups + 1 :]
+        outs, (whole, rows_ref, sem) = refs[:3], refs[3:]
 
         def body(b):
             fetch = pltpu.make_async_copy(
@@ -801,20 +823,22 @@
         by_branch(where, body)
         for g in range(groups):
             outs[0][g] = dot_w(order_ref[...], rows_ref[g]).astype(BF)
-            outs[1 + g][...] = dot_w(order_ref[...], rows_ref[groups + g]).astype(BF)
+            ref, i = (outs[1], 0) if g == 0 else (outs[2], g - 1)
+            ref[i] = dot_w(order_ref[...], rows_ref[groups + g]).astype(BF)
 
     return pl.pallas_call(
         kernel,
-        out_shape=[jax.ShapeDtypeStruct((groups, length, width), BF)]
-        + [jax.ShapeDtypeStruct((length, width), BF)] * groups,
+        out_shape=[
+            jax.ShapeDtypeStruct((c, length, width), BF) for c in (groups, 1, groups - 1)
+        ],
         in_specs=[smem_spec()] + [vmem_spec()] * 4 + [any_spec()],
-        out_specs=[vmem_spec()] * (1 + groups),
+        out_specs=[vmem_spec()] * 3,
         scratch_shapes=[
             pltpu.VMEM((most, width), BF),
             pltpu.VMEM((2 * groups, length, width), BF),
             pltpu.SemaphoreType.DMA,
         ],
-        compiler_params=pltpu.CompilerParams(vmem_limit_bytes=60 * MIB),
+        compiler_params=pltpu.CompilerParams(vmem_limit_bytes=VMEM),
         cost_estimate=cost(
             4 * groups * length * width * (width + length),
             2 * most * width + 24 * groups * length * width,
@@ -823,10 +847,41 @@
     )(where, order, pre, sum_own, sum_other, whole)
 
 
+def give_out(lay, member_ids, mine, over_y, sibling, sibling_over_y):
+    n, width = lay.n, lay.width
+
+    def kernel(where, mine, over_y, sibling, sibling_over_y, *outs):
+        for y in range(2):
+            for core in range(2):
+
+                @pl.when((where[0] == y) & (where[1] == core))
+                def _(y=y, core=core):
+                    for b in range(2):
+                        own, other = (mine, sibling) if b == y else (over_y, sibling_over_y)
+                        for i, (first, half, _, _) in enumerate(lay.si_parts(b)):
+                            for h in range(2):
+                                source = own if h == core else other
+                                outs[2 * i + b][h * half : (h + 1) * half, :] = source[
+                                    first : first + half, :
+                                ].astype(F32)
+
+    return pl.pallas_call(
+        kernel,
+        out_shape=[
+            jax.ShapeDtypeStruct((rows // n, width), F32) for rows in (*lay.shrink, *lay.iso)
+        ],
+        in_specs=[smem_spec()] + [vmem_spec()] * 4,
+        out_specs=[vmem_spec()] * 4,
+        compiler_params=pltpu.CompilerParams(vmem_limit_bytes=VMEM),
+        cost_estimate=cost(0, 12 * MIB),
+        name="give_out",
+    )(member_ids, mine, over_y, sibling, sibling_over_y)
+
+
 def dense_whole(lay, where, gf):
     width, ff = lay.width, lay.width * lay.chunks
     count = len(gf.arrays)
-    sizes = (2 * width, ff, width, ff)
+    shapes = ((2 * width, width), (ff, width), (width, width), (width, ff))
 
     def kernel(where, *refs):
         pieces, wholes, sems = refs[:count], refs[count:-1], refs[-1]
@@ -835,16 +890,16 @@
                 functools.partial(load_f, lay, c, where, gf.meta, pieces, wholes, sems)
             )
         for t in range(4):
-            wait_rows(wholes[t], 0, sizes[t], sems.at[t])
+            wait_rows(wholes[t], 0, shapes[t][0], sems.at[t])
 
     return pl.pallas_call(
         kernel,
-        out_shape=[jax.ShapeDtypeStruct((r, width), BF) for r in sizes],
+        out_shape=[jax.ShapeDtypeStruct(v, BF) for v in shapes],
         in_specs=[smem_spec()] + [any_spec()] * count,
         out_specs=[vmem_spec()] * 4,
         scratch_shapes=[pltpu.SemaphoreType.DMA((4,))],
-        compiler_params=pltpu.CompilerParams(vmem_limit_bytes=60 * MIB),
-        cost_estimate=cost(0, 4 * sum(sizes) * width),
+        compiler_params=pltpu.CompilerParams(vmem_limit_bytes=VMEM),
+        cost_estimate=cost(0, 4 * sum(r * c for r, c in shapes)),
         name="dense_whole",
     )(where, *gf.arrays)
 
@@ -854,74 +909,104 @@
     cuts = 2
     part = length // cuts
     ff = width * chunks
+    strip = 32
 
     def kernel(where, tile_ref, gm_ref, go_ref, merge, contract, trend, expand, *refs):
         mine_ref, got_ref, trend_ref, grad_ref = refs[:4]
-        (out_ref, jm_ref, js_ref, tb_ref, ml_ref, hid_ref, hg_ref, ll_ref, mg_ref) = refs[4:13]
-        gains_ref, slope_ref = refs[13:]
+        (hid_ref, hg_ref, ml_ref, ll_ref, mg_ref, tb_ref, out_ref, jm_ref, js_ref) = refs[4:13]
+        gains_ref, h_ref, slope_ref, a_ref, b_ref, c_ref = refs[13:]
         b = where[0]
         gm, go = gm_ref[...], go_ref[...]
         at_mine = pl.multiple_of(b * width, width)
         at_other = pl.multiple_of((1 - b) * width, width)
 
-        merged = dot(mine_ref[...], merge[pl.ds(at_mine, width)])
-        merged += dot(got_ref[...], merge[pl.ds(at_other, width)])
-        mhat, minv = normal(merged)
-        middle = mhat * gm
-        mlow = middle.astype(BF)
-        ml_ref[...] = mlow
-        lifted = jnp.zeros((part, width), F32)
+        def strips(body):
+            for r in range(0, part, strip):
+                body(slice(r, r + strip))
+
+        a_ref[...] = dot(mine_ref[...], merge[pl.ds(at_mine, width)]) + dot(
+            got_ref[...], merge[pl.ds(at_other, width)]
+        )
+        inverses = {}
+
+        def middle_norm(r):
+            hat, inverses[r.start] = normal(a_ref[r, :])
+            a_ref[r, :] = hat
+            ml_ref[r, :] = (hat * gm).astype(BF)
+
+        strips(middle_norm)
         for j in range(chunks):
             cols = slice(j * width, (j + 1) * width)
-            h = dot(mlow, expand[cols])
-            phi, dens = erf_pair(h)
-            hid = (h * phi).astype(BF)
-            slope_ref[:, cols] = phi + dens
-            hid_ref[:, cols] = hid
-            lifted += dot(hid, contract[cols])
-        ohat, oinv = normal(middle + lifted)
-        g_low = grad_ref[0]
-        projected = dot(trend_ref[0], trend[...])
-        out_ref[...] = (ohat * go + projected).astype(BF)
-        g = g_low.astype(F32)
-        tb_ref[...] = dot_t(g_low, trend[...])
-        d = normal_back(g, ohat, oinv, go)
-        llow = d.astype(BF)
-        ll_ref[...] = llow
-        back = d
+            h_ref[:, cols] = dot(ml_ref[...], expand[:, cols])
+
+            def gelu(r, cols=cols):
+                h = h_ref[r, cols]
+                phi, dens = erf_pair(h)
+                hid_ref[r, cols] = (h * phi).astype(BF)
+                slope_ref[r, cols] = phi + dens
+
+            strips(gelu)
+        b_ref[...] = dot(hid_ref[...], contract[...])
+        c_ref[...] = dot(trend_ref[0], trend[...])
+        sums = [jnp.zeros((8, width), F32), jnp.zeros((8, width), F32)]
+
+        def rows8(v):
+            return jnp.sum(v.reshape(strip // 8, 8, width), axis=0)
+
+        def output_norm(r):
+            hat, inverse = normal(a_ref[r, :] * gm + b_ref[r, :])
+            out_ref[r, :] = (hat * go + c_ref[r, :]).astype(BF)
+            g = grad_ref[0, r, :].astype(F32)
+            sums[1] += rows8(g * hat)
+            d = normal_back(g, hat, inverse, go)
+            b_ref[r, :] = d
+            ll_ref[r, :] = d.astype(BF)
+
+        strips(output_norm)
+        tb_ref[...] = dot_t(grad_ref[0], trend[...])
         for j in range(chunks):
             cols = slice(j * width, (j + 1) * width)
-            hg = (dot_t(llow, contract[cols]) * slope_ref[:, cols]).astype(BF)
-            hg_ref[:, cols] = hg
-            back += dot_t(hg, expand[cols])
-        mg = normal_back(back, mhat, minv, gm).astype(BF)
-        mg_ref[...] = mg
-        jm_ref[...] = dot_t(mg, merge[pl.ds(at_mine, width)]).astype(BF)
-        js_ref[...] = dot_t(mg, merge[pl.ds(at_other, width)]).astype(BF)
+            h_ref[:, cols] = dot_t(ll_ref[...], contract[cols])
+
+            def gelu_back(r, cols=cols):
+                hg_ref[r, cols] = (h_ref[r, cols] * slope_ref[r, cols]).astype(BF)
+
+            strips(gelu_back)
+        c_ref[...] = dot_t(hg_ref[...], expand[...])
+
+        def middle_back(r):
+            hat = a_ref[r, :]
+            back = b_ref[r, :] + c_ref[r, :]
+            sums[0] += rows8(back * hat)
+            mg_ref[r, :] = normal_back(back, hat, inverses[r.start], gm).astype(BF)
+
+        strips(middle_back)
+        jm_ref[...] = dot_t(mg_ref[...], merge[pl.ds(at_mine, width)]).astype(BF)
+        js_ref[...] = dot_t(mg_ref[...], merge[pl.ds(at_other, width)]).astype(BF)
 
         @pl.when(pl.program_id(0) == 0)
         def _():
             gains_ref[...] = jnp.zeros_like(gains_ref)
 
-        gains_ref[0:1, :] += jnp.sum(back * mhat, axis=0, keepdims=True)
-        gains_ref[1:2, :] += jnp.sum(g * ohat, axis=0, keepdims=True)
+        gains_ref[0:1, :] += jnp.sum(sums[0], axis=0, keepdims=True)
+        gains_ref[1:2, :] += jnp.sum(sums[1], axis=0, keepdims=True)
 
     of_tile = pl.BlockSpec((1, part, width), lambda i, w, t: (t[0], i, 0))
     alone = pl.BlockSpec((part, width), lambda i, w, t: (i, 0))
-    shapes = [(width, BF)] * 3 + [(width, F32), (width, BF), (ff, BF), (ff, BF), (width, BF), (width, BF)]
+    shapes = [(ff, BF)] * 2 + [(width, BF)] * 3 + [(width, F32)] + [(width, BF)] * 3
     return pl.pallas_call(
         kernel,
         grid_spec=pltpu.PrefetchScalarGridSpec(
             num_scalar_prefetch=2,
             grid=(cuts,),
             in_specs=[vmem_spec()] * 6 + [alone, alone, of_tile, of_tile],
-            out_specs=[pl.BlockSpec((part, w), lambda i, w, t: (i, 0)) for w, _ in shapes]
+            out_specs=[pl.BlockSpec((part, c), lambda i, w, t: (i, 0)) for c, _ in shapes]
             + [pl.BlockSpec((2, width), lambda i, w, t: (0, 0))],
-            scratch_shapes=[pltpu.VMEM((part, ff), F32)],
+            scratch_shapes=[pltpu.VMEM((part, ff), F32)] * 2 + [pltpu.VMEM((part, width), F32)] * 3,
         ),
         out_shape=[jax.ShapeDtypeStruct((length, w), t) for w, t in shapes]
         + [jax.ShapeDtypeStruct((2, width), F32)],
-        compiler_params=pltpu.CompilerParams(vmem_limit_bytes=60 * MIB),
+        compiler_params=pltpu.CompilerParams(vmem_limit_bytes=VMEM),
         cost_estimate=cost(
             2 * length * width * (4 * width + 4 * ff + 2 * width), 12 * MIB + 20 * MIB
         ),
@@ -1029,7 +1114,7 @@
         scratch_shapes=outlet.scratch()
         + [square] * 5
         + [pltpu.SemaphoreType.DMA((3 * groups + 2,))],
-        compiler_params=pltpu.CompilerParams(vmem_limit_bytes=60 * MIB),
+        compiler_params=pltpu.CompilerParams(vmem_limit_bytes=VMEM),
         cost_estimate=cost(
             2 * groups * length * width * (2 * width + 2 * ff + width), 45 * MIB
         ),
@@ -1194,7 +1279,7 @@
     cut_at = middle + half_rows
     sends = {"r": (whole_r[middle:cut_at], right), "l": (whole_l[cut_at:], left)}
     arrived, done = slot(sends, run_shrink, (low_own, low_other, *pieces.arrays))
-    shrunk, iso, mixed, age, si_whole = done
+    shrunk, iso, mixed, age, stacked_rows, si_whole = done
     gf_r, gf_l = arrived["r"], arrived["l"]
     pieces.add(source(last), 0, middle, gf_r)
     pieces.add(source(last), 0, cut_at, gf_l)
@@ -1239,11 +1324,11 @@
             received.append(arrived["b"])
         if "j" in arrived:
             back_got.append(arrived["j"])
-        outs.append(made[0])
-        back_own.append(made[1])
-        waiting.append(made[2])
-        trend_back.append(made[3])
-        saved.append(made[4:9])
+        outs.append(made[6])
+        back_own.append(made[7])
+        waiting.append(made[8])
+        trend_back.append(made[5])
+        saved.append((made[2], made[0], made[1], made[3], made[4]))
         dense_gains = made[9] if dense_gains is None else dense_gains + made[9]
     series_out = jnp.concatenate(outs)
 
@@ -1265,13 +1350,6 @@
         return dense_weights(
             lay, where, spot, mine, list(got), trend_low, grads_in, kept, f_outlet
         )
-
-    arrived, (f_keep, f_give) = slot(
-        {"j": (waiting.pop(0), swap_y)},
-        run_dense_weights,
-        (*branch_own, *received, *[v for k in saved for v in k]),
-    )
-    back_got.append(arrived["j"])
 
     class Chain:
         def __init__(self, keep):
@@ -1311,23 +1389,31 @@
     def back_of(grads, g_whole, up, season):
         return grow_backward(lay, where, g_whole, grads, up, season, order, gain_b)
 
+    def weights_and_own(g_whole, up, season, *rest):
+        return (
+            *run_dense_weights(*rest[groups:]),
+            *back_of(rest[:groups], g_whole, up, season),
+        )
+
+    sends = {"j%d" % i: (v, swap_y) for i, v in enumerate(waiting)}
     arrived, done = slot(
-        {"j": (waiting.pop(0), swap_y), "f": (f_give, swap_core)},
-        lambda g_whole, up, season, *grads: back_of(grads, g_whole, up, season),
-        (g_whole, up_own, season_own, *back_own),
+        sends,
+        weights_and_own,
+        (g_whole, up_own, season_own, *back_own, *branch_own, *received)
+        + tuple(v for k in saved for v in k),
     )
-    back_got.append(arrived["j"])
-    pre_own, mixed_back_own, sum_own, gains_own = done
-    f = Chain(f_keep)
-    f.got = [arrived["f"]]
-    chains = {"f": f}
-    starts = {"g": 3, "s": 5}
+    back_got += [arrived[k] for k in sends]
+    f_keep, f_give = done[:2]
+    pre_own, mixed_back_own, sum_own, gains_own = done[2:]
+    chains = {}
     kept = {}
     finals = {}
     t = 0
     while True:
         active = {k: c for k, c in chains.items() if c.step > 0}
         finishing = [k for k, c in chains.items() if c.step == 0 and k + "mine" not in finals]
+        if len(active) > 1:
+            finishing = []
         if not active and not finishing and "smine" in finals:
             break
         sends, work, given = {}, None, ()
@@ -1341,13 +1427,13 @@
             if name != "f":
                 sends[name + "c"] = (mine, swap_core)
         for name in ("f", "g"):
-            ready = name + "late" in finals and (t > 6 or name == "g")
-            if ready and name + "sent" not in finals:
+            if name + "late" in finals and name + "sent" not in finals:
                 sends[name + "d"] = (finals[name + "late"], swap_core)
                 finals[name + "sent"] = True
         if t == 0:
             work = lambda g_whole, up, season, *grads: back_of(grads, g_whole, up, season)
             given = (g_whole, up_other, season_other, *back_got)
+            sends["f0"] = (f_give, swap_core)
         elif t == 1:
             work = lambda *v: grow_weight(lay, where, spot, *v, g_outlet)
             given = (mixed, pre_own, pre_other)
@@ -1356,20 +1442,21 @@
             given = (si_whole, mixed_back_own, mixed_back_other, shrunk, iso)
             sends["g"] = (g_give, swap_core)
         elif t == 3:
-            work = lambda *v: shrink_weight(lay, where, spot, *v, age, s_outlet)
-            given = (iso_pre, shrink_pre, shrunk, low_own, low_other, grad_gains)
+            work = lambda *v: shrink_weight(lay, where, spot, *v, s_outlet)
+            given = (iso_pre, shrink_pre, stacked_rows, low_own, low_other, grad_gains)
         elif t == 4:
             work = lambda *v: season_backward(lay, where, *v, order)
             given = (si_whole, shrink_pre, sum_own, sum_other)
             sends["s0"] = (s_give, swap_core)
-        if t in (5, 6, 8) and tail_sends:
-            for i in range(len(tail_sends) if t == 8 else 1):
-                sends["x%d" % i] = (tail_sends.pop(0), swap_y)
+        if t in (5, 6):
+            sends["x"] = (tail_sends[t - 5], swap_y)
         if "s" in finishing:
             work, given = finish, (season_mine, own_counts, *trend_back, *tail)
         arrived, done = slot(sends, work, given)
         if t == 0:
             pre_other, mixed_back_other, sum_other, gains_other = done
+            chains["f"] = Chain(f_keep)
+            chains["f"].got = [arrived["f0"]]
         elif t == 1:
             g_keep, g_give = done
             chains["g"] = None
@@ -1390,7 +1477,7 @@
 
             def finish(season_mine, own_counts, *rest):
                 backs, tail = rest[:groups], rest[groups:]
-                total = season_mine.astype(F32) + jnp.stack(tail).astype(F32)
+                total = season_mine.astype(F32) + jnp.concatenate(tail).astype(F32)
                 rest = jnp.stack(backs) - total
                 spread = (rest * (1.0 / WINDOW)).astype(BF)
                 averaged = jnp.einsum(
@@ -1398,9 +1485,8 @@
                 )
                 return ((total + averaged).astype(BF),)
 
-        for i in range(groups):
-            if "x%d" % i in arrived:
-                tail.append(arrived["x%d" % i])
+        if "x" in arrived:
+            tail.append(arrived["x"])
         for name, chain in active.items():
             chain.r, chain.l = arrived[name + "r"], arrived[name + "l"]
             chain.step -= 1
@@ -1433,24 +1519,17 @@
     def branches(mine, over_y):
         return jnp.where(fine, mine, over_y), jnp.where(fine, over_y, mine)
 
-    s_fine, s_coarse = branches(s_mine, s_y)
-    t_fine, t_coarse = branches(*s_core)
     g_fine, g_coarse = branches(g_mine, g_y)
     h_fine, h_coarse = branches(*g_core)
-
-    def si_out(b, mine, other):
-        lo, hi = both(mine, other)
-        (f0, r0, _, _), (f1, r1, _, _) = lay.si_parts(b)
-        shrink = jnp.concatenate([lo[f0 : f0 + r0], hi[f0 : f0 + r0]])
-        return shrink.astype(F32), jnp.concatenate([lo[f1 : f1 + r1], hi[f1 : f1 + r1]]).astype(F32)
 
     def g_out(b, mine, other):
         lo, hi = both(mine, other)
         cols = [v[r : r + k] for v in (lo, hi) for r, k, _ in lay.g_parts(b)]
         return jnp.concatenate(cols, axis=1).astype(F32)
 
-    fine_shrink_grad, fine_iso_grad = si_out(0, s_fine, t_fine)
-    coarse_shrink_grad, coarse_iso_grad = si_out(1, s_coarse, t_coarse)
+    fine_shrink_grad, coarse_shrink_grad, fine_iso_grad, coarse_iso_grad = give_out(
+        lay, member_ids, s_mine, s_y, *s_core
+    )
     fine_grow_grad, coarse_grow_grad = g_out(0, g_fine, h_fine), g_out(1, g_coarse, h_coarse)
     lo, hi = both(f_half, f_other)
     (a0, a1, _, _), (b0, b1, _, _) = lay.f_parts(0)

time: 612 us -> 596 us (0.974)
  starting transfers between devices: 72.8 us -> 63.8 us
  Pallas kernels: 256 us -> 248 us
    pallas_call x3, Pallas kernels: 80.5 us -> 65.3 us  [dense(): pl.pallas_call(kernel, grid_spec=pltpu.PrefetchScalarGridSpec(num_scalar_...]
    ppermute x16 -> x15, starting transfers between devices: 29.1 us -> 20.2 us  [swap_y(): return lax.ppermute(v, 'group', Y_SWAP)]
    ppermute x16 -> x15, waiting for transfers between devices: 62.6 us -> 55.6 us  [swap_y(): return lax.ppermute(v, 'group', Y_SWAP)]
    pallas_call x2 -> x3, Pallas kernels: 20.6 us -> 26.4 us  [the longest x1 15 us: season_backward(): pl.pallas_call(kernel, out_shape=[jax.ShapeDtypeStruct((c, length, width)...]
  transfers between devices with their start and end apart: 71 -> 70, of which waited for: 25 -> 24; matrix products, arithmetic and copies ran while one was open for 5% -> 6% of each run, Pallas kernels for 40% -> 39%
where the time goes in v4:
time: 596 us; the launch traced here: 586 us
  Pallas kernels  248 us (42%)
  waiting for transfers between devices  185 us (31%)
  starting transfers between devices  63.8 us (11%)
  other arithmetic  62.6 us (11%)
  local copies, waits for them, and re-layouts  17.6 us (3%)
  matrix products  7 us (1%)
    ppermute x17, waiting for transfers between devices, right(): return lax.ppermute(v, 'dp', ring.right)  94.2 us
    pallas_call x3, Pallas kernels, dense(): pl.pallas_call(kernel, grid_spec=pltpu.PrefetchScalarGridSpec(num_scalar_...  65.3 us
    ppermute x15, waiting for transfers between devices, swap_y(): return lax.ppermute(v, 'group', Y_SWAP)  55.6 us
    pallas_call x2, Pallas kernels, grow_backward(): pl.pallas_call(kernel, out_shape=[jax.ShapeDtypeStruct((groups, length, w...  25.3 us
    pallas_call x1, Pallas kernels, dense_weights(): pl.pallas_call(kernel, grid=(chunks,), out_shape=outlet.shapes(), in_spec...  24.3 us
    ppermute x3, waiting for transfers between devices, exchange(): return lambda v: lax.ppermute(v, axis, [(i, i ^ step) for i in range(size)])  24.1 us
    pallas_call x2, Pallas kernels, season_kernel(): pl.pallas_call(kernel, grid=(groups,), out_shape=shapes, in_specs=[smem_s...  22.5 us
    pallas_call x2, Pallas kernels, grow_forward(): pl.pallas_call(kernel, out_shape=shapes, in_specs=[smem_spec()] + [vmem_s...  22.1 us
  transfers between devices with their start and end apart: 70, of which 24 were waited for; matrix products, arithmetic and copies ran while one was open for 6% of the time, Pallas kernels for 39%

profile of v4, /device:TPU:0, one launch (start us, length us, event | category | flops | bytes accessed | tf_op | source)
XLA Modules:
  0.0 585.7 jit_solution(13748774584769806767)
XLA Ops:
  1.3 3.1 fusion.52
  5.2 3.5 own_half.1.refs_0_
  8.7 3.1 collective-permute-start
  15.8 3.5 sibling_half.1.refs_1_
  19.3 11.8 %collective-permute-done.3 = f32[12]{0:T(128)S(1)} collective-permute-done((f32[12]{0:T(128)S(1)}, f32[12]{0:T(128)S(1)}, u32[]{:S(2)}, u32[]{:S(2)}) %collective-permute-start.3) | collective-permute-done | bytes 80 | tf_op jit(solution)/shard_map/ppermute | solution.py:93
  31.1 21.1 %collective-permute-done.4 = f32[3,512]{1,0:T(4,128)} collective-permute-done((f32[3,512]{1,0:T(4,128)S(1)}, f32[3,512]{1,0:T(4,128)}, u32[]{:S(2)}, u32[]{:S(2)}) %collective-permute-start.4) | collective-permute-done | bytes 6176 | tf_op jit(solution)/shard_map/ppermute | solution.py:1126
  57.6 8.1 %fusion.36.step_ref = s32[768,1]{1,0:T(8,128)} fusion(s32[]{:T(128)S(6)} %select_n.223, s32[]{:T(128)S(6)} %sign.30, s32[]{:T(128)S(6)} %select_n.226, s32[]{:T(128)S(6)} %select_n.224), kind=kLoop, calls=%fused_computation.88 | loop fusion | flops 12288 | bytes 3088 | tf_op jit(solution)/shard_map/add | solution.py:1190
  65.8 12.8 %season_trend.1 = (f32[3,768,512]{2,1,0:T(8,128)}, bf16[3,768,512]{2,1,0:T(8,128)(2,1)}, bf16[3,768,768]{2,1,0:T(8,128)(2,1)}, bf16[3,768,512]{2,1,0:T(8,128)(2,1)}, bf16[768,768]{1,0:T(8,128)(2,1)}) custom-call(s32[12]{0:T(128)} %kinds_own.1, s32[768,1]{1,0:T(8,128)} %fusion.36.step_ref, bf16[3,768,512]{2,1,0:T(8,128)(2,1)} %bitcast.163), custom_call_target="tpu_custom_call" | custom-call | flops 5435817984 | bytes 14155776 | tf_op jit(solution)/shard_map/season_trend/pallas_call | solution.py:332
  78.5 15.8 %collective-permute-done.5.refs_6_ = bf16[1792,512]{1,0:T(8,128)(2,1)} collective-permute-done((bf16[1792,512]{1,0:T(8,128)(2,1)}, bf16[1792,512]{1,0:T(8,128)(2,1)}, u32[]{:S(2)}, u32[]{:S(2)}) %collective-permute-start.5) | collective-permute-done | bytes 1835040 | tf_op jit(solution)/shard_map/ppermute | solution.py:1161
  102.0 16.0 %collective-permute-done.14 = bf16[768,512]{1,0:T(8,128)(2,1)S(1)} collective-permute-done((bf16[768,512]{1,0:T(8,128)(2,1)}, bf16[768,512]{1,0:T(8,128)(2,1)S(1)}, u32[]{:S(2)}, u32[]{:S(2)}) %collective-permute-start.14) | collective-permute-done | bytes 786464 | tf_op jit(solution)/shard_map/ppermute | solution.py:93
  118.0 17.2 %collective-permute-done.10.refs_10_ = bf16[1792,512]{1,0:T(8,128)(2,1)} collective-permute-done((bf16[1792,512]{1,0:T(8,128)(2,1)}, bf16[1792,512]{1,0:T(8,128)(2,1)}, u32[]{:S(2)}, u32[]{:S(2)}) %collective-permute-start.10) | collective-permute-done | bytes 1835040 | tf_op jit(solution)/shard_map/ppermute | solution.py:1161
  136.9 2.7 fusion.53
  144.3 3.0 pad_maximum_fusion.x_ref
  147.3 9.8 %season.1 = (f32[3,768,512]{2,1,0:T(8,128)}, bf16[3,768,512]{2,1,0:T(8,128)(2,1)}) custom-call(s32[12]{0:T(128)} %convert_element_type.396.kinds_ref.kinds_other, s32[768,1]{1,0:T(8,128)} %fusion.36.step_ref, bf16[3,768,512]{2,1,0:T(8,128)(2,1)} %pad_maximum_fusion.x_ref), custom_call_target="tpu_custom_call" | custom-call | flops 5435817984 | bytes 14155776 | tf_op jit(solution)/shard_map/season/pallas_call | solution.py:332
  160.0 3.0 collective-permute-done.22
  167.2 18.9 %shrink_forward.1 = (f32[384,512]{1,0:T(8,128)}, f32[384,512]{1,0:T(8,128)}, bf16[384,512]{1,0:T(8,128)(2,1)}, s32[384,1]{1,0:T(8,128)}, bf16[16,384,512]{2,1,0:T(8,128)(2,1)}, /*index=5*/bf16[14336,512]{1,0:T(8,128)(2,1)}) custom-call(s32[10]{0:T(128)} %stack.84.where, s32[12]{0:T(128)} %kinds_own.1, s32[12]{0:T(128)} %convert_element_type.396.kinds_ref.kinds_other, ...), custom_call_target="tpu_custom_call" | custom-call | flops 5637144576 | bytes 29360128 | tf_op jit(solution)/shard_map/shrink_forward/pallas_call | solution.py:418
  189.0 11.4 %grow_forward.2 = (bf16[1,768,512]{2,1,0:T(8,128)(2,1)}, bf16[1,768,512]{2,1,0:T(8,128)(2,1)}, bf16[1,768,512]{2,1,0:T(8,128)(2,1)}, f32[3,768,512]{2,1,0:T(8,128)}, bf16[8192,512]{1,0:T(8,128)(2,1)}) custom-call(s32[10]{0:T(128)} %stack.84.where, f32[1,512]{1,0:T(1,128)} %get-tuple-element.924.gain_ref, bf16[768,768]{1,0:T(8,128)(2,1)} %get-tuple-element.509.order_ref, ...), custom_call_target="tpu_custom_call" | custom-call | flops 3019898880 | bytes 24903680 | tf_op jit(solution)/shard_map/grow_forward/pallas_call | solution.py:520
  200.5 2.4 collective-permute-start.27
  203.4 5.8 dense_whole.1
  209.2 10.6 %grow_forward.3 = (bf16[1,768,512]{2,1,0:T(8,128)(2,1)}, bf16[1,768,512]{2,1,0:T(8,128)(2,1)}, bf16[1,768,512]{2,1,0:T(8,128)(2,1)}, f32[3,768,512]{2,1,0:T(8,128)}) custom-call(s32[10]{0:T(128)} %stack.84.where, f32[1,512]{1,0:T(1,128)} %get-tuple-element.924.gain_ref, bf16[768,768]{1,0:T(8,128)(2,1)} %get-tuple-element.509.order_ref, ...), custom_call_target="tpu_custom_call" | custom-call | flops 3019898880 | bytes 24903680 | tf_op jit(solution)/shard_map/grow_forward/pallas_call | solution.py:520
  222.8 21.7 %dense.3 = (bf16[768,2048]{1,0:T(8,128)(2,1)}, bf16[768,2048]{1,0:T(8,128)(2,1)}, bf16[768,512]{1,0:T(8,128)(2,1)}, bf16[768,512]{1,0:T(8,128)(2,1)}, bf16[768,5...) custom-call(s32[10]{0:T(128)} %stack.84.where, ...), custom_call_target="tpu_custom_call" | custom-call | flops 8858370048 | bytes 33554432 | tf_op jit(solution)/shard_map/dense/pallas_call | solution.py:997
  244.9 21.9 %dense.4 = (bf16[768,2048]{1,0:T(8,128)(2,1)}, bf16[768,2048]{1,0:T(8,128)(2,1)}, bf16[768,512]{1,0:T(8,128)(2,1)}, bf16[768,512]{1,0:T(8,128)(2,1)}, bf16[768,5...) custom-call(s32[10]{0:T(128)} %stack.84.where, ...), custom_call_target="tpu_custom_call" | custom-call | flops 8858370048 | bytes 33554432 | tf_op jit(solution)/shard_map/dense/pallas_call | solution.py:997
  268.6 21.7 %dense.5 = (bf16[768,2048]{1,0:T(8,128)(2,1)}, bf16[768,2048]{1,0:T(8,128)(2,1)}, bf16[768,512]{1,0:T(8,128)(2,1)}, bf16[768,512]{1,0:T(8,128)(2,1)}, bf16[768,5...) custom-call(s32[10]{0:T(128)} %stack.84.where, ...), custom_call_target="tpu_custom_call" | custom-call | flops 8858370048 | bytes 33554432 | tf_op jit(solution)/shard_map/dense/pallas_call | solution.py:997
  292.4 12.7 %grow_backward.2 = (bf16[3,768,512]{2,1,0:T(8,128)(2,1)}, f32[192,512]{1,0:T(8,128)}, f32[3,768,512]{2,1,0:T(8,128)}, f32[1,512]{1,0:T(1,128)}) custom-call(s32[10]{0:T(128)} %stack.84.where, f32[1,512]{1,0:T(1,128)} %get-tuple-element.924.gain_ref, bf16[768,768]{1,0:T(8,128)(2,1)} %get-tuple-element.509.order_ref, f32[3,768,512]{2,1,0:T(8,128)} %get-tuple-element.709.up_in, ...), custom_call_target="tpu_custom_call" | custom-call | flops 3019898880 | bytes 29622272 | tf_op jit(solution)/shard_map/grow_backward/pallas_call | solution.py:596
  305.1 24.3 %dense_weights.1 = (bf16[8,384,512]{2,1,0:T(8,128)(2,1)}, bf16[8,384,512]{2,1,0:T(8,128)(2,1)}) custom-call(s32[10]{0:T(128)} %stack.84.where, s32[8]{0:T(128)} %compare_select_fusion.6.places_ref, bf16[768,512]{1,0:T(8,128)(2,1)} %get-tuple-element.686.refs_0_, bf16[768,512]{1,0:T(8,128)(2,1)} %get-tuple-element.687.refs_1_, ...), custom_call_target="tpu_custom_call" | custom-call | flops 13287555072 | bytes 47185920 | tf_op jit(solution)/shard_map/dense_weights/pallas_call | solution.py:1105
  329.6 12.6 %grow_backward.3 = (bf16[3,768,512]{2,1,0:T(8,128)(2,1)}, f32[192,512]{1,0:T(8,128)}, f32[3,768,512]{2,1,0:T(8,128)}, f32[1,512]{1,0:T(1,128)}) custom-call(s32[10]{0:T(128)} %stack.84.where, f32[1,512]{1,0:T(1,128)} %get-tuple-element.924.gain_ref, bf16[768,768]{1,0:T(8,128)(2,1)} %get-tuple-element.509.order_ref, f32[3,768,512]{2,1,0:T(8,128)} %get-tuple-element.726.up_in, ...), custom_call_target="tpu_custom_call" | custom-call | flops 3019898880 | bytes 29622272 | tf_op jit(solution)/shard_map/grow_backward/pallas_call | solution.py:596
  347.5 9.8 %grow_weight.1 = (bf16[8,512,512]{2,1,0:T(8,128)(2,1)}, bf16[8,512,512]{2,1,0:T(8,128)(2,1)}) custom-call(s32[10]{0:T(128)} %stack.84.where, s32[8]{0:T(128)} %compare_select_fusion.6.places_ref, bf16[384,512]{1,0:T(8,128)(2,1)} %get-tuple-element.741.mixed_ref, bf16[3,768,512]{2,1,0:T(8,128)(2,1)} %get-tuple-element.742.own_ref, ...), custom_call_target="tpu_custom_call" | custom-call | flops 2415919104 | bytes 8388608 | tf_op jit(solution)/shard_map/grow_weight/pallas_call | solution.py:678
  363.2 9.8 %shrink_backward.1 = (bf16[384,512]{1,0:T(8,128)(2,1)}, bf16[384,512]{1,0:T(8,128)(2,1)}, f32[1,512]{1,0:T(1,128)}) custom-call(s32[10]{0:T(128)} %stack.84.where, s32[384,1]{1,0:T(8,128)} %get-tuple-element.757.age_ref, f32[1,512]{1,0:T(1,128)} %get-tuple-element.924.gain_ref, f32[192,512]{1,0:T(8,128)} %get-tuple-element.758.b0, ...), custom_call_target="tpu_custom_call" | custom-call | flops 3221225472 | bytes 8388608 | tf_op jit(solution)/shard_map/shrink_backward/pallas_call | solution.py:724
  373.1 3.7 convert_add_fusion.3
  377.6 2.6 fusion.27
  385.1 16.1 %shrink_weight.1 = (bf16[8,912,512]{2,1,0:T(8,128)(2,1)}, bf16[8,912,512]{2,1,0:T(8,128)(2,1)}) custom-call(s32[10]{0:T(128)} %stack.84.where, s32[8]{0:T(128)} %compare_select_fusion.6.places_ref, f32[16,512]{1,0:T(8,128)} %maximum_maximum_fusion.gains_ref, bf16[384,512]{1,0:T(8,128)(2,1)} %get-tuple-element.784.iso_pre_ref, ...), custom_call_target="tpu_custom_call" | custom-call | flops 5637144576 | bytes 31457280 | tf_op jit(solution)/shard_map/shrink_weight/pallas_call | solution.py:784
  407.4 2.6 fusion.25
  414.1 15.0 %season_backward.1 = (bf16[3,768,512]{2,1,0:T(8,128)(2,1)}, bf16[1,768,512]{2,1,0:T(8,128)(2,1)}, bf16[2,768,512]{2,1,0:T(8,128)(2,1)}) custom-call(s32[10]{0:T(128)} %stack.84.where, bf16[768,768]{1,0:T(8,128)(2,1)} %get-tuple-element.509.order_ref, bf16[384,512]{1,0:T(8,128)(2,1)} %get-tuple-element.804.pre_ref, ...), custom_call_target="tpu_custom_call" | custom-call | flops 6039797760 | bytes 36700160 | tf_op jit(solution)/shard_map/season_backward/pallas_call | solution.py:829
  429.1 4.0 collective-permute-done.45
  433.8 3.6 convert_add_fusion.1
  437.6 2.0 fusion.16
  439.7 2.6 collective-permute-start.52
  446.4 18.8 %collective-permute-done.50 = bf16[456,512]{1,0:T(8,128)(2,1)S(1)} collective-permute-done((bf16[456,512]{1,0:T(8,128)(2,1)S(1)}, bf16[456,512]{1,0:T(8,128)(2,1)S(1)}, u32[]{:S(2)}, u32[]{:S(2)}) %collective-permute-start.50) | collective-permute-done | bytes 466976 | tf_op jit(solution)/shard_map/ppermute | solution.py:1161
  475.6 26.2 %collective-permute-done.53 = bf16[512,512]{1,0:T(8,128)(2,1)S(1)} collective-permute-done((bf16[512,512]{1,0:T(8,128)(2,1)S(1)}, bf16[512,512]{1,0:T(8,128)(2,1)S(1)}, u32[]{:S(2)}, u32[]{:S(2)}) %collective-permute-start.53) | collective-permute-done | bytes 524320 | tf_op jit(solution)/shard_map/ppermute | solution.py:1161
  505.3 2.3 fusion.8
  511.7 16.7 %collective-permute-done.60 = bf16[384,512]{1,0:T(8,128)(2,1)S(1)} collective-permute-done((bf16[384,512]{1,0:T(8,128)(2,1)S(1)}, bf16[384,512]{1,0:T(8,128)(2,1)S(1)}, u32[]{:S(2)}, u32[]{:S(2)}) %collective-permute-start.60) | collective-permute-done | bytes 393248 | tf_op jit(solution)/shard_map/ppermute | solution.py:93
  529.3 2.3 fusion.7
  534.3 3.2 pad_maximum_fusion.1
  537.5 12.3 %collective-permute-done.63 = bf16[912,512]{1,0:T(8,128)(2,1)} collective-permute-done((bf16[912,512]{1,0:T(8,128)(2,1)S(1)}, bf16[912,512]{1,0:T(8,128)(2,1)}, u32[]{:S(2)}, u32[]{:S(2)}) %collective-permute-start.63) | collective-permute-done | bytes 933920 | tf_op jit(solution)/shard_map/ppermute | solution.py:1161
  551.5 2.5 fusion.12.mine
  560.1 7.0 %add_convert_fusion = bf16[3,768,512]{2,1,0:T(8,128)(2,1)} fusion(bf16[3,768,512]{2,1,0:T(8,128)(2,1)S(1)} %copy-done.23, bf16[3,768,768]{2,1,0:T(8,128)(2,1)} %get-tuple-element.863, f32[1,768,512]{2,1,0:T(8,128)S(1)} %bitcast.187, f32[1,768,512]{2,1,0:T(8,128)S(1)} %bitcast.186, f32[1,768,512]{2,1,0:T(8,128)S(1)} %bitcast.185, ...), kind=kOutput, calls=%fused_computation.3 | convolution fusion | flops 1829634048 | bytes 15335424 | tf_op jit(solution)/shard_map/gij,gid->gjd/dot_general | solution.py:1483
  567.1 8.6 %collective-permute-done.67.over_y = bf16[912,512]{1,0:T(8,128)(2,1)S(1)} collective-permute-done((bf16[912,512]{1,0:T(8,128)(2,1)S(1)}, bf16[912,512]{1,0:T(8,128)(2,1)S(1)}, u32[]{:S(2)}, u32[]{:S(2)}) %collective-permute-start.67) | collective-permute-done | bytes 933920 | tf_op jit(solution)/shard_map/ppermute | solution.py:93
  579.7 5.6 give_out.1
  (276 shorter events, 107.8 us)
Async XLA Ops:
  8.7 43.5 %collective-permute-start = (bf16[1792,512]{1,0:T(8,128)(2,1)}, bf16[1792,512]{1,0:T(8,128)(2,1)}, u32[]{:S(2)}, u32[]{:S(2)}) collective-permute-start(bf16[1792,512]{1,0:T(8,128)(2,1)} %own_half.1.refs_0_), channel_id=1, source_target_pairs={{0,8},{8,16},{16,24},{24,28},{28,20},{20,12},{12,4},{4,0},{1,9},{9... | collective-permute-start | bytes 5505032 | tf_op jit(solution)/shard_map/ppermute | solution.py:1161
  11.8 41.7 %collective-permute-start.1 = (bf16[1792,512]{1,0:T(8,128)(2,1)}, bf16[1792,512]{1,0:T(8,128)(2,1)}, u32[]{:S(2)}, u32[]{:S(2)}) collective-permute-start(bf16[1792,512]{1,0:T(8,128)(2,1)} %own_half.1.refs_0_), channel_id=1, source_target_pairs={{8,0},{16,8},{24,16},{28,24},{20,28},{12,20},{4,12},{0,4},{9,1},{1... | collective-permute-start | bytes 5505032 | tf_op jit(solution)/shard_map/ppermute | solution.py:1164
  11.8 40.4 %collective-permute-start.2 = (bf16[768,512]{1,0:T(8,128)(2,1)}, bf16[768,512]{1,0:T(8,128)(2,1)}, u32[]{:S(2)}, u32[]{:S(2)}) collective-permute-start(bf16[768,512]{1,0:T(8,128)(2,1)} %get-tuple-element.448), channel_id=1, source_target_pairs={{0,2},{2,0},{1,3},{3,1},{4,6},{6,4},{5,7},{7,5},{8,10},{10,8},{9,1... | collective-permute-start | bytes 2359304 | tf_op jit(solution)/shard_map/ppermute | solution.py:93
  13.8 38.4 %collective-permute-start.4 = (f32[3,512]{1,0:T(4,128)S(1)}, f32[3,512]{1,0:T(4,128)}, u32[]{:S(2)}, u32[]{:S(2)}) collective-permute-start(f32[3,512]{1,0:T(4,128)S(1)} %dynamic_update_slice.5), channel_id=1, source_target_pairs={{0,4},{4,0},{8,12},{12,8},{16,20},{20,16},{24,28},{28,24},{1,5},{5... | collective-permute-start | bytes 18440 | tf_op jit(solution)/shard_map/ppermute | solution.py:1126
  53.5 40.8 %collective-permute-start.5 = (bf16[1792,512]{1,0:T(8,128)(2,1)}, bf16[1792,512]{1,0:T(8,128)(2,1)}, u32[]{:S(2)}, u32[]{:S(2)}) collective-permute-start(bf16[1792,512]{1,0:T(8,128)(2,1)} %collective-permute-done.refs_2_), channel_id=1, source_target_pairs={{0,8},{8,16},{16,24},{24,28},{28,20},{20,12},{12,4},{4,0},{1,9},{9... | collective-permute-start | bytes 5505032 | tf_op jit(solution)/shard_map/ppermute | solution.py:1161
  55.1 40.5 %collective-permute-start.6 = (bf16[1792,512]{1,0:T(8,128)(2,1)}, bf16[1792,512]{1,0:T(8,128)(2,1)}, u32[]{:S(2)}, u32[]{:S(2)}) collective-permute-start(bf16[1792,512]{1,0:T(8,128)(2,1)} %collective-permute-done.1.refs_3_), channel_id=1, source_target_pairs={{8,0},{16,8},{24,16},{28,24},{20,28},{12,20},{4,12},{0,4},{9,1},{1... | collective-permute-start | bytes 5505032 | tf_op jit(solution)/shard_map/ppermute | solution.py:1164
  55.5 40.1 %collective-permute-start.7 = (bf16[1792,512]{1,0:T(8,128)(2,1)}, bf16[1792,512]{1,0:T(8,128)(2,1)}, u32[]{:S(2)}, u32[]{:S(2)}) collective-permute-start(bf16[1792,512]{1,0:T(8,128)(2,1)} %collective-permute-done.refs_2_), channel_id=1, source_target_pairs={{0,1},{1,0},{2,3},{3,2},{4,5},{5,4},{6,7},{7,6},{8,9},{9,8},{10,11... | collective-permute-start | bytes 5505032 | tf_op jit(solution)/shard_map/ppermute | solution.py:89
  55.5 40.1 %collective-permute-start.8 = (bf16[1792,512]{1,0:T(8,128)(2,1)}, bf16[1792,512]{1,0:T(8,128)(2,1)}, u32[]{:S(2)}, u32[]{:S(2)}) collective-permute-start(bf16[1792,512]{1,0:T(8,128)(2,1)} %collective-permute-done.1.refs_3_), channel_id=1, source_target_pairs={{0,1},{1,0},{2,3},{3,2},{4,5},{5,4},{6,7},{7,6},{8,9},{9,8},{10,11... | collective-permute-start | bytes 5505032 | tf_op jit(solution)/shard_map/ppermute | solution.py:89
  56.0 22.5 %collective-permute-start.9 = (bf16[768,512]{1,0:T(8,128)(2,1)}, bf16[768,512]{1,0:T(8,128)(2,1)}, u32[]{:S(2)}, u32[]{:S(2)}) collective-permute-start(bf16[768,512]{1,0:T(8,128)(2,1)} %get-tuple-element.468), channel_id=1, source_target_pairs={{0,2},{2,0},{1,3},{3,1},{4,6},{6,4},{5,7},{7,5},{8,10},{10,8},{9,1... | collective-permute-start | bytes 2359304 | tf_op jit(solution)/shard_map/ppermute | solution.py:93
  95.6 39.6 %collective-permute-start.10 = (bf16[1792,512]{1,0:T(8,128)(2,1)}, bf16[1792,512]{1,0:T(8,128)(2,1)}, u32[]{:S(2)}, u32[]{:S(2)}) collective-permute-start(bf16[1792,512]{1,0:T(8,128)(2,1)} %collective-permute-done.5.refs_6_), channel_id=1, source_target_pairs={{0,8},{8,16},{16,24},{24,28},{28,20},{20,12},{12,4},{4,0},{1,9},{9... | collective-permute-start | bytes 5505032 | tf_op jit(solution)/shard_map/ppermute | solution.py:1161
  97.3 39.6 %collective-permute-start.11 = (bf16[1792,512]{1,0:T(8,128)(2,1)}, bf16[1792,512]{1,0:T(8,128)(2,1)}, u32[]{:S(2)}, u32[]{:S(2)}) collective-permute-start(bf16[1792,512]{1,0:T(8,128)(2,1)} %collective-permute-done.6.refs_7_), channel_id=1, source_target_pairs={{8,0},{16,8},{24,16},{28,24},{20,28},{12,20},{4,12},{0,4},{9,1},{1... | collective-permute-start | bytes 5505032 | tf_op jit(solution)/shard_map/ppermute | solution.py:1164
  97.8 39.0 %collective-permute-start.12 = (bf16[1792,512]{1,0:T(8,128)(2,1)}, bf16[1792,512]{1,0:T(8,128)(2,1)}, u32[]{:S(2)}, u32[]{:S(2)}) collective-permute-start(bf16[1792,512]{1,0:T(8,128)(2,1)} %collective-permute-done.5.refs_6_), channel_id=1, source_target_pairs={{0,1},{1,0},{2,3},{3,2},{4,5},{5,4},{6,7},{7,6},{8,9},{9,8},{10,11... | collective-permute-start | bytes 5505032 | tf_op jit(solution)/shard_map/ppermute | solution.py:89
  97.8 39.0 %collective-permute-start.13 = (bf16[1792,512]{1,0:T(8,128)(2,1)}, bf16[1792,512]{1,0:T(8,128)(2,1)}, u32[]{:S(2)}, u32[]{:S(2)}) collective-permute-start(bf16[1792,512]{1,0:T(8,128)(2,1)} %collective-permute-done.6.refs_7_), channel_id=1, source_target_pairs={{0,1},{1,0},{2,3},{3,2},{4,5},{5,4},{6,7},{7,6},{8,9},{9,8},{10,11... | collective-permute-start | bytes 5505032 | tf_op jit(solution)/shard_map/ppermute | solution.py:89
  98.4 19.7 %collective-permute-start.14 = (bf16[768,512]{1,0:T(8,128)(2,1)}, bf16[768,512]{1,0:T(8,128)(2,1)S(1)}, u32[]{:S(2)}, u32[]{:S(2)}) collective-permute-start(bf16[768,512]{1,0:T(8,128)(2,1)} %get-tuple-element.482), channel_id=1, source_target_pairs={{0,2},{2,0},{1,3},{3,1},{4,6},{6,4},{5,7},{7,5},{8,10},{10,8},{9,1... | collective-permute-start | bytes 2359304 | tf_op jit(solution)/shard_map/ppermute | solution.py:93
  165.1 21.0 %collective-permute-start.23 = (bf16[448,512]{1,0:T(8,128)(2,1)}, bf16[448,512]{1,0:T(8,128)(2,1)}, u32[]{:S(2)}, u32[]{:S(2)}) collective-permute-start(bf16[448,512]{1,0:T(8,128)(2,1)} %get-tuple-element.521), channel_id=1, source_target_pairs={{0,8},{8,16},{16,24},{24,28},{28,20},{20,12},{12,4},{4,0},{1,9},{9... | collective-permute-start | bytes 1376264 | tf_op jit(solution)/shard_map/ppermute | solution.py:1161
  165.5 20.6 %collective-permute-start.24 = (bf16[448,512]{1,0:T(8,128)(2,1)}, bf16[448,512]{1,0:T(8,128)(2,1)}, u32[]{:S(2)}, u32[]{:S(2)}) collective-permute-start(bf16[448,512]{1,0:T(8,128)(2,1)} %get-tuple-element.522), channel_id=1, source_target_pairs={{8,0},{16,8},{24,16},{28,24},{20,28},{12,20},{4,12},{0,4},{9,1},{1... | collective-permute-start | bytes 1376264 | tf_op jit(solution)/shard_map/ppermute | solution.py:1164
  200.5 20.6 %collective-permute-start.27 = (bf16[768,512]{1,0:T(8,128)(2,1)}, bf16[768,512]{1,0:T(8,128)(2,1)}, u32[]{:S(2)}, u32[]{:S(2)}) collective-permute-start(bf16[768,512]{1,0:T(8,128)(2,1)} %bitcast.183), channel_id=1, source_target_pairs={{0,2},{2,0},{1,3},{3,1},{4,6},{6,4},{5,7},{7,5},{8,10},{10,8},{9,1... | collective-permute-start | bytes 2359304 | tf_op jit(solution)/shard_map/ppermute | solution.py:93
  221.0 23.5 %collective-permute-start.28 = (bf16[768,512]{1,0:T(8,128)(2,1)}, bf16[768,512]{1,0:T(8,128)(2,1)}, u32[]{:S(2)}, u32[]{:S(2)}) collective-permute-start(bf16[768,512]{1,0:T(8,128)(2,1)} %bitcast.182), channel_id=1, source_target_pairs={{0,2},{2,0},{1,3},{3,1},{4,6},{6,4},{5,7},{7,5},{8,10},{10,8},{9,1... | collective-permute-start | bytes 2359304 | tf_op jit(solution)/shard_map/ppermute | solution.py:93
  244.5 22.2 %collective-permute-start.29 = (bf16[768,512]{1,0:T(8,128)(2,1)}, bf16[768,512]{1,0:T(8,128)(2,1)}, u32[]{:S(2)}, u32[]{:S(2)}) collective-permute-start(bf16[768,512]{1,0:T(8,128)(2,1)} %bitcast.181), channel_id=1, source_target_pairs={{0,2},{2,0},{1,3},{3,1},{4,6},{6,4},{5,7},{7,5},{8,10},{10,8},{9,1... | collective-permute-start | bytes 2359304 | tf_op jit(solution)/shard_map/ppermute | solution.py:93
  266.8 23.6 %collective-permute-start.30 = (bf16[768,512]{1,0:T(8,128)(2,1)}, bf16[768,512]{1,0:T(8,128)(2,1)}, u32[]{:S(2)}, u32[]{:S(2)}) collective-permute-start(bf16[768,512]{1,0:T(8,128)(2,1)} %get-tuple-element.645), channel_id=1, source_target_pairs={{0,2},{2,0},{1,3},{3,1},{4,6},{6,4},{5,7},{7,5},{8,10},{10,8},{9,1... | collective-permute-start | bytes 2359304 | tf_op jit(solution)/shard_map/ppermute | solution.py:93
  290.3 39.2 %collective-permute-start.31 = (bf16[768,512]{1,0:T(8,128)(2,1)}, bf16[768,512]{1,0:T(8,128)(2,1)}, u32[]{:S(2)}, u32[]{:S(2)}) collective-permute-start(bf16[768,512]{1,0:T(8,128)(2,1)} %get-tuple-element.684), channel_id=1, source_target_pairs={{0,2},{2,0},{1,3},{3,1},{4,6},{6,4},{5,7},{7,5},{8,10},{10,8},{9,1... | collective-permute-start | bytes 2359304 | tf_op jit(solution)/shard_map/ppermute | solution.py:93
  290.6 38.9 %collective-permute-start.32 = (bf16[768,512]{1,0:T(8,128)(2,1)}, bf16[768,512]{1,0:T(8,128)(2,1)}, u32[]{:S(2)}, u32[]{:S(2)}) collective-permute-start(bf16[768,512]{1,0:T(8,128)(2,1)} %get-tuple-element.685), channel_id=1, source_target_pairs={{0,2},{2,0},{1,3},{3,1},{4,6},{6,4},{5,7},{7,5},{8,10},{10,8},{9,1... | collective-permute-start | bytes 2359304 | tf_op jit(solution)/shard_map/ppermute | solution.py:93
  381.0 22.4 %collective-permute-start.41 = (bf16[256,512]{1,0:T(8,128)(2,1)}, bf16[256,512]{1,0:T(8,128)(2,1)}, u32[]{:S(2)}, u32[]{:S(2)}) collective-permute-start(bf16[256,512]{1,0:T(8,128)(2,1)} %get-tuple-element.781), channel_id=1, source_target_pairs={{0,8},{8,16},{16,24},{24,28},{28,20},{20,12},{12,4},{4,0},{1,9},{9... | collective-permute-start | bytes 786440 | tf_op jit(solution)/shard_map/ppermute | solution.py:1161
  382.2 21.3 %collective-permute-start.42 = (bf16[256,512]{1,0:T(8,128)(2,1)}, bf16[256,512]{1,0:T(8,128)(2,1)}, u32[]{:S(2)}, u32[]{:S(2)}) collective-permute-start(bf16[256,512]{1,0:T(8,128)(2,1)} %get-tuple-element.782), channel_id=1, source_target_pairs={{8,0},{16,8},{24,16},{28,24},{20,28},{12,20},{4,12},{0,4},{9,1},{1... | collective-permute-start | bytes 786440 | tf_op jit(solution)/shard_map/ppermute | solution.py:1164
  383.0 20.4 %collective-permute-start.39 = (bf16[384,512]{1,0:T(8,128)(2,1)}, bf16[384,512]{1,0:T(8,128)(2,1)}, u32[]{:S(2)}, u32[]{:S(2)}) collective-permute-start(bf16[384,512]{1,0:T(8,128)(2,1)} %get-tuple-element.779), channel_id=1, source_target_pairs={{0,8},{8,16},{16,24},{24,28},{28,20},{20,12},{12,4},{4,0},{1,9},{9... | collective-permute-start | bytes 1179656 | tf_op jit(solution)/shard_map/ppermute | solution.py:1161
  384.2 19.3 %collective-permute-start.40 = (bf16[384,512]{1,0:T(8,128)(2,1)S(1)}, bf16[384,512]{1,0:T(8,128)(2,1)}, u32[]{:S(2)}, u32[]{:S(2)}) collective-permute-start(bf16[384,512]{1,0:T(8,128)(2,1)S(1)} %get-tuple-element.780), channel_id=1, source_target_pairs={{8,0},{16,8},{24,16},{28,24},{20,28},{12,20},{4,12},{0,4},{9,1},{1... | collective-permute-start | bytes 1179656 | tf_op jit(solution)/shard_map/ppermute | solution.py:1164
  410.0 23.8 %collective-permute-start.47 = (bf16[8,912,512]{2,1,0:T(8,128)(2,1)}, bf16[8,912,512]{2,1,0:T(8,128)(2,1)}, u32[]{:S(2)}, u32[]{:S(2)}) collective-permute-start(bf16[8,912,512]{2,1,0:T(8,128)(2,1)} %get-tuple-element.803), channel_id=1, source_target_pairs={{0,1},{1,0},{2,3},{3,2},{4,5},{5,4},{6,7},{7,6},{8,9},{9,8},{10,11... | collective-permute-start | bytes 22413320 | tf_op jit(solution)/shard_map/ppermute | solution.py:89
  410.0 19.1 %collective-permute-start.43 = (bf16[384,512]{1,0:T(8,128)(2,1)}, bf16[384,512]{1,0:T(8,128)(2,1)}, u32[]{:S(2)}, u32[]{:S(2)}) collective-permute-start(bf16[384,512]{1,0:T(8,128)(2,1)} %get-tuple-element.799), channel_id=1, source_target_pairs={{0,8},{8,16},{16,24},{24,28},{28,20},{20,12},{12,4},{4,0},{1,9},{9... | collective-permute-start | bytes 1179656 | tf_op jit(solution)/shard_map/ppermute | solution.py:1161
  411.2 17.9 %collective-permute-start.44 = (bf16[384,512]{1,0:T(8,128)(2,1)S(1)}, bf16[384,512]{1,0:T(8,128)(2,1)}, u32[]{:S(2)}, u32[]{:S(2)}) collective-permute-start(bf16[384,512]{1,0:T(8,128)(2,1)S(1)} %get-tuple-element.800), channel_id=1, source_target_pairs={{8,0},{16,8},{24,16},{28,24},{20,28},{12,20},{4,12},{0,4},{9,1},{1... | collective-permute-start | bytes 1179656 | tf_op jit(solution)/shard_map/ppermute | solution.py:1164
  412.0 21.1 %collective-permute-start.45 = (bf16[512,512]{1,0:T(8,128)(2,1)}, bf16[512,512]{1,0:T(8,128)(2,1)}, u32[]{:S(2)}, u32[]{:S(2)}) collective-permute-start(bf16[512,512]{1,0:T(8,128)(2,1)} %pad_maximum_fusion.6), channel_id=1, source_target_pairs={{0,8},{8,16},{16,24},{24,28},{28,20},{20,12},{12,4},{4,0},{1,9},{9... | collective-permute-start | bytes 1572872 | tf_op jit(solution)/shard_map/ppermute | solution.py:1161
  413.2 20.6 %collective-permute-start.46 = (bf16[512,512]{1,0:T(8,128)(2,1)}, bf16[512,512]{1,0:T(8,128)(2,1)}, u32[]{:S(2)}, u32[]{:S(2)}) collective-permute-start(bf16[512,512]{1,0:T(8,128)(2,1)} %pad_maximum_fusion.7), channel_id=1, source_target_pairs={{8,0},{16,8},{24,16},{28,24},{20,28},{12,20},{4,12},{0,4},{9,1},{1... | collective-permute-start | bytes 1572872 | tf_op jit(solution)/shard_map/ppermute | solution.py:1164
  439.7 26.7 %collective-permute-start.52 = (bf16[1,768,512]{2,1,0:T(8,128)(2,1)S(1)}, bf16[1,768,512]{2,1,0:T(8,128)(2,1)S(1)}, u32[]{:S(2)}, u32[]{:S(2)}) collective-permute-start(bf16[1,768,512]{2,1,0:T(8,128)(2,1)S(1)} %copy-done.27), channel_id=1, source_target_pairs={{0,2},{2,0},{1,3},{3,1},{4,6},{6,4},{5,7},{7,5},{8,10},{10,8},{9,1... | collective-permute-start | bytes 2359304 | tf_op jit(solution)/shard_map/ppermute | solution.py:93
  442.2 24.1 %collective-permute-start.48 = (bf16[512,512]{1,0:T(8,128)(2,1)S(1)}, bf16[512,512]{1,0:T(8,128)(2,1)S(1)}, u32[]{:S(2)}, u32[]{:S(2)}) collective-permute-start(bf16[512,512]{1,0:T(8,128)(2,1)S(1)} %get-tuple-element.815), channel_id=1, source_target_pairs={{0,8},{8,16},{16,24},{24,28},{28,20},{20,12},{12,4},{4,0},{1,9},{9... | collective-permute-start | bytes 1572872 | tf_op jit(solution)/shard_map/ppermute | solution.py:1161
  443.6 22.7 %collective-permute-start.49 = (bf16[512,512]{1,0:T(8,128)(2,1)S(1)}, bf16[512,512]{1,0:T(8,128)(2,1)S(1)}, u32[]{:S(2)}, u32[]{:S(2)}) collective-permute-start(bf16[512,512]{1,0:T(8,128)(2,1)S(1)} %get-tuple-element.816), channel_id=1, source_target_pairs={{8,0},{16,8},{24,16},{28,24},{20,28},{12,20},{4,12},{0,4},{9,1},{1... | collective-permute-start | bytes 1572872 | tf_op jit(solution)/shard_map/ppermute | solution.py:1164
  444.3 20.9 %collective-permute-start.50 = (bf16[456,512]{1,0:T(8,128)(2,1)S(1)}, bf16[456,512]{1,0:T(8,128)(2,1)S(1)}, u32[]{:S(2)}, u32[]{:S(2)}) collective-permute-start(bf16[456,512]{1,0:T(8,128)(2,1)S(1)} %get-tuple-element.817), channel_id=1, source_target_pairs={{0,8},{8,16},{16,24},{24,28},{28,20},{20,12},{12,4},{4,0},{1,9},{9... | collective-permute-start | bytes 1400840 | tf_op jit(solution)/shard_map/ppermute | solution.py:1161
  445.7 20.7 %collective-permute-start.51 = (bf16[456,512]{1,0:T(8,128)(2,1)S(1)}, bf16[456,512]{1,0:T(8,128)(2,1)S(1)}, u32[]{:S(2)}, u32[]{:S(2)}) collective-permute-start(bf16[456,512]{1,0:T(8,128)(2,1)S(1)} %get-tuple-element.818), channel_id=1, source_target_pairs={{8,0},{16,8},{24,16},{28,24},{20,28},{12,20},{4,12},{0,4},{9,1},{1... | collective-permute-start | bytes 1400840 | tf_op jit(solution)/shard_map/ppermute | solution.py:1164
  469.6 34.4 %collective-permute-start.57 = (bf16[2,768,512]{2,1,0:T(8,128)(2,1)S(1)}, bf16[2,768,512]{2,1,0:T(8,128)(2,1)}, u32[]{:S(2)}, u32[]{:S(2)}) collective-permute-start(bf16[2,768,512]{2,1,0:T(8,128)(2,1)S(1)} %copy-done.24), channel_id=1, source_target_pairs={{0,2},{2,0},{1,3},{3,1},{4,6},{6,4},{5,7},{7,5},{8,10},{10,8},{9,1... | collective-permute-start | bytes 4718600 | tf_op jit(solution)/shard_map/ppermute | solution.py:93
  470.0 32.6 %collective-permute-start.55 = (bf16[912,512]{1,0:T(8,128)(2,1)S(1)}, bf16[912,512]{1,0:T(8,128)(2,1)S(1)}, u32[]{:S(2)}, u32[]{:S(2)}) collective-permute-start(bf16[912,512]{1,0:T(8,128)(2,1)S(1)} %pad_maximum_fusion.4), channel_id=1, source_target_pairs={{0,8},{8,16},{16,24},{24,28},{28,20},{20,12},{12,4},{4,0},{1,9},{9... | collective-permute-start | bytes 2801672 | tf_op jit(solution)/shard_map/ppermute | solution.py:1161
  470.8 31.8 %collective-permute-start.56 = (bf16[912,512]{1,0:T(8,128)(2,1)S(1)}, bf16[912,512]{1,0:T(8,128)(2,1)S(1)}, u32[]{:S(2)}, u32[]{:S(2)}) collective-permute-start(bf16[912,512]{1,0:T(8,128)(2,1)S(1)} %pad_maximum_fusion.5), channel_id=1, source_target_pairs={{8,0},{16,8},{24,16},{28,24},{20,28},{12,20},{4,12},{0,4},{9,1},{1... | collective-permute-start | bytes 2801672 | tf_op jit(solution)/shard_map/ppermute | solution.py:1164
  472.0 29.7 %collective-permute-start.53 = (bf16[512,512]{1,0:T(8,128)(2,1)S(1)}, bf16[512,512]{1,0:T(8,128)(2,1)S(1)}, u32[]{:S(2)}, u32[]{:S(2)}) collective-permute-start(bf16[512,512]{1,0:T(8,128)(2,1)S(1)} %get-tuple-element.825), channel_id=1, source_target_pairs={{0,8},{8,16},{16,24},{24,28},{28,20},{20,12},{12,4},{4,0},{1,9},{9... | collective-permute-start | bytes 1572872 | tf_op jit(solution)/shard_map/ppermute | solution.py:1161
  472.8 29.8 %collective-permute-start.54 = (bf16[512,512]{1,0:T(8,128)(2,1)S(1)}, bf16[512,512]{1,0:T(8,128)(2,1)S(1)}, u32[]{:S(2)}, u32[]{:S(2)}) collective-permute-start(bf16[512,512]{1,0:T(8,128)(2,1)S(1)} %get-tuple-element.826), channel_id=1, source_target_pairs={{8,0},{16,8},{24,16},{28,24},{20,28},{12,20},{4,12},{0,4},{9,1},{1... | collective-permute-start | bytes 1572872 | tf_op jit(solution)/shard_map/ppermute | solution.py:1164
  507.6 20.8 %collective-permute-start.58 = (bf16[912,512]{1,0:T(8,128)(2,1)S(1)}, bf16[912,512]{1,0:T(8,128)(2,1)S(1)}, u32[]{:S(2)}, u32[]{:S(2)}) collective-permute-start(bf16[912,512]{1,0:T(8,128)(2,1)S(1)} %get-tuple-element.836), channel_id=1, source_target_pairs={{0,8},{8,16},{16,24},{24,28},{28,20},{20,12},{12,4},{4,0},{1,9},{9... | collective-permute-start | bytes 2801672 | tf_op jit(solution)/shard_map/ppermute | solution.py:1161
  508.8 20.4 %collective-permute-start.59 = (bf16[912,512]{1,0:T(8,128)(2,1)S(1)}, bf16[912,512]{1,0:T(8,128)(2,1)S(1)}, u32[]{:S(2)}, u32[]{:S(2)}) collective-permute-start(bf16[912,512]{1,0:T(8,128)(2,1)S(1)} %get-tuple-element.837), channel_id=1, source_target_pairs={{8,0},{16,8},{24,16},{28,24},{20,28},{12,20},{4,12},{0,4},{9,1},{1... | collective-permute-start | bytes 2801672 | tf_op jit(solution)/shard_map/ppermute | solution.py:1164
  509.7 18.7 %collective-permute-start.61 = (bf16[512,512]{1,0:T(8,128)(2,1)S(1)}, bf16[512,512]{1,0:T(8,128)(2,1)S(1)}, u32[]{:S(2)}, u32[]{:S(2)}) collective-permute-start(bf16[512,512]{1,0:T(8,128)(2,1)S(1)} %fusion.14), channel_id=1, source_target_pairs={{0,2},{2,0},{1,3},{3,1},{4,6},{6,4},{5,7},{7,5},{8,10},{10,8},{9,1... | collective-permute-start | bytes 1572872 | tf_op jit(solution)/shard_map/ppermute | solution.py:93
  510.3 18.1 %collective-permute-start.62 = (bf16[512,512]{1,0:T(8,128)(2,1)S(1)}, bf16[512,512]{1,0:T(8,128)(2,1)S(1)}, u32[]{:S(2)}, u32[]{:S(2)}) collective-permute-start(bf16[512,512]{1,0:T(8,128)(2,1)S(1)} %fusion.14), channel_id=1, source_target_pairs={{0,1},{1,0},{2,3},{3,2},{4,5},{5,4},{6,7},{7,6},{8,9},{9,8},{10,11... | collective-permute-start | bytes 1572872 | tf_op jit(solution)/shard_map/ppermute | solution.py:89
  510.3 18.1 %collective-permute-start.60 = (bf16[384,512]{1,0:T(8,128)(2,1)S(1)}, bf16[384,512]{1,0:T(8,128)(2,1)S(1)}, u32[]{:S(2)}, u32[]{:S(2)}) collective-permute-start(bf16[384,512]{1,0:T(8,128)(2,1)S(1)} %fusion.24), channel_id=1, source_target_pairs={{0,2},{2,0},{1,3},{3,1},{4,6},{6,4},{5,7},{7,5},{8,10},{10,8},{9,1... | collective-permute-start | bytes 1179656 | tf_op jit(solution)/shard_map/ppermute | solution.py:93
  531.5 18.3 %collective-permute-start.63 = (bf16[912,512]{1,0:T(8,128)(2,1)S(1)}, bf16[912,512]{1,0:T(8,128)(2,1)}, u32[]{:S(2)}, u32[]{:S(2)}) collective-permute-start(bf16[912,512]{1,0:T(8,128)(2,1)S(1)} %get-tuple-element.845), channel_id=1, source_target_pairs={{0,8},{8,16},{16,24},{24,28},{28,20},{20,12},{12,4},{4,0},{1,9},{9... | collective-permute-start | bytes 2801672 | tf_op jit(solution)/shard_map/ppermute | solution.py:1161
  533.0 18.5 %collective-permute-start.64 = (bf16[912,512]{1,0:T(8,128)(2,1)S(1)}, bf16[912,512]{1,0:T(8,128)(2,1)}, u32[]{:S(2)}, u32[]{:S(2)}) collective-permute-start(bf16[912,512]{1,0:T(8,128)(2,1)S(1)} %get-tuple-element.846), channel_id=1, source_target_pairs={{8,0},{16,8},{24,16},{28,24},{20,28},{12,20},{4,12},{0,4},{9,1},{1... | collective-permute-start | bytes 2801672 | tf_op jit(solution)/shard_map/ppermute | solution.py:1164
  (55 other events, 409.9 us)

commit v5 on v4

--- a/solution.py
+++ b/solution.py
@@ -341,10 +341,13 @@
     )(kinds, step, x)
 
 
-def tap_rows(x, age, k):
-    if k == 0:
-        return x
-    return jnp.where(age >= k, pltpu.roll(x, k, 0), 0.0)
+def all_taps(x, age, taps):
+    rolled = [x] + [pltpu.roll(x, k, 0) for k in range(1, min(8, taps))]
+    for k in range(taps):
+        v = rolled[k % 8]
+        if k >= 8:
+            v = jnp.concatenate([jnp.zeros_like(v[: k - k % 8]), v[: v.shape[0] - (k - k % 8)]])
+        yield k, jnp.where(age >= k, v, 0.0) if k else v
 
 
 def step_rows(own, other, s, npos):
@@ -397,9 +400,9 @@
                     age = jnp.where(inside, row - lo + (i - firsts[i]) * taps, age)
             age_ref[:m] = age
             e = jnp.zeros((m, width), F32)
-            for k in range(taps):
+            for k, x in all_taps(low, age, taps):
                 at = base + (taps - 1 - k) * width
-                x = tap_rows(low, age, k).astype(BF)
+                x = x.astype(BF)
                 taps_ref[k, :m, :] = x
                 if m < most:
                     taps_ref[k, m:, :] = jnp.zeros((most - m, width), BF)
@@ -621,12 +624,12 @@
 
 
 class Outlet:
-    def __init__(self, n, rows, width, cuts):
+    def __init__(self, n, rows, width):
         self.n, self.rows, self.width = n, rows, width
-        self.bounds = [(0, n)] if cuts is None else cuts
+        self.bounds = [(0, 1)] + [(i, i + 2) for i in range(1, n - 1, 2)] + [(n - 1, n)]
 
     def shapes(self):
-        sizes = [self.n] + [hi - lo for lo, hi in self.bounds]
+        sizes = [hi - lo for lo, hi in self.bounds] + [self.n]
         return [jax.ShapeDtypeStruct((c, self.rows, self.width), BF) for c in sizes]
 
     def scratch(self):
@@ -636,10 +639,12 @@
         ]
 
     def copies(self, held_ref, outs, sems):
-        found = [pltpu.make_async_copy(held_ref.at[0], outs[0], sems.at[0])]
+        found = []
         for i, (lo, hi) in enumerate(self.bounds):
-            source = held_ref.at[1, pl.ds(lo, hi - lo)]
-            found.append(pltpu.make_async_copy(source, outs[1 + i], sems.at[1 + i]))
+            source = held_ref.at[0, pl.ds(lo, hi - lo)]
+            found.append(pltpu.make_async_copy(source, outs[i], sems.at[i]))
+        last = len(self.bounds)
+        found.append(pltpu.make_async_copy(held_ref.at[1], outs[last], sems.at[last]))
         return found
 
     def flush(self, held_ref, outs, sems):
@@ -711,12 +716,17 @@
             age = age_ref[:m]
             total = joint
             fetch.wait()
-            for k in range(taps):
-                tap = taps - 1 - k
-                back = dot_t(iso_pre, whole[tap * width : (tap + 1) * width])
-                if k:
-                    back = pltpu.roll(jnp.where(age >= k, back, 0.0), m - k, 0)
-                total += back
+            for r in range(min(8, taps)):
+                both = None
+                for k in range(r, taps, 8):
+                    tap = taps - 1 - k
+                    back = dot_t(iso_pre, whole[tap * width : (tap + 1) * width])
+                    if k:
+                        back = jnp.where(age >= k, back, 0.0)
+                    if k >= 8:
+                        back = jnp.concatenate([back[k - r :], jnp.zeros_like(back[: k - r])])
+                    both = back if both is None else both + back
+                total += pltpu.roll(both, m - r, 0) if r else both
             pre_ref[:m] = (total * (1.0 - shrunk * shrunk)).astype(BF)
 
         by_branch(where, body)
@@ -845,6 +855,66 @@
         ),
         name="season_backward",
     )(where, order, pre, sum_own, sum_other, whole)
+
+
+def ring_add(jobs):
+    specs, arrays, shapes = [], [], []
+    for first, rows, terms in jobs:
+        width = terms[0][0].shape[-1]
+        shapes.append(jax.ShapeDtypeStruct((rows, width), BF))
+        for array, place, _ in terms:
+            arrays.append(array)
+            if place is None:
+                specs.append(vmem_spec())
+            else:
+                index = functools.partial(lambda p, q, g: (p, q, 0), place, first // rows)
+                specs.append(pl.BlockSpec((1, rows, width), index))
+
+    def kernel(*refs):
+        ins, outs = list(refs[: len(arrays)]), refs[len(arrays) :]
+        for (first, rows, terms), out in zip(jobs, outs):
+            mine = [ins.pop(0) for _ in terms]
+            for r in range(0, rows, 16):
+                total = None
+                for (array, place, at), ref in zip(terms, mine):
+                    count = rows if place is not None else array.shape[0]
+                    if not at <= r < at + count:
+                        continue
+                    v = ref[0, r : r + 16, :] if place is not None else ref[r - at : r - at + 16, :]
+                    v = v.astype(F32)
+                    total = v if total is None else total + v
+                out[r : r + 16, :] = total.astype(BF)
+
+    moved = sum(2 * s.shape[0] * s.shape[1] for s in shapes) * 4
+    return pl.pallas_call(
+        kernel,
+        grid=(1,),
+        out_shape=shapes,
+        in_specs=specs,
+        out_specs=[vmem_spec()] * len(shapes),
+        compiler_params=pltpu.CompilerParams(vmem_limit_bytes=VMEM),
+        cost_estimate=cost(0, moved),
+        name="ring_add",
+    )(*arrays)
+
+
+def plain_add(jobs):
+    found = []
+    for first, rows, terms in jobs:
+        total, late = None, None
+        for array, place, at in terms:
+            v = array if place is None else array[place, first : first + rows]
+            v = v.astype(F32)
+            if v.shape[0] < rows:
+                late = (v, at)
+            else:
+                total = v if total is None else total + v
+        if late is not None:
+            v, at = late
+            lo, hi = total[:at], total[at + v.shape[0] :]
+            total = jnp.concatenate([lo, total[at : at + v.shape[0]] + v, hi])
+        found.append(total.astype(BF))
+    return found
 
 
 def give_out(lay, member_ids, mine, over_y, sibling, sibling_over_y):
@@ -1340,9 +1410,9 @@
     for place, offset in enumerate(ring_order):
         spot = jnp.where(jnp.arange(n) == ring.index(offset), place, spot)
 
-    f_outlet = Outlet(n, lay.f_half, width, None)
-    g_outlet = Outlet(n, lay.g_half, width, None)
-    s_outlet = Outlet(n, lay.si_half + 16, width, None)
+    f_outlet = Outlet(n, lay.f_half, width)
+    g_outlet = Outlet(n, lay.g_half, width)
+    s_outlet = Outlet(n, lay.si_half + 32, width)
 
     def run_dense_weights(*arrays):
         mine, got, flat = arrays[:groups], arrays[groups : 2 * groups], arrays[2 * groups :]
@@ -1352,39 +1422,31 @@
         )
 
     class Chain:
-        def __init__(self, keep):
-            self.keep = keep
-            self.got = []
+        def __init__(self, keep, got, halved=True):
+            self.keep, self.got, self.halved = keep, got, halved
             self.step = last
             self.r = self.l = None
-            self.half = keep.shape[1] // 2
-
-        def here(self, place):
-            first = 0
-            for v in self.got:
-                if place < first + v.shape[0]:
-                    got = v[place - first]
-                    break
-                first += v.shape[0]
-            return self.keep[place].astype(F32) + got.astype(F32)
-
-        def sends(self):
-            k = self.step
+            self.half = got.shape[1] // 2
+
+        def here(self, place, first=0, rows=None):
+            array, i = (place + 1) // 2, 0 if place == 0 else (place - 1) % 2
+            rows = self.got.shape[1] if rows is None else rows
+            return (first, rows, [(self.keep[array], i, 0), (self.got, place, 0)])
+
+        def jobs(self):
+            k, h = self.step, self.half
+            if k == 0:
+                job = self.here(n - 1)
+                job[2].extend([(self.r, None, 0), (self.l, None, 0)])
+                return [job]
             if k == last:
-                part = self.here(0)
-                return part[: self.half].astype(BF), part[self.half :].astype(BF)
+                return [self.here(0, 0, h), self.here(0, h, h)] if self.halved else [self.here(0)]
             place = 1 + 2 * (last - 1 - k)
             a, b = self.here(place), self.here(place + 1)
-            if k == last - 1:
-                h = self.half
-                a = jnp.concatenate([a[:h] + self.r.astype(F32), a[h:]])
-                b = jnp.concatenate([b[:h], b[h:] + self.l.astype(F32)])
-            else:
-                a, b = a + self.r.astype(F32), b + self.l.astype(F32)
-            return a.astype(BF), b.astype(BF)
-
-        def total(self):
-            return (self.here(n - 1) + self.r.astype(F32) + self.l.astype(F32)).astype(BF)
+            a[2].append((self.r, None, 0))
+            if self.l is not None:
+                b[2].append((self.l, None, h if k == last - 1 else 0))
+            return [a, b]
 
     def back_of(grads, g_whole, up, season):
         return grow_backward(lay, where, g_whole, grads, up, season, order, gain_b)
@@ -1403,8 +1465,9 @@
         + tuple(v for k in saved for v in k),
     )
     back_got += [arrived[k] for k in sends]
-    f_keep, f_give = done[:2]
-    pre_own, mixed_back_own, sum_own, gains_own = done[2:]
+    steps = last + 1
+    f_keep, f_give = done[:steps], done[steps]
+    pre_own, mixed_back_own, sum_own, gains_own = done[steps + 1 :]
     chains = {}
     kept = {}
     finals = {}
@@ -1417,11 +1480,16 @@
         if not active and not finishing and "smine" in finals:
             break
         sends, work, given = {}, None, ()
-        for name, chain in active.items():
-            a, b = chain.sends()
-            sends[name + "r"], sends[name + "l"] = (a, right), (b, left)
+        names = [*active, *finishing]
+        jobs = {name: chains[name].jobs() for name in names}
+        adder = ring_add if t < 6 else plain_add
+        summed = list(adder([j for name in names for j in jobs[name]])) if names else []
+        for name in active:
+            sends[name + "r"] = (summed.pop(0), right)
+            if len(jobs[name]) > 1:
+                sends[name + "l"] = (summed.pop(0), left)
         for name in finishing:
-            mine = chains[name].total()
+            mine = summed.pop(0)
             finals[name + "mine"] = mine
             sends[name + "y"] = (mine, swap_y)
             if name != "f":
@@ -1451,29 +1519,28 @@
         if t in (5, 6):
             sends["x"] = (tail_sends[t - 5], swap_y)
         if "s" in finishing:
-            work, given = finish, (season_mine, own_counts, *trend_back, *tail)
+            work = lambda *v: (*finish(*v[6:]), *grow_out(*v[2:6]), *dense_out(*v[:2]))
+            given = tuple(finals[k] for k in ("flate", "fd", "gmine", "gy", "gc", "gd"))
+            given += (season_mine, own_counts, *trend_back, *tail)
         arrived, done = slot(sends, work, given)
         if t == 0:
             pre_other, mixed_back_other, sum_other, gains_other = done
-            chains["f"] = Chain(f_keep)
-            chains["f"].got = [arrived["f0"]]
+            chains["f"] = Chain(f_keep, arrived["f0"], False)
         elif t == 1:
-            g_keep, g_give = done
+            *g_keep, g_give = done
             chains["g"] = None
         elif t == 2:
             shrink_pre, iso_pre, gains_si = done
-            chains["g"] = Chain(g_keep)
-            chains["g"].got = [arrived["g"]]
+            chains["g"] = Chain(g_keep, arrived["g"])
             grad_gains = jnp.concatenate(
-                [gains_own + gains_other + gains_si, dense_gains, jnp.zeros((13, width), F32)]
+                [gains_own + gains_other + gains_si, dense_gains, jnp.zeros((29, width), F32)]
             )
         elif t == 3:
-            s_keep, s_give = done
+            *s_keep, s_give = done
         elif t == 4:
             season_mine, *tail_sends = done
             tail = []
-            chains["s"] = Chain(s_keep)
-            chains["s"].got = [arrived["s0"]]
+            chains["s"] = Chain(s_keep, arrived["s0"])
 
             def finish(season_mine, own_counts, *rest):
                 backs, tail = rest[:groups], rest[groups:]
@@ -1485,10 +1552,31 @@
                 )
                 return ((total + averaged).astype(BF),)
 
+            def both(mine, other):
+                return jnp.where(core == 0, mine, other), jnp.where(core == 0, other, mine)
+
+            def grow_out(mine, over_y, sibling, sibling_over_y):
+                found = []
+                for b in range(2):
+                    here = (y == 0) if b == 0 else (y == 1)
+                    lo, hi = both(
+                        jnp.where(here, mine, over_y), jnp.where(here, sibling, sibling_over_y)
+                    )
+                    cols = [v[r : r + k] for v in (lo, hi) for r, k, _ in lay.g_parts(b)]
+                    found.append(jnp.concatenate(cols, axis=1).astype(F32))
+                return found
+
+            def dense_out(mine, other):
+                lo, hi = both(mine, other)
+                z = lay.g_half
+                first = [lo[r - z : r - z + k].astype(F32) for r, k, _, _ in lay.f_parts(0)]
+                rest = [hi[r - z : r - z + k].astype(F32) for r, k, _, _ in lay.f_parts(1)]
+                return (*first, rest[0], jnp.concatenate(rest[1:], axis=1))
+
         if "x" in arrived:
             tail.append(arrived["x"])
         for name, chain in active.items():
-            chain.r, chain.l = arrived[name + "r"], arrived[name + "l"]
+            chain.r, chain.l = arrived[name + "r"], arrived.get(name + "l")
             chain.step -= 1
         for name in ("f", "g"):
             if name + "d" in arrived:
@@ -1503,42 +1591,17 @@
             elif name == "g":
                 finals["glate"] = arrived["gy"]
             else:
-                (series_grad,) = done
+                series_grad, *others = done
         if chains.get("g", 0) is None:
             del chains["g"]
         t += 1
     s_mine, s_y = finals["smine"], finals["sy"]
     s_core = (finals["sc"], swap_core(s_y))
-    f_half, f_other = finals["flate"], finals["fd"]
-    g_mine, g_y = finals["gmine"], finals["gy"]
-    g_core = (finals["gc"], finals["gd"])
-
-    def both(mine, other):
-        return jnp.where(core == 0, mine, other), jnp.where(core == 0, other, mine)
-
-    def branches(mine, over_y):
-        return jnp.where(fine, mine, over_y), jnp.where(fine, over_y, mine)
-
-    g_fine, g_coarse = branches(g_mine, g_y)
-    h_fine, h_coarse = branches(*g_core)
-
-    def g_out(b, mine, other):
-        lo, hi = both(mine, other)
-        cols = [v[r : r + k] for v in (lo, hi) for r, k, _ in lay.g_parts(b)]
-        return jnp.concatenate(cols, axis=1).astype(F32)
+    fine_grow_grad, coarse_grow_grad, contract_grad, merge_grad, trend_grad, expand_grad = others
 
     fine_shrink_grad, coarse_shrink_grad, fine_iso_grad, coarse_iso_grad = give_out(
         lay, member_ids, s_mine, s_y, *s_core
     )
-    fine_grow_grad, coarse_grow_grad = g_out(0, g_fine, h_fine), g_out(1, g_coarse, h_coarse)
-    lo, hi = both(f_half, f_other)
-    (a0, a1, _, _), (b0, b1, _, _) = lay.f_parts(0)
-    z = lay.g_half
-    contract_grad = lo[a0 - z : a0 - z + a1].astype(F32)
-    merge_grad = lo[b0 - z : b0 - z + b1].astype(F32)
-    rest = [hi[a - z : a - z + rows].astype(F32) for a, rows, _, _ in lay.f_parts(1)]
-    trend_grad, expand_grad = rest[0], jnp.concatenate(rest[1:], axis=1)
-
     at = lay.si_half
     gain_grads = s_mine[at : at + 3].astype(F32) + s_y[at : at + 3].astype(F32)
     gain_grads = lax.dynamic_slice(gain_grads, (jnp.int32(0), ring.me * share), (3, share))

time: 596 us -> 586 us (0.983)
  other arithmetic: 62.6 us -> 42.4 us
  Pallas kernels: 248 us -> 264 us
    pallas_call x0 -> x5, Pallas kernels: none -> 15.3 us  [ring_add(): pl.pallas_call(kernel, grid=(1,), out_shape=shapes, in_specs=specs, out_s...]
    convert_element_type x14 -> x10, other arithmetic: 24.2 us -> 16.7 us  [the longest x6 12.4 us: plain_add(): found.append(total.astype(BF))]
    add x3 -> x1, other arithmetic: 9.16 us -> 2.64 us  [plain_add(): total = v if total is None else total + v]
    ppermute x17 -> x16, starting transfers between devices: 16.6 us -> 18.3 us  [left(): return lax.ppermute(v, 'dp', ring.left)]
  transfers between devices with their start and end apart: 70 -> 69, of which waited for: 24 -> 28; matrix products, arithmetic and copies ran while one was open for 6% -> 5% of each run, Pallas kernels for 39% -> 40%
where the time goes in v5:
time: 586 us; the launch traced here: 576 us
  Pallas kernels  264 us (45%)
  waiting for transfers between devices  183 us (31%)
  starting transfers between devices  63 us (11%)
  other arithmetic  42.4 us (7%)
  local copies, waits for them, and re-layouts  14.7 us (3%)
  matrix products  7.03 us (1%)
    ppermute x17, waiting for transfers between devices, right(): return lax.ppermute(v, 'dp', ring.right)  93.3 us
    pallas_call x3, Pallas kernels, dense(): pl.pallas_call(kernel, grid_spec=pltpu.PrefetchScalarGridSpec(num_scalar_...  65.3 us
    ppermute x15, waiting for transfers between devices, swap_y(): return lax.ppermute(v, 'group', Y_SWAP)  52.5 us
    pallas_call x2, Pallas kernels, grow_backward(): pl.pallas_call(kernel, out_shape=[jax.ShapeDtypeStruct((groups, length, w...  25.2 us
    pallas_call x1, Pallas kernels, dense_weights(): pl.pallas_call(kernel, grid=(chunks,), out_shape=outlet.shapes(), in_spec...  24.4 us
    ppermute x3, waiting for transfers between devices, exchange(): return lambda v: lax.ppermute(v, axis, [(i, i ^ step) for i in range(size)])  24.1 us
    pallas_call x2, Pallas kernels, season_kernel(): pl.pallas_call(kernel, grid=(groups,), out_shape=shapes, in_specs=[smem_s...  22.5 us
    pallas_call x2, Pallas kernels, grow_forward(): pl.pallas_call(kernel, out_shape=shapes, in_specs=[smem_spec()] + [vmem_s...  22.1 us
  transfers between devices with their start and end apart: 69, of which 28 were waited for; matrix products, arithmetic and copies ran while one was open for 5% of the time, Pallas kernels for 40%

profile of v5, /device:TPU:0, one launch (start us, length us, event | category | flops | bytes accessed | tf_op | source)
XLA Modules:
  0.0 576.1 jit_solution(10860495348456870926)
XLA Ops:
  1.3 3.1 fusion.34
  5.3 3.5 own_half.1.refs_0_
  8.8 3.1 collective-permute-start
  15.9 3.4 sibling_half.1.refs_1_
  19.3 11.9 %collective-permute-done.3 = f32[12]{0:T(128)S(1)} collective-permute-done((f32[12]{0:T(128)S(1)}, f32[12]{0:T(128)S(1)}, u32[]{:S(2)}, u32[]{:S(2)}) %collective-permute-start.3) | collective-permute-done | bytes 80 | tf_op jit(solution)/shard_map/ppermute | solution.py:93
  31.2 21.1 %collective-permute-done.4 = f32[3,512]{1,0:T(4,128)} collective-permute-done((f32[3,512]{1,0:T(4,128)S(1)}, f32[3,512]{1,0:T(4,128)}, u32[]{:S(2)}, u32[]{:S(2)}) %collective-permute-start.4) | collective-permute-done | bytes 6176 | tf_op jit(solution)/shard_map/ppermute | solution.py:1196
  57.7 8.1 %fusion.26.step_ref = s32[768,1]{1,0:T(8,128)} fusion(s32[]{:T(128)S(6)} %select_n.225, s32[]{:T(128)S(6)} %sign.30, s32[]{:T(128)S(6)} %select_n.228, s32[]{:T(128)S(6)} %select_n.226), kind=kLoop, calls=%fused_computation.57 | loop fusion | flops 12288 | bytes 3088 | tf_op jit(solution)/shard_map/add | solution.py:1260
  65.9 12.8 %season_trend.1 = (f32[3,768,512]{2,1,0:T(8,128)}, bf16[3,768,512]{2,1,0:T(8,128)(2,1)}, bf16[3,768,768]{2,1,0:T(8,128)(2,1)}, bf16[3,768,512]{2,1,0:T(8,128)(2,1)}, bf16[768,768]{1,0:T(8,128)(2,1)}) custom-call(s32[12]{0:T(128)} %kinds_own.1, s32[768,1]{1,0:T(8,128)} %fusion.26.step_ref, bf16[3,768,512]{2,1,0:T(8,128)(2,1)} %bitcast.93), custom_call_target="tpu_custom_call" | custom-call | flops 5435817984 | bytes 14155776 | tf_op jit(solution)/shard_map/season_trend/pallas_call | solution.py:332
  78.6 15.8 %collective-permute-done.5.refs_6_ = bf16[1792,512]{1,0:T(8,128)(2,1)} collective-permute-done((bf16[1792,512]{1,0:T(8,128)(2,1)}, bf16[1792,512]{1,0:T(8,128)(2,1)}, u32[]{:S(2)}, u32[]{:S(2)}) %collective-permute-start.5) | collective-permute-done | bytes 1835040 | tf_op jit(solution)/shard_map/ppermute | solution.py:1231
  102.1 16.0 %collective-permute-done.14 = bf16[768,512]{1,0:T(8,128)(2,1)S(1)} collective-permute-done((bf16[768,512]{1,0:T(8,128)(2,1)}, bf16[768,512]{1,0:T(8,128)(2,1)S(1)}, u32[]{:S(2)}, u32[]{:S(2)}) %collective-permute-start.14) | collective-permute-done | bytes 786464 | tf_op jit(solution)/shard_map/ppermute | solution.py:93
  118.1 17.2 %collective-permute-done.10.refs_10_ = bf16[1792,512]{1,0:T(8,128)(2,1)} collective-permute-done((bf16[1792,512]{1,0:T(8,128)(2,1)}, bf16[1792,512]{1,0:T(8,128)(2,1)}, u32[]{:S(2)}, u32[]{:S(2)}) %collective-permute-start.10) | collective-permute-done | bytes 1835040 | tf_op jit(solution)/shard_map/ppermute | solution.py:1231
  137.0 2.7 fusion.35
  144.5 3.0 pad_maximum_fusion.x_ref
  147.5 9.7 %season.1 = (f32[3,768,512]{2,1,0:T(8,128)}, bf16[3,768,512]{2,1,0:T(8,128)(2,1)}) custom-call(s32[12]{0:T(128)} %convert_element_type.216.kinds_ref.kinds_other, s32[768,1]{1,0:T(8,128)} %fusion.26.step_ref, bf16[3,768,512]{2,1,0:T(8,128)(2,1)} %pad_maximum_fusion.x_ref), custom_call_target="tpu_custom_call" | custom-call | flops 5435817984 | bytes 14155776 | tf_op jit(solution)/shard_map/season/pallas_call | solution.py:332
  160.1 3.0 collective-permute-done.22
  167.3 19.0 %shrink_forward.1 = (f32[384,512]{1,0:T(8,128)}, f32[384,512]{1,0:T(8,128)}, bf16[384,512]{1,0:T(8,128)(2,1)}, s32[384,1]{1,0:T(8,128)}, bf16[16,384,512]{2,1,0:T(8,128)(2,1)}, /*index=5*/bf16[14336,512]{1,0:T(8,128)(2,1)}) custom-call(s32[10]{0:T(128)} %stack.84.where, s32[12]{0:T(128)} %kinds_own.1, s32[12]{0:T(128)} %convert_element_type.216.kinds_ref.kinds_other, ...), custom_call_target="tpu_custom_call" | custom-call | flops 5637144576 | bytes 29360128 | tf_op jit(solution)/shard_map/shrink_forward/pallas_call | solution.py:421
  189.2 11.5 %grow_forward.2 = (bf16[1,768,512]{2,1,0:T(8,128)(2,1)}, bf16[1,768,512]{2,1,0:T(8,128)(2,1)}, bf16[1,768,512]{2,1,0:T(8,128)(2,1)}, f32[3,768,512]{2,1,0:T(8,128)}, bf16[8192,512]{1,0:T(8,128)(2,1)}) custom-call(s32[10]{0:T(128)} %stack.84.where, f32[1,512]{1,0:T(1,128)} %get-tuple-element.1001.gain_ref, bf16[768,768]{1,0:T(8,128)(2,1)} %get-tuple-element.557.order_ref, ...), custom_call_target="tpu_custom_call" | custom-call | flops 3019898880 | bytes 24903680 | tf_op jit(solution)/shard_map/grow_forward/pallas_call | solution.py:523
  200.7 2.6 collective-permute-start.27
  203.7 5.8 %dense_whole.1 = (bf16[1024,512]{1,0:T(8,128)(2,1)}, bf16[2048,512]{1,0:T(8,128)(2,1)}, bf16[512,512]{1,0:T(8,128)(2,1)}, bf16[512,2048]{1,0:T(8,128)(2,1)}) custom-call(s32[10]{0:T(128)} %stack.84.where, bf16[1792,512]{1,0:T(8,128)(2,1)} %own_half.1.refs_0_, bf16[1792,512]{1,0:T(8,128)(2,1)} %sibling_half.1.refs_1_, ...), custom_call_target="tpu_custom_call" | custom-call | bytes 11534336 | tf_op jit(solution)/shard_map/dense_whole/pallas_call | solution.py:965
  209.6 10.6 %grow_forward.3 = (bf16[1,768,512]{2,1,0:T(8,128)(2,1)}, bf16[1,768,512]{2,1,0:T(8,128)(2,1)}, bf16[1,768,512]{2,1,0:T(8,128)(2,1)}, f32[3,768,512]{2,1,0:T(8,128)}) custom-call(s32[10]{0:T(128)} %stack.84.where, f32[1,512]{1,0:T(1,128)} %get-tuple-element.1001.gain_ref, bf16[768,768]{1,0:T(8,128)(2,1)} %get-tuple-element.557.order_ref, ...), custom_call_target="tpu_custom_call" | custom-call | flops 3019898880 | bytes 24903680 | tf_op jit(solution)/shard_map/grow_forward/pallas_call | solution.py:523
  223.1 21.7 %dense.3 = (bf16[768,2048]{1,0:T(8,128)(2,1)}, bf16[768,2048]{1,0:T(8,128)(2,1)}, bf16[768,512]{1,0:T(8,128)(2,1)}, bf16[768,512]{1,0:T(8,128)(2,1)}, bf16[768,5...) custom-call(s32[10]{0:T(128)} %stack.84.where, ...), custom_call_target="tpu_custom_call" | custom-call | flops 8858370048 | bytes 33554432 | tf_op jit(solution)/shard_map/dense/pallas_call | solution.py:1067
  245.2 21.9 %dense.4 = (bf16[768,2048]{1,0:T(8,128)(2,1)}, bf16[768,2048]{1,0:T(8,128)(2,1)}, bf16[768,512]{1,0:T(8,128)(2,1)}, bf16[768,512]{1,0:T(8,128)(2,1)}, bf16[768,5...) custom-call(s32[10]{0:T(128)} %stack.84.where, ...), custom_call_target="tpu_custom_call" | custom-call | flops 8858370048 | bytes 33554432 | tf_op jit(solution)/shard_map/dense/pallas_call | solution.py:1067
  268.9 21.7 %dense.5 = (bf16[768,2048]{1,0:T(8,128)(2,1)}, bf16[768,2048]{1,0:T(8,128)(2,1)}, bf16[768,512]{1,0:T(8,128)(2,1)}, bf16[768,512]{1,0:T(8,128)(2,1)}, bf16[768,5...) custom-call(s32[10]{0:T(128)} %stack.84.where, ...), custom_call_target="tpu_custom_call" | custom-call | flops 8858370048 | bytes 33554432 | tf_op jit(solution)/shard_map/dense/pallas_call | solution.py:1067
  292.7 12.7 %grow_backward.2 = (bf16[3,768,512]{2,1,0:T(8,128)(2,1)}, f32[192,512]{1,0:T(8,128)}, f32[3,768,512]{2,1,0:T(8,128)}, f32[1,512]{1,0:T(1,128)}) custom-call(s32[10]{0:T(128)} %stack.84.where, f32[1,512]{1,0:T(1,128)} %get-tuple-element.1001.gain_ref, bf16[768,768]{1,0:T(8,128)(2,1)} %get-tuple-element.557.order_ref, ...), custom_call_target="tpu_custom_call" | custom-call | flops 3019898880 | bytes 29622272 | tf_op jit(solution)/shard_map/grow_backward/pallas_call | solution.py:599
  305.4 24.4 %dense_weights.1 = (bf16[1,384,512]{2,1,0:T(8,128)(2,1)}, bf16[2,384,512]{2,1,0:T(8,128)(2,1)}, bf16[2,384,512]{2,1,0:T(8,128)(2,1)}, bf16[2,384,512]{2,1,0:T(8,...) custom-call(s32[10]{0:T(128)} %stack.84.where, s32[8]{0:T(128)} %compare_select_fusion.6.places_ref, ...), custom_call_target="tpu_custom_call" | custom-call | flops 13287555072 | bytes 47185920 | tf_op jit(solution)/shard_map/dense_weights/pallas_call | solution.py:1175
  329.9 12.5 %grow_backward.3 = (bf16[3,768,512]{2,1,0:T(8,128)(2,1)}, f32[192,512]{1,0:T(8,128)}, f32[3,768,512]{2,1,0:T(8,128)}, f32[1,512]{1,0:T(1,128)}) custom-call(s32[10]{0:T(128)} %stack.84.where, f32[1,512]{1,0:T(1,128)} %get-tuple-element.1001.gain_ref, bf16[768,768]{1,0:T(8,128)(2,1)} %get-tuple-element.557.order_ref, ...), custom_call_target="tpu_custom_call" | custom-call | flops 3019898880 | bytes 29622272 | tf_op jit(solution)/shard_map/grow_backward/pallas_call | solution.py:599
  344.8 9.6 %grow_weight.1 = (bf16[1,512,512]{2,1,0:T(8,128)(2,1)}, bf16[2,512,512]{2,1,0:T(8,128)(2,1)}, bf16[2,512,512]{2,1,0:T(8,128)(2,1)}, bf16[2,512,512]{2,1,0:T(8,12...) custom-call(s32[10]{0:T(128)} %stack.84.where, s32[8]{0:T(128)} %compare_select_fusion.6.places_ref, ...), custom_call_target="tpu_custom_call" | custom-call | flops 2415919104 | bytes 8388608 | tf_op jit(solution)/shard_map/grow_weight/pallas_call | solution.py:683
  356.9 2.5 ring_add.6
  361.6 10.5 %shrink_backward.1 = (bf16[384,512]{1,0:T(8,128)(2,1)}, bf16[384,512]{1,0:T(8,128)(2,1)}, f32[1,512]{1,0:T(1,128)}) custom-call(s32[10]{0:T(128)} %stack.84.where, s32[384,1]{1,0:T(8,128)} %get-tuple-element.815.age_ref, f32[1,512]{1,0:T(1,128)} %get-tuple-element.1001.gain_ref, f32[192,512]{1,0:T(8,128)} %get-tuple-element.816.b0, ...), custom_call_target="tpu_custom_call" | custom-call | flops 3221225472 | bytes 8388608 | tf_op jit(solution)/shard_map/shrink_backward/pallas_call | solution.py:734
  373.5 3.1 ring_add.7
  380.7 16.5 %shrink_weight.1 = (bf16[1,928,512]{2,1,0:T(8,128)(2,1)}, bf16[2,928,512]{2,1,0:T(8,128)(2,1)}, bf16[2,928,512]{2,1,0:T(8,128)(2,1)}, bf16[2,928,512]{2,1,0:T(8,...) custom-call(s32[10]{0:T(128)} %stack.84.where, s32[8]{0:T(128)} %compare_select_fusion.6.places_ref, ...), custom_call_target="tpu_custom_call" | custom-call | flops 5637144576 | bytes 31457280 | tf_op jit(solution)/shard_map/shrink_weight/pallas_call | solution.py:794
  398.0 3.8 ring_add.8
  405.8 15.0 %season_backward.1 = (bf16[3,768,512]{2,1,0:T(8,128)(2,1)}, bf16[1,768,512]{2,1,0:T(8,128)(2,1)}, bf16[2,768,512]{2,1,0:T(8,128)(2,1)}) custom-call(s32[10]{0:T(128)} %stack.84.where, bf16[768,768]{1,0:T(8,128)(2,1)} %get-tuple-element.557.order_ref, bf16[384,512]{1,0:T(8,128)(2,1)} %get-tuple-element.876.pre_ref, ...), custom_call_target="tpu_custom_call" | custom-call | flops 6039797760 | bytes 36700160 | tf_op jit(solution)/shard_map/season_backward/pallas_call | solution.py:839
  420.9 3.9 collective-permute-done.44.refs_2_
  425.0 3.9 ring_add.9
  434.8 2.6 convert_add_fusion.1
  437.6 5.3 collective-permute-done.49
  444.3 8.3 %collective-permute-done.47 = bf16[512,512]{1,0:T(8,128)(2,1)S(1)} collective-permute-done((bf16[512,512]{1,0:T(8,128)(2,1)}, bf16[512,512]{1,0:T(8,128)(2,1)S(1)}, u32[]{:S(2)}, u32[]{:S(2)}) %collective-permute-start.47) | collective-permute-done | bytes 524320 | tf_op jit(solution)/shard_map/ppermute | solution.py:1231
  464.0 26.7 %collective-permute-done.52 = bf16[512,512]{1,0:T(8,128)(2,1)S(1)} collective-permute-done((bf16[512,512]{1,0:T(8,128)(2,1)S(1)}, bf16[512,512]{1,0:T(8,128)(2,1)S(1)}, u32[]{:S(2)}, u32[]{:S(2)}) %collective-permute-start.52) | collective-permute-done | bytes 524320 | tf_op jit(solution)/shard_map/ppermute | solution.py:1231
  492.9 2.4 fusion.8
  499.4 16.9 %collective-permute-done.59 = bf16[384,512]{1,0:T(8,128)(2,1)S(1)} collective-permute-done((bf16[384,512]{1,0:T(8,128)(2,1)S(1)}, bf16[384,512]{1,0:T(8,128)(2,1)S(1)}, u32[]{:S(2)}, u32[]{:S(2)}) %collective-permute-start.59) | collective-permute-done | bytes 393248 | tf_op jit(solution)/shard_map/ppermute | solution.py:93
  516.5 3.6 fusion.7
  522.9 2.1 collective-permute-done.64
  524.9 14.3 %collective-permute-done.62 = bf16[928,512]{1,0:T(8,128)(2,1)S(1)} collective-permute-done((bf16[928,512]{1,0:T(8,128)(2,1)}, bf16[928,512]{1,0:T(8,128)(2,1)S(1)}, u32[]{:S(2)}, u32[]{:S(2)}) %collective-permute-start.62) | collective-permute-done | bytes 950304 | tf_op jit(solution)/shard_map/ppermute | solution.py:1231
  540.9 2.0 fusion.12.mine
  554.1 7.0 %add_convert_fusion = bf16[3,768,512]{2,1,0:T(8,128)(2,1)} fusion(bf16[3,768,512]{2,1,0:T(8,128)(2,1)S(1)} %copy-done.29, bf16[3,768,768]{2,1,0:T(8,128)(2,1)} %get-tuple-element.950, f32[1,768,512]{2,1,0:T(8,128)S(1)} %bitcast.117, f32[1,768,512]{2,1,0:T(8,128)S(1)} %bitcast.116, f32[1,768,512]{2,1,0:T(8,128)S(1)} %bitcast.115, ...), kind=kOutput, calls=%fused_computation.3 | convolution fusion | flops 1829634048 | bytes 15335424 | tf_op jit(solution)/shard_map/gij,gid->gjd/dot_general | solution.py:1550
  561.1 6.2 %collective-permute-done.66.over_y = bf16[928,512]{1,0:T(8,128)(2,1)S(1)} collective-permute-done((bf16[928,512]{1,0:T(8,128)(2,1)S(1)}, bf16[928,512]{1,0:T(8,128)(2,1)S(1)}, u32[]{:S(2)}, u32[]{:S(2)}) %collective-permute-start.66) | collective-permute-done | bytes 950304 | tf_op jit(solution)/shard_map/ppermute | solution.py:93
  570.0 5.6 give_out.1
  (264 shorter events, 103.5 us)
Async XLA Ops:
  8.8 43.5 %collective-permute-start = (bf16[1792,512]{1,0:T(8,128)(2,1)}, bf16[1792,512]{1,0:T(8,128)(2,1)}, u32[]{:S(2)}, u32[]{:S(2)}) collective-permute-start(bf16[1792,512]{1,0:T(8,128)(2,1)} %own_half.1.refs_0_), channel_id=1, source_target_pairs={{0,8},{8,16},{16,24},{24,28},{28,20},{20,12},{12,4},{4,0},{1,9},{9... | collective-permute-start | bytes 5505032 | tf_op jit(solution)/shard_map/ppermute | solution.py:1231
  11.9 41.7 %collective-permute-start.1 = (bf16[1792,512]{1,0:T(8,128)(2,1)}, bf16[1792,512]{1,0:T(8,128)(2,1)}, u32[]{:S(2)}, u32[]{:S(2)}) collective-permute-start(bf16[1792,512]{1,0:T(8,128)(2,1)} %own_half.1.refs_0_), channel_id=1, source_target_pairs={{8,0},{16,8},{24,16},{28,24},{20,28},{12,20},{4,12},{0,4},{9,1},{1... | collective-permute-start | bytes 5505032 | tf_op jit(solution)/shard_map/ppermute | solution.py:1234
  11.9 40.4 %collective-permute-start.2 = (bf16[768,512]{1,0:T(8,128)(2,1)}, bf16[768,512]{1,0:T(8,128)(2,1)}, u32[]{:S(2)}, u32[]{:S(2)}) collective-permute-start(bf16[768,512]{1,0:T(8,128)(2,1)} %get-tuple-element.496), channel_id=1, source_target_pairs={{0,2},{2,0},{1,3},{3,1},{4,6},{6,4},{5,7},{7,5},{8,10},{10,8},{9,1... | collective-permute-start | bytes 2359304 | tf_op jit(solution)/shard_map/ppermute | solution.py:93
  13.9 38.4 %collective-permute-start.4 = (f32[3,512]{1,0:T(4,128)S(1)}, f32[3,512]{1,0:T(4,128)}, u32[]{:S(2)}, u32[]{:S(2)}) collective-permute-start(f32[3,512]{1,0:T(4,128)S(1)} %dynamic_update_slice.5), channel_id=1, source_target_pairs={{0,4},{4,0},{8,12},{12,8},{16,20},{20,16},{24,28},{28,24},{1,5},{5... | collective-permute-start | bytes 18440 | tf_op jit(solution)/shard_map/ppermute | solution.py:1196
  53.6 40.8 %collective-permute-start.5 = (bf16[1792,512]{1,0:T(8,128)(2,1)}, bf16[1792,512]{1,0:T(8,128)(2,1)}, u32[]{:S(2)}, u32[]{:S(2)}) collective-permute-start(bf16[1792,512]{1,0:T(8,128)(2,1)} %collective-permute-done.refs_2_), channel_id=1, source_target_pairs={{0,8},{8,16},{16,24},{24,28},{28,20},{20,12},{12,4},{4,0},{1,9},{9... | collective-permute-start | bytes 5505032 | tf_op jit(solution)/shard_map/ppermute | solution.py:1231
  55.2 40.5 %collective-permute-start.6 = (bf16[1792,512]{1,0:T(8,128)(2,1)}, bf16[1792,512]{1,0:T(8,128)(2,1)}, u32[]{:S(2)}, u32[]{:S(2)}) collective-permute-start(bf16[1792,512]{1,0:T(8,128)(2,1)} %collective-permute-done.1.refs_3_), channel_id=1, source_target_pairs={{8,0},{16,8},{24,16},{28,24},{20,28},{12,20},{4,12},{0,4},{9,1},{1... | collective-permute-start | bytes 5505032 | tf_op jit(solution)/shard_map/ppermute | solution.py:1234
  55.6 40.1 %collective-permute-start.7 = (bf16[1792,512]{1,0:T(8,128)(2,1)}, bf16[1792,512]{1,0:T(8,128)(2,1)}, u32[]{:S(2)}, u32[]{:S(2)}) collective-permute-start(bf16[1792,512]{1,0:T(8,128)(2,1)} %collective-permute-done.refs_2_), channel_id=1, source_target_pairs={{0,1},{1,0},{2,3},{3,2},{4,5},{5,4},{6,7},{7,6},{8,9},{9,8},{10,11... | collective-permute-start | bytes 5505032 | tf_op jit(solution)/shard_map/ppermute | solution.py:89
  55.6 40.1 %collective-permute-start.8 = (bf16[1792,512]{1,0:T(8,128)(2,1)}, bf16[1792,512]{1,0:T(8,128)(2,1)}, u32[]{:S(2)}, u32[]{:S(2)}) collective-permute-start(bf16[1792,512]{1,0:T(8,128)(2,1)} %collective-permute-done.1.refs_3_), channel_id=1, source_target_pairs={{0,1},{1,0},{2,3},{3,2},{4,5},{5,4},{6,7},{7,6},{8,9},{9,8},{10,11... | collective-permute-start | bytes 5505032 | tf_op jit(solution)/shard_map/ppermute | solution.py:89
  56.1 22.5 %collective-permute-start.9 = (bf16[768,512]{1,0:T(8,128)(2,1)}, bf16[768,512]{1,0:T(8,128)(2,1)}, u32[]{:S(2)}, u32[]{:S(2)}) collective-permute-start(bf16[768,512]{1,0:T(8,128)(2,1)} %get-tuple-element.516), channel_id=1, source_target_pairs={{0,2},{2,0},{1,3},{3,1},{4,6},{6,4},{5,7},{7,5},{8,10},{10,8},{9,1... | collective-permute-start | bytes 2359304 | tf_op jit(solution)/shard_map/ppermute | solution.py:93
  95.7 39.6 %collective-permute-start.10 = (bf16[1792,512]{1,0:T(8,128)(2,1)}, bf16[1792,512]{1,0:T(8,128)(2,1)}, u32[]{:S(2)}, u32[]{:S(2)}) collective-permute-start(bf16[1792,512]{1,0:T(8,128)(2,1)} %collective-permute-done.5.refs_6_), channel_id=1, source_target_pairs={{0,8},{8,16},{16,24},{24,28},{28,20},{20,12},{12,4},{4,0},{1,9},{9... | collective-permute-start | bytes 5505032 | tf_op jit(solution)/shard_map/ppermute | solution.py:1231
  97.4 39.6 %collective-permute-start.11 = (bf16[1792,512]{1,0:T(8,128)(2,1)}, bf16[1792,512]{1,0:T(8,128)(2,1)}, u32[]{:S(2)}, u32[]{:S(2)}) collective-permute-start(bf16[1792,512]{1,0:T(8,128)(2,1)} %collective-permute-done.6.refs_7_), channel_id=1, source_target_pairs={{8,0},{16,8},{24,16},{28,24},{20,28},{12,20},{4,12},{0,4},{9,1},{1... | collective-permute-start | bytes 5505032 | tf_op jit(solution)/shard_map/ppermute | solution.py:1234
  97.9 39.0 %collective-permute-start.12 = (bf16[1792,512]{1,0:T(8,128)(2,1)}, bf16[1792,512]{1,0:T(8,128)(2,1)}, u32[]{:S(2)}, u32[]{:S(2)}) collective-permute-start(bf16[1792,512]{1,0:T(8,128)(2,1)} %collective-permute-done.5.refs_6_), channel_id=1, source_target_pairs={{0,1},{1,0},{2,3},{3,2},{4,5},{5,4},{6,7},{7,6},{8,9},{9,8},{10,11... | collective-permute-start | bytes 5505032 | tf_op jit(solution)/shard_map/ppermute | solution.py:89
  97.9 39.0 %collective-permute-start.13 = (bf16[1792,512]{1,0:T(8,128)(2,1)}, bf16[1792,512]{1,0:T(8,128)(2,1)}, u32[]{:S(2)}, u32[]{:S(2)}) collective-permute-start(bf16[1792,512]{1,0:T(8,128)(2,1)} %collective-permute-done.6.refs_7_), channel_id=1, source_target_pairs={{0,1},{1,0},{2,3},{3,2},{4,5},{5,4},{6,7},{7,6},{8,9},{9,8},{10,11... | collective-permute-start | bytes 5505032 | tf_op jit(solution)/shard_map/ppermute | solution.py:89
  98.5 19.7 %collective-permute-start.14 = (bf16[768,512]{1,0:T(8,128)(2,1)}, bf16[768,512]{1,0:T(8,128)(2,1)S(1)}, u32[]{:S(2)}, u32[]{:S(2)}) collective-permute-start(bf16[768,512]{1,0:T(8,128)(2,1)} %get-tuple-element.530), channel_id=1, source_target_pairs={{0,2},{2,0},{1,3},{3,1},{4,6},{6,4},{5,7},{7,5},{8,10},{10,8},{9,1... | collective-permute-start | bytes 2359304 | tf_op jit(solution)/shard_map/ppermute | solution.py:93
  139.7 17.5 %collective-permute-start.17 = (bf16[1792,512]{1,0:T(8,128)(2,1)}, bf16[1792,512]{1,0:T(8,128)(2,1)}, u32[]{:S(2)}, u32[]{:S(2)}) collective-permute-start(bf16[1792,512]{1,0:T(8,128)(2,1)} %collective-permute-done.10.refs_10_), channel_id=1, source_target_pairs={{0,1},{1,0},{2,3},{3,2},{4,5},{5,4},{6,7},{7,6},{8,9},{9,8},{10,11... | collective-permute-start | bytes 5505032 | tf_op jit(solution)/shard_map/ppermute | solution.py:89
  139.7 17.5 %collective-permute-start.18 = (bf16[1792,512]{1,0:T(8,128)(2,1)}, bf16[1792,512]{1,0:T(8,128)(2,1)}, u32[]{:S(2)}, u32[]{:S(2)}) collective-permute-start(bf16[1792,512]{1,0:T(8,128)(2,1)} %collective-permute-done.11.refs_11_), channel_id=1, source_target_pairs={{0,1},{1,0},{2,3},{3,2},{4,5},{5,4},{6,7},{7,6},{8,9},{9,8},{10,11... | collective-permute-start | bytes 5505032 | tf_op jit(solution)/shard_map/ppermute | solution.py:89
  165.3 21.0 %collective-permute-start.23 = (bf16[448,512]{1,0:T(8,128)(2,1)}, bf16[448,512]{1,0:T(8,128)(2,1)}, u32[]{:S(2)}, u32[]{:S(2)}) collective-permute-start(bf16[448,512]{1,0:T(8,128)(2,1)} %get-tuple-element.569), channel_id=1, source_target_pairs={{0,8},{8,16},{16,24},{24,28},{28,20},{20,12},{12,4},{4,0},{1,9},{9... | collective-permute-start | bytes 1376264 | tf_op jit(solution)/shard_map/ppermute | solution.py:1231
  165.6 20.7 %collective-permute-start.24 = (bf16[448,512]{1,0:T(8,128)(2,1)}, bf16[448,512]{1,0:T(8,128)(2,1)}, u32[]{:S(2)}, u32[]{:S(2)}) collective-permute-start(bf16[448,512]{1,0:T(8,128)(2,1)} %get-tuple-element.570), channel_id=1, source_target_pairs={{8,0},{16,8},{24,16},{28,24},{20,28},{12,20},{4,12},{0,4},{9,1},{1... | collective-permute-start | bytes 1376264 | tf_op jit(solution)/shard_map/ppermute | solution.py:1234
  200.7 20.7 %collective-permute-start.27 = (bf16[768,512]{1,0:T(8,128)(2,1)}, bf16[768,512]{1,0:T(8,128)(2,1)}, u32[]{:S(2)}, u32[]{:S(2)}) collective-permute-start(bf16[768,512]{1,0:T(8,128)(2,1)} %bitcast.113), channel_id=1, source_target_pairs={{0,2},{2,0},{1,3},{3,1},{4,6},{6,4},{5,7},{7,5},{8,10},{10,8},{9,1... | collective-permute-start | bytes 2359304 | tf_op jit(solution)/shard_map/ppermute | solution.py:93
  221.4 23.5 %collective-permute-start.28 = (bf16[768,512]{1,0:T(8,128)(2,1)}, bf16[768,512]{1,0:T(8,128)(2,1)}, u32[]{:S(2)}, u32[]{:S(2)}) collective-permute-start(bf16[768,512]{1,0:T(8,128)(2,1)} %bitcast.112), channel_id=1, source_target_pairs={{0,2},{2,0},{1,3},{3,1},{4,6},{6,4},{5,7},{7,5},{8,10},{10,8},{9,1... | collective-permute-start | bytes 2359304 | tf_op jit(solution)/shard_map/ppermute | solution.py:93
  244.9 22.2 %collective-permute-start.29 = (bf16[768,512]{1,0:T(8,128)(2,1)}, bf16[768,512]{1,0:T(8,128)(2,1)}, u32[]{:S(2)}, u32[]{:S(2)}) collective-permute-start(bf16[768,512]{1,0:T(8,128)(2,1)} %bitcast.111), channel_id=1, source_target_pairs={{0,2},{2,0},{1,3},{3,1},{4,6},{6,4},{5,7},{7,5},{8,10},{10,8},{9,1... | collective-permute-start | bytes 2359304 | tf_op jit(solution)/shard_map/ppermute | solution.py:93
  267.1 23.5 %collective-permute-start.30 = (bf16[768,512]{1,0:T(8,128)(2,1)}, bf16[768,512]{1,0:T(8,128)(2,1)}, u32[]{:S(2)}, u32[]{:S(2)}) collective-permute-start(bf16[768,512]{1,0:T(8,128)(2,1)} %get-tuple-element.693), channel_id=1, source_target_pairs={{0,2},{2,0},{1,3},{3,1},{4,6},{6,4},{5,7},{7,5},{8,10},{10,8},{9,1... | collective-permute-start | bytes 2359304 | tf_op jit(solution)/shard_map/ppermute | solution.py:93
  290.6 39.2 %collective-permute-start.31 = (bf16[768,512]{1,0:T(8,128)(2,1)}, bf16[768,512]{1,0:T(8,128)(2,1)}, u32[]{:S(2)}, u32[]{:S(2)}) collective-permute-start(bf16[768,512]{1,0:T(8,128)(2,1)} %get-tuple-element.732), channel_id=1, source_target_pairs={{0,2},{2,0},{1,3},{3,1},{4,6},{6,4},{5,7},{7,5},{8,10},{10,8},{9,1... | collective-permute-start | bytes 2359304 | tf_op jit(solution)/shard_map/ppermute | solution.py:93
  291.0 38.9 %collective-permute-start.32 = (bf16[768,512]{1,0:T(8,128)(2,1)}, bf16[768,512]{1,0:T(8,128)(2,1)}, u32[]{:S(2)}, u32[]{:S(2)}) collective-permute-start(bf16[768,512]{1,0:T(8,128)(2,1)} %get-tuple-element.733), channel_id=1, source_target_pairs={{0,2},{2,0},{1,3},{3,1},{4,6},{6,4},{5,7},{7,5},{8,10},{10,8},{9,1... | collective-permute-start | bytes 2359304 | tf_op jit(solution)/shard_map/ppermute | solution.py:93
  376.6 20.5 %collective-permute-start.40 = (bf16[256,512]{1,0:T(8,128)(2,1)}, bf16[256,512]{1,0:T(8,128)(2,1)}, u32[]{:S(2)}, u32[]{:S(2)}) collective-permute-start(bf16[256,512]{1,0:T(8,128)(2,1)} %get-tuple-element.843), channel_id=1, source_target_pairs={{0,8},{8,16},{16,24},{24,28},{28,20},{20,12},{12,4},{4,0},{1,9},{9... | collective-permute-start | bytes 786440 | tf_op jit(solution)/shard_map/ppermute | solution.py:1231
  377.2 20.0 %collective-permute-start.41 = (bf16[256,512]{1,0:T(8,128)(2,1)}, bf16[256,512]{1,0:T(8,128)(2,1)}, u32[]{:S(2)}, u32[]{:S(2)}) collective-permute-start(bf16[256,512]{1,0:T(8,128)(2,1)} %get-tuple-element.844), channel_id=1, source_target_pairs={{8,0},{16,8},{24,16},{28,24},{20,28},{12,20},{4,12},{0,4},{9,1},{1... | collective-permute-start | bytes 786440 | tf_op jit(solution)/shard_map/ppermute | solution.py:1234
  378.7 18.5 %collective-permute-start.38 = (bf16[384,512]{1,0:T(8,128)(2,1)}, bf16[384,512]{1,0:T(8,128)(2,1)S(1)}, u32[]{:S(2)}, u32[]{:S(2)}) collective-permute-start(bf16[384,512]{1,0:T(8,128)(2,1)} %get-tuple-element.841), channel_id=1, source_target_pairs={{0,8},{8,16},{16,24},{24,28},{28,20},{20,12},{12,4},{4,0},{1,9},{9... | collective-permute-start | bytes 1179656 | tf_op jit(solution)/shard_map/ppermute | solution.py:1231
  379.2 18.0 %collective-permute-start.39 = (bf16[384,512]{1,0:T(8,128)(2,1)}, bf16[384,512]{1,0:T(8,128)(2,1)}, u32[]{:S(2)}, u32[]{:S(2)}) collective-permute-start(bf16[384,512]{1,0:T(8,128)(2,1)} %get-tuple-element.842), channel_id=1, source_target_pairs={{8,0},{16,8},{24,16},{28,24},{20,28},{12,20},{4,12},{0,4},{9,1},{1... | collective-permute-start | bytes 1179656 | tf_op jit(solution)/shard_map/ppermute | solution.py:1234
  401.7 23.3 %collective-permute-start.46 = (bf16[8,928,512]{2,1,0:T(8,128)(2,1)}, bf16[8,928,512]{2,1,0:T(8,128)(2,1)}, u32[]{:S(2)}, u32[]{:S(2)}) collective-permute-start(bf16[8,928,512]{2,1,0:T(8,128)(2,1)} %get-tuple-element.875), channel_id=1, source_target_pairs={{0,1},{1,0},{2,3},{3,2},{4,5},{5,4},{6,7},{7,6},{8,9},{9,8},{10,11... | collective-permute-start | bytes 22806536 | tf_op jit(solution)/shard_map/ppermute | solution.py:89
  401.7 19.1 %collective-permute-start.42 = (bf16[384,512]{1,0:T(8,128)(2,1)}, bf16[384,512]{1,0:T(8,128)(2,1)S(1)}, u32[]{:S(2)}, u32[]{:S(2)}) collective-permute-start(bf16[384,512]{1,0:T(8,128)(2,1)} %get-tuple-element.871), channel_id=1, source_target_pairs={{0,8},{8,16},{16,24},{24,28},{28,20},{20,12},{12,4},{4,0},{1,9},{9... | collective-permute-start | bytes 1179656 | tf_op jit(solution)/shard_map/ppermute | solution.py:1231
  402.3 18.6 %collective-permute-start.43 = (bf16[384,512]{1,0:T(8,128)(2,1)}, bf16[384,512]{1,0:T(8,128)(2,1)}, u32[]{:S(2)}, u32[]{:S(2)}) collective-permute-start(bf16[384,512]{1,0:T(8,128)(2,1)} %get-tuple-element.872), channel_id=1, source_target_pairs={{8,0},{16,8},{24,16},{28,24},{20,28},{12,20},{4,12},{0,4},{9,1},{1... | collective-permute-start | bytes 1179656 | tf_op jit(solution)/shard_map/ppermute | solution.py:1234
  403.8 21.0 %collective-permute-start.44 = (bf16[512,512]{1,0:T(8,128)(2,1)}, bf16[512,512]{1,0:T(8,128)(2,1)}, u32[]{:S(2)}, u32[]{:S(2)}) collective-permute-start(bf16[512,512]{1,0:T(8,128)(2,1)} %get-tuple-element.873), channel_id=1, source_target_pairs={{0,8},{8,16},{16,24},{24,28},{28,20},{20,12},{12,4},{4,0},{1,9},{9... | collective-permute-start | bytes 1572872 | tf_op jit(solution)/shard_map/ppermute | solution.py:1231
  404.3 20.7 %collective-permute-start.45 = (bf16[512,512]{1,0:T(8,128)(2,1)}, bf16[512,512]{1,0:T(8,128)(2,1)}, u32[]{:S(2)}, u32[]{:S(2)}) collective-permute-start(bf16[512,512]{1,0:T(8,128)(2,1)} %get-tuple-element.874), channel_id=1, source_target_pairs={{8,0},{16,8},{24,16},{28,24},{20,28},{12,20},{4,12},{0,4},{9,1},{1... | collective-permute-start | bytes 1572872 | tf_op jit(solution)/shard_map/ppermute | solution.py:1234
  431.0 21.6 %collective-permute-start.47 = (bf16[512,512]{1,0:T(8,128)(2,1)}, bf16[512,512]{1,0:T(8,128)(2,1)S(1)}, u32[]{:S(2)}, u32[]{:S(2)}) collective-permute-start(bf16[512,512]{1,0:T(8,128)(2,1)} %get-tuple-element.896), channel_id=1, source_target_pairs={{0,8},{8,16},{16,24},{24,28},{28,20},{20,12},{12,4},{4,0},{1,9},{9... | collective-permute-start | bytes 1572872 | tf_op jit(solution)/shard_map/ppermute | solution.py:1231
  432.3 21.3 %collective-permute-start.48 = (bf16[512,512]{1,0:T(8,128)(2,1)}, bf16[512,512]{1,0:T(8,128)(2,1)S(1)}, u32[]{:S(2)}, u32[]{:S(2)}) collective-permute-start(bf16[512,512]{1,0:T(8,128)(2,1)} %get-tuple-element.897), channel_id=1, source_target_pairs={{8,0},{16,8},{24,16},{28,24},{20,28},{12,20},{4,12},{0,4},{9,1},{1... | collective-permute-start | bytes 1572872 | tf_op jit(solution)/shard_map/ppermute | solution.py:1234
  433.0 20.6 %collective-permute-start.51 = (bf16[1,768,512]{2,1,0:T(8,128)(2,1)}, bf16[1,768,512]{2,1,0:T(8,128)(2,1)S(1)}, u32[]{:S(2)}, u32[]{:S(2)}) collective-permute-start(bf16[1,768,512]{2,1,0:T(8,128)(2,1)} %get-tuple-element.900), channel_id=1, source_target_pairs={{0,2},{2,0},{1,3},{3,1},{4,6},{6,4},{5,7},{7,5},{8,10},{10,8},{9,1... | collective-permute-start | bytes 2359304 | tf_op jit(solution)/shard_map/ppermute | solution.py:93
  457.0 34.6 %collective-permute-start.56 = (bf16[2,768,512]{2,1,0:T(8,128)(2,1)S(1)}, bf16[2,768,512]{2,1,0:T(8,128)(2,1)}, u32[]{:S(2)}, u32[]{:S(2)}) collective-permute-start(bf16[2,768,512]{2,1,0:T(8,128)(2,1)S(1)} %copy-done.30), channel_id=1, source_target_pairs={{0,2},{2,0},{1,3},{3,1},{4,6},{6,4},{5,7},{7,5},{8,10},{10,8},{9,1... | collective-permute-start | bytes 4718600 | tf_op jit(solution)/shard_map/ppermute | solution.py:93
  458.6 32.7 %collective-permute-start.54 = (bf16[928,512]{1,0:T(8,128)(2,1)S(1)}, bf16[928,512]{1,0:T(8,128)(2,1)S(1)}, u32[]{:S(2)}, u32[]{:S(2)}) collective-permute-start(bf16[928,512]{1,0:T(8,128)(2,1)S(1)} %pad_maximum_fusion.4), channel_id=1, source_target_pairs={{0,8},{8,16},{16,24},{24,28},{28,20},{20,12},{12,4},{4,0},{1,9},{9... | collective-permute-start | bytes 2850824 | tf_op jit(solution)/shard_map/ppermute | solution.py:1231
  459.2 32.1 %collective-permute-start.55 = (bf16[928,512]{1,0:T(8,128)(2,1)S(1)}, bf16[928,512]{1,0:T(8,128)(2,1)S(1)}, u32[]{:S(2)}, u32[]{:S(2)}) collective-permute-start(bf16[928,512]{1,0:T(8,128)(2,1)S(1)} %pad_maximum_fusion.5), channel_id=1, source_target_pairs={{8,0},{16,8},{24,16},{28,24},{20,28},{12,20},{4,12},{0,4},{9,1},{1... | collective-permute-start | bytes 2850824 | tf_op jit(solution)/shard_map/ppermute | solution.py:1234
  460.7 30.0 %collective-permute-start.52 = (bf16[512,512]{1,0:T(8,128)(2,1)S(1)}, bf16[512,512]{1,0:T(8,128)(2,1)S(1)}, u32[]{:S(2)}, u32[]{:S(2)}) collective-permute-start(bf16[512,512]{1,0:T(8,128)(2,1)S(1)} %get-tuple-element.907), channel_id=1, source_target_pairs={{0,8},{8,16},{16,24},{24,28},{28,20},{20,12},{12,4},{4,0},{1,9},{9... | collective-permute-start | bytes 1572872 | tf_op jit(solution)/shard_map/ppermute | solution.py:1231
  461.3 30.0 %collective-permute-start.53 = (bf16[512,512]{1,0:T(8,128)(2,1)S(1)}, bf16[512,512]{1,0:T(8,128)(2,1)S(1)}, u32[]{:S(2)}, u32[]{:S(2)}) collective-permute-start(bf16[512,512]{1,0:T(8,128)(2,1)S(1)} %get-tuple-element.908), channel_id=1, source_target_pairs={{8,0},{16,8},{24,16},{28,24},{20,28},{12,20},{4,12},{0,4},{9,1},{1... | collective-permute-start | bytes 1572872 | tf_op jit(solution)/shard_map/ppermute | solution.py:1234
  495.3 21.0 %collective-permute-start.57 = (bf16[928,512]{1,0:T(8,128)(2,1)S(1)}, bf16[928,512]{1,0:T(8,128)(2,1)S(1)}, u32[]{:S(2)}, u32[]{:S(2)}) collective-permute-start(bf16[928,512]{1,0:T(8,128)(2,1)S(1)} %get-tuple-element.920), channel_id=1, source_target_pairs={{0,8},{8,16},{16,24},{24,28},{28,20},{20,12},{12,4},{4,0},{1,9},{9... | collective-permute-start | bytes 2850824 | tf_op jit(solution)/shard_map/ppermute | solution.py:1231
  496.4 19.9 %collective-permute-start.58 = (bf16[928,512]{1,0:T(8,128)(2,1)S(1)}, bf16[928,512]{1,0:T(8,128)(2,1)S(1)}, u32[]{:S(2)}, u32[]{:S(2)}) collective-permute-start(bf16[928,512]{1,0:T(8,128)(2,1)S(1)} %get-tuple-element.921), channel_id=1, source_target_pairs={{8,0},{16,8},{24,16},{28,24},{20,28},{12,20},{4,12},{0,4},{9,1},{1... | collective-permute-start | bytes 2850824 | tf_op jit(solution)/shard_map/ppermute | solution.py:1234
  497.4 18.9 %collective-permute-start.60 = (bf16[512,512]{1,0:T(8,128)(2,1)S(1)}, bf16[512,512]{1,0:T(8,128)(2,1)S(1)}, u32[]{:S(2)}, u32[]{:S(2)}) collective-permute-start(bf16[512,512]{1,0:T(8,128)(2,1)S(1)} %fusion.14), channel_id=1, source_target_pairs={{0,2},{2,0},{1,3},{3,1},{4,6},{6,4},{5,7},{7,5},{8,10},{10,8},{9,1... | collective-permute-start | bytes 1572872 | tf_op jit(solution)/shard_map/ppermute | solution.py:93
  499.0 17.3 %collective-permute-start.61 = (bf16[512,512]{1,0:T(8,128)(2,1)S(1)}, bf16[512,512]{1,0:T(8,128)(2,1)S(1)}, u32[]{:S(2)}, u32[]{:S(2)}) collective-permute-start(bf16[512,512]{1,0:T(8,128)(2,1)S(1)} %fusion.14), channel_id=1, source_target_pairs={{0,1},{1,0},{2,3},{3,2},{4,5},{5,4},{6,7},{7,6},{8,9},{9,8},{10,11... | collective-permute-start | bytes 1572872 | tf_op jit(solution)/shard_map/ppermute | solution.py:89
  520.1 19.2 %collective-permute-start.62 = (bf16[928,512]{1,0:T(8,128)(2,1)}, bf16[928,512]{1,0:T(8,128)(2,1)S(1)}, u32[]{:S(2)}, u32[]{:S(2)}) collective-permute-start(bf16[928,512]{1,0:T(8,128)(2,1)} %get-tuple-element.929), channel_id=1, source_target_pairs={{0,8},{8,16},{16,24},{24,28},{28,20},{20,12},{12,4},{4,0},{1,9},{9... | collective-permute-start | bytes 2850824 | tf_op jit(solution)/shard_map/ppermute | solution.py:1231
  521.3 19.6 %collective-permute-start.63 = (bf16[928,512]{1,0:T(8,128)(2,1)}, bf16[928,512]{1,0:T(8,128)(2,1)}, u32[]{:S(2)}, u32[]{:S(2)}) collective-permute-start(bf16[928,512]{1,0:T(8,128)(2,1)} %get-tuple-element.930), channel_id=1, source_target_pairs={{8,0},{16,8},{24,16},{28,24},{20,28},{12,20},{4,12},{0,4},{9,1},{1... | collective-permute-start | bytes 2850824 | tf_op jit(solution)/shard_map/ppermute | solution.py:1234
  549.2 18.1 %collective-permute-start.66 = (bf16[928,512]{1,0:T(8,128)(2,1)S(1)}, bf16[928,512]{1,0:T(8,128)(2,1)S(1)}, u32[]{:S(2)}, u32[]{:S(2)}) collective-permute-start(bf16[928,512]{1,0:T(8,128)(2,1)S(1)} %fusion.12.mine), channel_id=1, source_target_pairs={{0,2},{2,0},{1,3},{3,1},{4,6},{6,4},{5,7},{7,5},{8,10},{10,8},{9,1... | collective-permute-start | bytes 2850824 | tf_op jit(solution)/shard_map/ppermute | solution.py:93
  (57 other events, 503.6 us)

commit v6 on v5

--- a/solution.py
+++ b/solution.py
@@ -76,12 +76,14 @@
         return jnp.where(r < self.n // 2, 2 * r, 2 * (self.n - 1 - r) + 1)
 
 
-def slot(sends, work=None, given=()):
-    names = list(sends)
+def slot(sends, work=None, given=(), free=()):
+    names = [k for k in sends if k not in free]
+    loose = [sends[k][1](sends[k][0]) for k in free]
     tied = held(*[sends[k][0] for k in names], *given)
     moved = [sends[k][1](v) for k, v in zip(names, tied)]
     done = tuple(work(*tied[len(names) :])) if work is not None else ()
-    out = held(*moved, *done)
+    names += free
+    out = held(*moved, *loose, *done)
     return dict(zip(names, out[: len(names)])), out[len(names) :]
 
 
@@ -1299,7 +1301,7 @@
             given = (*shards, *dense_shards)
         elif t == 2:
             work, given = prepare_own, (block_kinds, x_own)
-        arrived, done = slot(sends, work, given)
+        arrived, done = slot(sends, work, given, ("r", "l") if t == 1 else ())
         if t == 1:
             kinds_other = arrived["k"]
             pieces.add(0, 0, 0, own)

time: 586 us -> 581 us (level)
  transfers between devices with their start and end apart: 69 -> 69, of which waited for: 28 -> 27; matrix products, arithmetic and copies ran while one was open for 5% -> 6% of each run, Pallas kernels for 40% -> 40%
where the time goes in v6:
time: 581 us; the launch traced here: 571 us
  Pallas kernels  264 us (45%)
  waiting for transfers between devices  178 us (31%)
  starting transfers between devices  63.6 us (11%)
  other arithmetic  41.7 us (7%)
  local copies, waits for them, and re-layouts  14.7 us (3%)
  matrix products  7.03 us (1%)
    ppermute x17, waiting for transfers between devices, right(): return lax.ppermute(v, 'dp', ring.right)  93.8 us
    pallas_call x3, Pallas kernels, dense(): pl.pallas_call(kernel, grid_spec=pltpu.PrefetchScalarGridSpec(num_scalar_...  65.3 us
    ppermute x15, waiting for transfers between devices, swap_y(): return lax.ppermute(v, 'group', Y_SWAP)  52.3 us
    pallas_call x2, Pallas kernels, grow_backward(): pl.pallas_call(kernel, out_shape=[jax.ShapeDtypeStruct((groups, length, w...  25.2 us
    pallas_call x1, Pallas kernels, dense_weights(): pl.pallas_call(kernel, grid=(chunks,), out_shape=outlet.shapes(), in_spec...  24.4 us
    pallas_call x2, Pallas kernels, season_kernel(): pl.pallas_call(kernel, grid=(groups,), out_shape=shapes, in_specs=[smem_s...  22.4 us
    pallas_call x2, Pallas kernels, grow_forward(): pl.pallas_call(kernel, out_shape=shapes, in_specs=[smem_spec()] + [vmem_s...  22.1 us
    ppermute x3, waiting for transfers between devices, exchange(): return lambda v: lax.ppermute(v, axis, [(i, i ^ step) for i in range(size)])  21.3 us
  transfers between devices with their start and end apart: 69, of which 27 were waited for; matrix products, arithmetic and copies ran while one was open for 6% of the time, Pallas kernels for 40%

profile of v6, /device:TPU:0, one launch (start us, length us, event | category | flops | bytes accessed | tf_op | source)
XLA Modules:
  0.0 570.6 jit_solution(12246476123965763688)
XLA Ops:
  1.3 3.6 own_half.1.refs_0_
  5.0 3.0 collective-permute-start.4
  8.3 3.1 fusion.34
  15.4 3.4 sibling_half.1.refs_1_
  18.8 11.9 %collective-permute-done.1 = f32[12]{0:T(128)S(1)} collective-permute-done((f32[12]{0:T(128)S(1)}, f32[12]{0:T(128)S(1)}, u32[]{:S(2)}, u32[]{:S(2)}) %collective-permute-start.1) | collective-permute-done | bytes 80 | tf_op jit(solution)/shard_map/ppermute | solution.py:95
  30.7 19.2 %collective-permute-done.2 = f32[3,512]{1,0:T(4,128)} collective-permute-done((f32[3,512]{1,0:T(4,128)S(1)}, f32[3,512]{1,0:T(4,128)}, u32[]{:S(2)}, u32[]{:S(2)}) %collective-permute-start.2) | collective-permute-done | bytes 6176 | tf_op jit(solution)/shard_map/ppermute | solution.py:1198
  54.1 8.1 %fusion.26.step_ref = s32[768,1]{1,0:T(8,128)} fusion(s32[]{:T(128)S(6)} %select_n.225, s32[]{:T(128)S(6)} %sign.30, s32[]{:T(128)S(6)} %select_n.228, s32[]{:T(128)S(6)} %select_n.226), kind=kLoop, calls=%fused_computation.57 | loop fusion | flops 12288 | bytes 3088 | tf_op jit(solution)/shard_map/add | solution.py:1262
  62.2 12.8 %season_trend.1 = (f32[3,768,512]{2,1,0:T(8,128)}, bf16[3,768,512]{2,1,0:T(8,128)(2,1)}, bf16[3,768,768]{2,1,0:T(8,128)(2,1)}, bf16[3,768,512]{2,1,0:T(8,128)(2,1)}, bf16[768,768]{1,0:T(8,128)(2,1)}) custom-call(s32[12]{0:T(128)} %kinds_own.1, s32[768,1]{1,0:T(8,128)} %fusion.26.step_ref, bf16[3,768,512]{2,1,0:T(8,128)(2,1)} %bitcast.93), custom_call_target="tpu_custom_call" | custom-call | flops 5435817984 | bytes 14155776 | tf_op jit(solution)/shard_map/season_trend/pallas_call | solution.py:334
  75.0 15.8 %collective-permute-done.5.refs_6_ = bf16[1792,512]{1,0:T(8,128)(2,1)} collective-permute-done((bf16[1792,512]{1,0:T(8,128)(2,1)}, bf16[1792,512]{1,0:T(8,128)(2,1)}, u32[]{:S(2)}, u32[]{:S(2)}) %collective-permute-start.5) | collective-permute-done | bytes 1835040 | tf_op jit(solution)/shard_map/ppermute | solution.py:1233
  97.3 16.1 %collective-permute-done.14 = bf16[768,512]{1,0:T(8,128)(2,1)S(1)} collective-permute-done((bf16[768,512]{1,0:T(8,128)(2,1)}, bf16[768,512]{1,0:T(8,128)(2,1)S(1)}, u32[]{:S(2)}, u32[]{:S(2)}) %collective-permute-start.14) | collective-permute-done | bytes 786464 | tf_op jit(solution)/shard_map/ppermute | solution.py:95
  113.4 17.5 %collective-permute-done.10.refs_10_ = bf16[1792,512]{1,0:T(8,128)(2,1)} collective-permute-done((bf16[1792,512]{1,0:T(8,128)(2,1)}, bf16[1792,512]{1,0:T(8,128)(2,1)}, u32[]{:S(2)}, u32[]{:S(2)}) %collective-permute-start.10) | collective-permute-done | bytes 1835040 | tf_op jit(solution)/shard_map/ppermute | solution.py:1233
  132.4 2.7 fusion.35
  140.0 3.0 pad_maximum_fusion.x_ref
  143.0 9.7 %season.1 = (f32[3,768,512]{2,1,0:T(8,128)}, bf16[3,768,512]{2,1,0:T(8,128)(2,1)}) custom-call(s32[12]{0:T(128)} %convert_element_type.216.kinds_ref.kinds_other, s32[768,1]{1,0:T(8,128)} %fusion.26.step_ref, bf16[3,768,512]{2,1,0:T(8,128)(2,1)} %pad_maximum_fusion.x_ref), custom_call_target="tpu_custom_call" | custom-call | flops 5435817984 | bytes 14155776 | tf_op jit(solution)/shard_map/season/pallas_call | solution.py:334
  156.4 2.1 collective-permute-done.22
  162.7 19.1 %shrink_forward.1 = (f32[384,512]{1,0:T(8,128)}, f32[384,512]{1,0:T(8,128)}, bf16[384,512]{1,0:T(8,128)(2,1)}, s32[384,1]{1,0:T(8,128)}, bf16[16,384,512]{2,1,0:T(8,128)(2,1)}, /*index=5*/bf16[14336,512]{1,0:T(8,128)(2,1)}) custom-call(s32[10]{0:T(128)} %stack.84.where, s32[12]{0:T(128)} %kinds_own.1, s32[12]{0:T(128)} %convert_element_type.216.kinds_ref.kinds_other, ...), custom_call_target="tpu_custom_call" | custom-call | flops 5637144576 | bytes 29360128 | tf_op jit(solution)/shard_map/shrink_forward/pallas_call | solution.py:423
  184.7 11.5 %grow_forward.2 = (bf16[1,768,512]{2,1,0:T(8,128)(2,1)}, bf16[1,768,512]{2,1,0:T(8,128)(2,1)}, bf16[1,768,512]{2,1,0:T(8,128)(2,1)}, f32[3,768,512]{2,1,0:T(8,128)}, bf16[8192,512]{1,0:T(8,128)(2,1)}) custom-call(s32[10]{0:T(128)} %stack.84.where, f32[1,512]{1,0:T(1,128)} %get-tuple-element.997.gain_ref, bf16[768,768]{1,0:T(8,128)(2,1)} %get-tuple-element.553.order_ref, ...), custom_call_target="tpu_custom_call" | custom-call | flops 3019898880 | bytes 24903680 | tf_op jit(solution)/shard_map/grow_forward/pallas_call | solution.py:525
  196.2 2.5 collective-permute-start.27
  199.2 5.8 %dense_whole.1 = (bf16[1024,512]{1,0:T(8,128)(2,1)}, bf16[2048,512]{1,0:T(8,128)(2,1)}, bf16[512,512]{1,0:T(8,128)(2,1)}, bf16[512,2048]{1,0:T(8,128)(2,1)}) custom-call(s32[10]{0:T(128)} %stack.84.where, bf16[1792,512]{1,0:T(8,128)(2,1)} %own_half.1.refs_0_, bf16[1792,512]{1,0:T(8,128)(2,1)} %sibling_half.1.refs_1_, ...), custom_call_target="tpu_custom_call" | custom-call | bytes 11534336 | tf_op jit(solution)/shard_map/dense_whole/pallas_call | solution.py:967
  205.1 10.6 %grow_forward.3 = (bf16[1,768,512]{2,1,0:T(8,128)(2,1)}, bf16[1,768,512]{2,1,0:T(8,128)(2,1)}, bf16[1,768,512]{2,1,0:T(8,128)(2,1)}, f32[3,768,512]{2,1,0:T(8,128)}) custom-call(s32[10]{0:T(128)} %stack.84.where, f32[1,512]{1,0:T(1,128)} %get-tuple-element.997.gain_ref, bf16[768,768]{1,0:T(8,128)(2,1)} %get-tuple-element.553.order_ref, ...), custom_call_target="tpu_custom_call" | custom-call | flops 3019898880 | bytes 24903680 | tf_op jit(solution)/shard_map/grow_forward/pallas_call | solution.py:525
  218.6 21.7 %dense.3 = (bf16[768,2048]{1,0:T(8,128)(2,1)}, bf16[768,2048]{1,0:T(8,128)(2,1)}, bf16[768,512]{1,0:T(8,128)(2,1)}, bf16[768,512]{1,0:T(8,128)(2,1)}, bf16[768,5...) custom-call(s32[10]{0:T(128)} %stack.84.where, ...), custom_call_target="tpu_custom_call" | custom-call | flops 8858370048 | bytes 33554432 | tf_op jit(solution)/shard_map/dense/pallas_call | solution.py:1069
  240.7 21.9 %dense.4 = (bf16[768,2048]{1,0:T(8,128)(2,1)}, bf16[768,2048]{1,0:T(8,128)(2,1)}, bf16[768,512]{1,0:T(8,128)(2,1)}, bf16[768,512]{1,0:T(8,128)(2,1)}, bf16[768,5...) custom-call(s32[10]{0:T(128)} %stack.84.where, ...), custom_call_target="tpu_custom_call" | custom-call | flops 8858370048 | bytes 33554432 | tf_op jit(solution)/shard_map/dense/pallas_call | solution.py:1069
  264.4 21.7 %dense.5 = (bf16[768,2048]{1,0:T(8,128)(2,1)}, bf16[768,2048]{1,0:T(8,128)(2,1)}, bf16[768,512]{1,0:T(8,128)(2,1)}, bf16[768,512]{1,0:T(8,128)(2,1)}, bf16[768,5...) custom-call(s32[10]{0:T(128)} %stack.84.where, ...), custom_call_target="tpu_custom_call" | custom-call | flops 8858370048 | bytes 33554432 | tf_op jit(solution)/shard_map/dense/pallas_call | solution.py:1069
  288.2 12.7 %grow_backward.2 = (bf16[3,768,512]{2,1,0:T(8,128)(2,1)}, f32[192,512]{1,0:T(8,128)}, f32[3,768,512]{2,1,0:T(8,128)}, f32[1,512]{1,0:T(1,128)}) custom-call(s32[10]{0:T(128)} %stack.84.where, f32[1,512]{1,0:T(1,128)} %get-tuple-element.997.gain_ref, bf16[768,768]{1,0:T(8,128)(2,1)} %get-tuple-element.553.order_ref, f32[3,768,512]{2,1,0:T(8,128)} %get-tuple-element.757.up_in, ...), custom_call_target="tpu_custom_call" | custom-call | flops 3019898880 | bytes 29622272 | tf_op jit(solution)/shard_map/grow_backward/pallas_call | solution.py:601
  300.9 24.4 %dense_weights.1 = (bf16[1,384,512]{2,1,0:T(8,128)(2,1)}, bf16[2,384,512]{2,1,0:T(8,128)(2,1)}, bf16[2,384,512]{2,1,0:T(8,128)(2,1)}, bf16[2,384,512]{2,1,0:T(8,...) custom-call(s32[10]{0:T(128)} %stack.84.where, s32[8]{0:T(128)} %compare_select_fusion.6.places_ref, ...), custom_call_target="tpu_custom_call" | custom-call | flops 13287555072 | bytes 47185920 | tf_op jit(solution)/shard_map/dense_weights/pallas_call | solution.py:1177
  325.4 12.5 %grow_backward.3 = (bf16[3,768,512]{2,1,0:T(8,128)(2,1)}, f32[192,512]{1,0:T(8,128)}, f32[3,768,512]{2,1,0:T(8,128)}, f32[1,512]{1,0:T(1,128)}) custom-call(s32[10]{0:T(128)} %stack.84.where, f32[1,512]{1,0:T(1,128)} %get-tuple-element.997.gain_ref, bf16[768,768]{1,0:T(8,128)(2,1)} %get-tuple-element.553.order_ref, f32[3,768,512]{2,1,0:T(8,128)} %get-tuple-element.774.up_in, ...), custom_call_target="tpu_custom_call" | custom-call | flops 3019898880 | bytes 29622272 | tf_op jit(solution)/shard_map/grow_backward/pallas_call | solution.py:601
  340.3 9.6 %grow_weight.1 = (bf16[1,512,512]{2,1,0:T(8,128)(2,1)}, bf16[2,512,512]{2,1,0:T(8,128)(2,1)}, bf16[2,512,512]{2,1,0:T(8,128)(2,1)}, bf16[2,512,512]{2,1,0:T(8,12...) custom-call(s32[10]{0:T(128)} %stack.84.where, s32[8]{0:T(128)} %compare_select_fusion.6.places_ref, ...), custom_call_target="tpu_custom_call" | custom-call | flops 2415919104 | bytes 8388608 | tf_op jit(solution)/shard_map/grow_weight/pallas_call | solution.py:685
  352.4 2.5 ring_add.6
  357.1 10.5 %shrink_backward.1 = (bf16[384,512]{1,0:T(8,128)(2,1)}, bf16[384,512]{1,0:T(8,128)(2,1)}, f32[1,512]{1,0:T(1,128)}) custom-call(s32[10]{0:T(128)} %stack.84.where, s32[384,1]{1,0:T(8,128)} %get-tuple-element.811.age_ref, f32[1,512]{1,0:T(1,128)} %get-tuple-element.997.gain_ref, f32[192,512]{1,0:T(8,128)} %get-tuple-element.812.b0, ...), custom_call_target="tpu_custom_call" | custom-call | flops 3221225472 | bytes 8388608 | tf_op jit(solution)/shard_map/shrink_backward/pallas_call | solution.py:736
  369.0 3.1 ring_add.7
  376.2 16.5 %shrink_weight.1 = (bf16[1,928,512]{2,1,0:T(8,128)(2,1)}, bf16[2,928,512]{2,1,0:T(8,128)(2,1)}, bf16[2,928,512]{2,1,0:T(8,128)(2,1)}, bf16[2,928,512]{2,1,0:T(8,...) custom-call(s32[10]{0:T(128)} %stack.84.where, s32[8]{0:T(128)} %compare_select_fusion.6.places_ref, ...), custom_call_target="tpu_custom_call" | custom-call | flops 5637144576 | bytes 31457280 | tf_op jit(solution)/shard_map/shrink_weight/pallas_call | solution.py:796
  393.5 3.8 ring_add.8
  401.3 15.0 %season_backward.1 = (bf16[3,768,512]{2,1,0:T(8,128)(2,1)}, bf16[1,768,512]{2,1,0:T(8,128)(2,1)}, bf16[2,768,512]{2,1,0:T(8,128)(2,1)}) custom-call(s32[10]{0:T(128)} %stack.84.where, bf16[768,768]{1,0:T(8,128)(2,1)} %get-tuple-element.553.order_ref, bf16[384,512]{1,0:T(8,128)(2,1)} %get-tuple-element.872.pre_ref, ...), custom_call_target="tpu_custom_call" | custom-call | flops 6039797760 | bytes 36700160 | tf_op jit(solution)/shard_map/season_backward/pallas_call | solution.py:841
  416.4 3.9 collective-permute-done.44.refs_2_
  421.3 3.9 ring_add.9
  430.9 2.6 convert_add_fusion.1
  433.7 5.6 collective-permute-done.49
  440.3 8.5 %collective-permute-done.47 = bf16[512,512]{1,0:T(8,128)(2,1)S(1)} collective-permute-done((bf16[512,512]{1,0:T(8,128)(2,1)}, bf16[512,512]{1,0:T(8,128)(2,1)S(1)}, u32[]{:S(2)}, u32[]{:S(2)}) %collective-permute-start.47) | collective-permute-done | bytes 524320 | tf_op jit(solution)/shard_map/ppermute | solution.py:1233
  459.8 26.7 %collective-permute-done.52 = bf16[512,512]{1,0:T(8,128)(2,1)S(1)} collective-permute-done((bf16[512,512]{1,0:T(8,128)(2,1)S(1)}, bf16[512,512]{1,0:T(8,128)(2,1)S(1)}, u32[]{:S(2)}, u32[]{:S(2)}) %collective-permute-start.52) | collective-permute-done | bytes 524320 | tf_op jit(solution)/shard_map/ppermute | solution.py:1233
  488.9 2.4 fusion.8
  495.4 16.9 %collective-permute-done.59 = bf16[384,512]{1,0:T(8,128)(2,1)S(1)} collective-permute-done((bf16[384,512]{1,0:T(8,128)(2,1)S(1)}, bf16[384,512]{1,0:T(8,128)(2,1)S(1)}, u32[]{:S(2)}, u32[]{:S(2)}) %collective-permute-start.59) | collective-permute-done | bytes 393248 | tf_op jit(solution)/shard_map/ppermute | solution.py:95
  512.5 3.6 fusion.7
  518.8 2.1 collective-permute-done.64
  520.9 14.1 %collective-permute-done.62 = bf16[928,512]{1,0:T(8,128)(2,1)S(1)} collective-permute-done((bf16[928,512]{1,0:T(8,128)(2,1)}, bf16[928,512]{1,0:T(8,128)(2,1)S(1)}, u32[]{:S(2)}, u32[]{:S(2)}) %collective-permute-start.62) | collective-permute-done | bytes 950304 | tf_op jit(solution)/shard_map/ppermute | solution.py:1233
  535.9 2.0 fusion.12.mine
  549.2 7.0 %add_convert_fusion = bf16[3,768,512]{2,1,0:T(8,128)(2,1)} fusion(bf16[3,768,512]{2,1,0:T(8,128)(2,1)S(1)} %copy-done.30, bf16[3,768,768]{2,1,0:T(8,128)(2,1)} %get-tuple-element.946, f32[1,768,512]{2,1,0:T(8,128)S(1)} %bitcast.117, f32[1,768,512]{2,1,0:T(8,128)S(1)} %bitcast.116, f32[1,768,512]{2,1,0:T(8,128)S(1)} %bitcast.115, ...), kind=kOutput, calls=%fused_computation.3 | convolution fusion | flops 1829634048 | bytes 15335424 | tf_op jit(solution)/shard_map/gij,gid->gjd/dot_general | solution.py:1552
  556.3 5.6 collective-permute-done.66.over_y
  564.6 5.6 give_out.1
  (266 shorter events, 100.9 us)
Async XLA Ops:
  5.0 44.9 %collective-permute-start.4 = (bf16[1792,512]{1,0:T(8,128)(2,1)}, bf16[1792,512]{1,0:T(8,128)(2,1)}, u32[]{:S(2)}, u32[]{:S(2)}) collective-permute-start(bf16[1792,512]{1,0:T(8,128)(2,1)} %own_half.1.refs_0_), channel_id=1, source_target_pairs={{8,0},{16,8},{24,16},{28,24},{20,28},{12,20},{4,12},{0,4},{9,1},{1... | collective-permute-start | bytes 5505032 | tf_op jit(solution)/shard_map/ppermute | solution.py:1236
  7.9 41.9 %collective-permute-start.3 = (bf16[1792,512]{1,0:T(8,128)(2,1)}, bf16[1792,512]{1,0:T(8,128)(2,1)}, u32[]{:S(2)}, u32[]{:S(2)}) collective-permute-start(bf16[1792,512]{1,0:T(8,128)(2,1)} %own_half.1.refs_0_), channel_id=1, source_target_pairs={{0,8},{8,16},{16,24},{24,28},{28,20},{20,12},{12,4},{4,0},{1,9},{9... | collective-permute-start | bytes 5505032 | tf_op jit(solution)/shard_map/ppermute | solution.py:1233
  11.4 38.5 %collective-permute-start = (bf16[768,512]{1,0:T(8,128)(2,1)}, bf16[768,512]{1,0:T(8,128)(2,1)}, u32[]{:S(2)}, u32[]{:S(2)}) collective-permute-start(bf16[768,512]{1,0:T(8,128)(2,1)} %get-tuple-element.492), channel_id=1, source_target_pairs={{0,2},{2,0},{1,3},{3,1},{4,6},{6,4},{5,7},{7,5},{8,10},{10,8},{9,1... | collective-permute-start | bytes 2359304 | tf_op jit(solution)/shard_map/ppermute | solution.py:95
  13.3 36.5 %collective-permute-start.2 = (f32[3,512]{1,0:T(4,128)S(1)}, f32[3,512]{1,0:T(4,128)}, u32[]{:S(2)}, u32[]{:S(2)}) collective-permute-start(f32[3,512]{1,0:T(4,128)S(1)} %dynamic_update_slice.5), channel_id=1, source_target_pairs={{0,4},{4,0},{8,12},{12,8},{16,20},{20,16},{24,28},{28,24},{1,5},{5... | collective-permute-start | bytes 18440 | tf_op jit(solution)/shard_map/ppermute | solution.py:1198
  49.9 40.9 %collective-permute-start.5 = (bf16[1792,512]{1,0:T(8,128)(2,1)}, bf16[1792,512]{1,0:T(8,128)(2,1)}, u32[]{:S(2)}, u32[]{:S(2)}) collective-permute-start(bf16[1792,512]{1,0:T(8,128)(2,1)} %collective-permute-done.3.refs_2_), channel_id=1, source_target_pairs={{0,8},{8,16},{16,24},{24,28},{28,20},{20,12},{12,4},{4,0},{1,9},{9... | collective-permute-start | bytes 5505032 | tf_op jit(solution)/shard_map/ppermute | solution.py:1233
  50.1 40.9 %collective-permute-start.6 = (bf16[1792,512]{1,0:T(8,128)(2,1)}, bf16[1792,512]{1,0:T(8,128)(2,1)}, u32[]{:S(2)}, u32[]{:S(2)}) collective-permute-start(bf16[1792,512]{1,0:T(8,128)(2,1)} %collective-permute-done.4.refs_3_), channel_id=1, source_target_pairs={{8,0},{16,8},{24,16},{28,24},{20,28},{12,20},{4,12},{0,4},{9,1},{1... | collective-permute-start | bytes 5505032 | tf_op jit(solution)/shard_map/ppermute | solution.py:1236
  52.0 39.0 %collective-permute-start.7 = (bf16[1792,512]{1,0:T(8,128)(2,1)}, bf16[1792,512]{1,0:T(8,128)(2,1)}, u32[]{:S(2)}, u32[]{:S(2)}) collective-permute-start(bf16[1792,512]{1,0:T(8,128)(2,1)} %collective-permute-done.3.refs_2_), channel_id=1, source_target_pairs={{0,1},{1,0},{2,3},{3,2},{4,5},{5,4},{6,7},{7,6},{8,9},{9,8},{10,11... | collective-permute-start | bytes 5505032 | tf_op jit(solution)/shard_map/ppermute | solution.py:91
  52.0 39.0 %collective-permute-start.8 = (bf16[1792,512]{1,0:T(8,128)(2,1)}, bf16[1792,512]{1,0:T(8,128)(2,1)}, u32[]{:S(2)}, u32[]{:S(2)}) collective-permute-start(bf16[1792,512]{1,0:T(8,128)(2,1)} %collective-permute-done.4.refs_3_), channel_id=1, source_target_pairs={{0,1},{1,0},{2,3},{3,2},{4,5},{5,4},{6,7},{7,6},{8,9},{9,8},{10,11... | collective-permute-start | bytes 5505032 | tf_op jit(solution)/shard_map/ppermute | solution.py:91
  52.5 22.5 %collective-permute-start.9 = (bf16[768,512]{1,0:T(8,128)(2,1)}, bf16[768,512]{1,0:T(8,128)(2,1)}, u32[]{:S(2)}, u32[]{:S(2)}) collective-permute-start(bf16[768,512]{1,0:T(8,128)(2,1)} %get-tuple-element.512), channel_id=1, source_target_pairs={{0,2},{2,0},{1,3},{3,1},{4,6},{6,4},{5,7},{7,5},{8,10},{10,8},{9,1... | collective-permute-start | bytes 2359304 | tf_op jit(solution)/shard_map/ppermute | solution.py:95
  91.0 39.9 %collective-permute-start.10 = (bf16[1792,512]{1,0:T(8,128)(2,1)}, bf16[1792,512]{1,0:T(8,128)(2,1)}, u32[]{:S(2)}, u32[]{:S(2)}) collective-permute-start(bf16[1792,512]{1,0:T(8,128)(2,1)} %collective-permute-done.5.refs_6_), channel_id=1, source_target_pairs={{0,8},{8,16},{16,24},{24,28},{28,20},{20,12},{12,4},{4,0},{1,9},{9... | collective-permute-start | bytes 5505032 | tf_op jit(solution)/shard_map/ppermute | solution.py:1233
  92.6 39.8 %collective-permute-start.11 = (bf16[1792,512]{1,0:T(8,128)(2,1)}, bf16[1792,512]{1,0:T(8,128)(2,1)}, u32[]{:S(2)}, u32[]{:S(2)}) collective-permute-start(bf16[1792,512]{1,0:T(8,128)(2,1)} %collective-permute-done.6.refs_7_), channel_id=1, source_target_pairs={{8,0},{16,8},{24,16},{28,24},{20,28},{12,20},{4,12},{0,4},{9,1},{1... | collective-permute-start | bytes 5505032 | tf_op jit(solution)/shard_map/ppermute | solution.py:1236
  93.2 39.2 %collective-permute-start.12 = (bf16[1792,512]{1,0:T(8,128)(2,1)}, bf16[1792,512]{1,0:T(8,128)(2,1)}, u32[]{:S(2)}, u32[]{:S(2)}) collective-permute-start(bf16[1792,512]{1,0:T(8,128)(2,1)} %collective-permute-done.5.refs_6_), channel_id=1, source_target_pairs={{0,1},{1,0},{2,3},{3,2},{4,5},{5,4},{6,7},{7,6},{8,9},{9,8},{10,11... | collective-permute-start | bytes 5505032 | tf_op jit(solution)/shard_map/ppermute | solution.py:91
  93.2 39.2 %collective-permute-start.13 = (bf16[1792,512]{1,0:T(8,128)(2,1)}, bf16[1792,512]{1,0:T(8,128)(2,1)}, u32[]{:S(2)}, u32[]{:S(2)}) collective-permute-start(bf16[1792,512]{1,0:T(8,128)(2,1)} %collective-permute-done.6.refs_7_), channel_id=1, source_target_pairs={{0,1},{1,0},{2,3},{3,2},{4,5},{5,4},{6,7},{7,6},{8,9},{9,8},{10,11... | collective-permute-start | bytes 5505032 | tf_op jit(solution)/shard_map/ppermute | solution.py:91
  93.7 19.7 %collective-permute-start.14 = (bf16[768,512]{1,0:T(8,128)(2,1)}, bf16[768,512]{1,0:T(8,128)(2,1)S(1)}, u32[]{:S(2)}, u32[]{:S(2)}) collective-permute-start(bf16[768,512]{1,0:T(8,128)(2,1)} %get-tuple-element.526), channel_id=1, source_target_pairs={{0,2},{2,0},{1,3},{3,1},{4,6},{6,4},{5,7},{7,5},{8,10},{10,8},{9,1... | collective-permute-start | bytes 2359304 | tf_op jit(solution)/shard_map/ppermute | solution.py:95
  135.1 17.5 %collective-permute-start.17 = (bf16[1792,512]{1,0:T(8,128)(2,1)}, bf16[1792,512]{1,0:T(8,128)(2,1)}, u32[]{:S(2)}, u32[]{:S(2)}) collective-permute-start(bf16[1792,512]{1,0:T(8,128)(2,1)} %collective-permute-done.10.refs_10_), channel_id=1, source_target_pairs={{0,1},{1,0},{2,3},{3,2},{4,5},{5,4},{6,7},{7,6},{8,9},{9,8},{10,11... | collective-permute-start | bytes 5505032 | tf_op jit(solution)/shard_map/ppermute | solution.py:91
  135.1 17.5 %collective-permute-start.18 = (bf16[1792,512]{1,0:T(8,128)(2,1)}, bf16[1792,512]{1,0:T(8,128)(2,1)}, u32[]{:S(2)}, u32[]{:S(2)}) collective-permute-start(bf16[1792,512]{1,0:T(8,128)(2,1)} %collective-permute-done.11.refs_11_), channel_id=1, source_target_pairs={{0,1},{1,0},{2,3},{3,2},{4,5},{5,4},{6,7},{7,6},{8,9},{9,8},{10,11... | collective-permute-start | bytes 5505032 | tf_op jit(solution)/shard_map/ppermute | solution.py:91
  160.7 21.1 %collective-permute-start.23 = (bf16[448,512]{1,0:T(8,128)(2,1)}, bf16[448,512]{1,0:T(8,128)(2,1)}, u32[]{:S(2)}, u32[]{:S(2)}) collective-permute-start(bf16[448,512]{1,0:T(8,128)(2,1)} %get-tuple-element.565), channel_id=1, source_target_pairs={{0,8},{8,16},{16,24},{24,28},{28,20},{20,12},{12,4},{4,0},{1,9},{9... | collective-permute-start | bytes 1376264 | tf_op jit(solution)/shard_map/ppermute | solution.py:1233
  161.1 20.7 %collective-permute-start.24 = (bf16[448,512]{1,0:T(8,128)(2,1)}, bf16[448,512]{1,0:T(8,128)(2,1)}, u32[]{:S(2)}, u32[]{:S(2)}) collective-permute-start(bf16[448,512]{1,0:T(8,128)(2,1)} %get-tuple-element.566), channel_id=1, source_target_pairs={{8,0},{16,8},{24,16},{28,24},{20,28},{12,20},{4,12},{0,4},{9,1},{1... | collective-permute-start | bytes 1376264 | tf_op jit(solution)/shard_map/ppermute | solution.py:1236
  196.2 20.7 %collective-permute-start.27 = (bf16[768,512]{1,0:T(8,128)(2,1)}, bf16[768,512]{1,0:T(8,128)(2,1)}, u32[]{:S(2)}, u32[]{:S(2)}) collective-permute-start(bf16[768,512]{1,0:T(8,128)(2,1)} %bitcast.113), channel_id=1, source_target_pairs={{0,2},{2,0},{1,3},{3,1},{4,6},{6,4},{5,7},{7,5},{8,10},{10,8},{9,1... | collective-permute-start | bytes 2359304 | tf_op jit(solution)/shard_map/ppermute | solution.py:95
  216.9 23.5 %collective-permute-start.28 = (bf16[768,512]{1,0:T(8,128)(2,1)}, bf16[768,512]{1,0:T(8,128)(2,1)}, u32[]{:S(2)}, u32[]{:S(2)}) collective-permute-start(bf16[768,512]{1,0:T(8,128)(2,1)} %bitcast.112), channel_id=1, source_target_pairs={{0,2},{2,0},{1,3},{3,1},{4,6},{6,4},{5,7},{7,5},{8,10},{10,8},{9,1... | collective-permute-start | bytes 2359304 | tf_op jit(solution)/shard_map/ppermute | solution.py:95
  240.4 22.2 %collective-permute-start.29 = (bf16[768,512]{1,0:T(8,128)(2,1)}, bf16[768,512]{1,0:T(8,128)(2,1)}, u32[]{:S(2)}, u32[]{:S(2)}) collective-permute-start(bf16[768,512]{1,0:T(8,128)(2,1)} %bitcast.111), channel_id=1, source_target_pairs={{0,2},{2,0},{1,3},{3,1},{4,6},{6,4},{5,7},{7,5},{8,10},{10,8},{9,1... | collective-permute-start | bytes 2359304 | tf_op jit(solution)/shard_map/ppermute | solution.py:95
  262.6 23.5 %collective-permute-start.30 = (bf16[768,512]{1,0:T(8,128)(2,1)}, bf16[768,512]{1,0:T(8,128)(2,1)}, u32[]{:S(2)}, u32[]{:S(2)}) collective-permute-start(bf16[768,512]{1,0:T(8,128)(2,1)} %get-tuple-element.689), channel_id=1, source_target_pairs={{0,2},{2,0},{1,3},{3,1},{4,6},{6,4},{5,7},{7,5},{8,10},{10,8},{9,1... | collective-permute-start | bytes 2359304 | tf_op jit(solution)/shard_map/ppermute | solution.py:95
  286.1 39.2 %collective-permute-start.31 = (bf16[768,512]{1,0:T(8,128)(2,1)}, bf16[768,512]{1,0:T(8,128)(2,1)}, u32[]{:S(2)}, u32[]{:S(2)}) collective-permute-start(bf16[768,512]{1,0:T(8,128)(2,1)} %get-tuple-element.728), channel_id=1, source_target_pairs={{0,2},{2,0},{1,3},{3,1},{4,6},{6,4},{5,7},{7,5},{8,10},{10,8},{9,1... | collective-permute-start | bytes 2359304 | tf_op jit(solution)/shard_map/ppermute | solution.py:95
  286.5 38.8 %collective-permute-start.32 = (bf16[768,512]{1,0:T(8,128)(2,1)}, bf16[768,512]{1,0:T(8,128)(2,1)}, u32[]{:S(2)}, u32[]{:S(2)}) collective-permute-start(bf16[768,512]{1,0:T(8,128)(2,1)} %get-tuple-element.729), channel_id=1, source_target_pairs={{0,2},{2,0},{1,3},{3,1},{4,6},{6,4},{5,7},{7,5},{8,10},{10,8},{9,1... | collective-permute-start | bytes 2359304 | tf_op jit(solution)/shard_map/ppermute | solution.py:95
  372.1 20.5 %collective-permute-start.40 = (bf16[256,512]{1,0:T(8,128)(2,1)}, bf16[256,512]{1,0:T(8,128)(2,1)}, u32[]{:S(2)}, u32[]{:S(2)}) collective-permute-start(bf16[256,512]{1,0:T(8,128)(2,1)} %get-tuple-element.839), channel_id=1, source_target_pairs={{0,8},{8,16},{16,24},{24,28},{28,20},{20,12},{12,4},{4,0},{1,9},{9... | collective-permute-start | bytes 786440 | tf_op jit(solution)/shard_map/ppermute | solution.py:1233
  373.4 19.2 %collective-permute-start.41 = (bf16[256,512]{1,0:T(8,128)(2,1)}, bf16[256,512]{1,0:T(8,128)(2,1)}, u32[]{:S(2)}, u32[]{:S(2)}) collective-permute-start(bf16[256,512]{1,0:T(8,128)(2,1)} %get-tuple-element.840), channel_id=1, source_target_pairs={{8,0},{16,8},{24,16},{28,24},{20,28},{12,20},{4,12},{0,4},{9,1},{1... | collective-permute-start | bytes 786440 | tf_op jit(solution)/shard_map/ppermute | solution.py:1236
  374.2 18.5 %collective-permute-start.38 = (bf16[384,512]{1,0:T(8,128)(2,1)}, bf16[384,512]{1,0:T(8,128)(2,1)S(1)}, u32[]{:S(2)}, u32[]{:S(2)}) collective-permute-start(bf16[384,512]{1,0:T(8,128)(2,1)} %get-tuple-element.837), channel_id=1, source_target_pairs={{0,8},{8,16},{16,24},{24,28},{28,20},{20,12},{12,4},{4,0},{1,9},{9... | collective-permute-start | bytes 1179656 | tf_op jit(solution)/shard_map/ppermute | solution.py:1233
  397.2 24.1 %collective-permute-start.46 = (bf16[8,928,512]{2,1,0:T(8,128)(2,1)}, bf16[8,928,512]{2,1,0:T(8,128)(2,1)}, u32[]{:S(2)}, u32[]{:S(2)}) collective-permute-start(bf16[8,928,512]{2,1,0:T(8,128)(2,1)} %get-tuple-element.871), channel_id=1, source_target_pairs={{0,1},{1,0},{2,3},{3,2},{4,5},{5,4},{6,7},{7,6},{8,9},{9,8},{10,11... | collective-permute-start | bytes 22806536 | tf_op jit(solution)/shard_map/ppermute | solution.py:91
  397.2 19.1 %collective-permute-start.42 = (bf16[384,512]{1,0:T(8,128)(2,1)}, bf16[384,512]{1,0:T(8,128)(2,1)S(1)}, u32[]{:S(2)}, u32[]{:S(2)}) collective-permute-start(bf16[384,512]{1,0:T(8,128)(2,1)} %get-tuple-element.867), channel_id=1, source_target_pairs={{0,8},{8,16},{16,24},{24,28},{28,20},{20,12},{12,4},{4,0},{1,9},{9... | collective-permute-start | bytes 1179656 | tf_op jit(solution)/shard_map/ppermute | solution.py:1233
  398.6 17.8 %collective-permute-start.43 = (bf16[384,512]{1,0:T(8,128)(2,1)}, bf16[384,512]{1,0:T(8,128)(2,1)}, u32[]{:S(2)}, u32[]{:S(2)}) collective-permute-start(bf16[384,512]{1,0:T(8,128)(2,1)} %get-tuple-element.868), channel_id=1, source_target_pairs={{8,0},{16,8},{24,16},{28,24},{20,28},{12,20},{4,12},{0,4},{9,1},{1... | collective-permute-start | bytes 1179656 | tf_op jit(solution)/shard_map/ppermute | solution.py:1236
  399.3 21.0 %collective-permute-start.44 = (bf16[512,512]{1,0:T(8,128)(2,1)}, bf16[512,512]{1,0:T(8,128)(2,1)}, u32[]{:S(2)}, u32[]{:S(2)}) collective-permute-start(bf16[512,512]{1,0:T(8,128)(2,1)} %get-tuple-element.869), channel_id=1, source_target_pairs={{0,8},{8,16},{16,24},{24,28},{28,20},{20,12},{12,4},{4,0},{1,9},{9... | collective-permute-start | bytes 1572872 | tf_op jit(solution)/shard_map/ppermute | solution.py:1233
  400.6 20.7 %collective-permute-start.45 = (bf16[512,512]{1,0:T(8,128)(2,1)}, bf16[512,512]{1,0:T(8,128)(2,1)}, u32[]{:S(2)}, u32[]{:S(2)}) collective-permute-start(bf16[512,512]{1,0:T(8,128)(2,1)} %get-tuple-element.870), channel_id=1, source_target_pairs={{8,0},{16,8},{24,16},{28,24},{20,28},{12,20},{4,12},{0,4},{9,1},{1... | collective-permute-start | bytes 1572872 | tf_op jit(solution)/shard_map/ppermute | solution.py:1236
  427.3 21.5 %collective-permute-start.47 = (bf16[512,512]{1,0:T(8,128)(2,1)}, bf16[512,512]{1,0:T(8,128)(2,1)S(1)}, u32[]{:S(2)}, u32[]{:S(2)}) collective-permute-start(bf16[512,512]{1,0:T(8,128)(2,1)} %get-tuple-element.892), channel_id=1, source_target_pairs={{0,8},{8,16},{16,24},{24,28},{28,20},{20,12},{12,4},{4,0},{1,9},{9... | collective-permute-start | bytes 1572872 | tf_op jit(solution)/shard_map/ppermute | solution.py:1233
  428.3 21.3 %collective-permute-start.48 = (bf16[512,512]{1,0:T(8,128)(2,1)}, bf16[512,512]{1,0:T(8,128)(2,1)S(1)}, u32[]{:S(2)}, u32[]{:S(2)}) collective-permute-start(bf16[512,512]{1,0:T(8,128)(2,1)} %get-tuple-element.893), channel_id=1, source_target_pairs={{8,0},{16,8},{24,16},{28,24},{20,28},{12,20},{4,12},{0,4},{9,1},{1... | collective-permute-start | bytes 1572872 | tf_op jit(solution)/shard_map/ppermute | solution.py:1236
  429.3 20.3 %collective-permute-start.51 = (bf16[1,768,512]{2,1,0:T(8,128)(2,1)}, bf16[1,768,512]{2,1,0:T(8,128)(2,1)S(1)}, u32[]{:S(2)}, u32[]{:S(2)}) collective-permute-start(bf16[1,768,512]{2,1,0:T(8,128)(2,1)} %get-tuple-element.896), channel_id=1, source_target_pairs={{0,2},{2,0},{1,3},{3,1},{4,6},{6,4},{5,7},{7,5},{8,10},{10,8},{9,1... | collective-permute-start | bytes 2359304 | tf_op jit(solution)/shard_map/ppermute | solution.py:95
  453.0 34.6 %collective-permute-start.56 = (bf16[2,768,512]{2,1,0:T(8,128)(2,1)S(1)}, bf16[2,768,512]{2,1,0:T(8,128)(2,1)}, u32[]{:S(2)}, u32[]{:S(2)}) collective-permute-start(bf16[2,768,512]{2,1,0:T(8,128)(2,1)S(1)} %copy-done.31), channel_id=1, source_target_pairs={{0,2},{2,0},{1,3},{3,1},{4,6},{6,4},{5,7},{7,5},{8,10},{10,8},{9,1... | collective-permute-start | bytes 4718600 | tf_op jit(solution)/shard_map/ppermute | solution.py:95
  454.4 32.5 %collective-permute-start.54 = (bf16[928,512]{1,0:T(8,128)(2,1)S(1)}, bf16[928,512]{1,0:T(8,128)(2,1)S(1)}, u32[]{:S(2)}, u32[]{:S(2)}) collective-permute-start(bf16[928,512]{1,0:T(8,128)(2,1)S(1)} %pad_maximum_fusion.4), channel_id=1, source_target_pairs={{0,8},{8,16},{16,24},{24,28},{28,20},{20,12},{12,4},{4,0},{1,9},{9... | collective-permute-start | bytes 2850824 | tf_op jit(solution)/shard_map/ppermute | solution.py:1233
  455.1 31.8 %collective-permute-start.55 = (bf16[928,512]{1,0:T(8,128)(2,1)S(1)}, bf16[928,512]{1,0:T(8,128)(2,1)S(1)}, u32[]{:S(2)}, u32[]{:S(2)}) collective-permute-start(bf16[928,512]{1,0:T(8,128)(2,1)S(1)} %pad_maximum_fusion.5), channel_id=1, source_target_pairs={{8,0},{16,8},{24,16},{28,24},{20,28},{12,20},{4,12},{0,4},{9,1},{1... | collective-permute-start | bytes 2850824 | tf_op jit(solution)/shard_map/ppermute | solution.py:1236
  456.5 30.0 %collective-permute-start.52 = (bf16[512,512]{1,0:T(8,128)(2,1)S(1)}, bf16[512,512]{1,0:T(8,128)(2,1)S(1)}, u32[]{:S(2)}, u32[]{:S(2)}) collective-permute-start(bf16[512,512]{1,0:T(8,128)(2,1)S(1)} %get-tuple-element.903), channel_id=1, source_target_pairs={{0,8},{8,16},{16,24},{24,28},{28,20},{20,12},{12,4},{4,0},{1,9},{9... | collective-permute-start | bytes 1572872 | tf_op jit(solution)/shard_map/ppermute | solution.py:1233
  457.1 29.8 %collective-permute-start.53 = (bf16[512,512]{1,0:T(8,128)(2,1)S(1)}, bf16[512,512]{1,0:T(8,128)(2,1)S(1)}, u32[]{:S(2)}, u32[]{:S(2)}) collective-permute-start(bf16[512,512]{1,0:T(8,128)(2,1)S(1)} %get-tuple-element.904), channel_id=1, source_target_pairs={{8,0},{16,8},{24,16},{28,24},{20,28},{12,20},{4,12},{0,4},{9,1},{1... | collective-permute-start | bytes 1572872 | tf_op jit(solution)/shard_map/ppermute | solution.py:1236
  491.3 21.0 %collective-permute-start.57 = (bf16[928,512]{1,0:T(8,128)(2,1)S(1)}, bf16[928,512]{1,0:T(8,128)(2,1)S(1)}, u32[]{:S(2)}, u32[]{:S(2)}) collective-permute-start(bf16[928,512]{1,0:T(8,128)(2,1)S(1)} %get-tuple-element.916), channel_id=1, source_target_pairs={{0,8},{8,16},{16,24},{24,28},{28,20},{20,12},{12,4},{4,0},{1,9},{9... | collective-permute-start | bytes 2850824 | tf_op jit(solution)/shard_map/ppermute | solution.py:1233
  492.2 20.2 %collective-permute-start.58 = (bf16[928,512]{1,0:T(8,128)(2,1)S(1)}, bf16[928,512]{1,0:T(8,128)(2,1)S(1)}, u32[]{:S(2)}, u32[]{:S(2)}) collective-permute-start(bf16[928,512]{1,0:T(8,128)(2,1)S(1)} %get-tuple-element.917), channel_id=1, source_target_pairs={{8,0},{16,8},{24,16},{28,24},{20,28},{12,20},{4,12},{0,4},{9,1},{1... | collective-permute-start | bytes 2850824 | tf_op jit(solution)/shard_map/ppermute | solution.py:1236
  493.4 18.9 %collective-permute-start.60 = (bf16[512,512]{1,0:T(8,128)(2,1)S(1)}, bf16[512,512]{1,0:T(8,128)(2,1)S(1)}, u32[]{:S(2)}, u32[]{:S(2)}) collective-permute-start(bf16[512,512]{1,0:T(8,128)(2,1)S(1)} %fusion.14), channel_id=1, source_target_pairs={{0,2},{2,0},{1,3},{3,1},{4,6},{6,4},{5,7},{7,5},{8,10},{10,8},{9,1... | collective-permute-start | bytes 1572872 | tf_op jit(solution)/shard_map/ppermute | solution.py:95
  494.8 17.5 %collective-permute-start.61 = (bf16[512,512]{1,0:T(8,128)(2,1)S(1)}, bf16[512,512]{1,0:T(8,128)(2,1)S(1)}, u32[]{:S(2)}, u32[]{:S(2)}) collective-permute-start(bf16[512,512]{1,0:T(8,128)(2,1)S(1)} %fusion.14), channel_id=1, source_target_pairs={{0,1},{1,0},{2,3},{3,2},{4,5},{5,4},{6,7},{7,6},{8,9},{9,8},{10,11... | collective-permute-start | bytes 1572872 | tf_op jit(solution)/shard_map/ppermute | solution.py:91
  494.8 17.5 %collective-permute-start.59 = (bf16[384,512]{1,0:T(8,128)(2,1)S(1)}, bf16[384,512]{1,0:T(8,128)(2,1)S(1)}, u32[]{:S(2)}, u32[]{:S(2)}) collective-permute-start(bf16[384,512]{1,0:T(8,128)(2,1)S(1)} %fusion.22), channel_id=1, source_target_pairs={{0,2},{2,0},{1,3},{3,1},{4,6},{6,4},{5,7},{7,5},{8,10},{10,8},{9,1... | collective-permute-start | bytes 1179656 | tf_op jit(solution)/shard_map/ppermute | solution.py:95
  516.1 18.9 %collective-permute-start.62 = (bf16[928,512]{1,0:T(8,128)(2,1)}, bf16[928,512]{1,0:T(8,128)(2,1)S(1)}, u32[]{:S(2)}, u32[]{:S(2)}) collective-permute-start(bf16[928,512]{1,0:T(8,128)(2,1)} %get-tuple-element.925), channel_id=1, source_target_pairs={{0,8},{8,16},{16,24},{24,28},{28,20},{20,12},{12,4},{4,0},{1,9},{9... | collective-permute-start | bytes 2850824 | tf_op jit(solution)/shard_map/ppermute | solution.py:1233
  516.9 19.0 %collective-permute-start.63 = (bf16[928,512]{1,0:T(8,128)(2,1)}, bf16[928,512]{1,0:T(8,128)(2,1)}, u32[]{:S(2)}, u32[]{:S(2)}) collective-permute-start(bf16[928,512]{1,0:T(8,128)(2,1)} %get-tuple-element.926), channel_id=1, source_target_pairs={{8,0},{16,8},{24,16},{28,24},{20,28},{12,20},{4,12},{0,4},{9,1},{1... | collective-permute-start | bytes 2850824 | tf_op jit(solution)/shard_map/ppermute | solution.py:1236
  544.2 17.6 %collective-permute-start.66 = (bf16[928,512]{1,0:T(8,128)(2,1)S(1)}, bf16[928,512]{1,0:T(8,128)(2,1)S(1)}, u32[]{:S(2)}, u32[]{:S(2)}) collective-permute-start(bf16[928,512]{1,0:T(8,128)(2,1)S(1)} %fusion.12.mine), channel_id=1, source_target_pairs={{0,2},{2,0},{1,3},{3,1},{4,6},{6,4},{5,7},{7,5},{8,10},{10,8},{9,1... | collective-permute-start | bytes 2850824 | tf_op jit(solution)/shard_map/ppermute | solution.py:95
  (58 other events, 515.6 us)
